TPU v7x, 128 devices: a whole 4x4x4 slice. The times are simulated.
128 devices in a mesh: phase: 2 (over core), ctx: 32 (over y, x, z_hi), fsdp: 2 (over z_lo).
Axes of the slice: x: 4, y: 4, z: 4 (z_hi: 2, z_lo: 2; z = z_hi * 2 + z_lo), core: 2. Of those that a mesh axis runs over, the one named last changes fastest.
Arguments:
- layer_in: bfloat16 [2, 4096, 960], P('fsdp', 'ctx'), may hold values from -6 to 6
- out_grad: float32 [2, 4096, 960], P('fsdp', 'ctx'), may hold values from -6 to 6
- segment_ids: int32 [2, 4096], P('fsdp'), may hold values from 0 to 3, never falling along the last dimension, each value on 1 to 2048 neighbouring positions
- block_pair: int32 [32], replicated, may hold values from 0 to 31, each once
- params: bfloat16 [2, 9830400], P('phase', ('ctx', 'fsdp')), may hold values from -2 to 2
- norm_gains: bfloat16 [2, 1920], P('phase', ('ctx', 'fsdp')), may hold values from 0.099609375 to 1.8984375
Outputs:
- phase_out: bfloat16 [2, 2, 4096, 960], P('phase', 'fsdp', 'ctx')
- phase_grad: float32 [2, 2, 4096, 960], P('phase', 'fsdp', 'ctx')
- param_grad: float32 [2, 9830400], P('phase', ('ctx', 'fsdp'))
- gain_grad: float32 [2, 1920], P('phase', ('ctx', 'fsdp'))
Inputs may be any that keep to these rules, and one draw needn't show every extreme that they name: segment_ids[s] never falls along a sequence; each id covers 1 to half of 4096 positions, and one covers exactly half of 4096. `block_pair`: each value once.
All inputs are finite; a program needn't handle non-finite values.
Results may differ from a plain program's by a relative error of at most 0.03.
Values may be sent and summed in bfloat16 or wider, within the bound.
No kernel may reach another device: no remote copies, remote signals or barrier semaphores. Data moves between devices by JAX's collectives and lax.ppermute only.
A program may use at most 256 MiB of HBM per device.

v0:
```python
import math

import jax
import jax.numpy as jnp
from jax import lax
from jax.sharding import PartitionSpec as P

H = 15
KVH = 5
HD = 64
D = 960
FF = 2560


eps = 1e-05
rope_theta = 100000.0
masked_fill = -1e30


def passed_along(block, axis, distance):
    devices = range(lax.axis_size(axis))
    route = [(i - distance, i) for i in devices if i - distance in devices]
    return lax.ppermute(block, axis, route)


def norm_scale(values):
    return lax.rsqrt(jnp.mean(values * values, axis=-1, keepdims=True) + eps)


def norm_back(d_out, values, scales, gain_vec):
    scaled = d_out * gain_vec
    d_gain = jnp.sum(d_out * values * scales, axis=0)
    d_values = scales * scaled - values * (scales * scales * scales) * jnp.mean(
        scaled * values, axis=-1, keepdims=True
    )
    return (d_values, d_gain)


def rotate(values, offsets, head_count, inverse):
    row_count = values.shape[0]
    shaped = values.reshape(row_count, head_count, HD)
    half_dim = HD // 2
    frequency = rope_theta ** (-2.0 * jnp.arange(half_dim, dtype=jnp.float32) / HD)
    angles = offsets.astype(jnp.float32)[:, None] * frequency[None, :]
    cosine = jnp.cos(angles)[:, None, :]
    sine = jnp.sin(angles)[:, None, :]
    left = shaped[..., :half_dim]
    right = shaped[..., half_dim:]
    if inverse:
        merged = jnp.concatenate(
            [left * cosine + right * sine, right * cosine - left * sine], axis=-1
        )
    else:
        merged = jnp.concatenate(
            [left * cosine - right * sine, right * cosine + left * sine], axis=-1
        )
    return merged.reshape(row_count, head_count * HD)


def unpack(flat_row, gain_row):
    query_width = H * HD
    qkv_width = (H + 2 * KVH) * HD
    cut_one = D * qkv_width
    cut_two = cut_one + query_width * D
    cut_three = cut_two + D * 2 * FF
    cut_four = cut_three + FF * D
    return (
        flat_row[:cut_one].reshape(D, qkv_width),
        flat_row[cut_one:cut_two].reshape(query_width, D),
        flat_row[cut_two:cut_three].reshape(D, 2 * FF),
        flat_row[cut_three:cut_four].reshape(FF, D),
        gain_row[:D].astype(jnp.float32),
        gain_row[D:].astype(jnp.float32),
    )


def layout(seg_row, block_pair, block_len):
    pair_count = block_pair.shape[0]
    seq_len = seg_row.shape[0]
    blocks_dealt = jnp.stack([block_pair, 2 * pair_count - 1 - block_pair], axis=1).reshape(-1)
    within = jnp.arange(block_len, dtype=jnp.int32)
    places = (blocks_dealt[:, None] * block_len + within[None, :]).reshape(-1)
    cell_ids = jnp.arange(seq_len, dtype=jnp.int32)
    begins = jnp.concatenate([jnp.ones((1,), dtype=jnp.bool_), seg_row[1:] != seg_row[:-1]])
    starts = lax.cummax(jnp.where(begins, cell_ids, jnp.zeros_like(cell_ids)), axis=0)
    offsets = cell_ids - starts
    dealt_seg = seg_row.reshape(2 * pair_count, block_len)[blocks_dealt].reshape(-1)
    dealt_off = offsets.reshape(2 * pair_count, block_len)[blocks_dealt].reshape(-1)
    return (places, dealt_seg, dealt_off)


def key_fold(query_g, query_meta, meta, state_in, key_piece):
    run_peak, run_total, run_acc = state_in
    count = key_piece.shape[0]
    key_width = KVH * HD
    keys = key_piece[:, :key_width].reshape(count, KVH, HD)
    vals = key_piece[:, key_width:].reshape(count, KVH, HD).astype(jnp.float32)
    key_place = meta[0]
    key_seg = meta[1]
    allowed = (key_place[None, :] <= query_meta[0][:, None]) & (
        key_seg[None, :] == query_meta[1][:, None]
    )
    scores = jnp.einsum("rkgd,nkd->kgrn", query_g, keys, preferred_element_type=jnp.float32) * (
        1.0 / math.sqrt(HD)
    )
    scores = jnp.where(allowed, scores, masked_fill)
    new_peak = jnp.maximum(run_peak, jnp.max(scores, axis=-1))
    weights_now = jnp.where(allowed, jnp.exp(scores - new_peak[..., None]), 0.0)
    run_total = jnp.sum(weights_now, axis=-1)
    update = jnp.einsum(
        "kgrn,nkd->kgrd",
        weights_now,
        vals,
        precision=lax.Precision.HIGHEST,
        preferred_element_type=jnp.float32,
    )
    run_acc = update
    return (new_peak, run_total, run_acc)


def layer_forward(entering, weights, meta, query_meta):
    w_qkv, w_out, w_gu, w_down, gain_one, gain_two = weights
    row_count = entering.shape[0]
    query_width = H * HD
    key_width = KVH * HD
    group_size = H // KVH
    resid = entering.astype(jnp.float32)
    scale_one = norm_scale(resid)
    normed = (resid * scale_one * gain_one).astype(jnp.bfloat16)
    proj = jnp.dot(normed, w_qkv, preferred_element_type=jnp.float32)
    query = rotate(proj[:, :query_width], query_meta[2], H, False).astype(jnp.bfloat16)
    keys = rotate(proj[:, query_width : query_width + key_width], query_meta[2], KVH, False)
    kv_local = jnp.concatenate([keys, proj[:, query_width + key_width :]], axis=1).astype(
        jnp.bfloat16
    )
    query_g = query.reshape(row_count, KVH, group_size, HD)
    initial = (
        jnp.full((KVH, group_size, row_count), masked_fill, jnp.float32),
        jnp.zeros((KVH, group_size, row_count), jnp.float32),
        jnp.zeros((KVH, group_size, row_count, HD), jnp.float32),
    )
    peak, totals, accum = key_fold(
        query_g, query_meta, meta, initial, lax.all_gather(kv_local, "ctx", axis=0, tiled=True)
    )
    lse = peak + jnp.log(totals)
    mixed = (
        jnp.transpose(accum / totals[..., None], (2, 0, 1, 3))
        .reshape(row_count, query_width)
        .astype(jnp.bfloat16)
    )
    hidden = resid + jnp.dot(mixed, w_out, preferred_element_type=jnp.float32)
    scale_two = norm_scale(hidden)
    normed_two = (hidden * scale_two * gain_two).astype(jnp.bfloat16)
    gate_up = jnp.dot(normed_two, w_gu, preferred_element_type=jnp.float32)
    gate = gate_up[:, :FF]
    up_proj = gate_up[:, FF:]
    inner = (gate * jax.nn.sigmoid(gate) * up_proj).astype(jnp.bfloat16)
    result = hidden + jnp.dot(inner, w_down, preferred_element_type=jnp.float32)
    saved = (
        resid,
        scale_one,
        normed,
        query,
        kv_local,
        mixed,
        lse,
        hidden,
        scale_two,
        normed_two,
        gate,
        up_proj,
        inner,
        meta,
        query_meta,
        kv_local,
    )
    return (result.astype(jnp.bfloat16), saved)


def attention_back(query, mixed, lse, d_mixed, whole, query_meta, meta):
    row_count = query.shape[0]
    group_size = H // KVH
    key_width = KVH * HD
    score_scale = 1.0 / math.sqrt(HD)
    total_rows = whole.shape[0]
    block_rows = min(512, total_rows)
    query_g = query.reshape(row_count, KVH, group_size, HD)
    delta = jnp.transpose(
        jnp.sum(
            (d_mixed * mixed.astype(jnp.float32)).reshape(row_count, KVH, group_size, HD), axis=-1
        ),
        (1, 2, 0),
    )
    d_mix_g = d_mixed.astype(jnp.bfloat16).reshape(row_count, KVH, group_size, HD)

    def step(d_query, block_index):
        first_row = block_index * block_rows
        key_piece = lax.dynamic_slice_in_dim(whole, first_row, block_rows)
        keys = key_piece[:, :key_width].reshape(block_rows, KVH, HD)
        vals = key_piece[:, key_width:].reshape(block_rows, KVH, HD)
        key_place = lax.dynamic_slice_in_dim(meta[0], first_row, block_rows)
        key_seg = lax.dynamic_slice_in_dim(meta[1], first_row, block_rows)
        allowed = (key_place[None, :] <= query_meta[0][:, None]) & (
            key_seg[None, :] == query_meta[1][:, None]
        )
        scores = (
            jnp.einsum("rkgd,nkd->kgrn", query_g, keys, preferred_element_type=jnp.float32)
            * score_scale
        )
        probs = jnp.exp(jnp.where(allowed, scores, masked_fill) - lse[..., None])
        d_vals = jnp.einsum(
            "kgrn,rkgd->nkd",
            probs.astype(jnp.bfloat16),
            d_mix_g,
            preferred_element_type=jnp.float32,
        )
        d_probs = jnp.einsum("rkgd,nkd->kgrn", d_mix_g, vals, preferred_element_type=jnp.float32)
        d_scores = (probs * (d_probs - delta[..., None]) * score_scale).astype(jnp.bfloat16)
        d_query = d_query + jnp.einsum(
            "kgrn,nkd->rkgd", d_scores, keys, preferred_element_type=jnp.float32
        )
        d_keys = jnp.einsum("kgrn,rkgd->nkd", d_scores, query_g, preferred_element_type=jnp.float32)
        return (
            d_query,
            jnp.concatenate(
                [d_keys.reshape(block_rows, key_width), d_vals.reshape(block_rows, key_width)],
                axis=1,
            ),
        )

    d_query, d_pieces = lax.scan(
        step,
        jnp.zeros((row_count, KVH, group_size, HD), jnp.float32),
        jnp.arange(total_rows // block_rows, dtype=jnp.int32),
    )
    return (d_query.reshape(row_count, H * HD), d_pieces.reshape(total_rows, 2 * key_width))


def no_hook(d_wgu, d_down):
    return None


def layer_backward(cotangent, saved, weights, tail_hook):
    w_qkv, w_out, w_gu, w_down, gain_one, gain_two = weights
    (
        resid,
        scale_one,
        normed,
        query,
        kv_local,
        mixed,
        lse,
        hidden,
        scale_two,
        normed_two,
        gate,
        up_proj,
        inner,
        meta,
        query_meta,
        whole,
    ) = saved
    key_width = KVH * HD
    cot_b = cotangent.astype(jnp.bfloat16)
    d_down = jnp.dot(inner.T, cot_b, preferred_element_type=jnp.float32)
    d_inner = jnp.dot(cot_b, w_down.T, preferred_element_type=jnp.float32)
    sigma = jax.nn.sigmoid(gate)
    d_gate = d_inner * up_proj * sigma * (1.0 + gate * (1.0 - sigma))
    d_up = d_inner * gate * sigma
    d_gu = jnp.concatenate([d_gate, d_up], axis=1).astype(jnp.bfloat16)
    d_wgu = jnp.dot(normed_two.T, d_gu, preferred_element_type=jnp.float32)
    tail_part = tail_hook(d_wgu, d_down)
    d_norm_two = jnp.dot(d_gu, w_gu.T, preferred_element_type=jnp.float32)
    d_hidden, d_gain_two = norm_back(d_norm_two, hidden, scale_two, gain_two)
    d_hidden = cotangent + d_hidden
    d_hidden_b = d_hidden.astype(jnp.bfloat16)
    d_wout = jnp.dot(mixed.T, d_hidden_b, preferred_element_type=jnp.float32)
    d_mixed = jnp.dot(d_hidden_b, w_out.T, preferred_element_type=jnp.float32)
    keys_all = lax.all_gather(kv_local, "ctx", axis=0, tiled=True)
    d_query, d_kv_all = attention_back(query, mixed, lse, d_mixed, keys_all, query_meta, meta)
    d_kv = lax.psum_scatter(
        d_kv_all.astype(jnp.bfloat16), "ctx", scatter_dimension=0, tiled=True
    ).astype(jnp.float32)
    d_query = rotate(d_query, query_meta[2], H, True)
    d_keys = rotate(d_kv[:, :key_width], query_meta[2], KVH, True)
    d_proj = jnp.concatenate([d_query, d_keys, d_kv[:, key_width:]], axis=1).astype(jnp.bfloat16)
    d_wqkv = jnp.dot(normed.T, d_proj, preferred_element_type=jnp.float32)
    d_normed = jnp.dot(d_proj, w_qkv.T, preferred_element_type=jnp.float32)
    d_resid, d_gain_one = norm_back(d_normed, resid, scale_one, gain_one)
    return (d_hidden + d_resid, (d_wqkv, d_wout, d_wgu, d_down, d_gain_one, d_gain_two), tail_part)


def per_device(layer_in, out_grad, segment_ids, block_pair, params, norm_gains):
    phase_rank = lax.axis_index("phase")
    ctx_rank = lax.axis_index("ctx")
    micro_count, row_count, model_width = layer_in.shape
    block_len = row_count // 2
    gathered = (
        lax.all_gather(params, ("ctx", "fsdp"), axis=1, tiled=True),
        lax.all_gather(norm_gains, ("ctx", "fsdp"), axis=1, tiled=True),
    )
    weights = unpack(gathered[0][0], gathered[1][0])

    def tick_meta(micro_index):
        seg_row = lax.dynamic_index_in_dim(segment_ids, micro_index, 0, keepdims=False)
        meta = layout(seg_row, block_pair, block_len)
        query_meta = tuple(
            (lax.dynamic_slice_in_dim(member, ctx_rank * row_count, row_count) for member in meta)
        )
        return (meta, query_meta)

    received = jnp.zeros((row_count, model_width), jnp.bfloat16)
    results = []
    kept_list = []
    for tick_index in range(micro_count + 1):
        micro_index = jnp.clip(tick_index - phase_rank, 0, micro_count - 1)
        meta, query_meta = tick_meta(micro_index)
        own_input = layer_in[min(tick_index, micro_count - 1)]
        entering = jnp.where(phase_rank == 0, own_input, received)
        result, saved = layer_forward(entering, weights, meta, query_meta)
        results.append(result)
        kept_list.append(saved)
        if tick_index < micro_count:
            received = passed_along(result, "phase", 1)
    outputs = jnp.stack([jnp.where(phase_rank == 0, results[0], results[1])])
    regathered = (
        lax.all_gather(params, ("ctx", "fsdp"), axis=1, tiled=True),
        lax.all_gather(norm_gains, ("ctx", "fsdp"), axis=1, tiled=True),
    )
    weights = unpack(regathered[0][0], regathered[1][0])
    back_in = jnp.zeros((row_count, model_width), jnp.float32)
    grads_sum = None
    grads_list = []
    for back_tick in range(micro_count + 1):
        valid = jnp.where(phase_rank == 1, float(back_tick < micro_count), float(back_tick >= 1))
        given = out_grad[max(micro_count - 1 - back_tick, 0)]
        cotangent = jnp.where(phase_rank == 1, given, back_in) * valid
        tail_hook = no_hook
        if back_tick == micro_count:
            tail_hook = no_hook
        grad_input, parts, tail_part = layer_backward(
            cotangent, kept_list[micro_count - back_tick], weights, tail_hook
        )
        grads_list.append(grad_input)
        grads_sum = parts if grads_sum is None else jax.tree.map(jnp.add, grads_sum, parts)
        if back_tick < micro_count:
            back_in = passed_along(grad_input.astype(jnp.bfloat16), "phase", -1).astype(
                grad_input.dtype
            )
    input_grads = jnp.stack(
        [jnp.where(phase_rank == 1, grads_list[micro_count - 1], grads_list[micro_count])]
    )
    gains_grad = jnp.concatenate([grads_sum[4], grads_sum[5]])[None]
    flat_grad = jnp.concatenate([member.reshape(-1) for member in grads_sum[:4]])[None]
    param_part, gain_part = (
        lax.psum_scatter(flat_grad, ("ctx", "fsdp"), scatter_dimension=1, tiled=True),
        lax.psum_scatter(gains_grad, ("ctx", "fsdp"), scatter_dimension=1, tiled=True),
    )
    return (outputs[None], input_grads[None], param_part, gain_part)


def solution(mesh):
    return jax.shard_map(
        per_device,
        mesh=mesh,
        in_specs=(
            P("fsdp", "ctx", None),
            P("fsdp", "ctx", None),
            P("fsdp", None),
            P(),
            P("phase", ("ctx", "fsdp")),
            P("phase", ("ctx", "fsdp")),
        ),
        out_specs=(
            P("phase", "fsdp", "ctx", None),
            P("phase", "fsdp", "ctx", None),
            P("phase", ("ctx", "fsdp")),
            P("phase", ("ctx", "fsdp")),
        ),
        check_vma=False,
    )
```

profile of v0, /device:TPU:0, one launch (start us, length us, event | category | flops | bytes accessed | tf_op | source)
XLA Modules:
  0.0 1941.0 jit_solution(7361246854671286231)
XLA Ops:
  12.2 183.3 %all-reduce = bf16[1920]{0:T(1024)(128)(2,1)S(1)} all-reduce(bf16[1920]{0:T(1024)(128)(2,1)S(1)} %dynamic-update-slice), channel_id=1, replica_groups=mesh['phase'=2,'ctx'=32,'fsdp'=2] {'ctx','fsdp'}, use_global_device_ids=true, to_apply=%add | all-reduce | flops 1920 | bytes 7680
  200.2 54.0 %slice_reduce_fusion.2 = bf16[1536000]{0:T(1024)(128)(2,1)} fusion(bf16[1,9830400]{1,0:T(2,128)(2,1)} %all-gather.4.cloned.1.call-done), kind=kLoop, calls=%fused_computation.63 | loop fusion | bytes 6144000 | tf_op jit(solution)/shard_map/slice | solution.py:68
  254.1 4.9 reshape.466
  270.8 33.0 %slice_reduce_fusion.3 = bf16[921600]{0:T(1024)(128)(2,1)} fusion(bf16[1,9830400]{1,0:T(2,128)(2,1)} %all-gather.4.cloned.1.call-done), kind=kLoop, calls=%fused_computation.65 | loop fusion | bytes 3686400 | tf_op jit(solution)/shard_map/slice | solution.py:69
  303.8 3.3 reshape.476
  307.2 196.0 %slice_reduce_fusion = bf16[4915200]{0:T(1024)(128)(2,1)} fusion(bf16[1,9830400]{1,0:T(2,128)(2,1)} %all-gather.4.cloned.1.call-done), kind=kLoop, calls=%fused_computation.49 | loop fusion | bytes 19660800 | tf_op jit(solution)/shard_map/slice | solution.py:70
  503.1 14.9 reshape.477
  518.1 99.5 %slice_reduce_fusion.1 = bf16[2457600]{0:T(1024)(128)(2,1)} fusion(bf16[1,9830400]{1,0:T(2,128)(2,1)} %all-gather.4.cloned.1.call-done), kind=kLoop, calls=%fused_computation.61 | loop fusion | bytes 9830400 | tf_op jit(solution)/shard_map/slice | solution.py:71
  617.6 9.6 reshape.478
  627.3 4.6 fusion.137
  631.9 12.6 fusion.24
  644.5 14.1 fusion.26
  658.6 22.0 %fusion.47 = bf16[128,5,3,64]{0,3,2,1:T(8,128)(2,1)S(1)} fusion(bf16[4096,5,64,1]{0,2,3,1:T(8,128)(2,1)} %bitcast.411, f32[5,4096,128,3]{2,1,3,0:T(8,128)} %get-tuple-element.344, f32[5,3,128]{2,1,0:T(4,128)S(1)} %broadcast_maximum_fusion.1, pred[128,4096]{0,1:T(8,128)(4,1)S(1)} %compare_and_fusion.2, f32[128,5,3]{0,2,1:T(4,128)S(1)} %bitcast.449), kind=kOutput, calls=%fused_computation.99 | convolution fusion | flops 6071500800 | bytes 34864128 | tf_op jit(solution)/shard_map/kgrn,nkd->kgrd/dot_general | solution.py:110
  682.1 5.5 fusion.131
  699.1 103.8 %all-gather.8.cloned.1.call-done = bf16[4096,640]{0,1:T(8,128)(2,1)} async-done(((bf16[128,640]{0,1:T(8,128)(2,1)}), bf16[4096,640]{0,1:T(8,128)(2,1)}) %all-gather.8.cloned.1.call-update) | async-done | bytes 5242896 | tf_op jit(solution)/shard_map/all_gather | solution.py:143
  802.8 4.6 fusion.136
  807.4 12.8 fusion.25
  820.2 14.0 fusion.28
  834.8 22.1 %fusion.49 = bf16[128,5,3,64]{0,3,2,1:T(8,128)(2,1)S(1)} fusion(bf16[4096,5,64,1]{0,2,3,1:T(8,128)(2,1)} %bitcast.410, f32[5,4096,128,3]{2,1,3,0:T(8,128)} %get-tuple-element.348, f32[5,3,128]{2,1,0:T(4,128)S(1)} %broadcast_maximum_fusion, pred[128,4096]{0,1:T(8,128)(4,1)S(1)} %compare_and_fusion.2, f32[128,5,3]{0,2,1:T(4,128)S(1)} %bitcast.450), kind=kOutput, calls=%fused_computation.101 | convolution fusion | flops 6071500800 | bytes 34864128 | tf_op jit(solution)/shard_map/kgrn,nkd->kgrd/dot_general | solution.py:110
  858.0 5.7 fusion.132
  863.7 5.7 multiply_convert_fusion.3
  869.4 3.4 multiply_reduce_fusion.1
  876.3 2.8 broadcast.303.clone2
  879.1 112.5 %while.26 = (s32[]{:T(128)}, f32[128,5,3,64]{0,3,2,1:T(8,128)}, bf16[8,512,640]{2,1,0:T(8,128)(2,1)}, s32[8]{0:T(128)}, bf16[4096,640]{0,1:T(8,128)(2,1)}, /*ind...) while((s32[]{:T(128)}, f32[128,5,3,64]{0,3,2,1:T(8,128)}, ...), condition=%wide.region_13.14_spmd.clone, body=%wide.region_12.13_spmd.clone.sunk | while | flops 641712128 | bytes 26775312 | solution.py:231
  994.2 191.8 %reduce-scatter.9.cloned.1.call-done = bf16[128,640]{1,0:T(8,128)(2,1)} async-done(((bf16[4096,640]{1,0:T(8,128)(2,1)}), bf16[128,640]{1,0:T(8,128)(2,1)}) %reduce-scatter.9.cloned.1.call-update) | async-done | bytes 163856
  1187.5 3.7 fusion.72
  1196.4 5.4 multiply_convert_fusion.1
  1201.9 7.7 multiply_reduce_fusion
  1211.3 2.9 broadcast.303.clone
  1214.1 109.6 %while.27 = (s32[]{:T(128)}, f32[128,5,3,64]{0,3,2,1:T(8,128)}, bf16[8,512,640]{2,1,0:T(8,128)(2,1)}, s32[8]{0:T(128)S(1)}, bf16[4096,640]{0,1:T(8,128)(2,1)}, /...) while((s32[]{:T(128)}, f32[128,5,3,64]{0,3,2,1:T(8,128)}, ...), condition=%wide.region_19.20_spmd.clone, body=%wide.region_18.19_spmd.clone.sunk | while | flops 641712128 | bytes 26775312 | solution.py:231
  1325.5 5.1 fusion.77
  1330.7 8.4 fusion.51
  1339.2 3.7 fusion.99
  1342.9 2.6 convolution_add_fusion.2
  1345.5 5.6 reshape.497
  1351.1 9.0 convolution_add_fusion
  1360.0 11.2 copy.102
  1371.3 13.3 reshape.499
  1384.6 12.7 add_bitcast_fusion
  1397.3 18.5 copy.157
  1417.0 97.2 %reduce-scatter.11.cloned.1.call-done = bf16[128,640]{1,0:T(8,128)(2,1)} async-done(((bf16[4096,640]{1,0:T(8,128)(2,1)}), bf16[128,640]{1,0:T(8,128)(2,1)}) %reduce-scatter.11.cloned.1.call-update) | async-done | bytes 163856
  1515.6 6.5 convolution_add_fusion.1
  1522.2 8.2 reshape.496
  1530.4 35.0 %pad_maximum_fusion = f32[9830400]{0:T(1024)} fusion(f32[2457600]{0:T(1024)} %reshape.499, f32[4915200]{0:T(1024)} %bitcast.388, f32[921600]{0:T(1024)} %reshape.497, f32[1536000]{0:T(1024)} %reshape.496), kind=kLoop, calls=%fused_computation.38 | loop fusion | flops 29491200 | bytes 78643200 | tf_op jit(solution)/shard_map/concatenate | solution.py:354
  1567.1 6.4 fusion.45
  1576.1 180.0 %all-reduce.2 = f32[1,1920]{1,0:T(1,128)S(1)} all-reduce(f32[1,1920]{1,0:T(1,128)S(1)} %broadcast_in_dim.56), channel_id=5, replica_groups=mesh['phase'=2,'ctx'=32,'fsdp'=2] {'ctx','fsdp'}, use_global_device_ids=true, to_apply=%region_27.28.clone | all-reduce | flops 1920 | bytes 15360
  1757.3 2.7 fusion.58
  1760.0 171.9 %all-reduce.5.cloned.1.call-done = f32[1,9830400]{1,0:T(1,128)} async-done(((f32[1,9830400]{1,0:T(1,128)}), f32[1,9830400]{1,0:T(1,128)}) %all-reduce.5.cloned.1.call-update) | async-done | bytes 39321616
  (511 shorter events, 269.8 us)
Async XLA Ops:
  7.2 193.0 %all-gather.4.cloned.1.call-start = ((), (), s32[]{:S(2)}) async-start(), calls=%async_computation.2 | async-start | bytes 39936000 | tf_op jit(solution)/shard_map/all_gather | solution.py:299
  7.9 619.4 %all-gather.6.cloned.1.call-start = ((), (), s32[]{:S(2)}) async-start(), calls=%async_computation.3 | async-start | bytes 5406720 | tf_op jit(solution)/shard_map/all_gather | solution.py:143
  199.9 59.2 %copy-start.72 = (f32[128]{0:T(128)}, f32[128]{0:T(128)S(1)}, u32[]{:S(2)}) copy-start(f32[128]{0:T(128)S(1)} %get-tuple-element.336) | copy-start | bytes 1540
  200.1 61.5 %copy-start.36 = (f32[128,32]{0,1:T(8,128)}, f32[128,32]{0,1:T(8,128)S(1)}, u32[]{:S(2)}) copy-start(f32[128,32]{0,1:T(8,128)S(1)} %get-tuple-element.332) | copy-start | bytes 49156
  259.1 8.5 copy-start.2
  262.4 540.5 %all-gather.8.cloned.1.call-start = ((), (), s32[]{:S(2)}) async-start(), calls=%async_computation.4 | async-start | bytes 5406720 | tf_op jit(solution)/shard_map/all_gather | solution.py:143
  617.6 9.6 slice-start.5
  617.6 9.6 copy-start.37
  644.5 14.1 copy-start.62
  658.6 22.0 %copy-start.63 = (f32[5,3,128]{2,1,0:T(4,128)}, f32[5,3,128]{2,1,0:T(4,128)S(1)}, u32[]{:S(2)}) copy-start(f32[5,3,128]{2,1,0:T(4,128)S(1)} %fusion.26) | copy-start | bytes 23044
  680.6 9.0 slice-start.3
  681.5 8.0 copy-start.5
  691.3 2.4 collective-permute-start
  693.9 163.1 %copy-start.13 = (bf16[128,960]{0,1:T(8,128)(2,1)}, bf16[128,960]{0,1:T(8,128)(2,1)S(1)}, u32[]{:S(2)}) copy-start(bf16[128,960]{0,1:T(8,128)(2,1)S(1)} %get-tuple-element.289) | copy-start | bytes 737284
  697.8 488.2 %reduce-scatter.9.cloned.1.call-start = ((), (), s32[]{:S(2)}) async-start(), calls=%async_computation.5 | async-start | bytes 5406720
  857.0 16.0 copy-start.30
  857.9 14.9 copy-start.8
  857.9 14.9 copy-start.64
  857.9 11.4 slice-start
  857.9 11.4 slice-start.1
  991.6 195.8 %copy-start.14 = (bf16[128,960]{0,1:T(8,128)(2,1)S(1)}, bf16[128,960]{0,1:T(8,128)(2,1)}, u32[]{:S(2)}) copy-start(bf16[128,960]{0,1:T(8,128)(2,1)} %copy-done.13) | copy-start | bytes 737284
  991.6 195.8 %copy-start.70 = (f32[128]{0:T(128)S(1)}, f32[128]{0:T(128)}, u32[]{:S(2)}) copy-start(f32[128]{0:T(128)} %copy-done.69) | copy-start | bytes 1540
  991.7 522.5 %reduce-scatter.11.cloned.1.call-start = ((), (), s32[]{:S(2)}) async-start(), calls=%async_computation.6 | async-start | bytes 5406720
  1187.4 8.9 copy-start.18
  1192.7 3.6 collective-permute-start.1
  1201.9 7.7 copy-start.50
  1201.9 7.7 copy-start.52
  1201.9 7.7 copy-start.80
  1201.9 7.9 copy-start.33
  1323.7 608.1 %all-reduce.5.cloned.1.call-start = ((), (), s32[]{:S(2)}) async-start(), calls=%async_computation.7 | async-start | bytes 78643200
  1330.7 8.5 copy-start.15
  1330.7 8.5 copy-start.41
  1330.7 8.5 copy-start.55
  1330.7 8.5 copy-start.57
  1330.7 8.5 copy-start.71
  1371.2 13.3 copy-start.7
  1371.2 13.3 copy-start.51
  1371.3 13.3 copy-start.53
  1371.3 13.3 copy-start.68
  1397.3 18.5 copy-start.39
  1397.3 118.3 %copy-start.21 = (bf16[1,128,960]{1,2,0:T(8,128)(2,1)S(1)}, bf16[1,128,960]{1,2,0:T(8,128)(2,1)}, u32[]{:S(2)}) copy-start(bf16[1,128,960]{1,2,0:T(8,128)(2,1)} %param.10) | copy-start | bytes 737284
  1397.3 118.3 %copy-start.73 = (f32[128]{0:T(128)S(1)}, f32[128]{0:T(128)}, u32[]{:S(2)}) copy-start(f32[128]{0:T(128)} %copy-done.72) | copy-start | bytes 1540
  1417.0 105.2 %copy-start.42 = (bf16[128,15,64]{0,2,1:T(8,128)(2,1)}, bf16[128,15,64]{0,2,1:T(8,128)(2,1)S(1)}, u32[]{:S(2)}) copy-start(bf16[128,15,64]{0,2,1:T(8,128)(2,1)S(1)} %pad_maximum_fusion.12) | copy-start | bytes 737284
  1565.4 8.2 copy-start.74
  1565.4 8.1 copy-start.76
  1565.5 8.2 copy-start.4
  1565.5 8.2 copy-start.59
  1573.6 183.7 %copy-start.78 = (f32[128]{0:T(128)S(1)}, f32[128]{0:T(128)}, u32[]{:S(2)}) copy-start(f32[128]{0:T(128)} %get-tuple-element.339) | copy-start | bytes 1540
  (47 other events, 197.9 us)
Sparse Core Ops, SparseCore 0:
  10.8 185.3 all-gather.3
  262.5 104.3 all-gather.5
  697.9 104.8 all-gather.7
  991.8 194.1 reduce-scatter.8
  1323.9 190.2 reduce-scatter.10
  1565.6 366.2 all-reduce.4
where the time goes:
time: 1950 us; the launch traced here: 1940 us
  local copies, waits for them, and re-layouts  584 us (30%)
  waiting for transfers between devices  568 us (29%)
  blocking collectives  363 us (19%)
  matrix products  304 us (16%)
  other arithmetic  89.7 us (5%)
    unnamed x9, waiting for transfers between devices  462 us
    unnamed x2, blocking collectives  363 us
    slice x1, local copies, waits for them, and re-layouts, unpack(): flat_row[cut_two:cut_three].reshape(D, 2 * FF)  196 us
    all_gather x2, waiting for transfers between devices, layer_forward(): lax.all_gather(kv_local, 'ctx', axis=0, tiled=True)  104 us
    slice x1, local copies, waits for them, and re-layouts, unpack(): flat_row[cut_three:cut_four].reshape(FF, D)  99.5 us
    slice x1, local copies, waits for them, and re-layouts, unpack(): flat_row[:cut_one].reshape(D, qkv_width)  54 us
    dot_general x2, matrix products, key_fold(): jnp.einsum('kgrn,nkd->kgrd', weights_now, vals, precision=lax.Precision.H...  44.1 us
    dot_general x16, matrix products, step(): jnp.einsum('rkgd,nkd->kgrn', d_mix_g, vals, preferred_element_type=jnp.fl...  39.2 us
  transfers between devices with their start and end apart: 8, of which 6 were waited for; matrix products, arithmetic and copies ran while one was open for 25% of the time, Pallas kernels for 0%

commit v1 on v0

v1 whole, which is shorter than its diff:
```python
import functools

import jax
import jax.numpy as jnp
from jax import lax
from jax.experimental import pallas as pl
from jax.experimental.pallas import tpu as pltpu
from jax.sharding import PartitionSpec as P

H = 15
KVH = 5
HD = 64
D = 960
FF = 2560
GRP = H // KVH
R = 128
SHARDS = 64
SHARD = 153600
ROWS = 1280
KEYS = 4096
CHUNK = 512
PADD = 1024

eps = 1e-05
rope_theta = 100000.0
masked_fill = -1e30
f32 = jnp.float32
bf16 = jnp.bfloat16
ALL = ("phase", "ctx", "fsdp")

NT = (((1,), (1,)), ((), ()))


def mm(a, b):
    return jnp.dot(a, b, preferred_element_type=f32)


def mm_nt(a, b):
    return lax.dot_general(a, b, NT, preferred_element_type=f32)


def moved(block, shift, phases):
    dy, dx, dz = shift
    pairs = []
    for p in phases:
        for y in range(4):
            for x in range(4):
                for z in range(4):
                    to = (((y + dy) % 4) * 4 + (x + dx) % 4) * 4 + (z + dz) % 4
                    pairs.append((p * 64 + (y * 4 + x) * 4 + z, p * 64 + to))
    return lax.ppermute(block, ALL, pairs)


def unit(axis, step):
    shift = [0, 0, 0]
    shift[axis] = step
    return tuple(shift)


def ring_gather(block, axis, phases, half):
    low, high = half
    from_prev = moved(block, unit(axis, 1), phases)
    from_next = moved(block, unit(axis, -1), phases)
    far_low = moved(low(from_prev), unit(axis, 1), phases)
    far_high = moved(high(from_next), unit(axis, -1), phases)
    return from_next, far_low, far_high, from_prev


def ring_scatter(parts, axis, phases, half, joined):
    low, high = half
    add = lambda a, b: (a.astype(f32) + b.astype(f32)).astype(bf16)
    far_low = moved(low(parts[2]), unit(axis, 1), phases)
    far_high = moved(high(parts[2]), unit(axis, -1), phases)
    up = joined(add(low(parts[1]), far_low), high(parts[1]))
    down = joined(low(parts[3]), add(high(parts[3]), far_high))
    got_up = moved(up, unit(axis, 1), phases)
    got_down = moved(down, unit(axis, -1), phases)
    return parts[0].astype(f32) + got_up.astype(f32) + got_down.astype(f32)


def halves(dim, at):
    low = lambda v: lax.slice_in_dim(v, 0, at, axis=dim)
    high = lambda v: lax.slice_in_dim(v, at, v.shape[dim], axis=dim)
    return low, high


def gather_keys(kv, phases):
    half = halves(kv.ndim - 2, R // 2)

    def ring(block, axis):
        dim = block.ndim - 2
        nxt, flow, fhigh, prev = ring_gather(block, axis, phases, halves(dim, R // 2))
        return jnp.stack([block, nxt, jnp.concatenate([flow, fhigh], axis=dim), prev])

    far = moved(kv, (0, 0, 2), phases)
    first = ring(ring(kv, 0), 1)
    second = ring(ring(far, 1), 0)
    return jnp.concatenate(
        [first.reshape(16, R, 2 * KVH * HD), second.reshape(16, R, 2 * KVH * HD)]
    ).reshape(KEYS, 2 * KVH * HD)


def key_order(y, x, zh):
    order = []
    for bx in range(4):
        for by in range(4):
            order.append(((y + by) % 4) * 8 + ((x + bx) % 4) * 2 + zh)
    for by in range(4):
        for bx in range(4):
            order.append(((y + by) % 4) * 8 + ((x + bx) % 4) * 2 + (1 - zh))
    return jnp.stack(order)


def scatter_keys(d_kv, phases):
    parts = d_kv.reshape(2, 4, 4, R, 2 * KVH * HD)

    def ring(block, axis):
        dim = block.ndim - 3
        joined = lambda a, b: jnp.concatenate([a, b], axis=dim)
        return ring_scatter(
            [block[o] for o in range(4)], axis, phases, halves(dim, R // 2), joined
        )

    first = ring(ring(parts[0], 1).astype(bf16), 0)
    second = ring(ring(parts[1], 0).astype(bf16), 1)
    return first + moved(second.astype(bf16), (0, 0, 2), phases).astype(f32)


PART_ROWS = ((0, 432), (432, 864), (864, 1280))


def scatter_grads(rel):
    both = (0, 1)
    out = []
    for part, (begin, end) in enumerate(PART_ROWS):
        block = rel[:, :, :, begin:end]
        count = end - begin
        at = count // 32 * 16
        left = [0, 1, 2]
        for step in range(3):
            axis = (part + step) % 3
            where_axis = left.index(axis)
            left.remove(axis)
            pieces = [
                lax.index_in_dim(block, o, axis=where_axis, keepdims=False) for o in range(4)
            ]
            dim = pieces[0].ndim - 2
            joined = lambda a, b, dim=dim: jnp.concatenate([a, b], axis=dim)
            block = ring_scatter(pieces, axis, both, halves(dim, at), joined)
            if step < 2:
                block = block.astype(bf16)
        out.append(block)
    return jnp.concatenate(out)


def lane_of(shape):
    return lax.broadcasted_iota(jnp.int32, shape, len(shape) - 1)


def half_swapped(block):
    lane = lane_of(block.shape)
    return jnp.where(lane % HD < HD // 2, pltpu.roll(block, 96, 1), pltpu.roll(block, 32, 1))


def qkv_weight(w_ref, c):
    return w_ref[:, 96 * c : 96 * c + 96, :].reshape(D, 128)


def normed_of(u, gain):
    scale = lax.rsqrt(jnp.mean(u * u, axis=-1, keepdims=True) + eps)
    return scale, (u * scale * gain).astype(bf16)


def project_kernel(u_ref, g_ref, cos_ref, sin_ref, w_ref, qt_ref, kv_ref):
    u = u_ref[...].astype(f32)
    _, a = normed_of(u, g_ref[...])
    cos, sin = cos_ref[...], sin_ref[...]
    blocks = []
    for c in range(0, 13, 2):
        if c + 1 < 13:
            w = jnp.concatenate([qkv_weight(w_ref, c), qkv_weight(w_ref, c + 1)], axis=1)
        else:
            w = qkv_weight(w_ref, c)
        y = mm(a, w)
        for k in range(w.shape[1] // 128):
            b = y[:, 128 * k : 128 * k + 128]
            if c + k < 10:
                b = b * cos + half_swapped(b) * sin
            blocks.append(b)
    for c in range(8):
        t = (blocks[c].astype(bf16).astype(f32) * 0.125).T.astype(bf16)
        count = 128 if c < 7 else 64
        qt_ref[128 * c : 128 * c + count, :] = t[:count]
    lane = lane_of((R, 128))
    for g in range(KVH):
        k, v = blocks[(15 + g) // 2], blocks[(20 + g) // 2]
        if (15 + g) % 2:
            k = pltpu.roll(k, 64, 1)
        if (20 + g) % 2 == 0:
            v = pltpu.roll(v, 64, 1)
        kv_ref[:, 128 * g : 128 * g + 128] = jnp.where(lane < 64, k, v).astype(bf16)


def project(u, gain, cos, sin, weights):
    return pl.pallas_call(
        project_kernel,
        name="project",
        grid=(1,),
        in_specs=[
            pl.BlockSpec((R, D), lambda i: (0, 0)),
            pl.BlockSpec((1, D), lambda i: (0, 0)),
            pl.BlockSpec((R, 128), lambda i: (0, 0)),
            pl.BlockSpec((R, 128), lambda i: (0, 0)),
            pl.BlockSpec((10, ROWS, 128), lambda i: (0, 0, 0)),
        ],
        out_specs=[
            pl.BlockSpec((D, R), lambda i: (0, 0)),
            pl.BlockSpec((R, 640), lambda i: (0, 0)),
        ],
        out_shape=[
            jax.ShapeDtypeStruct((D, R), bf16),
            jax.ShapeDtypeStruct((R, 640), bf16),
        ],
        compiler_params=pltpu.CompilerParams(vmem_limit_bytes=48 << 20),
        cost_estimate=pl.CostEstimate(flops=400_000_000, bytes_accessed=4_000_000, transcendentals=0),
    )(u, gain, cos, sin, weights)


def heads_wide(ref, low):
    top = jnp.concatenate([ref[64 * h : 64 * h + 64, :] for h in range(GRP)], axis=1)
    zero = jnp.zeros_like(top)
    return jnp.concatenate([top, zero] if low else [zero, top], axis=0)


def attend_kernel(qt_ref, kv_ref, bias_ref, mixed_ref, lse_ref, s_ref):
    q = heads_wide(qt_ref, True)
    peak = jnp.full((1, GRP * R), masked_fill, f32)
    for i in range(KEYS // CHUNK):
        rows = slice(CHUNK * i, CHUNK * i + CHUNK)
        b = bias_ref[rows, :]
        s = mm(kv_ref[rows, :], q) + jnp.concatenate([b, b, b], axis=1)
        s_ref[rows, :] = s
        peak = jnp.maximum(peak, jnp.max(s, axis=0, keepdims=True))
    total = jnp.zeros((1, GRP * R), f32)
    acc = jnp.zeros((128, GRP * R), f32)
    for i in range(KEYS // CHUNK):
        rows = slice(CHUNK * i, CHUNK * i + CHUNK)
        p = jnp.exp(s_ref[rows, :] - peak)
        total = total + jnp.sum(p, axis=0, keepdims=True)
        acc = acc + mm(kv_ref[rows, :].T, p.astype(bf16))
    lse_ref[0] = peak + jnp.log(total)
    o = (acc[64:] / total).astype(bf16)
    for h in range(GRP):
        mixed_ref[64 * h : 64 * h + 64, :] = o[:, 128 * h : 128 * h + 128]


def attend(qt, kv_all, bias):
    return pl.pallas_call(
        attend_kernel,
        name="attend",
        grid=(KVH,),
        in_specs=[
            pl.BlockSpec((GRP * HD, R), lambda g: (g, 0)),
            pl.BlockSpec((KEYS, 128), lambda g: (0, g)),
            pl.BlockSpec((KEYS, R), lambda g: (0, 0)),
        ],
        out_specs=[
            pl.BlockSpec((GRP * HD, R), lambda g: (g, 0)),
            pl.BlockSpec((1, 1, GRP * R), lambda g: (g, 0, 0)),
        ],
        out_shape=[
            jax.ShapeDtypeStruct((D, R), bf16),
            jax.ShapeDtypeStruct((KVH, 1, GRP * R), f32),
        ],
        scratch_shapes=[pltpu.VMEM((KEYS, GRP * R), f32)],
        compiler_params=pltpu.CompilerParams(vmem_limit_bytes=48 << 20),
        cost_estimate=pl.CostEstimate(
            flops=4_000_000_000, bytes_accessed=8_000_000, transcendentals=7_900_000
        ),
    )(qt, kv_all, bias)


def out_weight(refs, c):
    return jnp.concatenate(
        [ref[:, 160 * c : 160 * c + 160, :].reshape(320, 128) for ref in refs], axis=0
    )


def gu_weight(refs, c):
    gl, gh, ul, uh = refs
    gate = jnp.concatenate([gl[:, c].reshape(512, 128), gh[:, c].reshape(512, 128)], axis=0)
    up = jnp.concatenate([ul[:, c].reshape(512, 128), uh[:, c].reshape(512, 128)], axis=0)
    return jnp.concatenate([gate, up], axis=1)


def down_weight(ref, c):
    return ref[:, 160 * c : 160 * c + 160, :].reshape(640, 128)


WEIGHT_SPECS = (
    [pl.BlockSpec((2, ROWS, 128), lambda j, k=k: (5 + k, 0, 0)) for k in range(3)]
    + [
        pl.BlockSpec((16, 5, 32, 128), lambda j, d=d, o=o: (1 + d, o + j, 0, 0))
        for o in (0, 4)
        for d in (0, 1)
    ]
    + [pl.BlockSpec((4, ROWS, 128), lambda j: (12 + j, 0, 0))]
)


def weight_args(gathered):
    fine = gathered.reshape(SHARDS, 40, 32, 128)
    return [gathered] * 3 + [fine] * 4 + [gathered]


def feed_kernel(
    mixed_ref, u_ref, g_ref, pad_ref, o0, o1, o2, gl, gh, ul, uh, wd,
    y_ref, h_ref, nt_ref, gate_ref, up_ref, mt_ref, n_scr, y_scr,
):
    step = pl.program_id(0)

    @pl.when(step == 0)
    def _():
        mixed = mixed_ref[...].T
        for c in range(0, 8, 2):
            w = jnp.concatenate(
                [out_weight((o0, o1, o2), c), out_weight((o0, o1, o2), c + 1)], axis=1
            )
            y = mm(mixed, w)
            end = min(128 * c + 256, D)
            h_ref[:, 128 * c : end] = u_ref[:, 128 * c : end].astype(f32) + y[:, : end - 128 * c]
        _, n = normed_of(h_ref[...], g_ref[...])
        padded = mm(n, pad_ref[...])
        n_scr[...] = padded.astype(bf16)
        nt_ref[...] = padded.T.astype(bf16)
        y_scr[...] = jnp.zeros_like(y_scr)

    n = n_scr[...]
    inner = []
    for c in range(5):
        gu = mm(n, gu_weight((gl, gh, ul, uh), c))
        gate, up = gu[:, :128], gu[:, 128:]
        cols = slice(128 * c, 128 * c + 128)
        gate_ref[:, cols] = gate
        up_ref[:, cols] = up
        m = gate * jax.nn.sigmoid(gate) * up
        mt_ref[cols, :] = m.T.astype(bf16)
        inner.append(m.astype(bf16))
    inner = jnp.concatenate(inner, axis=1)
    for c in range(0, 8, 2):
        w = jnp.concatenate([down_weight(wd, c), down_weight(wd, c + 1)], axis=1)
        y_scr[:, 128 * c : 128 * c + 256] += mm(inner, w)

    @pl.when(step == 3)
    def _():
        y_ref[...] = (h_ref[...] + y_scr[:, :D]).astype(bf16)


def feed(mixed, u, gain, pad, gathered):
    whole = lambda *shape: pl.BlockSpec(shape, lambda j: (0,) * len(shape))
    return pl.pallas_call(
        feed_kernel,
        name="feed",
        grid=(4,),
        in_specs=[whole(D, R), whole(R, D), whole(1, D), whole(D, PADD)] + WEIGHT_SPECS,
        out_specs=[
            whole(R, D),
            whole(R, D),
            whole(PADD, R),
            pl.BlockSpec((R, 640), lambda j: (0, j)),
            pl.BlockSpec((R, 640), lambda j: (0, j)),
            pl.BlockSpec((640, R), lambda j: (j, 0)),
        ],
        out_shape=[
            jax.ShapeDtypeStruct((R, D), bf16),
            jax.ShapeDtypeStruct((R, D), f32),
            jax.ShapeDtypeStruct((PADD, R), bf16),
            jax.ShapeDtypeStruct((R, FF), f32),
            jax.ShapeDtypeStruct((R, FF), f32),
            jax.ShapeDtypeStruct((FF, R), bf16),
        ],
        scratch_shapes=[pltpu.VMEM((R, PADD), bf16), pltpu.VMEM((R, PADD), f32)],
        compiler_params=pltpu.CompilerParams(vmem_limit_bytes=48 << 20),
        cost_estimate=pl.CostEstimate(
            flops=2_200_000_000, bytes_accessed=22_000_000, transcendentals=400_000
        ),
    )(mixed, u, gain, pad, *weight_args(gathered))


def norm_back(d_out, values, gain):
    scales = lax.rsqrt(jnp.mean(values * values, axis=-1, keepdims=True) + eps)
    scaled = d_out * gain
    d_gain = jnp.sum(d_out * values * scales, axis=0, keepdims=True)
    d_values = scales * scaled - values * (scales * scales * scales) * jnp.mean(
        scaled * values, axis=-1, keepdims=True
    )
    return d_values, d_gain


def feed_back_kernel(
    c_ref, gate_ref, up_ref, h_ref, g_ref, pad_ref, o0, o1, o2, gl, gh, ul, uh, wd,
    dgate_ref, dup_ref, dh_ref, dhb_ref, dg_ref, dot_ref, cb_ref, dn_scr,
):
    step = pl.program_id(0)

    @pl.when(step == 0)
    def _():
        cb_ref[...] = jnp.zeros_like(cb_ref)
        cb_ref[:, :D] = c_ref[...].astype(bf16)
        dn_scr[...] = jnp.zeros_like(dn_scr)

    d_inner = jnp.zeros((R, 640), f32)
    for c in range(0, 8, 2):
        w = jnp.concatenate([down_weight(wd, c), down_weight(wd, c + 1)], axis=1)
        d_inner = d_inner + mm_nt(cb_ref[:, 128 * c : 128 * c + 256], w)
    for c in range(5):
        cols = slice(128 * c, 128 * c + 128)
        gate, up, dm = gate_ref[:, cols], up_ref[:, cols], d_inner[:, cols]
        sigma = jax.nn.sigmoid(gate)
        d_gate = (dm * up * sigma * (1.0 + gate * (1.0 - sigma))).astype(bf16)
        d_up = (dm * gate * sigma).astype(bf16)
        dgate_ref[:, cols] = d_gate
        dup_ref[:, cols] = d_up
        both = jnp.concatenate([d_gate, d_up], axis=1)
        dn_scr[...] += mm_nt(both, gu_weight((gl, gh, ul, uh), c))

    @pl.when(step == 3)
    def _():
        padded = dn_scr[...]
        high = padded.astype(bf16)
        low = (padded - high.astype(f32)).astype(bf16)
        dn = mm_nt(high, pad_ref[...]) + mm_nt(low, pad_ref[...])
        d_h, d_gain = norm_back(dn, h_ref[...], g_ref[...])
        d_h = c_ref[...] + d_h
        dg_ref[...] = d_gain
        dh_ref[...] = d_h
        dhb_ref[...] = jnp.zeros_like(dhb_ref)
        dhb_ref[:, :D] = d_h.astype(bf16)
        d_mixed = jnp.zeros((R, D), f32)
        for c in range(0, 8, 2):
            w = jnp.concatenate(
                [out_weight((o0, o1, o2), c), out_weight((o0, o1, o2), c + 1)], axis=1
            )
            d_mixed = d_mixed + mm_nt(dhb_ref[:, 128 * c : 128 * c + 256], w)
        dot_ref[...] = d_mixed.T


def feed_back(cot, gate, up, hidden, gain, pad, gathered):
    whole = lambda *shape: pl.BlockSpec(shape, lambda j: (0,) * len(shape))
    block = pl.BlockSpec((R, 640), lambda j: (0, j))
    return pl.pallas_call(
        feed_back_kernel,
        name="feed_back",
        grid=(4,),
        in_specs=[whole(R, D), block, block, whole(R, D), whole(1, D), whole(D, PADD)]
        + WEIGHT_SPECS,
        out_specs=[
            block,
            block,
            whole(R, D),
            whole(R, PADD),
            whole(1, D),
            whole(D, R),
            whole(R, PADD),
        ],
        out_shape=[
            jax.ShapeDtypeStruct((R, FF), bf16),
            jax.ShapeDtypeStruct((R, FF), bf16),
            jax.ShapeDtypeStruct((R, D), f32),
            jax.ShapeDtypeStruct((R, PADD), bf16),
            jax.ShapeDtypeStruct((1, D), f32),
            jax.ShapeDtypeStruct((D, R), f32),
            jax.ShapeDtypeStruct((R, PADD), bf16),
        ],
        scratch_shapes=[pltpu.VMEM((R, PADD), f32)],
        compiler_params=pltpu.CompilerParams(vmem_limit_bytes=48 << 20),
        cost_estimate=pl.CostEstimate(
            flops=2_200_000_000, bytes_accessed=22_000_000, transcendentals=400_000
        ),
    )(cot, gate, up, hidden, gain, pad, *weight_args(gathered))


def attend_back_kernel(
    qt_ref, kv_ref, bias_ref, dot_ref, mixed_ref, lse_ref, dkv_ref, dqt_ref
):
    q = heads_wide(qt_ref, True)
    d_o = heads_wide(dot_ref, False)
    o = heads_wide(mixed_ref, False)
    delta = jnp.sum(d_o * o.astype(f32), axis=0, keepdims=True)
    d_o = d_o.astype(bf16)
    lse = lse_ref[0]
    both = jnp.concatenate([q, d_o], axis=1)
    acc = jnp.zeros((128, GRP * R), f32)
    for i in range(KEYS // CHUNK):
        rows = slice(CHUNK * i, CHUNK * i + CHUNK)
        b = bias_ref[rows, :]
        kv = kv_ref[rows, :]
        p = jnp.exp(mm(kv, q) + jnp.concatenate([b, b, b], axis=1) - lse)
        ds = (p * (mm(kv, d_o) - delta)).astype(bf16)
        dkv_ref[rows, :] = mm_nt(jnp.concatenate([ds, p.astype(bf16)], axis=1), both).astype(bf16)
        acc = acc + mm(kv.T, ds)
    acc = acc[:64] * 0.125
    for h in range(GRP):
        dqt_ref[64 * h : 64 * h + 64, :] = acc[:, 128 * h : 128 * h + 128]


def attend_back(qt, kv_all, bias, d_mixed, mixed, lse):
    heads = pl.BlockSpec((GRP * HD, R), lambda g: (g, 0))
    return pl.pallas_call(
        attend_back_kernel,
        name="attend_back",
        grid=(KVH,),
        in_specs=[
            heads,
            pl.BlockSpec((KEYS, 128), lambda g: (0, g)),
            pl.BlockSpec((KEYS, R), lambda g: (0, 0)),
            heads,
            heads,
            pl.BlockSpec((1, 1, GRP * R), lambda g: (g, 0, 0)),
        ],
        out_specs=[pl.BlockSpec((KEYS, 128), lambda g: (0, g)), heads],
        out_shape=[
            jax.ShapeDtypeStruct((KEYS, 640), bf16),
            jax.ShapeDtypeStruct((D, R), f32),
        ],
        compiler_params=pltpu.CompilerParams(vmem_limit_bytes=48 << 20),
        cost_estimate=pl.CostEstimate(
            flops=10_000_000_000, bytes_accessed=14_000_000, transcendentals=7_900_000
        ),
    )(qt, kv_all, bias, d_mixed, mixed, lse)


def project_back_kernel(
    dqt_ref, dkv_ref, cos_ref, sin_ref, u_ref, g_ref, dh_ref, w_ref,
    du_ref, dqkv_ref, at_ref, dg_ref,
):
    cos, sin = cos_ref[...], sin_ref[...]
    lane = lane_of((R, 128))
    dkv = [dkv_ref[:, 128 * g : 128 * g + 128] for g in range(KVH)]
    rolled = [pltpu.roll(b, 64, 1) for b in dkv]
    zero = jnp.zeros((R, 128), f32)
    blocks = [dqt_ref[128 * c : 128 * c + 128, :].T for c in range(7)]
    last = jnp.concatenate([dqt_ref[896:960, :], jnp.zeros((64, R), f32)], axis=0).T
    low = lane < 64
    blocks.append(jnp.where(low, last, rolled[0]))
    blocks.append(jnp.where(low, dkv[1], rolled[2]))
    blocks.append(jnp.where(low, dkv[3], rolled[4]))
    blocks = [b * cos - half_swapped(b) * sin for b in blocks]
    blocks.append(jnp.where(low, rolled[0], dkv[1]))
    blocks.append(jnp.where(low, rolled[2], dkv[3]))
    blocks.append(jnp.where(low, rolled[4], zero))
    da = jnp.zeros((R, D), f32)
    for c in range(0, 13, 2):
        if c + 1 < 13:
            d = jnp.concatenate([blocks[c], blocks[c + 1]], axis=1).astype(bf16)
            w = jnp.concatenate([qkv_weight(w_ref, c), qkv_weight(w_ref, c + 1)], axis=1)
        else:
            d, w = blocks[c].astype(bf16), qkv_weight(w_ref, c)
        dqkv_ref[:, 128 * c : 128 * c + d.shape[1]] = d
        da = da + mm_nt(d, w)
    u = u_ref[...].astype(f32)
    gain = g_ref[...]
    _, a = normed_of(u, gain)
    at_ref[...] = a.T
    d_u, d_gain = norm_back(da, u, gain)
    dg_ref[...] = d_gain
    du_ref[...] = dh_ref[...] + d_u


def project_back(d_query, d_kv, cos, sin, u, gain, d_hidden, weights):
    whole = lambda *shape: pl.BlockSpec(shape, lambda j: (0,) * len(shape))
    return pl.pallas_call(
        project_back_kernel,
        name="project_back",
        grid=(1,),
        in_specs=[
            whole(D, R),
            whole(R, 640),
            whole(R, 128),
            whole(R, 128),
            whole(R, D),
            whole(1, D),
            whole(R, D),
            whole(10, ROWS, 128),
        ],
        out_specs=[whole(R, D), whole(R, 13 * 128), whole(D, R), whole(1, D)],
        out_shape=[
            jax.ShapeDtypeStruct((R, D), f32),
            jax.ShapeDtypeStruct((R, 13 * 128), bf16),
            jax.ShapeDtypeStruct((D, R), bf16),
            jax.ShapeDtypeStruct((1, D), f32),
        ],
        compiler_params=pltpu.CompilerParams(vmem_limit_bytes=48 << 20),
        cost_estimate=pl.CostEstimate(flops=400_000_000, bytes_accessed=5_000_000, transcendentals=0),
    )(d_query, d_kv, cos, sin, u, gain, d_hidden, weights)


def outer_kernel(
    place_ref, at_ref, dqkv_ref, mixed_ref, dhb_ref, nt_ref, dgate_ref, dup_ref, mt_ref, cb_ref,
    gain_ref, out_ref,
):
    shard = pl.program_id(0)
    gains = gain_ref[pl.ds(shard, 1), :]

    def row_of(count, at):
        row = lax.broadcasted_iota(jnp.int32, (count, 128), 0)
        return jnp.where(row == at, gains, 0.0)

    @pl.when(shard < 10)
    def _():
        rows = at_ref[pl.ds(pl.multiple_of(96 * shard, 32), 96), :]
        res = mm(rows, dqkv_ref[...])
        for c in range(13):
            out_ref[0, 96 * c : 96 * c + 96, :] = res[:, 128 * c : 128 * c + 128].astype(bf16)
        out_ref[0, 1248:1280, :] = row_of(32, 0).astype(bf16)

    def wide(rows, cot):
        res = mm(rows, cot)
        for c in range(8):
            b = res[:, 128 * c : 128 * c + 128]
            if c == 7:
                b = b + row_of(160, 0)
            out_ref[0, 160 * c : 160 * c + 160, :] = b.astype(bf16)

    @pl.when((shard >= 10) & (shard < 16))
    def _():
        wide(mixed_ref[pl.ds(pl.multiple_of(160 * (shard - 10), 32), 160), :], dhb_ref[...])

    @pl.when((shard >= 16) & (shard < 48))
    def _():
        rows = nt_ref[pl.ds(pl.multiple_of(32 * (shard - 16), 32), 32), :]
        for part, ref in enumerate((dgate_ref, dup_ref)):
            res = mm(rows, ref[...])
            for c in range(20):
                b = res[:, 128 * c : 128 * c + 128]
                at = 32 * (20 * part + c)
                if part == 0 and c == 0:
                    b = b + row_of(32, 30)
                out_ref[0, at : at + 32, :] = b.astype(bf16)

    @pl.when(shard >= 48)
    def _():
        wide(mt_ref[pl.ds(pl.multiple_of(160 * (shard - 48), 32), 160), :], cb_ref[...])


def outer(places, at, dqkv, mixed, dhb, nt, dgate, dup, mt, cb, gains):
    whole = lambda v: pl.BlockSpec(v.shape, lambda s, place: (0,) * v.ndim)
    args = (at, dqkv, mixed, dhb, nt, dgate, dup, mt, cb, gains)
    return pl.pallas_call(
        outer_kernel,
        name="outer",
        grid_spec=pltpu.PrefetchScalarGridSpec(
            num_scalar_prefetch=1,
            grid=(SHARDS,),
            in_specs=[whole(v) for v in args],
            out_specs=pl.BlockSpec((1, ROWS, 128), lambda s, place: (place[s], 0, 0)),
        ),
        out_shape=jax.ShapeDtypeStruct((SHARDS, ROWS, 128), bf16),
        compiler_params=pltpu.CompilerParams(vmem_limit_bytes=48 << 20),
        cost_estimate=pl.CostEstimate(
            flops=2_600_000_000, bytes_accessed=24_000_000, transcendentals=0
        ),
    )(places, *args)


def shard_kind(rank):
    return jnp.where(rank < 10, 0, jnp.where((rank >= 16) & (rank < 48), 2, 1))


def shard_blocks(flat, gains, rank):
    g = jnp.zeros((1, 128), bf16).at[0, :30].set(gains)

    def narrow(_):
        w = jnp.pad(flat.reshape(96, 1600), ((0, 0), (0, 64)))
        w = w.reshape(96, 13, 128).transpose(1, 0, 2).reshape(1248, 128)
        return jnp.concatenate([w, jnp.pad(g, ((0, 31), (0, 0)))])

    def square(_):
        w = jnp.pad(flat.reshape(160, 960), ((0, 0), (0, 64)))
        w = w.reshape(160, 8, 128).transpose(1, 0, 2)
        last = jnp.concatenate([jnp.zeros((1, 64), bf16), g[:, :64]], axis=1)
        return w.at[7, 0].add(last[0]).reshape(ROWS, 128)

    def broad(_):
        w = jnp.pad(flat.reshape(30, 40, 128), ((0, 2), (0, 0), (0, 0))).transpose(1, 0, 2)
        return w.at[0, 30].set(g[0]).reshape(ROWS, 128)

    return lax.switch(shard_kind(rank), [narrow, square, broad], 0)


def blocks_shard(blocks, rank):
    def narrow(_):
        w = blocks[:1248].reshape(13, 96, 128).transpose(1, 0, 2).reshape(96, 1664)[:, :1600]
        return w.reshape(SHARD), blocks[1248, :30]

    def square(_):
        w = blocks.reshape(8, 160, 128).transpose(1, 0, 2).reshape(160, 1024)[:, :960]
        return w.reshape(SHARD), blocks[1120, 64:94]

    def broad(_):
        w = blocks.reshape(40, 32, 128).transpose(1, 0, 2)[:30]
        return w.reshape(SHARD), blocks[30, :30]

    return lax.switch(shard_kind(rank), [narrow, square, broad], 0)


def gathered_gains(gathered):
    rows = jnp.concatenate(
        [
            gathered[:10, 1248, :30],
            gathered[10:16, 1120, 64:94],
            gathered[16:48, 30, :30],
            gathered[48:, 1120, 64:94],
        ]
    ).astype(f32)
    flat = rows.reshape(1, 2 * D)
    return flat[:, :D], flat[:, D:]


def per_device(layer_in, out_grad, segment_ids, block_pair, params, norm_gains):
    phase = lax.axis_index("phase")
    ctx = lax.axis_index("ctx")
    rank = ctx * 2 + lax.axis_index("fsdp")
    y, x, z = rank // 16, (rank // 4) % 4, rank % 4
    zh = z // 2

    own = shard_blocks(params[0], norm_gains[0], rank)
    gathered = lax.all_gather(own, ("ctx", "fsdp"), axis=0)

    seg_row = segment_ids[0]
    pair = lax.dynamic_index_in_dim(block_pair, ctx, 0, keepdims=False)
    within = jnp.arange(HD, dtype=jnp.int32)
    place_q = jnp.concatenate([pair * 64 + within, (63 - pair) * 64 + within])
    seg_q = jnp.concatenate(
        [
            lax.dynamic_slice_in_dim(seg_row, pair * 64, 64),
            lax.dynamic_slice_in_dim(seg_row, (63 - pair) * 64, 64),
        ]
    )
    start_q = jnp.sum((seg_row[:, None] < seg_q[None, :]).astype(jnp.int32), axis=0)
    pairs_k = block_pair[key_order(y, x, zh)]
    place_k = (
        jnp.stack([pairs_k, 63 - pairs_k], axis=1)[:, :, None] * 64 + within[None, None, :]
    ).reshape(KEYS)
    bias = jnp.where(
        (place_k[:, None] <= place_q[None, :]) & (place_k[:, None] >= start_q[None, :]),
        0.0,
        masked_fill,
    ).astype(f32)
    frequency = rope_theta ** (-2.0 * jnp.arange(HD // 2, dtype=f32) / HD)
    angles = (place_q - start_q).astype(f32)[:, None] * frequency[None, :]
    cosine, sine = jnp.cos(angles), jnp.sin(angles)
    cos = jnp.concatenate([cosine] * 4, axis=1)
    sin = jnp.concatenate([-sine, sine, -sine, sine], axis=1)
    spread = jnp.arange(PADD, dtype=jnp.int32)
    target = jnp.where(spread % 32 < 30, (spread // 32) * 30 + spread % 32, -1)
    pad = (jnp.arange(D, dtype=jnp.int32)[:, None] == target[None, :]).astype(bf16)

    gain_one, gain_two = gathered_gains(gathered)
    first = phase == 0

    u = layer_in[0]
    kv_all = None
    for tick in range(2):
        qt, kv = project(u, gain_one, cos, sin, gathered)
        fetched = gather_keys(kv, (tick,))
        kv_all = fetched if tick == 0 else jnp.where(first, kv_all, fetched)
        mixed, lse = attend(qt, kv_all, bias)
        result, hidden, nt, gate, up, mt = feed(mixed, u, gain_two, pad, gathered)
        if tick == 0:
            u = jnp.where(first, u, lax.ppermute(result, "phase", [(0, 1)]))

    cot = out_grad[0]
    kept = None
    for tick in range(2):
        dgate, dup, dh, dhb, dg_two, d_mixed, cb = feed_back(
            cot, gate, up, hidden, gain_two, pad, gathered
        )
        d_kv_all, d_query = attend_back(qt, kv_all, bias, d_mixed, mixed, lse)
        d_kv = scatter_keys(d_kv_all, (1 - tick,))
        kept = d_kv if tick == 0 else jnp.where(first, d_kv, kept)
        d_u, dqkv, at, dg_one = project_back(
            d_query, kept, cos, sin, u, gain_one, dh, gathered
        )
        if tick == 0:
            back = lax.ppermute(d_u.astype(bf16), "phase", [(1, 0)])
            cot = jnp.where(first, back.astype(f32), cot)

    gains = jnp.concatenate([dg_one, dg_two], axis=1).reshape(SHARDS, 30)
    shards = jnp.arange(SHARDS, dtype=jnp.int32)
    square = (((shards >= 10) & (shards < 16)) | (shards >= 48))[:, None]
    gains = jnp.where(
        square, jnp.pad(gains, ((0, 0), (64, 34))), jnp.pad(gains, ((0, 0), (0, 98)))
    )
    sy, sx, sz = shards // 16, (shards // 4) % 4, shards % 4
    places = ((sy - y) % 4) * 16 + ((sx - x) % 4) * 4 + (sz - z) % 4
    grads = outer(places, at, dqkv, mixed, dhb, nt, dgate, dup, mt, cb, gains)
    total = scatter_grads(grads.reshape(4, 4, 4, ROWS, 128))
    param_part, gain_part = blocks_shard(total, rank)
    return (result[None, None], d_u[None, None], param_part[None], gain_part[None])


def solution(mesh):
    return jax.shard_map(
        per_device,
        mesh=mesh,
        in_specs=(
            P("fsdp", "ctx", None),
            P("fsdp", "ctx", None),
            P("fsdp", None),
            P(),
            P("phase", ("ctx", "fsdp")),
            P("phase", ("ctx", "fsdp")),
        ),
        out_specs=(
            P("phase", "fsdp", "ctx", None),
            P("phase", "fsdp", "ctx", None),
            P("phase", ("ctx", "fsdp")),
            P("phase", ("ctx", "fsdp")),
        ),
        check_vma=False,
    )
```

time: 1950 us -> 778 us (0.40)
  local copies, waits for them, and re-layouts: 584 us -> 44.7 us
  blocking collectives: 363 us -> 0 us
  matrix products: 304 us -> 0 us
  waiting for transfers between devices: 568 us -> 278 us
  starting transfers between devices: 3.21 us -> 187 us
  Pallas kernels: 0 us -> 182 us
  other arithmetic: 89.7 us -> 56.4 us
    unnamed x9 -> x1, waiting for transfers between devices: 462 us -> 0.02 us
    slice x32 -> x69, local copies, waits for them, and re-layouts: 413 us -> 20.7 us  [the longest x2 5.92 us: ring(): block[o]]
    unnamed x2 -> x0, blocking collectives: 363 us -> none
    dot_general x108 -> x0, matrix products: 304 us -> none  [the longest x2 44.1 us: key_fold(): jnp.einsum('kgrn,nkd->kgrd', weights_now, vals, precision=lax.Precision.H...]
    ppermute x2 -> x106, starting transfers between devices: 2.59 us -> 187 us  [the longest x104 185 us: moved(): return lax.ppermute(block, ALL, pairs)]
    pallas_call x0 -> x13, Pallas kernels: none -> 182 us  [the longest x2 52.8 us: attend_back(): pl.pallas_call(attend_back_kernel, name='attend_back', grid=(KVH,), in_sp...]
    ppermute x2 -> x106, waiting for transfers between devices: 2.08 us -> 159 us  [the longest x1 91.9 us: per_device(): back = lax.ppermute(d_u.astype(bf16), 'phase', [(1, 0)])]
    reshape x9 -> x3, local copies, waits for them, and re-layouts: 60 us -> 0.76 us  [the longest x1 0.38 us: narrow(): blocks[:1248].reshape(13, 96, 128).transpose(1, 0, 2).reshape(96, 1664)]
  transfers between devices with their start and end apart: 8 -> 107, of which waited for: 6 -> 25; matrix products, arithmetic and copies ran while one was open for 25% -> 7% of each run, Pallas kernels for 0% -> 0%
where the time goes in v1:
time: 778 us; the launch traced here: 768 us
  waiting for transfers between devices  278 us (36%)
  starting transfers between devices  187 us (24%)
  Pallas kernels  182 us (23%)
  other arithmetic  56.4 us (7%)
  local copies, waits for them, and re-layouts  44.7 us (6%)
  between operations  18.7 us (2%)
    ppermute x104, starting transfers between devices, moved(): return lax.ppermute(block, ALL, pairs)  185 us
    all_gather x1, waiting for transfers between devices, per_device(): gathered = lax.all_gather(own, ('ctx', 'fsdp'), axis=0)  119 us
    ppermute x1, waiting for transfers between devices, per_device(): back = lax.ppermute(d_u.astype(bf16), 'phase', [(1, 0)])  91.9 us
    ppermute x104, waiting for transfers between devices, moved(): return lax.ppermute(block, ALL, pairs)  66 us
    pallas_call x2, Pallas kernels, attend_back(): pl.pallas_call(attend_back_kernel, name='attend_back', grid=(KVH,), in_sp...  52.8 us
    pallas_call x1, Pallas kernels, outer(): pl.pallas_call(outer_kernel, name='outer', grid_spec=pltpu.PrefetchScalar...  33.1 us
    pallas_call x2, Pallas kernels, attend(): pl.pallas_call(attend_kernel, name='attend', grid=(KVH,), in_specs=[pl.Bl...  30.8 us
    pallas_call x2, Pallas kernels, feed_back(): pl.pallas_call(feed_back_kernel, name='feed_back', grid=(4,), in_specs=[w...  30.1 us
  transfers between devices with their start and end apart: 107, of which 25 were waited for; matrix products, arithmetic and copies ran while one was open for 7% of the time, Pallas kernels for 0%

profile of v1, /device:TPU:0, one launch (start us, length us, event | category | flops | bytes accessed | tf_op | source)
XLA Modules:
  0.0 767.6 jit_solution(12675611949296328010)
XLA Ops:
  9.2 8.4 %conditional.2 = (bf16[1280,128]{1,0:T(8,128)(2,1)S(1)}) conditional(s32[]{:T(128)} %clamp.4, (bf16[1,153600]{1,0:T(2,128)(2,1)}, bf16[1,128]{1,0:T(2,128)(2,1)S(1)}) %tuple.47, (bf16[1,153600]{1,0:T(2,128)(2,1)}, bf16[1,128]{1,0:T(2,128)(2,1)S(1)}) %tuple.47, (bf16[1,153600]{1,0:T(2,128)(2,1)}, bf16[1,128]{1,0:T(2,128)(2,1)S(1)}) %tuple.47), branch_computations={%region_1.2_spmd, %region_2.3_spmd, %region_3.5_spmd} | conditional | flops 983040 | bytes 3780876 | solution.py:688
  9.2 7.4 reduce.15
  24.1 118.9 %all-gather.3.cloned.1.call-done = bf16[81920,128]{1,0:T(8,128)(2,1)} async-done(((bf16[1280,128]{1,0:T(8,128)(2,1)}), bf16[81920,128]{1,0:T(8,128)(2,1)}) %all-gather.3.cloned.1.call-update) | async-done | bytes 20971536 | tf_op jit(solution)/shard_map/all_gather | solution.py:728
  149.6 4.8 collective-permute-start.8
  154.4 3.4 collective-permute-start.1
  157.8 3.7 collective-permute-start
  165.0 4.9 collective-permute-start.3
  172.8 4.2 collective-permute-start.9
  180.3 5.1 collective-permute-start.12
  187.5 3.9 collective-permute-start.5
  193.9 3.6 collective-permute-start.14
  206.2 3.4 collective-permute-start.16
  215.2 4.7 collective-permute-done.15
  223.2 15.5 %attend.2 = (bf16[960,128]{1,0:T(8,128)(2,1)S(1)}, f32[5,1,384]{2,1,0:T(1,128)}) custom-call(bf16[960,128]{1,0:T(8,128)(2,1)S(1)} %get-tuple-element.116.qt_ref, bf16[4096,640]{1,0:T(8,128)(2,1)} %bitcast.469, f32[4096,128]{1,0:T(8,128)S(1)} %and_select_fusion.bias_ref), custom_call_target="tpu_custom_call" | custom-call | flops 4000000000 | bytes 8000000 | tf_op jit(solution)/shard_map/attend/pallas_call | solution.py:258
  238.7 11.5 %feed.2 = (bf16[128,960]{1,0:T(8,128)(2,1)S(1)}, f32[128,960]{1,0:T(8,128)}, bf16[1024,128]{1,0:T(8,128)(2,1)}, f32[128,2560]{1,0:T(8,128)}, f32[128,2560]{1,0:T(8,128)}, /*index=5*/bf16[2560,128]{1,0:T(8,128)(2,1)}) custom-call(bf16[960,128]{1,0:T(8,128)(2,1)S(1)} %get-tuple-element.118.mixed_ref, bf16[128,960]{1,0:T(8,128)(2,1)S(1)} %bitcast.419, ...), custom_call_target="tpu_custom_call" | custom-call | flops 2200000000 | bytes 22000000 | tf_op jit(solution)/shard_map/feed/pallas_call | solution.py:361
  280.5 3.4 pad_maximum_fusion.5
  286.2 3.8 bitcast_select_fusion.kv_ref
  290.0 15.2 %attend.3 = (bf16[960,128]{1,0:T(8,128)(2,1)S(1)}, f32[5,1,384]{2,1,0:T(1,128)S(1)}) custom-call(bf16[960,128]{1,0:T(8,128)(2,1)S(1)} %get-tuple-element.120.qt_ref, bf16[4096,640]{1,0:T(8,128)(2,1)} %bitcast_select_fusion.kv_ref, f32[4096,128]{1,0:T(8,128)S(1)} %and_select_fusion.bias_ref), custom_call_target="tpu_custom_call" | custom-call | flops 4000000000 | bytes 8000000 | tf_op jit(solution)/shard_map/attend/pallas_call | solution.py:258
  305.2 10.0 %feed.3 = (bf16[128,960]{1,0:T(8,128)(2,1)S(1)}, f32[128,960]{1,0:T(8,128)S(1)}, bf16[1024,128]{1,0:T(8,128)(2,1)S(1)}, f32[128,2560]{1,0:T(8,128)S(1)}, f32[128...) custom-call(bf16[960,128]{1,0:T(8,128)(2,1)S(1)} %get-tuple-element.122.mixed_ref, ...), custom_call_target="tpu_custom_call" | custom-call | flops 2200000000 | bytes 22000000 | tf_op jit(solution)/shard_map/feed/pallas_call | solution.py:361
  317.2 15.3 %feed_back.2 = (bf16[128,2560]{1,0:T(8,128)(2,1)}, bf16[128,2560]{1,0:T(8,128)(2,1)}, f32[128,960]{1,0:T(8,128)S(1)}, bf16[128,1024]{1,0:T(8,128)(2,1)}, f32[1,9...) custom-call(f32[128,960]{1,0:T(8,128)S(1)} %bitcast.417, ...), custom_call_target="tpu_custom_call" | custom-call | flops 2200000000 | bytes 22000000 | tf_op jit(solution)/shard_map/feed_back/pallas_call | solution.py:451
  332.6 26.2 %attend_back.2 = (bf16[4096,640]{1,0:T(8,128)(2,1)}, f32[960,128]{1,0:T(8,128)S(1)}) custom-call(bf16[960,128]{1,0:T(8,128)(2,1)S(1)} %copy-done.18, bf16[4096,640]{1,0:T(8,128)(2,1)} %bitcast_select_fusion.kv_ref, f32[4096,128]{1,0:T(8,128)S(1)} %and_select_fusion.bias_ref, f32[960,128]{1,0:T(8,128)S(1)} %get-tuple-element.127.dot_ref, ...), custom_call_target="tpu_custom_call" | custom-call | flops 10000000000 | bytes 14000000 | tf_op jit(solution)/shard_map/attend_back/pallas_call | solution.py:509
  375.5 4.3 project_back.2
  381.1 91.9 %collective-permute-done.52 = bf16[128,960]{1,0:T(8,128)(2,1)S(1)} collective-permute-done((bf16[128,960]{1,0:T(8,128)(2,1)S(1)}, bf16[128,960]{1,0:T(8,128)(2,1)S(1)}, u32[]{:S(2)}, u32[]{:S(2)}) %collective-permute-start.52) | collective-permute-done | bytes 245792 | tf_op jit(solution)/shard_map/ppermute | solution.py:786
  473.1 14.8 %feed_back.3 = (bf16[128,2560]{1,0:T(8,128)(2,1)S(1)}, bf16[128,2560]{1,0:T(8,128)(2,1)S(1)}, f32[128,960]{1,0:T(8,128)S(1)}, bf16[128,1024]{1,0:T(8,128)(2,1)S(...) custom-call(f32[128,960]{1,0:T(8,128)S(1)} %convert_select_fusion.c_ref, ...), custom_call_target="tpu_custom_call" | custom-call | flops 2200000000 | bytes 22000000 | tf_op jit(solution)/shard_map/feed_back/pallas_call | solution.py:451
  487.9 26.6 %attend_back.3 = (bf16[4096,640]{1,0:T(8,128)(2,1)}, f32[960,128]{1,0:T(8,128)S(1)}) custom-call(bf16[960,128]{1,0:T(8,128)(2,1)S(1)} %copy-done.18, bf16[4096,640]{1,0:T(8,128)(2,1)} %bitcast_select_fusion.kv_ref, f32[4096,128]{1,0:T(8,128)S(1)} %and_select_fusion.bias_ref, f32[960,128]{1,0:T(8,128)S(1)} %get-tuple-element.133.dot_ref, ...), custom_call_target="tpu_custom_call" | custom-call | flops 10000000000 | bytes 14000000 | tf_op jit(solution)/shard_map/attend_back/pallas_call | solution.py:509
  517.6 3.4 collective-permute-start.63
  525.9 4.9 collective-permute-start.55
  530.9 4.6 collective-permute-start.64
  543.8 5.5 collective-permute-done.62
  551.6 5.1 collective-permute-start.67
  559.0 5.1 collective-permute-start.59
  566.2 3.9 collective-permute-start.66
  572.2 3.9 collective-permute-start.58
  576.2 4.8 collective-permute-start.69
  581.0 3.9 collective-permute-done.69
  585.0 3.7 project_back.3
  594.4 33.1 %outer.1 = bf16[64,1280,128]{2,1,0:T(8,128)(2,1)} custom-call(s32[64]{0:T(128)S(1)} %fusion.64.place_ref, bf16[960,128]{1,0:T(8,128)(2,1)S(1)} %copy-done.16, bf16[128,1664]{1,0:T(8,128)(2,1)S(1)} %copy-done.8, bf16[960,128]{1,0:T(8,128)(2,1)S(1)} %get-tuple-element.122.mixed_ref, bf16[128,1024]{1,0:T(8,128)(2,1)S(1)} %copy-done.10, ...), custom_call_target="tpu_custom_call" | custom-call | flops 2600000000 | bytes 24000000 | tf_op jit(solution)/shard_map/outer/pallas_call | solution.py:649
  631.7 4.3 collective-permute-start.96
  640.0 3.7 fusion.80
  649.1 3.3 collective-permute-start.84
  659.9 3.8 collective-permute-done.70
  673.9 5.7 collective-permute-done.97
  681.7 5.9 collective-permute-done.95
  697.6 5.1 collective-permute-done.85
  709.1 3.3 collective-permute-start.88
  716.4 4.3 collective-permute-done.101
  738.2 4.5 collective-permute-done.89
  752.4 3.3 collective-permute-start.93
  (480 shorter events, 214.3 us)
Async XLA Ops:
  7.2 135.9 %all-gather.3.cloned.1.call-start = ((), (), s32[]{:S(2)}) async-start(), calls=%async_computation | async-start | bytes 21299200 | tf_op jit(solution)/shard_map/all_gather | solution.py:728
  149.6 20.3 %collective-permute-start.8 = (bf16[128,640]{1,0:T(8,128)(2,1)S(1)}, bf16[128,640]{1,0:T(8,128)(2,1)S(1)}, u32[]{:S(2)}, u32[]{:S(2)}) collective-permute-start(bf16[128,640]{1,0:T(8,128)(2,1)S(1)} %get-tuple-element.117), channel_id=1, source_target_pairs={{0,2},{1,3},{2,0},{3,1},{4,6},{5,7},{6,4},{7,5},{8,10},{9,11},{10,... | collective-permute-start | bytes 491528 | tf_op jit(solution)/shard_map/ppermute | solution.py:51
  162.8 14.4 %collective-permute-start.2 = (bf16[64,640]{1,0:T(8,128)(2,1)S(1)}, bf16[64,640]{1,0:T(8,128)(2,1)S(1)}, u32[]{:S(2)}, u32[]{:S(2)}) collective-permute-start(bf16[64,640]{1,0:T(8,128)(2,1)S(1)} %slice.1028), channel_id=1, source_target_pairs={{0,16},{1,17},{2,18},{3,19},{4,20},{5,21},{6,22},{7,23},{8,24},{9,... | collective-permute-start | bytes 245768 | tf_op jit(solution)/shard_map/ppermute | solution.py:51
  165.0 12.2 %collective-permute-start.3 = (bf16[64,640]{1,0:T(8,128)(2,1)S(1)}, bf16[64,640]{1,0:T(8,128)(2,1)S(1)}, u32[]{:S(2)}, u32[]{:S(2)}) collective-permute-start(bf16[64,640]{1,0:T(8,128)(2,1)S(1)} %slice.1029), channel_id=1, source_target_pairs={{0,48},{1,49},{2,50},{3,51},{4,52},{5,53},{6,54},{7,55},{8,56},{9,... | collective-permute-start | bytes 245768 | tf_op jit(solution)/shard_map/ppermute | solution.py:51
  178.4 13.1 %collective-permute-start.11 = (bf16[64,640]{1,0:T(8,128)(2,1)S(1)}, bf16[64,640]{1,0:T(8,128)(2,1)S(1)}, u32[]{:S(2)}, u32[]{:S(2)}) collective-permute-start(bf16[64,640]{1,0:T(8,128)(2,1)S(1)} %slice.1032), channel_id=1, source_target_pairs={{0,4},{1,5},{2,6},{3,7},{4,8},{5,9},{6,10},{7,11},{8,12},{9,13},{1... | collective-permute-start | bytes 245768 | tf_op jit(solution)/shard_map/ppermute | solution.py:51
  180.3 11.1 %collective-permute-start.12 = (bf16[64,640]{1,0:T(8,128)(2,1)S(1)}, bf16[64,640]{1,0:T(8,128)(2,1)S(1)}, u32[]{:S(2)}, u32[]{:S(2)}) collective-permute-start(bf16[64,640]{1,0:T(8,128)(2,1)S(1)} %slice.1033), channel_id=1, source_target_pairs={{0,12},{1,13},{2,14},{3,15},{4,0},{5,1},{6,2},{7,3},{8,4},{9,5},{1... | collective-permute-start | bytes 245768 | tf_op jit(solution)/shard_map/ppermute | solution.py:51
  185.6 12.5 %collective-permute-start.4 = (bf16[4,128,640]{2,1,0:T(8,128)(2,1)S(1)}, bf16[4,128,640]{2,1,0:T(8,128)(2,1)S(1)}, u32[]{:S(2)}, u32[]{:S(2)}) collective-permute-start(bf16[4,128,640]{2,1,0:T(8,128)(2,1)S(1)} %get-tuple-element.248), channel_id=1, source_target_pairs={{0,12},{1,13},{2,14},{3,15},{4,0},{5,1},{6,2},{7,3},{8,4},{9,5},{1... | collective-permute-start | bytes 1966088 | tf_op jit(solution)/shard_map/ppermute | solution.py:51
  187.5 13.8 %collective-permute-start.5 = (bf16[4,128,640]{2,1,0:T(8,128)(2,1)S(1)}, bf16[4,128,640]{2,1,0:T(8,128)(2,1)S(1)}, u32[]{:S(2)}, u32[]{:S(2)}) collective-permute-start(bf16[4,128,640]{2,1,0:T(8,128)(2,1)S(1)} %get-tuple-element.248), channel_id=1, source_target_pairs={{0,4},{1,5},{2,6},{3,7},{4,8},{5,9},{6,10},{7,11},{8,12},{9,13},{1... | collective-permute-start | bytes 1966088 | tf_op jit(solution)/shard_map/ppermute | solution.py:51
  191.6 14.6 %collective-permute-start.13 = (bf16[4,128,640]{2,1,0:T(8,128)(2,1)S(1)}, bf16[4,128,640]{2,1,0:T(8,128)(2,1)S(1)}, u32[]{:S(2)}, u32[]{:S(2)}) collective-permute-start(bf16[4,128,640]{2,1,0:T(8,128)(2,1)S(1)} %get-tuple-element.250), channel_id=1, source_target_pairs={{0,48},{1,49},{2,50},{3,51},{4,52},{5,53},{6,54},{7,55},{8,56},{9,... | collective-permute-start | bytes 1966088 | tf_op jit(solution)/shard_map/ppermute | solution.py:51
  193.9 15.8 %collective-permute-start.14 = (bf16[4,128,640]{2,1,0:T(8,128)(2,1)S(1)}, bf16[4,128,640]{2,1,0:T(8,128)(2,1)S(1)}, u32[]{:S(2)}, u32[]{:S(2)}) collective-permute-start(bf16[4,128,640]{2,1,0:T(8,128)(2,1)S(1)} %get-tuple-element.250), channel_id=1, source_target_pairs={{0,16},{1,17},{2,18},{3,19},{4,20},{5,21},{6,22},{7,23},{8,24},{9,... | collective-permute-start | bytes 1966088 | tf_op jit(solution)/shard_map/ppermute | solution.py:51
  198.1 14.5 %collective-permute-start.7 = (bf16[4,64,640]{2,1,0:T(8,128)(2,1)S(1)}, bf16[4,64,640]{2,1,0:T(8,128)(2,1)S(1)}, u32[]{:S(2)}, u32[]{:S(2)}) collective-permute-start(bf16[4,64,640]{2,1,0:T(8,128)(2,1)S(1)} %slice.1031), channel_id=1, source_target_pairs={{0,12},{1,13},{2,14},{3,15},{4,0},{5,1},{6,2},{7,3},{8,4},{9,5},{1... | collective-permute-start | bytes 983048 | tf_op jit(solution)/shard_map/ppermute | solution.py:51
  201.3 11.3 %collective-permute-start.6 = (bf16[4,64,640]{2,1,0:T(8,128)(2,1)S(1)}, bf16[4,64,640]{2,1,0:T(8,128)(2,1)S(1)}, u32[]{:S(2)}, u32[]{:S(2)}) collective-permute-start(bf16[4,64,640]{2,1,0:T(8,128)(2,1)S(1)} %slice.1030), channel_id=1, source_target_pairs={{0,4},{1,5},{2,6},{3,7},{4,8},{5,9},{6,10},{7,11},{8,12},{9,13},{1... | collective-permute-start | bytes 983048 | tf_op jit(solution)/shard_map/ppermute | solution.py:51
  209.7 10.2 %collective-permute-start.15 = (bf16[4,64,640]{2,1,0:T(8,128)(2,1)S(1)}, bf16[4,64,640]{2,1,0:T(8,128)(2,1)S(1)}, u32[]{:S(2)}, u32[]{:S(2)}) collective-permute-start(bf16[4,64,640]{2,1,0:T(8,128)(2,1)S(1)} %slice.1034), channel_id=1, source_target_pairs={{0,16},{1,17},{2,18},{3,19},{4,20},{5,21},{6,22},{7,23},{8,24},{9,... | collective-permute-start | bytes 983048 | tf_op jit(solution)/shard_map/ppermute | solution.py:51
  379.8 93.2 %collective-permute-start.52 = (bf16[128,960]{1,0:T(8,128)(2,1)S(1)}, bf16[128,960]{1,0:T(8,128)(2,1)S(1)}, u32[]{:S(2)}, u32[]{:S(2)}) collective-permute-start(bf16[128,960]{1,0:T(8,128)(2,1)S(1)} %convert_element_type.697), channel_id=1, source_target_pairs={{64,0},{65,1},{66,2},{67,3},{68,4},{69,5},{70,6},{71,7},{72,8},{73... | collective-permute-start | bytes 737288 | tf_op jit(solution)/shard_map/ppermute | solution.py:786
  517.6 13.1 %collective-permute-start.63 = (bf16[4,64,640]{2,1,0:T(8,128)(2,1)S(1)}, bf16[4,64,640]{2,1,0:T(8,128)(2,1)S(1)}, u32[]{:S(2)}, u32[]{:S(2)}) collective-permute-start(bf16[4,64,640]{2,1,0:T(8,128)(2,1)S(1)} %get-tuple-element.226), channel_id=1, source_target_pairs={{0,48},{1,49},{2,50},{3,51},{4,52},{5,53},{6,54},{7,55},{8,56},{9,... | collective-permute-start | bytes 983048 | tf_op jit(solution)/shard_map/ppermute | solution.py:51
  521.2 14.4 %collective-permute-start.61 = (bf16[4,64,640]{2,1,0:T(8,128)(2,1)S(1)}, bf16[4,64,640]{2,1,0:T(8,128)(2,1)S(1)}, u32[]{:S(2)}, u32[]{:S(2)}) collective-permute-start(bf16[4,64,640]{2,1,0:T(8,128)(2,1)S(1)} %get-tuple-element.225), channel_id=1, source_target_pairs={{0,16},{1,17},{2,18},{3,19},{4,20},{5,21},{6,22},{7,23},{8,24},{9,... | collective-permute-start | bytes 983048 | tf_op jit(solution)/shard_map/ppermute | solution.py:51
  523.7 17.4 %collective-permute-start.53 = (bf16[4,64,640]{2,1,0:T(8,128)(2,1)S(1)}, bf16[4,64,640]{2,1,0:T(8,128)(2,1)S(1)}, u32[]{:S(2)}, u32[]{:S(2)}) collective-permute-start(bf16[4,64,640]{2,1,0:T(8,128)(2,1)S(1)} %get-tuple-element.217), channel_id=1, source_target_pairs={{0,4},{1,5},{2,6},{3,7},{4,8},{5,9},{6,10},{7,11},{8,12},{9,13},{1... | collective-permute-start | bytes 983048 | tf_op jit(solution)/shard_map/ppermute | solution.py:51
  525.9 11.8 %collective-permute-start.55 = (bf16[4,64,640]{2,1,0:T(8,128)(2,1)S(1)}, bf16[4,64,640]{2,1,0:T(8,128)(2,1)S(1)}, u32[]{:S(2)}, u32[]{:S(2)}) collective-permute-start(bf16[4,64,640]{2,1,0:T(8,128)(2,1)S(1)} %get-tuple-element.218), channel_id=1, source_target_pairs={{0,12},{1,13},{2,14},{3,15},{4,0},{5,1},{6,2},{7,3},{8,4},{9,5},{1... | collective-permute-start | bytes 983048 | tf_op jit(solution)/shard_map/ppermute | solution.py:51
  530.9 12.9 %collective-permute-start.64 = (bf16[4,128,640]{2,1,0:T(8,128)(2,1)S(1)}, bf16[4,128,640]{2,1,0:T(8,128)(2,1)S(1)}, u32[]{:S(2)}, u32[]{:S(2)}) collective-permute-start(bf16[4,128,640]{2,1,0:T(8,128)(2,1)S(1)} %pad_maximum_fusion.23), channel_id=1, source_target_pairs={{0,48},{1,49},{2,50},{3,51},{4,52},{5,53},{6,54},{7,55},{8,56},{9,... | collective-permute-start | bytes 1966088 | tf_op jit(solution)/shard_map/ppermute | solution.py:51
  535.7 13.7 %collective-permute-start.62 = (bf16[4,128,640]{2,1,0:T(8,128)(2,1)S(1)}, bf16[4,128,640]{2,1,0:T(8,128)(2,1)S(1)}, u32[]{:S(2)}, u32[]{:S(2)}) collective-permute-start(bf16[4,128,640]{2,1,0:T(8,128)(2,1)S(1)} %pad_maximum_fusion.22), channel_id=1, source_target_pairs={{0,16},{1,17},{2,18},{3,19},{4,20},{5,21},{6,22},{7,23},{8,24},{9,... | collective-permute-start | bytes 1966088 | tf_op jit(solution)/shard_map/ppermute | solution.py:51
  537.8 19.0 %collective-permute-start.56 = (bf16[4,128,640]{2,1,0:T(8,128)(2,1)S(1)}, bf16[4,128,640]{2,1,0:T(8,128)(2,1)S(1)}, u32[]{:S(2)}, u32[]{:S(2)}) collective-permute-start(bf16[4,128,640]{2,1,0:T(8,128)(2,1)S(1)} %pad_maximum_fusion.21), channel_id=1, source_target_pairs={{0,12},{1,13},{2,14},{3,15},{4,0},{5,1},{6,2},{7,3},{8,4},{9,5},{1... | collective-permute-start | bytes 1966088 | tf_op jit(solution)/shard_map/ppermute | solution.py:51
  541.2 15.5 %collective-permute-start.54 = (bf16[4,128,640]{2,1,0:T(8,128)(2,1)S(1)}, bf16[4,128,640]{2,1,0:T(8,128)(2,1)S(1)}, u32[]{:S(2)}, u32[]{:S(2)}) collective-permute-start(bf16[4,128,640]{2,1,0:T(8,128)(2,1)S(1)} %pad_maximum_fusion.20), channel_id=1, source_target_pairs={{0,4},{1,5},{2,6},{3,7},{4,8},{5,9},{6,10},{7,11},{8,12},{9,13},{1... | collective-permute-start | bytes 1966088 | tf_op jit(solution)/shard_map/ppermute | solution.py:51
  549.7 14.5 %collective-permute-start.65 = (bf16[64,640]{1,0:T(8,128)(2,1)S(1)}, bf16[64,640]{1,0:T(8,128)(2,1)S(1)}, u32[]{:S(2)}, u32[]{:S(2)}) collective-permute-start(bf16[64,640]{1,0:T(8,128)(2,1)S(1)} %get-tuple-element.221), channel_id=1, source_target_pairs={{0,4},{1,5},{2,6},{3,7},{4,8},{5,9},{6,10},{7,11},{8,12},{9,13},{1... | collective-permute-start | bytes 245768 | tf_op jit(solution)/shard_map/ppermute | solution.py:51
  551.6 12.5 %collective-permute-start.67 = (bf16[64,640]{1,0:T(8,128)(2,1)S(1)}, bf16[64,640]{1,0:T(8,128)(2,1)S(1)}, u32[]{:S(2)}, u32[]{:S(2)}) collective-permute-start(bf16[64,640]{1,0:T(8,128)(2,1)S(1)} %get-tuple-element.222), channel_id=1, source_target_pairs={{0,12},{1,13},{2,14},{3,15},{4,0},{5,1},{6,2},{7,3},{8,4},{9,5},{1... | collective-permute-start | bytes 245768 | tf_op jit(solution)/shard_map/ppermute | solution.py:51
  557.1 13.1 %collective-permute-start.57 = (bf16[64,640]{1,0:T(8,128)(2,1)S(1)}, bf16[64,640]{1,0:T(8,128)(2,1)S(1)}, u32[]{:S(2)}, u32[]{:S(2)}) collective-permute-start(bf16[64,640]{1,0:T(8,128)(2,1)S(1)} %get-tuple-element.213), channel_id=1, source_target_pairs={{0,16},{1,17},{2,18},{3,19},{4,20},{5,21},{6,22},{7,23},{8,24},{9,... | collective-permute-start | bytes 245768 | tf_op jit(solution)/shard_map/ppermute | solution.py:51
  559.0 11.1 %collective-permute-start.59 = (bf16[64,640]{1,0:T(8,128)(2,1)S(1)}, bf16[64,640]{1,0:T(8,128)(2,1)S(1)}, u32[]{:S(2)}, u32[]{:S(2)}) collective-permute-start(bf16[64,640]{1,0:T(8,128)(2,1)S(1)} %get-tuple-element.214), channel_id=1, source_target_pairs={{0,48},{1,49},{2,50},{3,51},{4,52},{5,53},{6,54},{7,55},{8,56},{9,... | collective-permute-start | bytes 245768 | tf_op jit(solution)/shard_map/ppermute | solution.py:51
  564.2 11.9 %collective-permute-start.68 = (bf16[128,640]{1,0:T(8,128)(2,1)S(1)}, bf16[128,640]{1,0:T(8,128)(2,1)S(1)}, u32[]{:S(2)}, u32[]{:S(2)}) collective-permute-start(bf16[128,640]{1,0:T(8,128)(2,1)S(1)} %pad_maximum_fusion.38), channel_id=1, source_target_pairs={{0,12},{1,13},{2,14},{3,15},{4,0},{5,1},{6,2},{7,3},{8,4},{9,5},{1... | collective-permute-start | bytes 491528 | tf_op jit(solution)/shard_map/ppermute | solution.py:51
  570.2 10.8 %collective-permute-start.60 = (bf16[128,640]{1,0:T(8,128)(2,1)S(1)}, bf16[128,640]{1,0:T(8,128)(2,1)S(1)}, u32[]{:S(2)}, u32[]{:S(2)}) collective-permute-start(bf16[128,640]{1,0:T(8,128)(2,1)S(1)} %pad_maximum_fusion.36), channel_id=1, source_target_pairs={{0,48},{1,49},{2,50},{3,51},{4,52},{5,53},{6,54},{7,55},{8,56},{9,... | collective-permute-start | bytes 491528 | tf_op jit(solution)/shard_map/ppermute | solution.py:51
  631.7 17.4 %collective-permute-start.96 = (bf16[4,4,208,128]{3,2,1,0:T(8,128)(2,1)}, bf16[4,4,208,128]{3,2,1,0:T(8,128)(2,1)}, u32[]{:S(2)}, u32[]{:S(2)}) collective-permute-start(bf16[4,4,208,128]{3,2,1,0:T(8,128)(2,1)} %get-tuple-element.210), channel_id=1, source_target_pairs={{0,3},{1,0},{2,1},{3,2},{4,7},{5,4},{6,5},{7,6},{8,11},{9,8},{10,9... | collective-permute-start | bytes 2555912 | tf_op jit(solution)/shard_map/ppermute | solution.py:51
  639.9 16.6 %collective-permute-start.94 = (bf16[4,4,208,128]{3,2,1,0:T(8,128)(2,1)}, bf16[4,4,208,128]{3,2,1,0:T(8,128)(2,1)}, u32[]{:S(2)}, u32[]{:S(2)}) collective-permute-start(bf16[4,4,208,128]{3,2,1,0:T(8,128)(2,1)} %get-tuple-element.209), channel_id=1, source_target_pairs={{0,1},{1,2},{2,3},{3,0},{4,5},{5,6},{6,7},{7,4},{8,9},{9,10},{10,1... | collective-permute-start | bytes 2555912 | tf_op jit(solution)/shard_map/ppermute | solution.py:51
  645.2 18.5 %collective-permute-start.70 = (bf16[4,4,208,128]{3,2,1,0:T(8,128)(2,1)S(1)}, bf16[4,4,208,128]{3,2,1,0:T(8,128)(2,1)S(1)}, u32[]{:S(2)}, u32[]{:S(2)}) collective-permute-start(bf16[4,4,208,128]{3,2,1,0:T(8,128)(2,1)S(1)} %copy-done.27), channel_id=1, source_target_pairs={{0,16},{1,17},{2,18},{3,19},{4,20},{5,21},{6,22},{7,23},{8,24},{9,... | collective-permute-start | bytes 2555912 | tf_op jit(solution)/shard_map/ppermute | solution.py:51
  645.3 20.5 %collective-permute-start.72 = (bf16[4,4,224,128]{3,2,1,0:T(8,128)(2,1)S(1)}, bf16[4,4,224,128]{3,2,1,0:T(8,128)(2,1)S(1)}, u32[]{:S(2)}, u32[]{:S(2)}) collective-permute-start(bf16[4,4,224,128]{3,2,1,0:T(8,128)(2,1)S(1)} %slice.1106), channel_id=1, source_target_pairs={{0,48},{1,49},{2,50},{3,51},{4,52},{5,53},{6,54},{7,55},{8,56},{9,... | collective-permute-start | bytes 2752520 | tf_op jit(solution)/shard_map/ppermute | solution.py:51
  648.8 18.7 %collective-permute-start.82 = (bf16[4,4,208,128]{3,2,0,1:T(8,128)(2,1)S(1)}, bf16[4,4,208,128]{3,2,0,1:T(8,128)(2,1)S(1)}, u32[]{:S(2)}, u32[]{:S(2)}) collective-permute-start(bf16[4,4,208,128]{3,2,0,1:T(8,128)(2,1)S(1)} %slice.1128), channel_id=1, source_target_pairs={{0,4},{1,5},{2,6},{3,7},{4,8},{5,9},{6,10},{7,11},{8,12},{9,13},{1... | collective-permute-start | bytes 2555912 | tf_op jit(solution)/shard_map/ppermute | solution.py:51
  649.1 23.3 %collective-permute-start.84 = (bf16[4,4,224,128]{3,2,0,1:T(8,128)(2,1)S(1)}, bf16[4,4,224,128]{3,2,0,1:T(8,128)(2,1)S(1)}, u32[]{:S(2)}, u32[]{:S(2)}) collective-permute-start(bf16[4,4,224,128]{3,2,0,1:T(8,128)(2,1)S(1)} %slice.1133), channel_id=1, source_target_pairs={{0,12},{1,13},{2,14},{3,15},{4,0},{5,1},{6,2},{7,3},{8,4},{9,5},{1... | collective-permute-start | bytes 2752520 | tf_op jit(solution)/shard_map/ppermute | solution.py:51
  656.5 23.2 %collective-permute-start.97 = (bf16[4,4,416,128]{3,2,1,0:T(8,128)(2,1)S(1)}, bf16[4,4,416,128]{3,2,1,0:T(8,128)(2,1)}, u32[]{:S(2)}, u32[]{:S(2)}) collective-permute-start(bf16[4,4,416,128]{3,2,1,0:T(8,128)(2,1)S(1)} %pad_maximum_fusion.11), channel_id=1, source_target_pairs={{0,3},{1,0},{2,1},{3,2},{4,7},{5,4},{6,5},{7,6},{8,11},{9,8},{10,9... | collective-permute-start | bytes 5111816 | tf_op jit(solution)/shard_map/ppermute | solution.py:51
  663.7 23.9 %collective-permute-start.95 = (bf16[4,4,416,128]{3,2,1,0:T(8,128)(2,1)}, bf16[4,4,416,128]{3,2,1,0:T(8,128)(2,1)}, u32[]{:S(2)}, u32[]{:S(2)}) collective-permute-start(bf16[4,4,416,128]{3,2,1,0:T(8,128)(2,1)} %pad_maximum_fusion.10), channel_id=1, source_target_pairs={{0,1},{1,2},{2,3},{3,0},{4,5},{5,6},{6,7},{7,4},{8,9},{9,10},{10,1... | collective-permute-start | bytes 5111816 | tf_op jit(solution)/shard_map/ppermute | solution.py:51
  665.8 25.2 %collective-permute-start.71 = (bf16[4,4,432,128]{3,2,1,0:T(8,128)(2,1)}, bf16[4,4,432,128]{3,2,1,0:T(8,128)(2,1)}, u32[]{:S(2)}, u32[]{:S(2)}) collective-permute-start(bf16[4,4,432,128]{3,2,1,0:T(8,128)(2,1)} %pad_maximum_fusion.6), channel_id=1, source_target_pairs={{0,16},{1,17},{2,18},{3,19},{4,20},{5,21},{6,22},{7,23},{8,24},{9,... | collective-permute-start | bytes 5308424 | tf_op jit(solution)/shard_map/ppermute | solution.py:51
  667.5 26.8 %collective-permute-start.73 = (bf16[4,4,432,128]{3,2,1,0:T(8,128)(2,1)}, bf16[4,4,432,128]{3,2,1,0:T(8,128)(2,1)}, u32[]{:S(2)}, u32[]{:S(2)}) collective-permute-start(bf16[4,4,432,128]{3,2,1,0:T(8,128)(2,1)} %pad_maximum_fusion.7), channel_id=1, source_target_pairs={{0,48},{1,49},{2,50},{3,51},{4,52},{5,53},{6,54},{7,55},{8,56},{9,... | collective-permute-start | bytes 5308424 | tf_op jit(solution)/shard_map/ppermute | solution.py:51
  672.3 25.3 %collective-permute-start.83 = (bf16[4,4,432,128]{3,2,0,1:T(8,128)(2,1)}, bf16[4,4,432,128]{3,2,0,1:T(8,128)(2,1)}, u32[]{:S(2)}, u32[]{:S(2)}) collective-permute-start(bf16[4,4,432,128]{3,2,0,1:T(8,128)(2,1)} %pad_maximum_fusion.8), channel_id=1, source_target_pairs={{0,4},{1,5},{2,6},{3,7},{4,8},{5,9},{6,10},{7,11},{8,12},{9,13},{1... | collective-permute-start | bytes 5308424 | tf_op jit(solution)/shard_map/ppermute | solution.py:51
  679.7 23.0 %collective-permute-start.85 = (bf16[4,4,432,128]{3,2,0,1:T(8,128)(2,1)}, bf16[4,4,432,128]{3,2,0,1:T(8,128)(2,1)}, u32[]{:S(2)}, u32[]{:S(2)}) collective-permute-start(bf16[4,4,432,128]{3,2,0,1:T(8,128)(2,1)} %pad_maximum_fusion.9), channel_id=1, source_target_pairs={{0,12},{1,13},{2,14},{3,15},{4,0},{5,1},{6,2},{7,3},{8,4},{9,5},{1... | collective-permute-start | bytes 5308424 | tf_op jit(solution)/shard_map/ppermute | solution.py:51
  690.9 21.6 %collective-permute-start.98 = (bf16[4,208,128]{2,1,0:T(8,128)(2,1)S(1)}, bf16[4,208,128]{2,1,0:T(8,128)(2,1)S(1)}, u32[]{:S(2)}, u32[]{:S(2)}) collective-permute-start(bf16[4,208,128]{2,1,0:T(8,128)(2,1)S(1)} %get-tuple-element.265), channel_id=1, source_target_pairs={{0,16},{1,17},{2,18},{3,19},{4,20},{5,21},{6,22},{7,23},{8,24},{9,... | collective-permute-start | bytes 638984 | tf_op jit(solution)/shard_map/ppermute | solution.py:51
  691.0 18.1 %collective-permute-start.100 = (bf16[4,208,128]{2,1,0:T(8,128)(2,1)S(1)}, bf16[4,208,128]{2,1,0:T(8,128)(2,1)S(1)}, u32[]{:S(2)}, u32[]{:S(2)}) collective-permute-start(bf16[4,208,128]{2,1,0:T(8,128)(2,1)S(1)} %get-tuple-element.266), channel_id=1, source_target_pairs={{0,48},{1,49},{2,50},{3,51},{4,52},{5,53},{6,54},{7,55},{8,56},{9,... | collective-permute-start | bytes 638984 | tf_op jit(solution)/shard_map/ppermute | solution.py:51
  706.2 10.0 %collective-permute-start.76 = (bf16[4,224,128]{2,1,0:T(8,128)(2,1)S(1)}, bf16[4,224,128]{2,1,0:T(8,128)(2,1)S(1)}, u32[]{:S(2)}, u32[]{:S(2)}) collective-permute-start(bf16[4,224,128]{2,1,0:T(8,128)(2,1)S(1)} %slice.1116), channel_id=1, source_target_pairs={{0,12},{1,13},{2,14},{3,15},{4,0},{5,1},{6,2},{7,3},{8,4},{9,5},{1... | collective-permute-start | bytes 688136 | tf_op jit(solution)/shard_map/ppermute | solution.py:51
  709.1 14.0 %collective-permute-start.88 = (bf16[4,224,128]{2,1,0:T(8,128)(2,1)S(1)}, bf16[4,224,128]{2,1,0:T(8,128)(2,1)S(1)}, u32[]{:S(2)}, u32[]{:S(2)}) collective-permute-start(bf16[4,224,128]{2,1,0:T(8,128)(2,1)S(1)} %slice.1143), channel_id=1, source_target_pairs={{0,3},{1,0},{2,1},{3,2},{4,7},{5,4},{6,5},{7,6},{8,11},{9,8},{10,9... | collective-permute-start | bytes 688136 | tf_op jit(solution)/shard_map/ppermute | solution.py:51
  716.1 21.8 %collective-permute-start.75 = (bf16[4,432,128]{2,1,0:T(8,128)(2,1)S(1)}, bf16[4,432,128]{2,1,0:T(8,128)(2,1)S(1)}, u32[]{:S(2)}, u32[]{:S(2)}) collective-permute-start(bf16[4,432,128]{2,1,0:T(8,128)(2,1)S(1)} %pad_maximum_fusion.25), channel_id=1, source_target_pairs={{0,4},{1,5},{2,6},{3,7},{4,8},{5,9},{6,10},{7,11},{8,12},{9,13},{1... | collective-permute-start | bytes 1327112 | tf_op jit(solution)/shard_map/ppermute | solution.py:51
  716.2 22.0 %collective-permute-start.87 = (bf16[4,432,128]{2,1,0:T(8,128)(2,1)S(1)}, bf16[4,432,128]{2,1,0:T(8,128)(2,1)S(1)}, u32[]{:S(2)}, u32[]{:S(2)}) collective-permute-start(bf16[4,432,128]{2,1,0:T(8,128)(2,1)S(1)} %pad_maximum_fusion.27), channel_id=1, source_target_pairs={{0,1},{1,2},{2,3},{3,0},{4,5},{5,6},{6,7},{7,4},{8,9},{9,10},{10,1... | collective-permute-start | bytes 1327112 | tf_op jit(solution)/shard_map/ppermute | solution.py:51
  720.7 17.2 %collective-permute-start.77 = (bf16[4,432,128]{2,1,0:T(8,128)(2,1)S(1)}, bf16[4,432,128]{2,1,0:T(8,128)(2,1)S(1)}, u32[]{:S(2)}, u32[]{:S(2)}) collective-permute-start(bf16[4,432,128]{2,1,0:T(8,128)(2,1)S(1)} %pad_maximum_fusion.26), channel_id=1, source_target_pairs={{0,12},{1,13},{2,14},{3,15},{4,0},{5,1},{6,2},{7,3},{8,4},{9,5},{1... | collective-permute-start | bytes 1327112 | tf_op jit(solution)/shard_map/ppermute | solution.py:51
  738.1 10.4 %collective-permute-start.78 = (bf16[208,128]{1,0:T(8,128)(2,1)S(1)}, bf16[208,128]{1,0:T(8,128)(2,1)S(1)}, u32[]{:S(2)}, u32[]{:S(2)}) collective-permute-start(bf16[208,128]{1,0:T(8,128)(2,1)S(1)} %get-tuple-element.251), channel_id=1, source_target_pairs={{0,1},{1,2},{2,3},{3,0},{4,5},{5,6},{6,7},{7,4},{8,9},{9,10},{10,1... | collective-permute-start | bytes 159752 | tf_op jit(solution)/shard_map/ppermute | solution.py:51
  (93 other events, 556.5 us)
Sparse Core Ops, SparseCore 0:
  18.4 124.5 all-gather.2

commit v2 on v1

--- a/solution.py
+++ b/solution.py
@@ -20,6 +20,9 @@
 KEYS = 4096
 CHUNK = 512
 PADD = 1024
+SIDE = 3
+QSIDE = SIDE * GRP * HD
+QPAD = 2 * QSIDE
 
 eps = 1e-05
 rope_theta = 100000.0
@@ -39,118 +42,113 @@
     return lax.dot_general(a, b, NT, preferred_element_type=f32)
 
 
-def moved(block, shift, phases):
-    dy, dx, dz = shift
+STEPS = ((1, 3), (3, 1))
+
+
+def swapped(block, way):
     pairs = []
-    for p in phases:
+    for p in range(2):
+        dy, dx, dz = way(p)
         for y in range(4):
             for x in range(4):
                 for z in range(4):
-                    to = (((y + dy) % 4) * 4 + (x + dx) % 4) * 4 + (z + dz) % 4
+                    to = ((y ^ dy) * 4 + (x ^ dx)) * 4 + (z ^ dz)
                     pairs.append((p * 64 + (y * 4 + x) * 4 + z, p * 64 + to))
     return lax.ppermute(block, ALL, pairs)
 
 
-def unit(axis, step):
-    shift = [0, 0, 0]
-    shift[axis] = step
-    return tuple(shift)
-
-
-def ring_gather(block, axis, phases, half):
-    low, high = half
-    from_prev = moved(block, unit(axis, 1), phases)
-    from_next = moved(block, unit(axis, -1), phases)
-    far_low = moved(low(from_prev), unit(axis, 1), phases)
-    far_high = moved(high(from_next), unit(axis, -1), phases)
-    return from_next, far_low, far_high, from_prev
-
-
-def ring_scatter(parts, axis, phases, half, joined):
-    low, high = half
-    add = lambda a, b: (a.astype(f32) + b.astype(f32)).astype(bf16)
-    far_low = moved(low(parts[2]), unit(axis, 1), phases)
-    far_high = moved(high(parts[2]), unit(axis, -1), phases)
-    up = joined(add(low(parts[1]), far_low), high(parts[1]))
-    down = joined(low(parts[3]), add(high(parts[3]), far_high))
-    got_up = moved(up, unit(axis, 1), phases)
-    got_down = moved(down, unit(axis, -1), phases)
-    return parts[0].astype(f32) + got_up.astype(f32) + got_down.astype(f32)
-
-
-def halves(dim, at):
-    low = lambda v: lax.slice_in_dim(v, 0, at, axis=dim)
-    high = lambda v: lax.slice_in_dim(v, at, v.shape[dim], axis=dim)
-    return low, high
-
-
-def gather_keys(kv, phases):
-    half = halves(kv.ndim - 2, R // 2)
-
-    def ring(block, axis):
-        dim = block.ndim - 2
-        nxt, flow, fhigh, prev = ring_gather(block, axis, phases, halves(dim, R // 2))
-        return jnp.stack([block, nxt, jnp.concatenate([flow, fhigh], axis=dim), prev])
-
-    far = moved(kv, (0, 0, 2), phases)
-    first = ring(ring(kv, 0), 1)
-    second = ring(ring(far, 1), 0)
-    return jnp.concatenate(
-        [first.reshape(16, R, 2 * KVH * HD), second.reshape(16, R, 2 * KVH * HD)]
-    ).reshape(KEYS, 2 * KVH * HD)
-
-
-def key_order(y, x, zh):
-    order = []
-    for bx in range(4):
-        for by in range(4):
-            order.append(((y + by) % 4) * 8 + ((x + bx) % 4) * 2 + zh)
-    for by in range(4):
-        for bx in range(4):
-            order.append(((y + by) % 4) * 8 + ((x + bx) % 4) * 2 + (1 - zh))
-    return jnp.stack(order)
-
-
-def scatter_keys(d_kv, phases):
-    parts = d_kv.reshape(2, 4, 4, R, 2 * KVH * HD)
-
-    def ring(block, axis):
-        dim = block.ndim - 3
-        joined = lambda a, b: jnp.concatenate([a, b], axis=dim)
-        return ring_scatter(
-            [block[o] for o in range(4)], axis, phases, halves(dim, R // 2), joined
-        )
-
-    first = ring(ring(parts[0], 1).astype(bf16), 0)
-    second = ring(ring(parts[1], 0).astype(bf16), 1)
-    return first + moved(second.astype(bf16), (0, 0, 2), phases).astype(f32)
+def over(block, source):
+    return lax.ppermute(block, "phase", [(source, 1 - source)])
+
+
+def along(axes, number):
+    def way(p):
+        shift = [0, 0, 0]
+        shift[axes[p]] = STEPS[p][number]
+        return tuple(shift)
+
+    return way
+
+
+def far_z(p):
+    return (0, 0, 2)
+
+
+def gather_keys(kv):
+    tail = kv.shape
+    far = swapped(kv, far_z)
+    near = kv
+    orders = (((0, 1), (1, 0)), ((1, 0), (0, 1)))
+    blocks = [near[None], far[None]]
+    for leg in range(2):
+        for number in range(2):
+            for k in range(2):
+                got = swapped(blocks[k], along(orders[k][leg], number))
+                blocks[k] = jnp.concatenate([blocks[k], got], axis=0)
+    return jnp.concatenate(blocks, axis=0).reshape(KEYS, tail[1])
+
+
+def scatter_keys(d_kv):
+    parts = d_kv.reshape(2, 16, R, d_kv.shape[1])
+    orders = (((0, 1), (1, 0)), ((1, 0), (0, 1)))
+    blocks = [parts[0], parts[1]]
+    for leg in (1, 0):
+        for number in (1, 0):
+            for k in (1, 0):
+                half = blocks[k].shape[0] // 2
+                got = swapped(blocks[k][half:], along(orders[k][leg], number))
+                total = blocks[k][:half].astype(f32) + got.astype(f32)
+                last = k == 0 and half == 1
+                blocks[k] = total if last else total.astype(bf16)
+    return blocks[0][0] + swapped(blocks[1][0], far_z).astype(f32)
+
+
+def slot_offsets(phase):
+    return jnp.where(phase == 0, jnp.array([0, 1, 3, 2]), jnp.array([0, 3, 1, 2]))
+
+
+def slot_of(offset, phase):
+    at = jnp.where(phase == 0, jnp.array([0, 1, 3, 2]), jnp.array([0, 2, 3, 1]))
+    return at[offset]
+
+
+def key_order(y, x, zh, phase):
+    off = slot_offsets(phase)
+    outer = jnp.repeat(off, 4)
+    inner = jnp.tile(off, 4)
+    out = []
+    for k in range(2):
+        first_y = phase == k
+        oy = jnp.where(first_y, inner, outer)
+        ox = jnp.where(first_y, outer, inner)
+        out.append((y ^ oy) * 8 + (x ^ ox) * 2 + (zh ^ k))
+    return jnp.concatenate(out)
 
 
 PART_ROWS = ((0, 432), (432, 864), (864, 1280))
 
 
 def scatter_grads(rel):
-    both = (0, 1)
-    out = []
-    for part, (begin, end) in enumerate(PART_ROWS):
-        block = rel[:, :, :, begin:end]
-        count = end - begin
-        at = count // 32 * 16
-        left = [0, 1, 2]
-        for step in range(3):
-            axis = (part + step) % 3
-            where_axis = left.index(axis)
-            left.remove(axis)
-            pieces = [
-                lax.index_in_dim(block, o, axis=where_axis, keepdims=False) for o in range(4)
-            ]
-            dim = pieces[0].ndim - 2
-            joined = lambda a, b, dim=dim: jnp.concatenate([a, b], axis=dim)
-            block = ring_scatter(pieces, axis, both, halves(dim, at), joined)
-            if step < 2:
-                block = block.astype(bf16)
-        out.append(block)
-    return jnp.concatenate(out)
+    blocks = [rel[:, :, :, begin:end] for begin, end in PART_ROWS]
+    left = [[0, 1, 2], [0, 1, 2], [0, 1, 2]]
+    for leg in range(3):
+        for number in (1, 0):
+            for part in range(3):
+                axis = (part + leg) % 3
+                dim = left[part].index(axis)
+                block = blocks[part]
+                half = block.shape[dim] // 2
+                keep = lax.slice_in_dim(block, 0, half, axis=dim)
+                send = lax.slice_in_dim(block, half, 2 * half, axis=dim)
+                got = swapped(send, along((axis, axis), number))
+                total = keep.astype(f32) + got.astype(f32)
+                if number == 0:
+                    total = lax.squeeze(total, (dim,))
+                    left[part].remove(axis)
+                if leg < 2 or number:
+                    total = total.astype(bf16)
+                blocks[part] = total
+    return jnp.concatenate(blocks)
 
 
 def lane_of(shape):
@@ -191,6 +189,8 @@
         t = (blocks[c].astype(bf16).astype(f32) * 0.125).T.astype(bf16)
         count = 128 if c < 7 else 64
         qt_ref[128 * c : 128 * c + count, :] = t[:count]
+    qt_ref[D:, :] = jnp.zeros((QPAD - D, R), bf16)
+    kv_ref[:, 640:] = jnp.zeros((R, 128), bf16)
     lane = lane_of((R, 128))
     for g in range(KVH):
         k, v = blocks[(15 + g) // 2], blocks[(20 + g) // 2]
@@ -214,12 +214,12 @@
             pl.BlockSpec((10, ROWS, 128), lambda i: (0, 0, 0)),
         ],
         out_specs=[
-            pl.BlockSpec((D, R), lambda i: (0, 0)),
-            pl.BlockSpec((R, 640), lambda i: (0, 0)),
+            pl.BlockSpec((QPAD, R), lambda i: (0, 0)),
+            pl.BlockSpec((R, 768), lambda i: (0, 0)),
         ],
         out_shape=[
-            jax.ShapeDtypeStruct((D, R), bf16),
-            jax.ShapeDtypeStruct((R, 640), bf16),
+            jax.ShapeDtypeStruct((QPAD, R), bf16),
+            jax.ShapeDtypeStruct((R, 768), bf16),
         ],
         compiler_params=pltpu.CompilerParams(vmem_limit_bytes=48 << 20),
         cost_estimate=pl.CostEstimate(flops=400_000_000, bytes_accessed=4_000_000, transcendentals=0),
@@ -258,7 +258,7 @@
     return pl.pallas_call(
         attend_kernel,
         name="attend",
-        grid=(KVH,),
+        grid=(SIDE,),
         in_specs=[
             pl.BlockSpec((GRP * HD, R), lambda g: (g, 0)),
             pl.BlockSpec((KEYS, 128), lambda g: (0, g)),
@@ -269,8 +269,8 @@
             pl.BlockSpec((1, 1, GRP * R), lambda g: (g, 0, 0)),
         ],
         out_shape=[
-            jax.ShapeDtypeStruct((D, R), bf16),
-            jax.ShapeDtypeStruct((KVH, 1, GRP * R), f32),
+            jax.ShapeDtypeStruct((QSIDE, R), bf16),
+            jax.ShapeDtypeStruct((SIDE, 1, GRP * R), f32),
         ],
         scratch_shapes=[pltpu.VMEM((KEYS, GRP * R), f32)],
         compiler_params=pltpu.CompilerParams(vmem_limit_bytes=48 << 20),
@@ -442,7 +442,8 @@
                 [out_weight((o0, o1, o2), c), out_weight((o0, o1, o2), c + 1)], axis=1
             )
             d_mixed = d_mixed + mm_nt(dhb_ref[:, 128 * c : 128 * c + 256], w)
-        dot_ref[...] = d_mixed.T
+        dot_ref[:D, :] = d_mixed.T
+        dot_ref[D:, :] = jnp.zeros((QPAD - D, R), f32)
 
 
 def feed_back(cot, gate, up, hidden, gain, pad, gathered):
@@ -460,7 +461,7 @@
             whole(R, D),
             whole(R, PADD),
             whole(1, D),
-            whole(D, R),
+            whole(QPAD, R),
             whole(R, PADD),
         ],
         out_shape=[
@@ -469,7 +470,7 @@
             jax.ShapeDtypeStruct((R, D), f32),
             jax.ShapeDtypeStruct((R, PADD), bf16),
             jax.ShapeDtypeStruct((1, D), f32),
-            jax.ShapeDtypeStruct((D, R), f32),
+            jax.ShapeDtypeStruct((QPAD, R), f32),
             jax.ShapeDtypeStruct((R, PADD), bf16),
         ],
         scratch_shapes=[pltpu.VMEM((R, PADD), f32)],
@@ -509,7 +510,7 @@
     return pl.pallas_call(
         attend_back_kernel,
         name="attend_back",
-        grid=(KVH,),
+        grid=(SIDE,),
         in_specs=[
             heads,
             pl.BlockSpec((KEYS, 128), lambda g: (0, g)),
@@ -520,8 +521,8 @@
         ],
         out_specs=[pl.BlockSpec((KEYS, 128), lambda g: (0, g)), heads],
         out_shape=[
-            jax.ShapeDtypeStruct((KEYS, 640), bf16),
-            jax.ShapeDtypeStruct((D, R), f32),
+            jax.ShapeDtypeStruct((KEYS, SIDE * 128), bf16),
+            jax.ShapeDtypeStruct((QSIDE, R), f32),
         ],
         compiler_params=pltpu.CompilerParams(vmem_limit_bytes=48 << 20),
         cost_estimate=pl.CostEstimate(
@@ -596,71 +597,91 @@
 
 
 def outer_kernel(
-    place_ref, at_ref, dqkv_ref, mixed_ref, dhb_ref, nt_ref, dgate_ref, dup_ref, mt_ref, cb_ref,
-    gain_ref, out_ref,
+    place_ref, slot_ref, at_ref, dqkv_ref, mixed_ref, dhb_ref, nt_ref, dgate_ref, dup_ref, mt_ref,
+    cb_ref, gain_ref, out_ref,
 ):
-    shard = pl.program_id(0)
-    gains = gain_ref[pl.ds(shard, 1), :]
-
-    def row_of(count, at):
+    step = pl.program_id(0)
+
+    def row_of(k, count, at):
         row = lax.broadcasted_iota(jnp.int32, (count, 128), 0)
-        return jnp.where(row == at, gains, 0.0)
-
-    @pl.when(shard < 10)
+        return jnp.where(row == at, gain_ref[pl.ds(4 * step + k, 1), :], 0.0)
+
+    def narrow(start, ks):
+        count = len(ks)
+        rows = at_ref[pl.ds(pl.multiple_of(start, 32), 96 * count), :]
+        for c in range(0, 13, 2):
+            width = min(256, 1664 - 128 * c)
+            res = mm(rows, dqkv_ref[:, 128 * c : 128 * c + width])
+            for i, k in enumerate(ks):
+                for h in range(width // 128):
+                    out_ref[0, slot_ref[k], 96 * (c + h) : 96 * (c + h) + 96, :] = res[
+                        96 * i : 96 * i + 96, 128 * h : 128 * h + 128
+                    ].astype(bf16)
+        for k in ks:
+            out_ref[0, slot_ref[k], 1248:1280, :] = row_of(k, 32, 0).astype(bf16)
+
+    def wide(ref, start, cot_ref, ks):
+        rows = ref[pl.ds(pl.multiple_of(start, 32), 160 * len(ks)), :]
+        for c in range(0, 8, 2):
+            res = mm(rows, cot_ref[:, 128 * c : 128 * c + 256])
+            for i, k in enumerate(ks):
+                for h in range(2):
+                    b = res[160 * i : 160 * i + 160, 128 * h : 128 * h + 128]
+                    if c + h == 7:
+                        b = b + row_of(k, 160, 0)
+                    at = 160 * (c + h)
+                    out_ref[0, slot_ref[k], at : at + 160, :] = b.astype(bf16)
+
+    @pl.when(step < 2)
     def _():
-        rows = at_ref[pl.ds(pl.multiple_of(96 * shard, 32), 96), :]
-        res = mm(rows, dqkv_ref[...])
-        for c in range(13):
-            out_ref[0, 96 * c : 96 * c + 96, :] = res[:, 128 * c : 128 * c + 128].astype(bf16)
-        out_ref[0, 1248:1280, :] = row_of(32, 0).astype(bf16)
-
-    def wide(rows, cot):
-        res = mm(rows, cot)
-        for c in range(8):
-            b = res[:, 128 * c : 128 * c + 128]
-            if c == 7:
-                b = b + row_of(160, 0)
-            out_ref[0, 160 * c : 160 * c + 160, :] = b.astype(bf16)
-
-    @pl.when((shard >= 10) & (shard < 16))
+        narrow(384 * step, (0, 1, 2, 3))
+
+    @pl.when(step == 2)
     def _():
-        wide(mixed_ref[pl.ds(pl.multiple_of(160 * (shard - 10), 32), 160), :], dhb_ref[...])
-
-    @pl.when((shard >= 16) & (shard < 48))
+        narrow(768, (0, 1))
+        wide(mixed_ref, 0, dhb_ref, (2, 3))
+
+    @pl.when(step == 3)
     def _():
-        rows = nt_ref[pl.ds(pl.multiple_of(32 * (shard - 16), 32), 32), :]
+        wide(mixed_ref, 320, dhb_ref, (0, 1, 2, 3))
+
+    @pl.when((step >= 4) & (step < 12))
+    def _():
+        rows = nt_ref[pl.ds(pl.multiple_of(128 * (step - 4), 128), 128), :]
         for part, ref in enumerate((dgate_ref, dup_ref)):
-            res = mm(rows, ref[...])
-            for c in range(20):
-                b = res[:, 128 * c : 128 * c + 128]
-                at = 32 * (20 * part + c)
-                if part == 0 and c == 0:
-                    b = b + row_of(32, 30)
-                out_ref[0, at : at + 32, :] = b.astype(bf16)
-
-    @pl.when(shard >= 48)
+            for c in range(0, 20, 2):
+                res = mm(rows, ref[:, 128 * c : 128 * c + 256])
+                for k in range(4):
+                    for h in range(2):
+                        b = res[32 * k : 32 * k + 32, 128 * h : 128 * h + 128]
+                        at = 32 * (20 * part + c + h)
+                        if at == 0:
+                            b = b + row_of(k, 32, 30)
+                        out_ref[0, slot_ref[k], at : at + 32, :] = b.astype(bf16)
+
+    @pl.when(step >= 12)
     def _():
-        wide(mt_ref[pl.ds(pl.multiple_of(160 * (shard - 48), 32), 160), :], cb_ref[...])
-
-
-def outer(places, at, dqkv, mixed, dhb, nt, dgate, dup, mt, cb, gains):
-    whole = lambda v: pl.BlockSpec(v.shape, lambda s, place: (0,) * v.ndim)
+        wide(mt_ref, 640 * (step - 12), cb_ref, (0, 1, 2, 3))
+
+
+def outer(places, slots, at, dqkv, mixed, dhb, nt, dgate, dup, mt, cb, gains):
+    whole = lambda v: pl.BlockSpec(v.shape, lambda s, place, slot: (0,) * v.ndim)
     args = (at, dqkv, mixed, dhb, nt, dgate, dup, mt, cb, gains)
     return pl.pallas_call(
         outer_kernel,
         name="outer",
         grid_spec=pltpu.PrefetchScalarGridSpec(
-            num_scalar_prefetch=1,
-            grid=(SHARDS,),
+            num_scalar_prefetch=2,
+            grid=(16,),
             in_specs=[whole(v) for v in args],
-            out_specs=pl.BlockSpec((1, ROWS, 128), lambda s, place: (place[s], 0, 0)),
+            out_specs=pl.BlockSpec((1, 4, ROWS, 128), lambda s, place, slot: (place[s], 0, 0, 0)),
         ),
-        out_shape=jax.ShapeDtypeStruct((SHARDS, ROWS, 128), bf16),
+        out_shape=jax.ShapeDtypeStruct((16, 4, ROWS, 128), bf16),
         compiler_params=pltpu.CompilerParams(vmem_limit_bytes=48 << 20),
         cost_estimate=pl.CostEstimate(
             flops=2_600_000_000, bytes_accessed=24_000_000, transcendentals=0
         ),
-    )(places, *args)
+    )(places, slots, *args)
 
 
 def shard_kind(rank):
@@ -738,7 +759,7 @@
         ]
     )
     start_q = jnp.sum((seg_row[:, None] < seg_q[None, :]).astype(jnp.int32), axis=0)
-    pairs_k = block_pair[key_order(y, x, zh)]
+    pairs_k = block_pair[key_order(y, x, zh, phase)]
     place_k = (
         jnp.stack([pairs_k, 63 - pairs_k], axis=1)[:, :, None] * 64 + within[None, None, :]
     ).reshape(KEYS)
@@ -760,31 +781,44 @@
     first = phase == 0
 
     u = layer_in[0]
-    kv_all = None
+    mixed = None
+    kept = []
     for tick in range(2):
+        active = phase == tick
         qt, kv = project(u, gain_one, cos, sin, gathered)
-        fetched = gather_keys(kv, (tick,))
-        kv_all = fetched if tick == 0 else jnp.where(first, kv_all, fetched)
-        mixed, lse = attend(qt, kv_all, bias)
+        kv_side = jnp.where(active, kv[:, :384], over(kv[:, 384:], tick))
+        qt_side = jnp.where(active, qt[:QSIDE], over(qt[QSIDE:], tick))
+        kv_all = gather_keys(kv_side)
+        mixed_side, lse = attend(qt_side, kv_all, bias)
+        kept.append((qt_side, kv_all, mixed_side, lse))
+        far = over(mixed_side[: D - QSIDE], 1 - tick)
+        whole = jnp.concatenate([mixed_side, far])
+        mixed = whole if tick == 0 else jnp.where(active, whole, mixed)
         result, hidden, nt, gate, up, mt = feed(mixed, u, gain_two, pad, gathered)
         if tick == 0:
-            u = jnp.where(first, u, lax.ppermute(result, "phase", [(0, 1)]))
+            u = jnp.where(first, u, over(result, 0))
 
     cot = out_grad[0]
-    kept = None
+    d_query = d_kv = None
     for tick in range(2):
+        layer = 1 - tick
+        active = phase == layer
+        qt_side, kv_all, mixed_side, lse = kept[layer]
         dgate, dup, dh, dhb, dg_two, d_mixed, cb = feed_back(
             cot, gate, up, hidden, gain_two, pad, gathered
         )
-        d_kv_all, d_query = attend_back(qt, kv_all, bias, d_mixed, mixed, lse)
-        d_kv = scatter_keys(d_kv_all, (1 - tick,))
-        kept = d_kv if tick == 0 else jnp.where(first, d_kv, kept)
+        d_side = jnp.where(active, d_mixed[:QSIDE], over(d_mixed[QSIDE:], layer))
+        d_kv_all, dq_side = attend_back(qt_side, kv_all, bias, d_side, mixed_side, lse)
+        dq_new = jnp.concatenate([dq_side, over(dq_side[: D - QSIDE], tick)])
+        dkv_side = scatter_keys(d_kv_all)
+        dkv_new = jnp.concatenate([dkv_side, over(dkv_side[:, :256], tick)], axis=1)
+        d_query = dq_new if tick == 0 else jnp.where(active, dq_new, d_query)
+        d_kv = dkv_new if tick == 0 else jnp.where(active, dkv_new, d_kv)
         d_u, dqkv, at, dg_one = project_back(
-            d_query, kept, cos, sin, u, gain_one, dh, gathered
+            d_query, d_kv, cos, sin, u, gain_one, dh, gathered
         )
         if tick == 0:
-            back = lax.ppermute(d_u.astype(bf16), "phase", [(1, 0)])
-            cot = jnp.where(first, back.astype(f32), cot)
+            cot = jnp.where(first, over(d_u.astype(bf16), 1).astype(f32), cot)
 
     gains = jnp.concatenate([dg_one, dg_two], axis=1).reshape(SHARDS, 30)
     shards = jnp.arange(SHARDS, dtype=jnp.int32)
@@ -792,9 +826,10 @@
     gains = jnp.where(
         square, jnp.pad(gains, ((0, 0), (64, 34))), jnp.pad(gains, ((0, 0), (0, 98)))
     )
-    sy, sx, sz = shards // 16, (shards // 4) % 4, shards % 4
-    places = ((sy - y) % 4) * 16 + ((sx - x) % 4) * 4 + (sz - z) % 4
-    grads = outer(places, at, dqkv, mixed, dhb, nt, dgate, dup, mt, cb, gains)
+    four = jnp.arange(4, dtype=jnp.int32)
+    slots_y, slots_x, slots_z = (slot_of(four ^ at_axis, phase) for at_axis in (y, x, z))
+    places = (slots_y[:, None] * 4 + slots_x[None, :]).reshape(16)
+    grads = outer(places, slots_z, at, dqkv, mixed, dhb, nt, dgate, dup, mt, cb, gains)
     total = scatter_grads(grads.reshape(4, 4, 4, ROWS, 128))
     param_part, gain_part = blocks_shard(total, rank)
     return (result[None, None], d_u[None, None], param_part[None], gain_part[None])

time: 778 us -> 668 us (0.86)
  starting transfers between devices: 187 us -> 82.8 us
  waiting for transfers between devices: 278 us -> 333 us
  Pallas kernels: 182 us -> 130 us
  other arithmetic: 56.4 us -> 40.3 us
  local copies, waits for them, and re-layouts: 44.7 us -> 55.9 us
    ppermute x106 -> x68, starting transfers between devices: 187 us -> 82.7 us  [the longest x54 62 us: swapped(): return lax.ppermute(block, ALL, pairs)]
    ppermute x106 -> x68, waiting for transfers between devices: 159 us -> 214 us  [the longest x54 200 us: swapped(): return lax.ppermute(block, ALL, pairs)]
    pallas_call x4, Pallas kernels: 83.6 us -> 50.6 us  [the longest x2 32.1 us: attend_back(): pl.pallas_call(attend_back_kernel, name='attend_back', grid=(SIDE,), in_s...]
    pallas_call x1, Pallas kernels: 33.1 us -> 14 us  [outer(): pl.pallas_call(outer_kernel, name='outer', grid_spec=pltpu.PrefetchScalar...]
    concatenate x37 -> x14, other arithmetic: 13 us -> 0.79 us  [the longest x12 0.72 us: gather_keys(): blocks[k] = jnp.concatenate([blocks[k], got], axis=0)]
    unnamed x79 -> x134, local copies, waits for them, and re-layouts: 14.2 us -> 22.9 us
    another operation x19 -> x3, other arithmetic: 17.7 us -> 9.35 us
    convert_element_type x42 -> x28, other arithmetic: 15.9 us -> 22.5 us  [the longest x15 16.4 us: scatter_grads(): total = total.astype(bf16)]
  transfers between devices with their start and end apart: 107 -> 69, of which waited for: 25 -> 48; matrix products, arithmetic and copies ran while one was open for 7% -> 8% of each run, Pallas kernels for 0% -> 0%
where the time goes in v2:
time: 668 us; the launch traced here: 659 us
  waiting for transfers between devices  333 us (50%)
  Pallas kernels  130 us (19%)
  starting transfers between devices  82.8 us (12%)
  local copies, waits for them, and re-layouts  55.9 us (8%)
  other arithmetic  40.3 us (6%)
  between operations  17.6 us (3%)
    ppermute x54, waiting for transfers between devices, swapped(): return lax.ppermute(block, ALL, pairs)  200 us
    all_gather x1, waiting for transfers between devices, per_device(): gathered = lax.all_gather(own, ('ctx', 'fsdp'), axis=0)  118 us
    ppermute x54, starting transfers between devices, swapped(): return lax.ppermute(block, ALL, pairs)  62 us
    pallas_call x2, Pallas kernels, attend_back(): pl.pallas_call(attend_back_kernel, name='attend_back', grid=(SIDE,), in_s...  32.1 us
    pallas_call x2, Pallas kernels, feed_back(): pl.pallas_call(feed_back_kernel, name='feed_back', grid=(4,), in_specs=[w...  29.7 us
    unnamed x134, local copies, waits for them, and re-layouts  22.9 us
    pallas_call x2, Pallas kernels, feed(): pl.pallas_call(feed_kernel, name='feed', grid=(4,), in_specs=[whole(D, R)...  21.6 us
    ppermute x14, starting transfers between devices, over(): return lax.ppermute(block, 'phase', [(source, 1 - source)])  20.7 us
  transfers between devices with their start and end apart: 69, of which 48 were waited for; matrix products, arithmetic and copies ran while one was open for 8% of the time, Pallas kernels for 0%

profile of v2, /device:TPU:0, one launch (start us, length us, event | category | flops | bytes accessed | tf_op | source)
XLA Modules:
  0.0 659.5 jit_solution(5967850297018856250)
XLA Ops:
  9.2 8.3 %conditional.2 = (bf16[1280,128]{1,0:T(8,128)(2,1)S(1)}) conditional(s32[]{:T(128)} %clamp.4, (bf16[1,153600]{1,0:T(2,128)(2,1)}, bf16[1,128]{1,0:T(2,128)(2,1)S(1)}) %tuple.47, (bf16[1,153600]{1,0:T(2,128)(2,1)}, bf16[1,128]{1,0:T(2,128)(2,1)S(1)}) %tuple.47, (bf16[1,153600]{1,0:T(2,128)(2,1)}, bf16[1,128]{1,0:T(2,128)(2,1)S(1)}) %tuple.47), branch_computations={%region_1.2_spmd, %region_2.3_spmd, %region_3.5_spmd} | conditional | flops 983040 | bytes 3780876 | solution.py:709
  9.2 7.4 %reduce.15 = bf16[153600]{0:T(1024)(128)(2,1)S(1)} reduce(bf16[1,153600]{1,0:T(2,128)(2,1)} %get-tuple-element.66, bf16[]{:T(256)} %constant.275), dimensions={0}, to_apply=%get-tuple-element.66.reduce_sub_computation | reduce | bytes 614402 | tf_op jit(solution)/shard_map
  24.7 118.3 %all-gather.3.cloned.1.call-done = bf16[81920,128]{1,0:T(8,128)(2,1)} async-done(((bf16[1280,128]{1,0:T(8,128)(2,1)}), bf16[81920,128]{1,0:T(8,128)(2,1)}) %all-gather.3.cloned.1.call-update) | async-done | bytes 20971536 | tf_op jit(solution)/shard_map/all_gather | solution.py:749
  146.5 3.0 project.2
  166.2 3.1 collective-permute-start.8
  172.8 3.5 collective-permute-start.5
  176.8 10.2 %collective-permute-done.9 = bf16[4,128,384]{2,1,0:T(8,128)(2,1)S(1)} collective-permute-done((bf16[4,128,384]{2,1,0:T(8,128)(2,1)S(1)}, bf16[4,128,384]{2,1,0:T(8,128)(2,1)S(1)}, u32[]{:S(2)}, u32[]{:S(2)}) %collective-permute-start.9) | collective-permute-done | bytes 393248 | tf_op jit(solution)/shard_map/ppermute | solution.py:57
  189.8 10.6 %collective-permute-done.10 = bf16[8,128,384]{2,1,0:T(8,128)(2,1)S(1)} collective-permute-done((bf16[8,128,384]{2,1,0:T(8,128)(2,1)S(1)}, bf16[8,128,384]{2,1,0:T(8,128)(2,1)S(1)}, u32[]{:S(2)}, u32[]{:S(2)}) %collective-permute-start.10) | collective-permute-done | bytes 786464 | tf_op jit(solution)/shard_map/ppermute | solution.py:57
  200.6 9.2 %attend.2 = (bf16[576,128]{1,0:T(8,128)(2,1)S(1)}, f32[3,1,384]{2,1,0:T(1,128)S(1)}) custom-call(bf16[576,128]{1,0:T(8,128)(2,1)S(1)} %slice_select_fusion.3.qt_ref, bf16[4096,384]{1,0:T(8,128)(2,1)S(1)} %bitcast.159, f32[4096,128]{1,0:T(8,128)S(1)} %and_select_fusion.bias_ref), custom_call_target="tpu_custom_call" | custom-call | flops 4000000000 | bytes 8000000 | tf_op jit(solution)/shard_map/attend/pallas_call | solution.py:258
  213.1 11.5 %feed.2 = (bf16[128,960]{1,0:T(8,128)(2,1)S(1)}, f32[128,960]{1,0:T(8,128)}, bf16[1024,128]{1,0:T(8,128)(2,1)}, f32[128,2560]{1,0:T(8,128)}, f32[128,2560]{1,0:T(8,128)}, /*index=5*/bf16[2560,128]{1,0:T(8,128)(2,1)}) custom-call(bf16[960,128]{1,0:T(8,128)(2,1)S(1)} %constant_dynamic-update-slice_fusion.10.mixed_ref, bf16[128,960]{1,0:T(8,128)(2,1)S(1)} %bitcast.156, ...), custom_call_target="tpu_custom_call" | custom-call | flops 2200000000 | bytes 22000000 | tf_op jit(solution)/shard_map/feed/pallas_call | solution.py:361
  227.8 3.0 project.3
  234.2 4.6 collective-permute-done.15
  241.1 4.7 collective-permute-done.16
  248.2 4.8 collective-permute-done.19
  254.1 3.5 collective-permute-done.20
  264.8 11.9 %collective-permute-done.22 = bf16[4,128,384]{2,1,0:T(8,128)(2,1)S(1)} collective-permute-done((bf16[4,128,384]{2,1,0:T(8,128)(2,1)S(1)}, bf16[4,128,384]{2,1,0:T(8,128)(2,1)S(1)}, u32[]{:S(2)}, u32[]{:S(2)}) %collective-permute-start.22) | collective-permute-done | bytes 393248 | tf_op jit(solution)/shard_map/ppermute | solution.py:57
  278.7 11.5 %collective-permute-done.23 = bf16[8,128,384]{2,1,0:T(8,128)(2,1)S(1)} collective-permute-done((bf16[8,128,384]{2,1,0:T(8,128)(2,1)S(1)}, bf16[8,128,384]{2,1,0:T(8,128)(2,1)S(1)}, u32[]{:S(2)}, u32[]{:S(2)}) %collective-permute-start.23) | collective-permute-done | bytes 786464 | tf_op jit(solution)/shard_map/ppermute | solution.py:57
  290.3 9.2 %attend.3 = (bf16[576,128]{1,0:T(8,128)(2,1)S(1)}, f32[3,1,384]{2,1,0:T(1,128)S(1)}) custom-call(bf16[576,128]{1,0:T(8,128)(2,1)S(1)} %slice_select_fusion.2.qt_ref, bf16[4096,384]{1,0:T(8,128)(2,1)S(1)} %bitcast.161, f32[4096,128]{1,0:T(8,128)S(1)} %and_select_fusion.bias_ref), custom_call_target="tpu_custom_call" | custom-call | flops 4000000000 | bytes 8000000 | tf_op jit(solution)/shard_map/attend/pallas_call | solution.py:258
  301.9 10.0 %feed.3 = (bf16[128,960]{1,0:T(8,128)(2,1)S(1)}, f32[128,960]{1,0:T(8,128)S(1)}, bf16[1024,128]{1,0:T(8,128)(2,1)S(1)}, f32[128,2560]{1,0:T(8,128)S(1)}, f32[128...) custom-call(bf16[960,128]{1,0:T(8,128)(2,1)S(1)} %maximum_select_fusion.2.mixed_ref, ...), custom_call_target="tpu_custom_call" | custom-call | flops 2200000000 | bytes 22000000 | tf_op jit(solution)/shard_map/feed/pallas_call | solution.py:361
  313.7 15.3 %feed_back.2 = (bf16[128,2560]{1,0:T(8,128)(2,1)}, bf16[128,2560]{1,0:T(8,128)(2,1)}, f32[128,960]{1,0:T(8,128)S(1)}, bf16[128,1024]{1,0:T(8,128)(2,1)}, f32[1,9...) custom-call(f32[128,960]{1,0:T(8,128)S(1)} %bitcast.154, ...), custom_call_target="tpu_custom_call" | custom-call | flops 2200000000 | bytes 22000000 | tf_op jit(solution)/shard_map/feed_back/pallas_call | solution.py:452
  332.6 16.1 %attend_back.2 = (bf16[4096,384]{1,0:T(8,128)(2,1)S(1)}, f32[576,128]{1,0:T(8,128)S(1)}) custom-call(bf16[576,128]{1,0:T(8,128)(2,1)S(1)} %slice_select_fusion.2.qt_ref, bf16[4096,384]{1,0:T(8,128)(2,1)} %bitcast.162, f32[4096,128]{1,0:T(8,128)S(1)} %copy-done.2, f32[576,128]{1,0:T(8,128)S(1)} %slice_select_fusion.1.dot_ref, ...), custom_call_target="tpu_custom_call" | custom-call | flops 10000000000 | bytes 14000000 | tf_op jit(solution)/shard_map/attend_back/pallas_call | solution.py:510
  352.5 9.8 %collective-permute-done.31 = bf16[8,128,384]{2,1,0:T(8,128)(2,1)S(1)} collective-permute-done((bf16[8,128,384]{2,1,0:T(8,128)(2,1)S(1)}, bf16[8,128,384]{2,1,0:T(8,128)(2,1)S(1)}, u32[]{:S(2)}, u32[]{:S(2)}) %collective-permute-start.31) | collective-permute-done | bytes 786464 | tf_op jit(solution)/shard_map/ppermute | solution.py:57
  363.9 6.4 collective-permute-done.32
  374.4 3.1 collective-permute-done.33
  385.3 3.2 collective-permute-done.35
  390.8 4.3 project_back.2
  398.7 14.4 %feed_back.3 = (bf16[128,2560]{1,0:T(8,128)(2,1)S(1)}, bf16[128,2560]{1,0:T(8,128)(2,1)S(1)}, f32[128,960]{1,0:T(8,128)S(1)}, bf16[128,1024]{1,0:T(8,128)(2,1)S(...) custom-call(f32[128,960]{1,0:T(8,128)S(1)} %convert_select_fusion.c_ref, ...), custom_call_target="tpu_custom_call" | custom-call | flops 2200000000 | bytes 22000000 | tf_op jit(solution)/shard_map/feed_back/pallas_call | solution.py:452
  416.5 16.1 %attend_back.3 = (bf16[4096,384]{1,0:T(8,128)(2,1)S(1)}, f32[576,128]{1,0:T(8,128)S(1)}) custom-call(bf16[576,128]{1,0:T(8,128)(2,1)S(1)} %copy-done.22, bf16[4096,384]{1,0:T(8,128)(2,1)} %bitcast.160, f32[4096,128]{1,0:T(8,128)S(1)} %copy-done.2, f32[576,128]{1,0:T(8,128)S(1)} %slice_select_fusion.dot_ref, bf16[576,128]{1,0:T(8,128)(2,1)S(1)} %copy-done.10, ...), custom_call_target="tpu_custom_call" | custom-call | flops 10000000000 | bytes 14000000 | tf_op jit(solution)/shard_map/attend_back/pallas_call | solution.py:510
  439.7 8.1 %collective-permute-done.44 = bf16[8,128,384]{2,1,0:T(8,128)(2,1)} collective-permute-done((bf16[8,128,384]{2,1,0:T(8,128)(2,1)}, bf16[8,128,384]{2,1,0:T(8,128)(2,1)}, u32[]{:S(2)}, u32[]{:S(2)}) %collective-permute-start.44) | collective-permute-done | bytes 786464 | tf_op jit(solution)/shard_map/ppermute | solution.py:57
  453.0 5.5 collective-permute-done.45
  474.7 3.1 collective-permute-done.48
  481.1 3.6 project_back.3
  491.2 14.0 %outer.1 = bf16[16,4,1280,128]{3,2,1,0:T(8,128)(2,1)} custom-call(s32[16]{0:T(128)S(1)} %add.411.place_ref, s32[4]{0:T(128)S(1)} %gather_fusion.3, bf16[960,128]{1,0:T(8,128)(2,1)S(1)} %copy-done.20, bf16[128,1664]{1,0:T(8,128)(2,1)S(1)} %copy-done.8, bf16[960,128]{1,0:T(8,128)(2,1)S(1)} %maximum_select_fusion.2.mixed_ref, bf16[128,1024]{1,0:T(8,128)(2,1)S(1)} %copy-done.14, ...), custom_call_target="tpu_custom_call" | custom-call | flops 2600000000 | bytes 24000000 | tf_op jit(solution)/shard_map/outer/pallas_call | solution.py:670
  505.2 7.2 %fusion.35 = (bf16[4,4,2,416,128]{4,3,2,1,0:T(8,128)(2,1)}, bf16[4,4,2,416,128]{4,3,2,1,0:T(8,128)(2,1)}) fusion(bf16[4,4,4,1280,128]{4,3,2,1,0:T(8,128)(2,1)} %bitcast.203), kind=kLoop, calls=%fused_computation.189 | loop fusion | bytes 13631488 | tf_op jit(solution)/shard_map/slice | solution.py:141
  512.4 4.7 copy.109
  518.4 4.1 slice.572
  524.7 3.4 fusion.34
  528.1 4.3 copy.107
  533.6 25.1 %collective-permute-done.62 = bf16[4,4,2,416,128]{4,3,1,0,2:T(8,128)(2,1)} collective-permute-done((bf16[4,4,2,416,128]{4,3,1,0,2:T(8,128)(2,1)}, bf16[4,4,2,416,128]{4,3,1,0,2:T(8,128)(2,1)}, u32[]{:S(2)}, u32[]{:S(2)}) %collective-permute-start.62) | collective-permute-done | bytes 3407904 | tf_op jit(solution)/shard_map/ppermute | solution.py:57
  565.4 3.0 add_convert_fusion.1
  569.0 6.5 collective-permute-done.56
  578.7 6.5 collective-permute-done.63
  588.5 6.4 collective-permute-done.51
  602.1 6.7 %collective-permute-done.57 = bf16[4,1,4,432,128]{4,3,0,2,1:T(8,128)(2,1)S(1)} collective-permute-done((bf16[4,1,4,432,128]{4,3,0,2,1:T(8,128)(2,1)S(1)}, bf16[4,1,4,432,128]{4,3,0,2,1:T(8,128)(2,1)S(1)}, u32[]{:S(2)}, u32[]{:S(2)}) %collective-permute-start.57) | collective-permute-done | bytes 1769504 | tf_op jit(solution)/shard_map/ppermute | solution.py:57
  619.4 8.4 %collective-permute-done.58 = bf16[4,2,432,128]{3,2,0,1:T(8,128)(2,1)} collective-permute-done((bf16[4,2,432,128]{3,2,0,1:T(8,128)(2,1)}, bf16[4,2,432,128]{3,2,0,1:T(8,128)(2,1)}, u32[]{:S(2)}, u32[]{:S(2)}) %collective-permute-start.58) | collective-permute-done | bytes 884768 | tf_op jit(solution)/shard_map/ppermute | solution.py:57
  630.6 7.0 %collective-permute-done.59 = bf16[4,1,432,128]{3,2,0,1:T(8,128)(2,1)S(1)} collective-permute-done((bf16[4,1,432,128]{3,2,0,1:T(8,128)(2,1)S(1)}, bf16[4,1,432,128]{3,2,0,1:T(8,128)(2,1)S(1)}, u32[]{:S(2)}, u32[]{:S(2)}) %collective-permute-start.59) | collective-permute-done | bytes 442400 | tf_op jit(solution)/shard_map/ppermute | solution.py:57
  638.2 6.7 %collective-permute-done.60 = bf16[2,432,128]{2,1,0:T(8,128)(2,1)S(1)} collective-permute-done((bf16[2,432,128]{2,1,0:T(8,128)(2,1)S(1)}, bf16[2,432,128]{2,1,0:T(8,128)(2,1)S(1)}, u32[]{:S(2)}, u32[]{:S(2)}) %collective-permute-start.60) | collective-permute-done | bytes 221216 | tf_op jit(solution)/shard_map/ppermute | solution.py:57
  645.2 4.7 collective-permute-done.61
  (409 shorter events, 175.1 us)
Async XLA Ops:
  7.2 135.9 %all-gather.3.cloned.1.call-start = ((), (), s32[]{:S(2)}) async-start(), calls=%async_computation | async-start | bytes 21299200 | tf_op jit(solution)/shard_map/all_gather | solution.py:749
  154.5 6.9 %collective-permute-start.6 = (bf16[128,384]{1,0:T(8,128)(2,1)S(1)}, bf16[128,384]{1,0:T(8,128)(2,1)S(1)}, u32[]{:S(2)}, u32[]{:S(2)}) collective-permute-start(bf16[128,384]{1,0:T(8,128)(2,1)S(1)} %get-tuple-element.175), channel_id=1, source_target_pairs={{0,2},{1,3},{2,0},{3,1},{4,6},{5,7},{6,4},{7,5},{8,10},{9,11},{10,... | collective-permute-start | bytes 294920 | tf_op jit(solution)/shard_map/ppermute | solution.py:57
  157.5 7.0 %collective-permute-start.3 = (bf16[2,128,384]{2,1,0:T(8,128)(2,1)S(1)}, bf16[2,128,384]{2,1,0:T(8,128)(2,1)S(1)}, u32[]{:S(2)}, u32[]{:S(2)}) collective-permute-start(bf16[2,128,384]{2,1,0:T(8,128)(2,1)S(1)} %pad_maximum_fusion.10), channel_id=1, source_target_pairs={{0,48},{1,49},{2,50},{3,51},{4,52},{5,53},{6,54},{7,55},{8,56},{9,... | collective-permute-start | bytes 589832 | tf_op jit(solution)/shard_map/ppermute | solution.py:57
  164.5 8.2 %collective-permute-start.4 = (bf16[4,128,384]{2,1,0:T(8,128)(2,1)S(1)}, bf16[4,128,384]{2,1,0:T(8,128)(2,1)S(1)}, u32[]{:S(2)}, u32[]{:S(2)}) collective-permute-start(bf16[4,128,384]{2,1,0:T(8,128)(2,1)S(1)} %pad_maximum_fusion.5), channel_id=1, source_target_pairs={{0,4},{1,5},{2,6},{3,7},{4,0},{5,1},{6,2},{7,3},{8,12},{9,13},{10,... | collective-permute-start | bytes 1179656 | tf_op jit(solution)/shard_map/ppermute | solution.py:57
  166.2 10.1 %collective-permute-start.8 = (bf16[2,128,384]{2,1,0:T(8,128)(2,1)S(1)}, bf16[2,128,384]{2,1,0:T(8,128)(2,1)S(1)}, u32[]{:S(2)}, u32[]{:S(2)}) collective-permute-start(bf16[2,128,384]{2,1,0:T(8,128)(2,1)S(1)} %pad_maximum_fusion.11), channel_id=1, source_target_pairs={{0,12},{1,13},{2,14},{3,15},{4,8},{5,9},{6,10},{7,11},{8,4},{9,5},... | collective-permute-start | bytes 589832 | tf_op jit(solution)/shard_map/ppermute | solution.py:57
  172.8 16.7 %collective-permute-start.5 = (bf16[8,128,384]{2,1,0:T(8,128)(2,1)S(1)}, bf16[8,128,384]{2,1,0:T(8,128)(2,1)S(1)}, u32[]{:S(2)}, u32[]{:S(2)}) collective-permute-start(bf16[8,128,384]{2,1,0:T(8,128)(2,1)S(1)} %pad_maximum_fusion), channel_id=1, source_target_pairs={{0,12},{1,13},{2,14},{3,15},{4,8},{5,9},{6,10},{7,11},{8,4},{9,5},... | collective-permute-start | bytes 2359304 | tf_op jit(solution)/shard_map/ppermute | solution.py:57
  176.4 10.7 %collective-permute-start.9 = (bf16[4,128,384]{2,1,0:T(8,128)(2,1)S(1)}, bf16[4,128,384]{2,1,0:T(8,128)(2,1)S(1)}, u32[]{:S(2)}, u32[]{:S(2)}) collective-permute-start(bf16[4,128,384]{2,1,0:T(8,128)(2,1)S(1)} %pad_maximum_fusion.6), channel_id=1, source_target_pairs={{0,16},{1,17},{2,18},{3,19},{4,20},{5,21},{6,22},{7,23},{8,24},{9,... | collective-permute-start | bytes 1179656 | tf_op jit(solution)/shard_map/ppermute | solution.py:57
  187.2 13.3 %collective-permute-start.10 = (bf16[8,128,384]{2,1,0:T(8,128)(2,1)S(1)}, bf16[8,128,384]{2,1,0:T(8,128)(2,1)S(1)}, u32[]{:S(2)}, u32[]{:S(2)}) collective-permute-start(bf16[8,128,384]{2,1,0:T(8,128)(2,1)S(1)} %pad_maximum_fusion.1), channel_id=1, source_target_pairs={{0,48},{1,49},{2,50},{3,51},{4,52},{5,53},{6,54},{7,55},{8,56},{9,... | collective-permute-start | bytes 2359304 | tf_op jit(solution)/shard_map/ppermute | solution.py:57
  238.8 7.0 %collective-permute-start.16 = (bf16[2,128,384]{2,1,0:T(8,128)(2,1)S(1)}, bf16[2,128,384]{2,1,0:T(8,128)(2,1)S(1)}, u32[]{:S(2)}, u32[]{:S(2)}) collective-permute-start(bf16[2,128,384]{2,1,0:T(8,128)(2,1)S(1)} %pad_maximum_fusion.12), channel_id=1, source_target_pairs={{0,48},{1,49},{2,50},{3,51},{4,52},{5,53},{6,54},{7,55},{8,56},{9,... | collective-permute-start | bytes 589832 | tf_op jit(solution)/shard_map/ppermute | solution.py:57
  245.8 14.4 %collective-permute-start.17 = (bf16[4,128,384]{2,1,0:T(8,128)(2,1)S(1)}, bf16[4,128,384]{2,1,0:T(8,128)(2,1)S(1)}, u32[]{:S(2)}, u32[]{:S(2)}) collective-permute-start(bf16[4,128,384]{2,1,0:T(8,128)(2,1)S(1)} %pad_maximum_fusion.7), channel_id=1, source_target_pairs={{0,4},{1,5},{2,6},{3,7},{4,0},{5,1},{6,2},{7,3},{8,12},{9,13},{10,... | collective-permute-start | bytes 1179656 | tf_op jit(solution)/shard_map/ppermute | solution.py:57
  246.9 6.1 collective-permute-start.19
  257.6 7.0 %collective-permute-start.21 = (bf16[2,128,384]{2,1,0:T(8,128)(2,1)S(1)}, bf16[2,128,384]{2,1,0:T(8,128)(2,1)S(1)}, u32[]{:S(2)}, u32[]{:S(2)}) collective-permute-start(bf16[2,128,384]{2,1,0:T(8,128)(2,1)S(1)} %pad_maximum_fusion.13), channel_id=1, source_target_pairs={{0,12},{1,13},{2,14},{3,15},{4,8},{5,9},{6,10},{7,11},{8,4},{9,5},... | collective-permute-start | bytes 589832 | tf_op jit(solution)/shard_map/ppermute | solution.py:57
  260.4 18.0 %collective-permute-start.18 = (bf16[8,128,384]{2,1,0:T(8,128)(2,1)S(1)}, bf16[8,128,384]{2,1,0:T(8,128)(2,1)S(1)}, u32[]{:S(2)}, u32[]{:S(2)}) collective-permute-start(bf16[8,128,384]{2,1,0:T(8,128)(2,1)S(1)} %pad_maximum_fusion.2), channel_id=1, source_target_pairs={{0,12},{1,13},{2,14},{3,15},{4,8},{5,9},{6,10},{7,11},{8,4},{9,5},... | collective-permute-start | bytes 2359304 | tf_op jit(solution)/shard_map/ppermute | solution.py:57
  264.6 12.1 %collective-permute-start.22 = (bf16[4,128,384]{2,1,0:T(8,128)(2,1)S(1)}, bf16[4,128,384]{2,1,0:T(8,128)(2,1)S(1)}, u32[]{:S(2)}, u32[]{:S(2)}) collective-permute-start(bf16[4,128,384]{2,1,0:T(8,128)(2,1)S(1)} %pad_maximum_fusion.8), channel_id=1, source_target_pairs={{0,16},{1,17},{2,18},{3,19},{4,20},{5,21},{6,22},{7,23},{8,24},{9,... | collective-permute-start | bytes 1179656 | tf_op jit(solution)/shard_map/ppermute | solution.py:57
  276.9 13.3 %collective-permute-start.23 = (bf16[8,128,384]{2,1,0:T(8,128)(2,1)S(1)}, bf16[8,128,384]{2,1,0:T(8,128)(2,1)S(1)}, u32[]{:S(2)}, u32[]{:S(2)}) collective-permute-start(bf16[8,128,384]{2,1,0:T(8,128)(2,1)S(1)} %pad_maximum_fusion.3), channel_id=1, source_target_pairs={{0,48},{1,49},{2,50},{3,51},{4,52},{5,53},{6,54},{7,55},{8,56},{9,... | collective-permute-start | bytes 2359304 | tf_op jit(solution)/shard_map/ppermute | solution.py:57
  349.0 13.3 %collective-permute-start.31 = (bf16[8,128,384]{2,1,0:T(8,128)(2,1)S(1)}, bf16[8,128,384]{2,1,0:T(8,128)(2,1)S(1)}, u32[]{:S(2)}, u32[]{:S(2)}) collective-permute-start(bf16[8,128,384]{2,1,0:T(8,128)(2,1)S(1)} %bitcast.243), channel_id=1, source_target_pairs={{0,48},{1,49},{2,50},{3,51},{4,52},{5,53},{6,54},{7,55},{8,56},{9,... | collective-permute-start | bytes 2359304 | tf_op jit(solution)/shard_map/ppermute | solution.py:57
  350.4 13.2 %collective-permute-start.27 = (bf16[8,128,384]{2,1,0:T(8,128)(2,1)S(1)}, bf16[8,128,384]{2,1,0:T(8,128)(2,1)S(1)}, u32[]{:S(2)}, u32[]{:S(2)}) collective-permute-start(bf16[8,128,384]{2,1,0:T(8,128)(2,1)S(1)} %bitcast.242), channel_id=1, source_target_pairs={{0,12},{1,13},{2,14},{3,15},{4,8},{5,9},{6,10},{7,11},{8,4},{9,5},... | collective-permute-start | bytes 2359304 | tf_op jit(solution)/shard_map/ppermute | solution.py:57
  362.5 7.9 %collective-permute-start.32 = (bf16[4,128,384]{2,1,0:T(8,128)(2,1)S(1)}, bf16[4,128,384]{2,1,0:T(8,128)(2,1)S(1)}, u32[]{:S(2)}, u32[]{:S(2)}) collective-permute-start(bf16[4,128,384]{2,1,0:T(8,128)(2,1)S(1)} %slice.552), channel_id=1, source_target_pairs={{0,16},{1,17},{2,18},{3,19},{4,20},{5,21},{6,22},{7,23},{8,24},{9,... | collective-permute-start | bytes 1179656 | tf_op jit(solution)/shard_map/ppermute | solution.py:57
  363.8 8.0 %collective-permute-start.28 = (bf16[4,128,384]{2,1,0:T(8,128)(2,1)S(1)}, bf16[4,128,384]{2,1,0:T(8,128)(2,1)S(1)}, u32[]{:S(2)}, u32[]{:S(2)}) collective-permute-start(bf16[4,128,384]{2,1,0:T(8,128)(2,1)S(1)} %slice.546), channel_id=1, source_target_pairs={{0,4},{1,5},{2,6},{3,7},{4,0},{5,1},{6,2},{7,3},{8,12},{9,13},{10,... | collective-permute-start | bytes 1179656 | tf_op jit(solution)/shard_map/ppermute | solution.py:57
  370.5 7.0 %collective-permute-start.33 = (bf16[2,128,384]{2,1,0:T(8,128)(2,1)S(1)}, bf16[2,128,384]{2,1,0:T(8,128)(2,1)S(1)}, u32[]{:S(2)}, u32[]{:S(2)}) collective-permute-start(bf16[2,128,384]{2,1,0:T(8,128)(2,1)S(1)} %slice.554), channel_id=1, source_target_pairs={{0,12},{1,13},{2,14},{3,15},{4,8},{5,9},{6,10},{7,11},{8,4},{9,5},... | collective-permute-start | bytes 589832 | tf_op jit(solution)/shard_map/ppermute | solution.py:57
  372.0 8.2 %collective-permute-start.29 = (bf16[2,128,384]{2,1,0:T(8,128)(2,1)S(1)}, bf16[2,128,384]{2,1,0:T(8,128)(2,1)S(1)}, u32[]{:S(2)}, u32[]{:S(2)}) collective-permute-start(bf16[2,128,384]{2,1,0:T(8,128)(2,1)S(1)} %slice.548), channel_id=1, source_target_pairs={{0,48},{1,49},{2,50},{3,51},{4,52},{5,53},{6,54},{7,55},{8,56},{9,... | collective-permute-start | bytes 589832 | tf_op jit(solution)/shard_map/ppermute | solution.py:57
  382.3 6.2 collective-permute-start.35
  384.0 5.9 collective-permute-start.26
  434.3 13.5 %collective-permute-start.44 = (bf16[8,128,384]{2,1,0:T(8,128)(2,1)}, bf16[8,128,384]{2,1,0:T(8,128)(2,1)}, u32[]{:S(2)}, u32[]{:S(2)}) collective-permute-start(bf16[8,128,384]{2,1,0:T(8,128)(2,1)} %bitcast.48), channel_id=1, source_target_pairs={{0,48},{1,49},{2,50},{3,51},{4,52},{5,53},{6,54},{7,55},{8,56},{9,... | collective-permute-start | bytes 2359304 | tf_op jit(solution)/shard_map/ppermute | solution.py:57
  435.7 14.8 %collective-permute-start.40 = (bf16[8,128,384]{2,1,0:T(8,128)(2,1)}, bf16[8,128,384]{2,1,0:T(8,128)(2,1)}, u32[]{:S(2)}, u32[]{:S(2)}) collective-permute-start(bf16[8,128,384]{2,1,0:T(8,128)(2,1)} %bitcast.45), channel_id=1, source_target_pairs={{0,12},{1,13},{2,14},{3,15},{4,8},{5,9},{6,10},{7,11},{8,4},{9,5},... | collective-permute-start | bytes 2359304 | tf_op jit(solution)/shard_map/ppermute | solution.py:57
  450.3 8.3 %collective-permute-start.45 = (bf16[4,128,384]{2,1,0:T(8,128)(2,1)}, bf16[4,128,384]{2,1,0:T(8,128)(2,1)}, u32[]{:S(2)}, u32[]{:S(2)}) collective-permute-start(bf16[4,128,384]{2,1,0:T(8,128)(2,1)} %slice.565), channel_id=1, source_target_pairs={{0,16},{1,17},{2,18},{3,19},{4,20},{5,21},{6,22},{7,23},{8,24},{9,... | collective-permute-start | bytes 1179656 | tf_op jit(solution)/shard_map/ppermute | solution.py:57
  452.7 8.4 %collective-permute-start.41 = (bf16[4,128,384]{2,1,0:T(8,128)(2,1)}, bf16[4,128,384]{2,1,0:T(8,128)(2,1)}, u32[]{:S(2)}, u32[]{:S(2)}) collective-permute-start(bf16[4,128,384]{2,1,0:T(8,128)(2,1)} %slice.559), channel_id=1, source_target_pairs={{0,4},{1,5},{2,6},{3,7},{4,0},{5,1},{6,2},{7,3},{8,12},{9,13},{10,... | collective-permute-start | bytes 1179656 | tf_op jit(solution)/shard_map/ppermute | solution.py:57
  459.8 7.0 %collective-permute-start.46 = (bf16[2,128,384]{2,1,0:T(8,128)(2,1)S(1)}, bf16[2,128,384]{2,1,0:T(8,128)(2,1)S(1)}, u32[]{:S(2)}, u32[]{:S(2)}) collective-permute-start(bf16[2,128,384]{2,1,0:T(8,128)(2,1)S(1)} %slice.567), channel_id=1, source_target_pairs={{0,12},{1,13},{2,14},{3,15},{4,8},{5,9},{6,10},{7,11},{8,4},{9,5},... | collective-permute-start | bytes 589832 | tf_op jit(solution)/shard_map/ppermute | solution.py:57
  462.4 7.5 %collective-permute-start.42 = (bf16[2,128,384]{2,1,0:T(8,128)(2,1)S(1)}, bf16[2,128,384]{2,1,0:T(8,128)(2,1)S(1)}, u32[]{:S(2)}, u32[]{:S(2)}) collective-permute-start(bf16[2,128,384]{2,1,0:T(8,128)(2,1)S(1)} %slice.561), channel_id=1, source_target_pairs={{0,48},{1,49},{2,50},{3,51},{4,52},{5,53},{6,54},{7,55},{8,56},{9,... | collective-permute-start | bytes 589832 | tf_op jit(solution)/shard_map/ppermute | solution.py:57
  471.6 6.2 collective-permute-start.48
  473.3 5.8 collective-permute-start.39
  517.1 41.6 %collective-permute-start.62 = (bf16[4,4,2,416,128]{4,3,1,0,2:T(8,128)(2,1)}, bf16[4,4,2,416,128]{4,3,1,0,2:T(8,128)(2,1)}, u32[]{:S(2)}, u32[]{:S(2)}) collective-permute-start(bf16[4,4,2,416,128]{4,3,1,0,2:T(8,128)(2,1)} %copy.109), channel_id=1, source_target_pairs={{0,3},{1,2},{2,1},{3,0},{4,7},{5,6},{6,5},{7,4},{8,11},{9,10},{10,... | collective-permute-start | bytes 10223624 | tf_op jit(solution)/shard_map/ppermute | solution.py:57
  522.4 43.0 %collective-permute-start.50 = (bf16[2,4,4,432,128]{4,3,2,1,0:T(8,128)(2,1)}, bf16[2,4,4,432,128]{4,3,2,1,0:T(8,128)(2,1)}, u32[]{:S(2)}, u32[]{:S(2)}) collective-permute-start(bf16[2,4,4,432,128]{4,3,2,1,0:T(8,128)(2,1)} %slice.572), channel_id=1, source_target_pairs={{0,48},{1,49},{2,50},{3,51},{4,52},{5,53},{6,54},{7,55},{8,56},{9,... | collective-permute-start | bytes 10616840 | tf_op jit(solution)/shard_map/ppermute | solution.py:57
  532.4 43.0 %collective-permute-start.56 = (bf16[4,2,4,432,128]{4,3,0,2,1:T(8,128)(2,1)}, bf16[4,2,4,432,128]{4,3,0,2,1:T(8,128)(2,1)}, u32[]{:S(2)}, u32[]{:S(2)}) collective-permute-start(bf16[4,2,4,432,128]{4,3,0,2,1:T(8,128)(2,1)} %copy.107), channel_id=1, source_target_pairs={{0,12},{1,13},{2,14},{3,15},{4,8},{5,9},{6,10},{7,11},{8,4},{9,5},... | collective-permute-start | bytes 10616840 | tf_op jit(solution)/shard_map/ppermute | solution.py:57
  563.0 22.1 %collective-permute-start.63 = (bf16[4,4,1,416,128]{4,3,1,0,2:T(8,128)(2,1)}, bf16[4,4,1,416,128]{4,3,1,0,2:T(8,128)(2,1)}, u32[]{:S(2)}, u32[]{:S(2)}) collective-permute-start(bf16[4,4,1,416,128]{4,3,1,0,2:T(8,128)(2,1)} %slice.598), channel_id=1, source_target_pairs={{0,1},{1,0},{2,3},{3,2},{4,5},{5,4},{6,7},{7,6},{8,9},{9,8},{10,11... | collective-permute-start | bytes 5111816 | tf_op jit(solution)/shard_map/ppermute | solution.py:57
  568.6 26.3 %collective-permute-start.51 = (bf16[1,4,4,432,128]{4,3,2,1,0:T(8,128)(2,1)S(1)}, bf16[1,4,4,432,128]{4,3,2,1,0:T(8,128)(2,1)S(1)}, u32[]{:S(2)}, u32[]{:S(2)}) collective-permute-start(bf16[1,4,4,432,128]{4,3,2,1,0:T(8,128)(2,1)S(1)} %slice.574), channel_id=1, source_target_pairs={{0,16},{1,17},{2,18},{3,19},{4,20},{5,21},{6,22},{7,23},{8,24},{9,... | collective-permute-start | bytes 5308424 | tf_op jit(solution)/shard_map/ppermute | solution.py:57
  578.6 30.2 %collective-permute-start.57 = (bf16[4,1,4,432,128]{4,3,0,2,1:T(8,128)(2,1)S(1)}, bf16[4,1,4,432,128]{4,3,0,2,1:T(8,128)(2,1)S(1)}, u32[]{:S(2)}, u32[]{:S(2)}) collective-permute-start(bf16[4,1,4,432,128]{4,3,0,2,1:T(8,128)(2,1)S(1)} %slice.586), channel_id=1, source_target_pairs={{0,4},{1,5},{2,6},{3,7},{4,0},{5,1},{6,2},{7,3},{8,12},{9,13},{10,... | collective-permute-start | bytes 5308424 | tf_op jit(solution)/shard_map/ppermute | solution.py:57
  587.1 14.0 %collective-permute-start.64 = (bf16[2,4,416,128]{3,2,1,0:T(8,128)(2,1)S(1)}, bf16[2,4,416,128]{3,2,1,0:T(8,128)(2,1)S(1)}, u32[]{:S(2)}, u32[]{:S(2)}) collective-permute-start(bf16[2,4,416,128]{3,2,1,0:T(8,128)(2,1)S(1)} %slice_bitcast_fusion.2), channel_id=1, source_target_pairs={{0,48},{1,49},{2,50},{3,51},{4,52},{5,53},{6,54},{7,55},{8,56},{9,... | collective-permute-start | bytes 2555912 | tf_op jit(solution)/shard_map/ppermute | solution.py:57
  596.5 17.8 %collective-permute-start.52 = (bf16[2,4,432,128]{3,2,1,0:T(8,128)(2,1)}, bf16[2,4,432,128]{3,2,1,0:T(8,128)(2,1)}, u32[]{:S(2)}, u32[]{:S(2)}) collective-permute-start(bf16[2,4,432,128]{3,2,1,0:T(8,128)(2,1)} %slice_bitcast_fusion), channel_id=1, source_target_pairs={{0,12},{1,13},{2,14},{3,15},{4,8},{5,9},{6,10},{7,11},{8,4},{9,5},... | collective-permute-start | bytes 2654216 | tf_op jit(solution)/shard_map/ppermute | solution.py:57
  602.1 13.9 %collective-permute-start.65 = (bf16[1,4,416,128]{3,2,1,0:T(8,128)(2,1)}, bf16[1,4,416,128]{3,2,1,0:T(8,128)(2,1)}, u32[]{:S(2)}, u32[]{:S(2)}) collective-permute-start(bf16[1,4,416,128]{3,2,1,0:T(8,128)(2,1)} %slice.602), channel_id=1, source_target_pairs={{0,16},{1,17},{2,18},{3,19},{4,20},{5,21},{6,22},{7,23},{8,24},{9,... | collective-permute-start | bytes 1277960 | tf_op jit(solution)/shard_map/ppermute | solution.py:57
  611.5 16.3 %collective-permute-start.58 = (bf16[4,2,432,128]{3,2,0,1:T(8,128)(2,1)}, bf16[4,2,432,128]{3,2,0,1:T(8,128)(2,1)}, u32[]{:S(2)}, u32[]{:S(2)}) collective-permute-start(bf16[4,2,432,128]{3,2,0,1:T(8,128)(2,1)} %slice.588), channel_id=1, source_target_pairs={{0,3},{1,2},{2,1},{3,0},{4,7},{5,6},{6,5},{7,4},{8,11},{9,10},{10,... | collective-permute-start | bytes 2654216 | tf_op jit(solution)/shard_map/ppermute | solution.py:57
  615.9 13.6 %collective-permute-start.53 = (bf16[1,4,432,128]{3,2,1,0:T(8,128)(2,1)S(1)}, bf16[1,4,432,128]{3,2,1,0:T(8,128)(2,1)S(1)}, u32[]{:S(2)}, u32[]{:S(2)}) collective-permute-start(bf16[1,4,432,128]{3,2,1,0:T(8,128)(2,1)S(1)} %slice.578), channel_id=1, source_target_pairs={{0,4},{1,5},{2,6},{3,7},{4,0},{5,1},{6,2},{7,3},{8,12},{9,13},{10,... | collective-permute-start | bytes 1327112 | tf_op jit(solution)/shard_map/ppermute | solution.py:57
  617.1 12.2 %collective-permute-start.66 = (bf16[2,416,128]{2,1,0:T(8,128)(2,1)S(1)}, bf16[2,416,128]{2,1,0:T(8,128)(2,1)S(1)}, u32[]{:S(2)}, u32[]{:S(2)}) collective-permute-start(bf16[2,416,128]{2,1,0:T(8,128)(2,1)S(1)} %slice_bitcast_fusion.8), channel_id=1, source_target_pairs={{0,12},{1,13},{2,14},{3,15},{4,8},{5,9},{6,10},{7,11},{8,4},{9,5},... | collective-permute-start | bytes 638984 | tf_op jit(solution)/shard_map/ppermute | solution.py:57
  629.2 8.4 %collective-permute-start.59 = (bf16[4,1,432,128]{3,2,0,1:T(8,128)(2,1)S(1)}, bf16[4,1,432,128]{3,2,0,1:T(8,128)(2,1)S(1)}, u32[]{:S(2)}, u32[]{:S(2)}) collective-permute-start(bf16[4,1,432,128]{3,2,0,1:T(8,128)(2,1)S(1)} %slice.590), channel_id=1, source_target_pairs={{0,1},{1,0},{2,3},{3,2},{4,5},{5,4},{6,7},{7,6},{8,9},{9,8},{10,11... | collective-permute-start | bytes 1327112 | tf_op jit(solution)/shard_map/ppermute | solution.py:57
  629.4 8.4 %collective-permute-start.67 = (bf16[1,416,128]{2,1,0:T(8,128)(2,1)S(1)}, bf16[1,416,128]{2,1,0:T(8,128)(2,1)S(1)}, u32[]{:S(2)}, u32[]{:S(2)}) collective-permute-start(bf16[1,416,128]{2,1,0:T(8,128)(2,1)S(1)} %slice.606), channel_id=1, source_target_pairs={{0,4},{1,5},{2,6},{3,7},{4,0},{5,1},{6,2},{7,3},{8,12},{9,13},{10,... | collective-permute-start | bytes 319496 | tf_op jit(solution)/shard_map/ppermute | solution.py:57
  629.6 8.4 %collective-permute-start.54 = (bf16[2,432,128]{2,1,0:T(8,128)(2,1)S(1)}, bf16[2,432,128]{2,1,0:T(8,128)(2,1)S(1)}, u32[]{:S(2)}, u32[]{:S(2)}) collective-permute-start(bf16[2,432,128]{2,1,0:T(8,128)(2,1)S(1)} %slice_bitcast_fusion.6), channel_id=1, source_target_pairs={{0,3},{1,2},{2,1},{3,0},{4,7},{5,6},{6,5},{7,4},{8,11},{9,10},{10,... | collective-permute-start | bytes 663560 | tf_op jit(solution)/shard_map/ppermute | solution.py:57
  637.7 7.2 %collective-permute-start.60 = (bf16[2,432,128]{2,1,0:T(8,128)(2,1)S(1)}, bf16[2,432,128]{2,1,0:T(8,128)(2,1)S(1)}, u32[]{:S(2)}, u32[]{:S(2)}) collective-permute-start(bf16[2,432,128]{2,1,0:T(8,128)(2,1)S(1)} %slice_bitcast_fusion.4), channel_id=1, source_target_pairs={{0,48},{1,49},{2,50},{3,51},{4,52},{5,53},{6,54},{7,55},{8,56},{9,... | collective-permute-start | bytes 663560 | tf_op jit(solution)/shard_map/ppermute | solution.py:57
  638.1 7.0 %collective-permute-start.55 = (bf16[1,432,128]{2,1,0:T(8,128)(2,1)S(1)}, bf16[1,432,128]{2,1,0:T(8,128)(2,1)S(1)}, u32[]{:S(2)}, u32[]{:S(2)}) collective-permute-start(bf16[1,432,128]{2,1,0:T(8,128)(2,1)S(1)} %slice.582), channel_id=1, source_target_pairs={{0,1},{1,0},{2,3},{3,2},{4,5},{5,4},{6,7},{7,6},{8,9},{9,8},{10,11... | collective-permute-start | bytes 331784 | tf_op jit(solution)/shard_map/ppermute | solution.py:57
  (74 other events, 700.8 us)
Sparse Core Ops, SparseCore 0:
  18.4 124.5 all-gather.2

commit v3 on v2

--- a/solution.py
+++ b/solution.py
@@ -82,6 +82,8 @@
     blocks = [near[None], far[None]]
     for leg in range(2):
         for number in range(2):
+            if leg and number:
+                blocks = list(lax.optimization_barrier(tuple(blocks)))
             for k in range(2):
                 got = swapped(blocks[k], along(orders[k][leg], number))
                 blocks[k] = jnp.concatenate([blocks[k], got], axis=0)
@@ -128,27 +130,30 @@
 PART_ROWS = ((0, 432), (432, 864), (864, 1280))
 
 
-def scatter_grads(rel):
-    blocks = [rel[:, :, :, begin:end] for begin, end in PART_ROWS]
-    left = [[0, 1, 2], [0, 1, 2], [0, 1, 2]]
+PART_AXES = ((0, 1, 2), (1, 2, 0), (2, 0, 1))
+
+
+def scatter_grads(keep, send):
+    keep, send = list(keep), list(send)
     for leg in range(3):
         for number in (1, 0):
-            for part in range(3):
-                axis = (part + leg) % 3
-                dim = left[part].index(axis)
-                block = blocks[part]
-                half = block.shape[dim] // 2
-                keep = lax.slice_in_dim(block, 0, half, axis=dim)
-                send = lax.slice_in_dim(block, half, 2 * half, axis=dim)
-                got = swapped(send, along((axis, axis), number))
-                total = keep.astype(f32) + got.astype(f32)
-                if number == 0:
-                    total = lax.squeeze(total, (dim,))
-                    left[part].remove(axis)
-                if leg < 2 or number:
-                    total = total.astype(bf16)
-                blocks[part] = total
-    return jnp.concatenate(blocks)
+            for part, axes in enumerate(PART_AXES):
+                axis = axes[leg]
+                got = swapped(send[part], along((axis, axis), number))
+                mine = keep[part]
+
+                def total(at, mine=mine, got=got):
+                    return mine[at].astype(f32) + got[at].astype(f32)
+
+                if number:
+                    keep[part] = total(0).astype(bf16)
+                    send[part] = total(1).astype(bf16)
+                elif leg < 2:
+                    keep[part] = total(slice(0, 2)).astype(bf16)
+                    send[part] = total(slice(2, 4)).astype(bf16)
+                else:
+                    keep[part] = total(slice(None))
+    return jnp.concatenate(keep)
 
 
 def lane_of(shape):
@@ -597,10 +602,32 @@
 
 
 def outer_kernel(
-    place_ref, slot_ref, at_ref, dqkv_ref, mixed_ref, dhb_ref, nt_ref, dgate_ref, dup_ref, mt_ref,
-    cb_ref, gain_ref, out_ref,
+    slot_ref, at_ref, dqkv_ref, mixed_ref, dhb_ref, nt_ref, dgate_ref, dup_ref, mt_ref, cb_ref,
+    gain_ref, k0, k1, k2, s0, s1, s2, stage, sems,
 ):
     step = pl.program_id(0)
+    buf = step % 2
+    slot_y, slot_x = slot_ref[step // 4], slot_ref[4 + step % 4]
+    zslot = [slot_ref[8 + k] for k in range(4)]
+    out_ref = stage.at[buf]
+    (a0, b0), (a1, b1), (a2, b2) = PART_ROWS
+
+    def copy(i, buf, half=0):
+        src = stage.at[buf]
+        if i == 0:
+            src, dst = src.at[:, a0:b0], (k0, s0)[half].at[slot_y % 2, slot_x]
+        elif i == 1:
+            src, dst = src.at[:, a1:b1], (k1, s1)[half].at[slot_x % 2, :, slot_y]
+        elif i == 2:
+            src, dst = src.at[0:2, a2:b2], k2.at[:, slot_y, slot_x]
+        else:
+            src, dst = src.at[2:4, a2:b2], s2.at[:, slot_y, slot_x]
+        return pltpu.make_async_copy(src, dst, sems.at[buf, i])
+
+    @pl.when(step >= 2)
+    def _():
+        for i in range(4):
+            copy(i, buf).wait()
 
     def row_of(k, count, at):
         row = lax.broadcasted_iota(jnp.int32, (count, 128), 0)
@@ -614,11 +641,11 @@
             res = mm(rows, dqkv_ref[:, 128 * c : 128 * c + width])
             for i, k in enumerate(ks):
                 for h in range(width // 128):
-                    out_ref[0, slot_ref[k], 96 * (c + h) : 96 * (c + h) + 96, :] = res[
+                    out_ref[zslot[k], 96 * (c + h) : 96 * (c + h) + 96, :] = res[
                         96 * i : 96 * i + 96, 128 * h : 128 * h + 128
                     ].astype(bf16)
         for k in ks:
-            out_ref[0, slot_ref[k], 1248:1280, :] = row_of(k, 32, 0).astype(bf16)
+            out_ref[zslot[k], 1248:1280, :] = row_of(k, 32, 0).astype(bf16)
 
     def wide(ref, start, cot_ref, ks):
         rows = ref[pl.ds(pl.multiple_of(start, 32), 160 * len(ks)), :]
@@ -630,7 +657,7 @@
                     if c + h == 7:
                         b = b + row_of(k, 160, 0)
                     at = 160 * (c + h)
-                    out_ref[0, slot_ref[k], at : at + 160, :] = b.astype(bf16)
+                    out_ref[zslot[k], at : at + 160, :] = b.astype(bf16)
 
     @pl.when(step < 2)
     def _():
@@ -657,31 +684,58 @@
                         at = 32 * (20 * part + c + h)
                         if at == 0:
                             b = b + row_of(k, 32, 30)
-                        out_ref[0, slot_ref[k], at : at + 32, :] = b.astype(bf16)
+                        out_ref[zslot[k], at : at + 32, :] = b.astype(bf16)
 
     @pl.when(step >= 12)
     def _():
         wide(mt_ref, 640 * (step - 12), cb_ref, (0, 1, 2, 3))
 
-
-def outer(places, slots, at, dqkv, mixed, dhb, nt, dgate, dup, mt, cb, gains):
-    whole = lambda v: pl.BlockSpec(v.shape, lambda s, place, slot: (0,) * v.ndim)
+    for half in range(2):
+
+        @pl.when(slot_y // 2 == half)
+        def _(half=half):
+            copy(0, buf, half).start()
+
+        @pl.when(slot_x // 2 == half)
+        def _(half=half):
+            copy(1, buf, half).start()
+
+    copy(2, buf).start()
+    copy(3, buf).start()
+
+    @pl.when(step == 15)
+    def _():
+        for last in (0, 1):
+            for i in range(4):
+                copy(i, last).wait()
+
+
+def outer(slots, at, dqkv, mixed, dhb, nt, dgate, dup, mt, cb, gains):
+    whole = lambda v: pl.BlockSpec(v.shape, lambda s, slot: (0,) * v.ndim)
     args = (at, dqkv, mixed, dhb, nt, dgate, dup, mt, cb, gains)
-    return pl.pallas_call(
+    shapes = [
+        jax.ShapeDtypeStruct((2, 4, 4, end - begin, 128), bf16) for begin, end in PART_ROWS
+    ]
+    out = pl.pallas_call(
         outer_kernel,
         name="outer",
         grid_spec=pltpu.PrefetchScalarGridSpec(
-            num_scalar_prefetch=2,
+            num_scalar_prefetch=1,
             grid=(16,),
             in_specs=[whole(v) for v in args],
-            out_specs=pl.BlockSpec((1, 4, ROWS, 128), lambda s, place, slot: (place[s], 0, 0, 0)),
+            out_specs=[pl.BlockSpec(memory_space=pl.ANY)] * 6,
+            scratch_shapes=[
+                pltpu.VMEM((2, 4, ROWS, 128), bf16),
+                pltpu.SemaphoreType.DMA((2, 4)),
+            ],
         ),
-        out_shape=jax.ShapeDtypeStruct((16, 4, ROWS, 128), bf16),
+        out_shape=shapes * 2,
         compiler_params=pltpu.CompilerParams(vmem_limit_bytes=48 << 20),
         cost_estimate=pl.CostEstimate(
             flops=2_600_000_000, bytes_accessed=24_000_000, transcendentals=0
         ),
-    )(places, slots, *args)
+    )(slots, *args)
+    return out[:3], out[3:]
 
 
 def shard_kind(rank):
@@ -827,10 +881,9 @@
         square, jnp.pad(gains, ((0, 0), (64, 34))), jnp.pad(gains, ((0, 0), (0, 98)))
     )
     four = jnp.arange(4, dtype=jnp.int32)
-    slots_y, slots_x, slots_z = (slot_of(four ^ at_axis, phase) for at_axis in (y, x, z))
-    places = (slots_y[:, None] * 4 + slots_x[None, :]).reshape(16)
-    grads = outer(places, slots_z, at, dqkv, mixed, dhb, nt, dgate, dup, mt, cb, gains)
-    total = scatter_grads(grads.reshape(4, 4, 4, ROWS, 128))
+    slots = jnp.concatenate([slot_of(four ^ at_axis, phase) for at_axis in (y, x, z)])
+    keep, send = outer(slots, at, dqkv, mixed, dhb, nt, dgate, dup, mt, cb, gains)
+    total = scatter_grads(keep, send)
     param_part, gain_part = blocks_shard(total, rank)
     return (result[None, None], d_u[None, None], param_part[None], gain_part[None])
 

time: 668 us -> 629 us (0.942)
  local copies, waits for them, and re-layouts: 55.9 us -> 26.9 us
    slice x18 -> x0, local copies, waits for them, and re-layouts: 19.3 us -> none  [the longest x2 10.6 us: scatter_grads(): keep = lax.slice_in_dim(block, 0, half, axis=dim)]
    ppermute x54, waiting for transfers between devices: 200 us -> 193 us  [swapped(): return lax.ppermute(block, ALL, pairs)]
    unnamed x134 -> x110, local copies, waits for them, and re-layouts: 22.9 us -> 16.4 us
  transfers between devices with their start and end apart: 69 -> 69, of which waited for: 48 -> 50; matrix products, arithmetic and copies ran while one was open for 8% -> 5% of each run, Pallas kernels for 0% -> 0%
where the time goes in v3:
time: 629 us; the launch traced here: 620 us
  waiting for transfers between devices  327 us (52%)
  Pallas kernels  129 us (21%)
  starting transfers between devices  83.5 us (13%)
  other arithmetic  35.8 us (6%)
  local copies, waits for them, and re-layouts  26.9 us (4%)
  between operations  17.4 us (3%)
    ppermute x54, waiting for transfers between devices, swapped(): return lax.ppermute(block, ALL, pairs)  193 us
    all_gather x1, waiting for transfers between devices, per_device(): gathered = lax.all_gather(own, ('ctx', 'fsdp'), axis=0)  119 us
    ppermute x54, starting transfers between devices, swapped(): return lax.ppermute(block, ALL, pairs)  62.1 us
    pallas_call x2, Pallas kernels, attend_back(): pl.pallas_call(attend_back_kernel, name='attend_back', grid=(SIDE,), in_s...  31.8 us
    pallas_call x2, Pallas kernels, feed_back(): pl.pallas_call(feed_back_kernel, name='feed_back', grid=(4,), in_specs=[w...  29.8 us
    pallas_call x2, Pallas kernels, feed(): pl.pallas_call(feed_kernel, name='feed', grid=(4,), in_specs=[whole(D, R)...  21.6 us
    ppermute x14, starting transfers between devices, over(): return lax.ppermute(block, 'phase', [(source, 1 - source)])  21.3 us
    pallas_call x2, Pallas kernels, attend(): pl.pallas_call(attend_kernel, name='attend', grid=(SIDE,), in_specs=[pl.B...  17.9 us
  transfers between devices with their start and end apart: 69, of which 50 were waited for; matrix products, arithmetic and copies ran while one was open for 5% of the time, Pallas kernels for 0%

profile of v3, /device:TPU:0, one launch (start us, length us, event | category | flops | bytes accessed | tf_op | source)
XLA Modules:
  0.0 620.4 jit_solution(3597762067484056060)
XLA Ops:
  9.2 8.3 %conditional.2 = (bf16[1280,128]{1,0:T(8,128)(2,1)S(1)}) conditional(s32[]{:T(128)} %clamp.4, (bf16[1,153600]{1,0:T(2,128)(2,1)}, bf16[1,128]{1,0:T(2,128)(2,1)S(1)}) %tuple.49, (bf16[1,153600]{1,0:T(2,128)(2,1)}, bf16[1,128]{1,0:T(2,128)(2,1)S(1)}) %tuple.49, (bf16[1,153600]{1,0:T(2,128)(2,1)}, bf16[1,128]{1,0:T(2,128)(2,1)S(1)}) %tuple.49), branch_computations={%region_1.2_spmd, %region_2.3_spmd, %region_3.5_spmd} | conditional | flops 983040 | bytes 3780876 | solution.py:763
  9.2 7.4 %reduce.15 = bf16[153600]{0:T(1024)(128)(2,1)S(1)} reduce(bf16[1,153600]{1,0:T(2,128)(2,1)} %get-tuple-element.66, bf16[]{:T(256)} %constant.274), dimensions={0}, to_apply=%get-tuple-element.66.reduce_sub_computation | reduce | bytes 614402 | tf_op jit(solution)/shard_map
  24.0 119.0 %all-gather.3.cloned.1.call-done = bf16[81920,128]{1,0:T(8,128)(2,1)} async-done(((bf16[1280,128]{1,0:T(8,128)(2,1)}), bf16[81920,128]{1,0:T(8,128)(2,1)}) %all-gather.3.cloned.1.call-update) | async-done | bytes 20971536 | tf_op jit(solution)/shard_map/all_gather | solution.py:803
  146.5 3.0 project.2
  152.2 3.0 collective-permute-start.5
  160.4 2.8 collective-permute-start.3
  163.5 2.8 collective-permute-start.7
  170.5 2.7 collective-permute-start.8
  175.3 4.5 collective-permute-done.8
  180.0 4.5 collective-permute-start.9
  190.0 4.5 collective-permute-done.9
  194.5 3.2 collective-permute-done.10
  198.2 9.0 %attend.2 = (bf16[576,128]{1,0:T(8,128)(2,1)S(1)}, f32[3,1,384]{2,1,0:T(1,128)S(1)}) custom-call(bf16[576,128]{1,0:T(8,128)(2,1)S(1)} %slice_select_fusion.3.qt_ref, bf16[4096,384]{1,0:T(8,128)(2,1)S(1)} %bitcast.202, f32[4096,128]{1,0:T(8,128)S(1)} %and_select_fusion.bias_ref), custom_call_target="tpu_custom_call" | custom-call | flops 4000000000 | bytes 8000000 | tf_op jit(solution)/shard_map/attend/pallas_call | solution.py:263
  210.5 11.5 %feed.2 = (bf16[128,960]{1,0:T(8,128)(2,1)S(1)}, f32[128,960]{1,0:T(8,128)}, bf16[1024,128]{1,0:T(8,128)(2,1)}, f32[128,2560]{1,0:T(8,128)}, f32[128,2560]{1,0:T(8,128)}, /*index=5*/bf16[2560,128]{1,0:T(8,128)(2,1)}) custom-call(bf16[960,128]{1,0:T(8,128)(2,1)S(1)} %constant_dynamic-update-slice_fusion.mixed_ref, bf16[128,960]{1,0:T(8,128)(2,1)S(1)} %bitcast.201, ...), custom_call_target="tpu_custom_call" | custom-call | flops 2200000000 | bytes 22000000 | tf_op jit(solution)/shard_map/feed/pallas_call | solution.py:366
  225.2 3.0 project.3
  234.3 3.6 collective-permute-done.18
  239.5 4.0 collective-permute-done.19
  247.1 3.4 collective-permute-done.20
  253.2 7.3 %collective-permute-done.21 = bf16[4,128,384]{2,1,0:T(8,128)(2,1)S(1)} collective-permute-done((bf16[4,128,384]{2,1,0:T(8,128)(2,1)S(1)}, bf16[4,128,384]{2,1,0:T(8,128)(2,1)S(1)}, u32[]{:S(2)}, u32[]{:S(2)}) %collective-permute-start.21) | collective-permute-done | bytes 393248 | tf_op jit(solution)/shard_map/ppermute | solution.py:57
  265.6 8.3 %collective-permute-done.22 = bf16[8,128,384]{2,1,0:T(8,128)(2,1)S(1)} collective-permute-done((bf16[8,128,384]{2,1,0:T(8,128)(2,1)S(1)}, bf16[8,128,384]{2,1,0:T(8,128)(2,1)S(1)}, u32[]{:S(2)}, u32[]{:S(2)}) %collective-permute-start.22) | collective-permute-done | bytes 786464 | tf_op jit(solution)/shard_map/ppermute | solution.py:57
  276.0 9.0 %attend.3 = (bf16[576,128]{1,0:T(8,128)(2,1)S(1)}, f32[3,1,384]{2,1,0:T(1,128)S(1)}) custom-call(bf16[576,128]{1,0:T(8,128)(2,1)S(1)} %slice_select_fusion.2.qt_ref, bf16[4096,384]{1,0:T(8,128)(2,1)S(1)} %bitcast.204, f32[4096,128]{1,0:T(8,128)S(1)} %and_select_fusion.bias_ref), custom_call_target="tpu_custom_call" | custom-call | flops 4000000000 | bytes 8000000 | tf_op jit(solution)/shard_map/attend/pallas_call | solution.py:263
  290.3 10.1 %feed.3 = (bf16[128,960]{1,0:T(8,128)(2,1)S(1)}, f32[128,960]{1,0:T(8,128)S(1)}, bf16[1024,128]{1,0:T(8,128)(2,1)S(1)}, f32[128,2560]{1,0:T(8,128)S(1)}, f32[128...) custom-call(bf16[960,128]{1,0:T(8,128)(2,1)S(1)} %maximum_select_fusion.2.mixed_ref, ...), custom_call_target="tpu_custom_call" | custom-call | flops 2200000000 | bytes 22000000 | tf_op jit(solution)/shard_map/feed/pallas_call | solution.py:366
  303.0 15.3 %feed_back.2 = (bf16[128,2560]{1,0:T(8,128)(2,1)}, bf16[128,2560]{1,0:T(8,128)(2,1)}, f32[128,960]{1,0:T(8,128)S(1)}, bf16[128,1024]{1,0:T(8,128)(2,1)}, f32[1,9...) custom-call(f32[128,960]{1,0:T(8,128)S(1)} %bitcast.199, ...), custom_call_target="tpu_custom_call" | custom-call | flops 2200000000 | bytes 22000000 | tf_op jit(solution)/shard_map/feed_back/pallas_call | solution.py:457
  321.9 15.9 %attend_back.2 = (bf16[4096,384]{1,0:T(8,128)(2,1)S(1)}, f32[576,128]{1,0:T(8,128)S(1)}) custom-call(bf16[576,128]{1,0:T(8,128)(2,1)S(1)} %copy-done.16, bf16[4096,384]{1,0:T(8,128)(2,1)} %bitcast.205, f32[4096,128]{1,0:T(8,128)S(1)} %and_select_fusion.bias_ref, f32[576,128]{1,0:T(8,128)S(1)} %slice_select_fusion.1.dot_ref, bf16[576,128]{1,0:T(8,128)(2,1)S(1)} %copy-done.8, ...), custom_call_target="tpu_custom_call" | custom-call | flops 10000000000 | bytes 14000000 | tf_op jit(solution)/shard_map/attend_back/pallas_call | solution.py:515
  340.4 11.0 %collective-permute-done.31 = bf16[8,128,384]{2,1,0:T(8,128)(2,1)S(1)} collective-permute-done((bf16[8,128,384]{2,1,0:T(8,128)(2,1)S(1)}, bf16[8,128,384]{2,1,0:T(8,128)(2,1)S(1)}, u32[]{:S(2)}, u32[]{:S(2)}) %collective-permute-start.31) | collective-permute-done | bytes 786464 | tf_op jit(solution)/shard_map/ppermute | solution.py:57
  352.2 7.4 %collective-permute-done.32 = bf16[4,128,384]{2,1,0:T(8,128)(2,1)S(1)} collective-permute-done((bf16[4,128,384]{2,1,0:T(8,128)(2,1)S(1)}, bf16[4,128,384]{2,1,0:T(8,128)(2,1)S(1)}, u32[]{:S(2)}, u32[]{:S(2)}) %collective-permute-start.32) | collective-permute-done | bytes 393248 | tf_op jit(solution)/shard_map/ppermute | solution.py:57
  361.6 3.3 collective-permute-start.29
  366.8 2.7 collective-permute-done.29
  374.3 3.3 collective-permute-done.35
  380.6 4.2 project_back.2
  388.4 14.4 %feed_back.3 = (bf16[128,2560]{1,0:T(8,128)(2,1)S(1)}, bf16[128,2560]{1,0:T(8,128)(2,1)S(1)}, f32[128,960]{1,0:T(8,128)S(1)}, bf16[128,1024]{1,0:T(8,128)(2,1)S(...) custom-call(f32[128,960]{1,0:T(8,128)S(1)} %convert_select_fusion.c_ref, ...), custom_call_target="tpu_custom_call" | custom-call | flops 2200000000 | bytes 22000000 | tf_op jit(solution)/shard_map/feed_back/pallas_call | solution.py:457
  407.6 15.9 %attend_back.3 = (bf16[4096,384]{1,0:T(8,128)(2,1)S(1)}, f32[576,128]{1,0:T(8,128)S(1)}) custom-call(bf16[576,128]{1,0:T(8,128)(2,1)S(1)} %copy-done.14, bf16[4096,384]{1,0:T(8,128)(2,1)} %bitcast.203, f32[4096,128]{1,0:T(8,128)S(1)} %and_select_fusion.bias_ref, f32[576,128]{1,0:T(8,128)S(1)} %slice_select_fusion.dot_ref, bf16[576,128]{1,0:T(8,128)(2,1)S(1)} %copy-done.10, ...), custom_call_target="tpu_custom_call" | custom-call | flops 10000000000 | bytes 14000000 | tf_op jit(solution)/shard_map/attend_back/pallas_call | solution.py:515
  426.1 11.0 %collective-permute-done.44 = bf16[8,128,384]{2,1,0:T(8,128)(2,1)S(1)} collective-permute-done((bf16[8,128,384]{2,1,0:T(8,128)(2,1)S(1)}, bf16[8,128,384]{2,1,0:T(8,128)(2,1)S(1)}, u32[]{:S(2)}, u32[]{:S(2)}) %collective-permute-start.44) | collective-permute-done | bytes 786464 | tf_op jit(solution)/shard_map/ppermute | solution.py:57
  440.4 5.1 collective-permute-done.45
  449.2 4.5 collective-permute-done.46
  453.9 2.8 collective-permute-done.42
  461.5 3.3 collective-permute-done.48
  468.2 3.7 project_back.3
  477.6 14.2 %outer.1 = (bf16[2,4,4,432,128]{4,3,2,1,0:T(8,128)(2,1)}, bf16[2,4,4,432,128]{4,3,2,1,0:T(8,128)(2,1)}, bf16[2,4,4,416,128]{4,3,2,1,0:T(8,128)(2,1)}, bf16[2,4,4...) custom-call(s32[12]{0:T(128)S(1)} %pad_add_fusion.2.slot_ref, ...), custom_call_target="tpu_custom_call" | custom-call | flops 2600000000 | bytes 24000000 | tf_op jit(solution)/shard_map/outer/pallas_call | solution.py:719
  495.8 37.6 %collective-permute-done.62 = bf16[2,4,4,416,128]{4,3,2,1,0:T(8,128)(2,1)S(1)} collective-permute-done((bf16[2,4,4,416,128]{4,3,2,1,0:T(8,128)(2,1)}, bf16[2,4,4,416,128]{4,3,2,1,0:T(8,128)(2,1)S(1)}, u32[]{:S(2)}, u32[]{:S(2)}) %collective-permute-start.62) | collective-permute-done | bytes 3407904 | tf_op jit(solution)/shard_map/ppermute | solution.py:57
  533.4 3.1 add_convert_fusion.5
  539.6 18.8 %collective-permute-done.63 = bf16[4,4,416,128]{3,2,1,0:T(8,128)(2,1)S(1)} collective-permute-done((bf16[4,4,416,128]{3,2,1,0:T(8,128)(2,1)S(1)}, bf16[4,4,416,128]{3,2,1,0:T(8,128)(2,1)S(1)}, u32[]{:S(2)}, u32[]{:S(2)}) %collective-permute-start.63) | collective-permute-done | bytes 1703968 | tf_op jit(solution)/shard_map/ppermute | solution.py:57
  566.3 6.7 %collective-permute-done.64 = bf16[2,4,416,128]{3,2,1,0:T(8,128)(2,1)S(1)} collective-permute-done((bf16[2,4,416,128]{3,2,1,0:T(8,128)(2,1)S(1)}, bf16[2,4,416,128]{3,2,1,0:T(8,128)(2,1)S(1)}, u32[]{:S(2)}, u32[]{:S(2)}) %collective-permute-start.64) | collective-permute-done | bytes 852000 | tf_op jit(solution)/shard_map/ppermute | solution.py:57
  577.8 4.7 collective-permute-done.65
  587.6 3.1 collective-permute-done.66
  592.5 5.0 collective-permute-done.59
  600.1 5.9 collective-permute-done.60
  606.2 4.7 collective-permute-done.61
  (364 shorter events, 149.8 us)
Async XLA Ops:
  7.2 135.9 %all-gather.3.cloned.1.call-start = ((), (), s32[]{:S(2)}) async-start(), calls=%async_computation | async-start | bytes 21299200 | tf_op jit(solution)/shard_map/all_gather | solution.py:803
  152.2 6.6 %collective-permute-start.5 = (bf16[128,384]{1,0:T(8,128)(2,1)S(1)}, bf16[128,384]{1,0:T(8,128)(2,1)S(1)}, u32[]{:S(2)}, u32[]{:S(2)}) collective-permute-start(bf16[128,384]{1,0:T(8,128)(2,1)S(1)} %slice_select_fusion.5), channel_id=1, source_target_pairs={{0,2},{1,3},{2,0},{3,1},{4,6},{5,7},{6,4},{7,5},{8,10},{9,11},{10,... | collective-permute-start | bytes 294920 | tf_op jit(solution)/shard_map/ppermute | solution.py:57
  160.4 7.0 %collective-permute-start.3 = (bf16[2,128,384]{2,1,0:T(8,128)(2,1)S(1)}, bf16[2,128,384]{2,1,0:T(8,128)(2,1)S(1)}, u32[]{:S(2)}, u32[]{:S(2)}) collective-permute-start(bf16[2,128,384]{2,1,0:T(8,128)(2,1)S(1)} %pad_maximum_fusion.12), channel_id=1, source_target_pairs={{0,48},{1,49},{2,50},{3,51},{4,52},{5,53},{6,54},{7,55},{8,56},{9,... | collective-permute-start | bytes 589832 | tf_op jit(solution)/shard_map/ppermute | solution.py:57
  163.5 7.0 %collective-permute-start.7 = (bf16[2,128,384]{2,1,0:T(8,128)(2,1)S(1)}, bf16[2,128,384]{2,1,0:T(8,128)(2,1)S(1)}, u32[]{:S(2)}, u32[]{:S(2)}) collective-permute-start(bf16[2,128,384]{2,1,0:T(8,128)(2,1)S(1)} %pad_maximum_fusion.13), channel_id=1, source_target_pairs={{0,12},{1,13},{2,14},{3,15},{4,8},{5,9},{6,10},{7,11},{8,4},{9,5},... | collective-permute-start | bytes 589832 | tf_op jit(solution)/shard_map/ppermute | solution.py:57
  167.4 7.9 %collective-permute-start.4 = (bf16[4,128,384]{2,1,0:T(8,128)(2,1)S(1)}, bf16[4,128,384]{2,1,0:T(8,128)(2,1)S(1)}, u32[]{:S(2)}, u32[]{:S(2)}) collective-permute-start(bf16[4,128,384]{2,1,0:T(8,128)(2,1)S(1)} %pad_maximum_fusion.7), channel_id=1, source_target_pairs={{0,4},{1,5},{2,6},{3,7},{4,0},{5,1},{6,2},{7,3},{8,12},{9,13},{10,... | collective-permute-start | bytes 1179656 | tf_op jit(solution)/shard_map/ppermute | solution.py:57
  170.5 9.3 %collective-permute-start.8 = (bf16[4,128,384]{2,1,0:T(8,128)(2,1)S(1)}, bf16[4,128,384]{2,1,0:T(8,128)(2,1)S(1)}, u32[]{:S(2)}, u32[]{:S(2)}) collective-permute-start(bf16[4,128,384]{2,1,0:T(8,128)(2,1)S(1)} %pad_maximum_fusion.8), channel_id=1, source_target_pairs={{0,16},{1,17},{2,18},{3,19},{4,20},{5,21},{6,22},{7,23},{8,24},{9,... | collective-permute-start | bytes 1179656 | tf_op jit(solution)/shard_map/ppermute | solution.py:57
  180.0 14.5 %collective-permute-start.9 = (bf16[8,128,384]{2,1,0:T(8,128)(2,1)S(1)}, bf16[8,128,384]{2,1,0:T(8,128)(2,1)S(1)}, u32[]{:S(2)}, u32[]{:S(2)}) collective-permute-start(bf16[8,128,384]{2,1,0:T(8,128)(2,1)S(1)} %pad_maximum_fusion.2), channel_id=1, source_target_pairs={{0,12},{1,13},{2,14},{3,15},{4,8},{5,9},{6,10},{7,11},{8,4},{9,5},... | collective-permute-start | bytes 2359304 | tf_op jit(solution)/shard_map/ppermute | solution.py:57
  184.5 13.2 %collective-permute-start.10 = (bf16[8,128,384]{2,1,0:T(8,128)(2,1)S(1)}, bf16[8,128,384]{2,1,0:T(8,128)(2,1)S(1)}, u32[]{:S(2)}, u32[]{:S(2)}) collective-permute-start(bf16[8,128,384]{2,1,0:T(8,128)(2,1)S(1)} %pad_maximum_fusion.3), channel_id=1, source_target_pairs={{0,48},{1,49},{2,50},{3,51},{4,52},{5,53},{6,54},{7,55},{8,56},{9,... | collective-permute-start | bytes 2359304 | tf_op jit(solution)/shard_map/ppermute | solution.py:57
  231.5 6.4 %collective-permute-start.18 = (bf16[128,384]{1,0:T(8,128)(2,1)S(1)}, bf16[128,384]{1,0:T(8,128)(2,1)S(1)}, u32[]{:S(2)}, u32[]{:S(2)}) collective-permute-start(bf16[128,384]{1,0:T(8,128)(2,1)S(1)} %slice_select_fusion.4), channel_id=1, source_target_pairs={{0,2},{1,3},{2,0},{3,1},{4,6},{5,7},{6,4},{7,5},{8,10},{9,11},{10,... | collective-permute-start | bytes 294920 | tf_op jit(solution)/shard_map/ppermute | solution.py:57
  238.0 7.0 %collective-permute-start.16 = (bf16[2,128,384]{2,1,0:T(8,128)(2,1)S(1)}, bf16[2,128,384]{2,1,0:T(8,128)(2,1)S(1)}, u32[]{:S(2)}, u32[]{:S(2)}) collective-permute-start(bf16[2,128,384]{2,1,0:T(8,128)(2,1)S(1)} %pad_maximum_fusion.14), channel_id=1, source_target_pairs={{0,48},{1,49},{2,50},{3,51},{4,52},{5,53},{6,54},{7,55},{8,56},{9,... | collective-permute-start | bytes 589832 | tf_op jit(solution)/shard_map/ppermute | solution.py:57
  243.5 7.0 %collective-permute-start.20 = (bf16[2,128,384]{2,1,0:T(8,128)(2,1)S(1)}, bf16[2,128,384]{2,1,0:T(8,128)(2,1)S(1)}, u32[]{:S(2)}, u32[]{:S(2)}) collective-permute-start(bf16[2,128,384]{2,1,0:T(8,128)(2,1)S(1)} %pad_maximum_fusion.15), channel_id=1, source_target_pairs={{0,12},{1,13},{2,14},{3,15},{4,8},{5,9},{6,10},{7,11},{8,4},{9,5},... | collective-permute-start | bytes 589832 | tf_op jit(solution)/shard_map/ppermute | solution.py:57
  245.0 8.1 %collective-permute-start.17 = (bf16[4,128,384]{2,1,0:T(8,128)(2,1)S(1)}, bf16[4,128,384]{2,1,0:T(8,128)(2,1)S(1)}, u32[]{:S(2)}, u32[]{:S(2)}) collective-permute-start(bf16[4,128,384]{2,1,0:T(8,128)(2,1)S(1)} %pad_maximum_fusion.9), channel_id=1, source_target_pairs={{0,4},{1,5},{2,6},{3,7},{4,0},{5,1},{6,2},{7,3},{8,12},{9,13},{10,... | collective-permute-start | bytes 1179656 | tf_op jit(solution)/shard_map/ppermute | solution.py:57
  250.6 9.9 %collective-permute-start.21 = (bf16[4,128,384]{2,1,0:T(8,128)(2,1)S(1)}, bf16[4,128,384]{2,1,0:T(8,128)(2,1)S(1)}, u32[]{:S(2)}, u32[]{:S(2)}) collective-permute-start(bf16[4,128,384]{2,1,0:T(8,128)(2,1)S(1)} %pad_maximum_fusion.10), channel_id=1, source_target_pairs={{0,16},{1,17},{2,18},{3,19},{4,20},{5,21},{6,22},{7,23},{8,24},{9,... | collective-permute-start | bytes 1179656 | tf_op jit(solution)/shard_map/ppermute | solution.py:57
  260.6 13.3 %collective-permute-start.22 = (bf16[8,128,384]{2,1,0:T(8,128)(2,1)S(1)}, bf16[8,128,384]{2,1,0:T(8,128)(2,1)S(1)}, u32[]{:S(2)}, u32[]{:S(2)}) collective-permute-start(bf16[8,128,384]{2,1,0:T(8,128)(2,1)S(1)} %pad_maximum_fusion.4), channel_id=1, source_target_pairs={{0,12},{1,13},{2,14},{3,15},{4,8},{5,9},{6,10},{7,11},{8,4},{9,5},... | collective-permute-start | bytes 2359304 | tf_op jit(solution)/shard_map/ppermute | solution.py:57
  262.3 13.2 %collective-permute-start.23 = (bf16[8,128,384]{2,1,0:T(8,128)(2,1)S(1)}, bf16[8,128,384]{2,1,0:T(8,128)(2,1)S(1)}, u32[]{:S(2)}, u32[]{:S(2)}) collective-permute-start(bf16[8,128,384]{2,1,0:T(8,128)(2,1)S(1)} %pad_maximum_fusion.5), channel_id=1, source_target_pairs={{0,48},{1,49},{2,50},{3,51},{4,52},{5,53},{6,54},{7,55},{8,56},{9,... | collective-permute-start | bytes 2359304 | tf_op jit(solution)/shard_map/ppermute | solution.py:57
  338.2 13.3 %collective-permute-start.31 = (bf16[8,128,384]{2,1,0:T(8,128)(2,1)S(1)}, bf16[8,128,384]{2,1,0:T(8,128)(2,1)S(1)}, u32[]{:S(2)}, u32[]{:S(2)}) collective-permute-start(bf16[8,128,384]{2,1,0:T(8,128)(2,1)S(1)} %bitcast.286), channel_id=1, source_target_pairs={{0,48},{1,49},{2,50},{3,51},{4,52},{5,53},{6,54},{7,55},{8,56},{9,... | collective-permute-start | bytes 2359304 | tf_op jit(solution)/shard_map/ppermute | solution.py:57
  338.2 13.6 %collective-permute-start.27 = (bf16[8,128,384]{2,1,0:T(8,128)(2,1)S(1)}, bf16[8,128,384]{2,1,0:T(8,128)(2,1)S(1)}, u32[]{:S(2)}, u32[]{:S(2)}) collective-permute-start(bf16[8,128,384]{2,1,0:T(8,128)(2,1)S(1)} %bitcast.284), channel_id=1, source_target_pairs={{0,12},{1,13},{2,14},{3,15},{4,8},{5,9},{6,10},{7,11},{8,4},{9,5},... | collective-permute-start | bytes 2359304 | tf_op jit(solution)/shard_map/ppermute | solution.py:57
  351.7 7.9 %collective-permute-start.32 = (bf16[4,128,384]{2,1,0:T(8,128)(2,1)S(1)}, bf16[4,128,384]{2,1,0:T(8,128)(2,1)S(1)}, u32[]{:S(2)}, u32[]{:S(2)}) collective-permute-start(bf16[4,128,384]{2,1,0:T(8,128)(2,1)S(1)} %slice.626), channel_id=1, source_target_pairs={{0,16},{1,17},{2,18},{3,19},{4,20},{5,21},{6,22},{7,23},{8,24},{9,... | collective-permute-start | bytes 1179656 | tf_op jit(solution)/shard_map/ppermute | solution.py:57
  352.1 9.4 %collective-permute-start.28 = (bf16[4,128,384]{2,1,0:T(8,128)(2,1)S(1)}, bf16[4,128,384]{2,1,0:T(8,128)(2,1)S(1)}, u32[]{:S(2)}, u32[]{:S(2)}) collective-permute-start(bf16[4,128,384]{2,1,0:T(8,128)(2,1)S(1)} %slice.620), channel_id=1, source_target_pairs={{0,4},{1,5},{2,6},{3,7},{4,0},{5,1},{6,2},{7,3},{8,12},{9,13},{10,... | collective-permute-start | bytes 1179656 | tf_op jit(solution)/shard_map/ppermute | solution.py:57
  359.7 7.0 %collective-permute-start.33 = (bf16[2,128,384]{2,1,0:T(8,128)(2,1)S(1)}, bf16[2,128,384]{2,1,0:T(8,128)(2,1)S(1)}, u32[]{:S(2)}, u32[]{:S(2)}) collective-permute-start(bf16[2,128,384]{2,1,0:T(8,128)(2,1)S(1)} %slice.628), channel_id=1, source_target_pairs={{0,12},{1,13},{2,14},{3,15},{4,8},{5,9},{6,10},{7,11},{8,4},{9,5},... | collective-permute-start | bytes 589832 | tf_op jit(solution)/shard_map/ppermute | solution.py:57
  361.6 8.0 %collective-permute-start.29 = (bf16[2,128,384]{2,1,0:T(8,128)(2,1)S(1)}, bf16[2,128,384]{2,1,0:T(8,128)(2,1)S(1)}, u32[]{:S(2)}, u32[]{:S(2)}) collective-permute-start(bf16[2,128,384]{2,1,0:T(8,128)(2,1)S(1)} %slice.622), channel_id=1, source_target_pairs={{0,48},{1,49},{2,50},{3,51},{4,52},{5,53},{6,54},{7,55},{8,56},{9,... | collective-permute-start | bytes 589832 | tf_op jit(solution)/shard_map/ppermute | solution.py:57
  371.5 6.2 collective-permute-start.35
  372.8 6.3 %collective-permute-start.26 = (f32[384,128]{1,0:T(8,128)S(1)}, f32[384,128]{1,0:T(8,128)S(1)}, u32[]{:S(2)}, u32[]{:S(2)}) collective-permute-start(f32[384,128]{1,0:T(8,128)S(1)} %slice.499), channel_id=1, source_target_pairs={{0,64},{1,65},{2,66},{3,67},{4,68},{5,69},{6,70},{7,71},{8,72},{9,... | collective-permute-start | bytes 589832 | tf_op jit(solution)/shard_map/ppermute | solution.py:61
  423.8 13.3 %collective-permute-start.44 = (bf16[8,128,384]{2,1,0:T(8,128)(2,1)S(1)}, bf16[8,128,384]{2,1,0:T(8,128)(2,1)S(1)}, u32[]{:S(2)}, u32[]{:S(2)}) collective-permute-start(bf16[8,128,384]{2,1,0:T(8,128)(2,1)S(1)} %bitcast.285), channel_id=1, source_target_pairs={{0,48},{1,49},{2,50},{3,51},{4,52},{5,53},{6,54},{7,55},{8,56},{9,... | collective-permute-start | bytes 2359304 | tf_op jit(solution)/shard_map/ppermute | solution.py:57
  424.4 13.3 %collective-permute-start.40 = (bf16[8,128,384]{2,1,0:T(8,128)(2,1)S(1)}, bf16[8,128,384]{2,1,0:T(8,128)(2,1)S(1)}, u32[]{:S(2)}, u32[]{:S(2)}) collective-permute-start(bf16[8,128,384]{2,1,0:T(8,128)(2,1)S(1)} %bitcast.283), channel_id=1, source_target_pairs={{0,12},{1,13},{2,14},{3,15},{4,8},{5,9},{6,10},{7,11},{8,4},{9,5},... | collective-permute-start | bytes 2359304 | tf_op jit(solution)/shard_map/ppermute | solution.py:57
  437.4 8.2 %collective-permute-start.45 = (bf16[4,128,384]{2,1,0:T(8,128)(2,1)S(1)}, bf16[4,128,384]{2,1,0:T(8,128)(2,1)}, u32[]{:S(2)}, u32[]{:S(2)}) collective-permute-start(bf16[4,128,384]{2,1,0:T(8,128)(2,1)S(1)} %slice.639), channel_id=1, source_target_pairs={{0,16},{1,17},{2,18},{3,19},{4,20},{5,21},{6,22},{7,23},{8,24},{9,... | collective-permute-start | bytes 1179656 | tf_op jit(solution)/shard_map/ppermute | solution.py:57
  438.3 10.3 %collective-permute-start.41 = (bf16[4,128,384]{2,1,0:T(8,128)(2,1)S(1)}, bf16[4,128,384]{2,1,0:T(8,128)(2,1)S(1)}, u32[]{:S(2)}, u32[]{:S(2)}) collective-permute-start(bf16[4,128,384]{2,1,0:T(8,128)(2,1)S(1)} %slice.633), channel_id=1, source_target_pairs={{0,4},{1,5},{2,6},{3,7},{4,0},{5,1},{6,2},{7,3},{8,12},{9,13},{10,... | collective-permute-start | bytes 1179656 | tf_op jit(solution)/shard_map/ppermute | solution.py:57
  446.8 7.0 %collective-permute-start.46 = (bf16[2,128,384]{2,1,0:T(8,128)(2,1)S(1)}, bf16[2,128,384]{2,1,0:T(8,128)(2,1)S(1)}, u32[]{:S(2)}, u32[]{:S(2)}) collective-permute-start(bf16[2,128,384]{2,1,0:T(8,128)(2,1)S(1)} %slice.641), channel_id=1, source_target_pairs={{0,12},{1,13},{2,14},{3,15},{4,8},{5,9},{6,10},{7,11},{8,4},{9,5},... | collective-permute-start | bytes 589832 | tf_op jit(solution)/shard_map/ppermute | solution.py:57
  448.7 8.0 %collective-permute-start.42 = (bf16[2,128,384]{2,1,0:T(8,128)(2,1)S(1)}, bf16[2,128,384]{2,1,0:T(8,128)(2,1)S(1)}, u32[]{:S(2)}, u32[]{:S(2)}) collective-permute-start(bf16[2,128,384]{2,1,0:T(8,128)(2,1)S(1)} %slice.635), channel_id=1, source_target_pairs={{0,48},{1,49},{2,50},{3,51},{4,52},{5,53},{6,54},{7,55},{8,56},{9,... | collective-permute-start | bytes 589832 | tf_op jit(solution)/shard_map/ppermute | solution.py:57
  458.6 6.2 collective-permute-start.48
  460.0 6.2 collective-permute-start.39
  491.8 41.6 %collective-permute-start.62 = (bf16[2,4,4,416,128]{4,3,2,1,0:T(8,128)(2,1)}, bf16[2,4,4,416,128]{4,3,2,1,0:T(8,128)(2,1)S(1)}, u32[]{:S(2)}, u32[]{:S(2)}) collective-permute-start(bf16[2,4,4,416,128]{4,3,2,1,0:T(8,128)(2,1)} %get-tuple-element.169), channel_id=1, source_target_pairs={{0,3},{1,2},{2,1},{3,0},{4,7},{5,6},{6,5},{7,4},{8,11},{9,10},{10,... | collective-permute-start | bytes 10223624 | tf_op jit(solution)/shard_map/ppermute | solution.py:57
  493.3 43.3 %collective-permute-start.50 = (bf16[2,4,4,432,128]{4,3,2,1,0:T(8,128)(2,1)}, bf16[2,4,4,432,128]{4,3,2,1,0:T(8,128)(2,1)S(1)}, u32[]{:S(2)}, u32[]{:S(2)}) collective-permute-start(bf16[2,4,4,432,128]{4,3,2,1,0:T(8,128)(2,1)} %get-tuple-element.165), channel_id=1, source_target_pairs={{0,48},{1,49},{2,50},{3,51},{4,52},{5,53},{6,54},{7,55},{8,56},{9,... | collective-permute-start | bytes 10616840 | tf_op jit(solution)/shard_map/ppermute | solution.py:57
  494.0 44.0 %collective-permute-start.56 = (bf16[2,4,4,432,128]{4,3,2,1,0:T(8,128)(2,1)}, bf16[2,4,4,432,128]{4,3,2,1,0:T(8,128)(2,1)S(1)}, u32[]{:S(2)}, u32[]{:S(2)}) collective-permute-start(bf16[2,4,4,432,128]{4,3,2,1,0:T(8,128)(2,1)} %get-tuple-element.167), channel_id=1, source_target_pairs={{0,12},{1,13},{2,14},{3,15},{4,8},{5,9},{6,10},{7,11},{8,4},{9,5},... | collective-permute-start | bytes 10616840 | tf_op jit(solution)/shard_map/ppermute | solution.py:57
  536.5 21.9 %collective-permute-start.63 = (bf16[4,4,416,128]{3,2,1,0:T(8,128)(2,1)S(1)}, bf16[4,4,416,128]{3,2,1,0:T(8,128)(2,1)S(1)}, u32[]{:S(2)}, u32[]{:S(2)}) collective-permute-start(bf16[4,4,416,128]{3,2,1,0:T(8,128)(2,1)S(1)} %get-tuple-element.201), channel_id=1, source_target_pairs={{0,1},{1,0},{2,3},{3,2},{4,5},{5,4},{6,7},{7,6},{8,9},{9,8},{10,11... | collective-permute-start | bytes 5111816 | tf_op jit(solution)/shard_map/ppermute | solution.py:57
  537.5 22.8 %collective-permute-start.51 = (bf16[4,4,432,128]{3,2,1,0:T(8,128)(2,1)S(1)}, bf16[4,4,432,128]{3,2,1,0:T(8,128)(2,1)S(1)}, u32[]{:S(2)}, u32[]{:S(2)}) collective-permute-start(bf16[4,4,432,128]{3,2,1,0:T(8,128)(2,1)S(1)} %get-tuple-element.197), channel_id=1, source_target_pairs={{0,16},{1,17},{2,18},{3,19},{4,20},{5,21},{6,22},{7,23},{8,24},{9,... | collective-permute-start | bytes 5308424 | tf_op jit(solution)/shard_map/ppermute | solution.py:57
  539.5 23.8 %collective-permute-start.57 = (bf16[4,4,432,128]{3,2,1,0:T(8,128)(2,1)S(1)}, bf16[4,4,432,128]{3,2,1,0:T(8,128)(2,1)S(1)}, u32[]{:S(2)}, u32[]{:S(2)}) collective-permute-start(bf16[4,4,432,128]{3,2,1,0:T(8,128)(2,1)S(1)} %get-tuple-element.199), channel_id=1, source_target_pairs={{0,4},{1,5},{2,6},{3,7},{4,0},{5,1},{6,2},{7,3},{8,12},{9,13},{10,... | collective-permute-start | bytes 5308424 | tf_op jit(solution)/shard_map/ppermute | solution.py:57
  558.8 14.2 %collective-permute-start.64 = (bf16[2,4,416,128]{3,2,1,0:T(8,128)(2,1)S(1)}, bf16[2,4,416,128]{3,2,1,0:T(8,128)(2,1)S(1)}, u32[]{:S(2)}, u32[]{:S(2)}) collective-permute-start(bf16[2,4,416,128]{3,2,1,0:T(8,128)(2,1)S(1)} %get-tuple-element.207), channel_id=1, source_target_pairs={{0,48},{1,49},{2,50},{3,51},{4,52},{5,53},{6,54},{7,55},{8,56},{9,... | collective-permute-start | bytes 2555912 | tf_op jit(solution)/shard_map/ppermute | solution.py:57
  561.8 14.6 %collective-permute-start.52 = (bf16[2,4,432,128]{3,2,1,0:T(8,128)(2,1)}, bf16[2,4,432,128]{3,2,1,0:T(8,128)(2,1)}, u32[]{:S(2)}, u32[]{:S(2)}) collective-permute-start(bf16[2,4,432,128]{3,2,1,0:T(8,128)(2,1)} %get-tuple-element.203), channel_id=1, source_target_pairs={{0,12},{1,13},{2,14},{3,15},{4,8},{5,9},{6,10},{7,11},{8,4},{9,5},... | collective-permute-start | bytes 2654216 | tf_op jit(solution)/shard_map/ppermute | solution.py:57
  564.8 20.6 %collective-permute-start.58 = (bf16[2,4,432,128]{3,2,1,0:T(8,128)(2,1)}, bf16[2,4,432,128]{3,2,1,0:T(8,128)(2,1)}, u32[]{:S(2)}, u32[]{:S(2)}) collective-permute-start(bf16[2,4,432,128]{3,2,1,0:T(8,128)(2,1)} %get-tuple-element.205), channel_id=1, source_target_pairs={{0,3},{1,2},{2,1},{3,0},{4,7},{5,6},{6,5},{7,4},{8,11},{9,10},{10,... | collective-permute-start | bytes 2654216 | tf_op jit(solution)/shard_map/ppermute | solution.py:57
  574.1 8.4 %collective-permute-start.65 = (bf16[4,416,128]{2,1,0:T(8,128)(2,1)}, bf16[4,416,128]{2,1,0:T(8,128)(2,1)}, u32[]{:S(2)}, u32[]{:S(2)}) collective-permute-start(bf16[4,416,128]{2,1,0:T(8,128)(2,1)} %get-tuple-element.221), channel_id=1, source_target_pairs={{0,16},{1,17},{2,18},{3,19},{4,20},{5,21},{6,22},{7,23},{8,24},{9,... | collective-permute-start | bytes 1277960 | tf_op jit(solution)/shard_map/ppermute | solution.py:57
  577.7 13.2 %collective-permute-start.53 = (bf16[4,432,128]{2,1,0:T(8,128)(2,1)S(1)}, bf16[4,432,128]{2,1,0:T(8,128)(2,1)S(1)}, u32[]{:S(2)}, u32[]{:S(2)}) collective-permute-start(bf16[4,432,128]{2,1,0:T(8,128)(2,1)S(1)} %get-tuple-element.217), channel_id=1, source_target_pairs={{0,4},{1,5},{2,6},{3,7},{4,0},{5,1},{6,2},{7,3},{8,12},{9,13},{10,... | collective-permute-start | bytes 1327112 | tf_op jit(solution)/shard_map/ppermute | solution.py:57
  583.6 7.1 %collective-permute-start.66 = (bf16[2,416,128]{2,1,0:T(8,128)(2,1)S(1)}, bf16[2,416,128]{2,1,0:T(8,128)(2,1)S(1)}, u32[]{:S(2)}, u32[]{:S(2)}) collective-permute-start(bf16[2,416,128]{2,1,0:T(8,128)(2,1)S(1)} %get-tuple-element.227), channel_id=1, source_target_pairs={{0,12},{1,13},{2,14},{3,15},{4,8},{5,9},{6,10},{7,11},{8,4},{9,5},... | collective-permute-start | bytes 638984 | tf_op jit(solution)/shard_map/ppermute | solution.py:57
  586.8 10.8 %collective-permute-start.59 = (bf16[4,432,128]{2,1,0:T(8,128)(2,1)S(1)}, bf16[4,432,128]{2,1,0:T(8,128)(2,1)S(1)}, u32[]{:S(2)}, u32[]{:S(2)}) collective-permute-start(bf16[4,432,128]{2,1,0:T(8,128)(2,1)S(1)} %get-tuple-element.219), channel_id=1, source_target_pairs={{0,1},{1,0},{2,3},{3,2},{4,5},{5,4},{6,7},{7,6},{8,9},{9,8},{10,11... | collective-permute-start | bytes 1327112 | tf_op jit(solution)/shard_map/ppermute | solution.py:57
  590.8 7.4 %collective-permute-start.67 = (bf16[416,128]{1,0:T(8,128)(2,1)S(1)}, bf16[416,128]{1,0:T(8,128)(2,1)S(1)}, u32[]{:S(2)}, u32[]{:S(2)}) collective-permute-start(bf16[416,128]{1,0:T(8,128)(2,1)S(1)} %fusion.32), channel_id=1, source_target_pairs={{0,4},{1,5},{2,6},{3,7},{4,0},{5,1},{6,2},{7,3},{8,12},{9,13},{10,... | collective-permute-start | bytes 319496 | tf_op jit(solution)/shard_map/ppermute | solution.py:57
  591.0 7.2 %collective-permute-start.54 = (bf16[2,432,128]{2,1,0:T(8,128)(2,1)S(1)}, bf16[2,432,128]{2,1,0:T(8,128)(2,1)S(1)}, u32[]{:S(2)}, u32[]{:S(2)}) collective-permute-start(bf16[2,432,128]{2,1,0:T(8,128)(2,1)S(1)} %get-tuple-element.223), channel_id=1, source_target_pairs={{0,3},{1,2},{2,1},{3,0},{4,7},{5,6},{6,5},{7,4},{8,11},{9,10},{10,... | collective-permute-start | bytes 663560 | tf_op jit(solution)/shard_map/ppermute | solution.py:57
  597.7 8.3 %collective-permute-start.60 = (bf16[2,432,128]{2,1,0:T(8,128)(2,1)S(1)}, bf16[2,432,128]{2,1,0:T(8,128)(2,1)S(1)}, u32[]{:S(2)}, u32[]{:S(2)}) collective-permute-start(bf16[2,432,128]{2,1,0:T(8,128)(2,1)S(1)} %get-tuple-element.225), channel_id=1, source_target_pairs={{0,48},{1,49},{2,50},{3,51},{4,52},{5,53},{6,54},{7,55},{8,56},{9,... | collective-permute-start | bytes 663560 | tf_op jit(solution)/shard_map/ppermute | solution.py:57
  598.3 7.8 %collective-permute-start.55 = (bf16[432,128]{1,0:T(8,128)(2,1)S(1)}, bf16[432,128]{1,0:T(8,128)(2,1)S(1)}, u32[]{:S(2)}, u32[]{:S(2)}) collective-permute-start(bf16[432,128]{1,0:T(8,128)(2,1)S(1)} %fusion.28), channel_id=1, source_target_pairs={{0,1},{1,0},{2,3},{3,2},{4,5},{5,4},{6,7},{7,6},{8,9},{9,8},{10,11... | collective-permute-start | bytes 331784 | tf_op jit(solution)/shard_map/ppermute | solution.py:57
  (71 other events, 443.2 us)
Sparse Core Ops, SparseCore 0:
  18.4 124.5 all-gather.2

commit v4 on v3

--- a/solution.py
+++ b/solution.py
@@ -90,7 +90,7 @@
     return jnp.concatenate(blocks, axis=0).reshape(KEYS, tail[1])
 
 
-def scatter_keys(d_kv):
+def scatter_keys(d_kv, beside=None):
     parts = d_kv.reshape(2, 16, R, d_kv.shape[1])
     orders = (((0, 1), (1, 0)), ((1, 0), (0, 1)))
     blocks = [parts[0], parts[1]]
@@ -102,7 +102,11 @@
                 total = blocks[k][:half].astype(f32) + got.astype(f32)
                 last = k == 0 and half == 1
                 blocks[k] = total if last else total.astype(bf16)
-    return blocks[0][0] + swapped(blocks[1][0], far_z).astype(f32)
+            if beside is not None and number == 0:
+                beside = planes_step(beside, 0, leg)
+                blocks, beside = lax.optimization_barrier((blocks, beside))
+    total = blocks[0][0] + swapped(blocks[1][0], far_z).astype(f32)
+    return total if beside is None else (total, beside)
 
 
 def slot_offsets(phase):
@@ -127,33 +131,45 @@
     return jnp.concatenate(out)
 
 
-PART_ROWS = ((0, 432), (432, 864), (864, 1280))
-
-
-PART_AXES = ((0, 1, 2), (1, 2, 0), (2, 0, 1))
-
-
-def scatter_grads(keep, send):
-    keep, send = list(keep), list(send)
-    for leg in range(3):
+HALF = ROWS // 2
+PLUS = ROWS + 16
+PART_AXES = ((1, 2), (2, 1))
+
+
+def summed(mine, got, at):
+    return (mine[at].astype(f32) + got[at].astype(f32)).astype(bf16)
+
+
+def planes_step(state, leg, number):
+    keep, send = list(state[0]), list(state[1])
+    for part, axes in enumerate(PART_AXES):
+        axis = axes[leg]
+        got = swapped(send[part], along((axis, axis), number))
+        mine = keep[part]
+        if number:
+            keep[part] = summed(mine, got, 0)
+            send[part] = summed(mine, got, 1)
+        elif leg == 0:
+            keep[part] = summed(mine, got, slice(0, 2))
+            send[part] = summed(mine, got, slice(2, 4))
+        else:
+            keep[part] = summed(mine, got, slice(None))
+    return keep, send
+
+
+def scatter_planes(state, legs=(0, 1)):
+    for leg in legs:
         for number in (1, 0):
-            for part, axes in enumerate(PART_AXES):
-                axis = axes[leg]
-                got = swapped(send[part], along((axis, axis), number))
-                mine = keep[part]
-
-                def total(at, mine=mine, got=got):
-                    return mine[at].astype(f32) + got[at].astype(f32)
-
-                if number:
-                    keep[part] = total(0).astype(bf16)
-                    send[part] = total(1).astype(bf16)
-                elif leg < 2:
-                    keep[part] = total(slice(0, 2)).astype(bf16)
-                    send[part] = total(slice(2, 4)).astype(bf16)
-                else:
-                    keep[part] = total(slice(None))
-    return jnp.concatenate(keep)
+            state = planes_step(state, leg, number)
+    return state[0]
+
+
+def scatter_last(planes, y, phase):
+    slots = planes[y ^ slot_offsets(phase)]
+    got = swapped(slots[2:], along((0, 0), 1))
+    send = summed(slots[1], got[1], slice(None))
+    keep = slots[0].astype(f32) + got[0].astype(f32)
+    return keep + swapped(send, along((0, 0), 0)).astype(f32)
 
 
 def lane_of(shape):
@@ -601,141 +617,148 @@
     )(d_query, d_kv, cos, sin, u, gain, d_hidden, weights)
 
 
-def outer_kernel(
-    slot_ref, at_ref, dqkv_ref, mixed_ref, dhb_ref, nt_ref, dgate_ref, dup_ref, mt_ref, cb_ref,
-    gain_ref, k0, k1, k2, s0, s1, s2, stage, sems,
-):
-    step = pl.program_id(0)
+def stage_out(step, slot_ref, planes, outs, stage, sems, fill):
     buf = step % 2
-    slot_y, slot_x = slot_ref[step // 4], slot_ref[4 + step % 4]
-    zslot = [slot_ref[8 + k] for k in range(4)]
-    out_ref = stage.at[buf]
-    (a0, b0), (a1, b1), (a2, b2) = PART_ROWS
+    plane = step // 4
+    slot_x = slot_ref[step % 4]
+    zslot = [slot_ref[4 + k] for k in range(4)]
+    ka, kb, sa, sb = outs
+    rows = stage.shape[2]
 
     def copy(i, buf, half=0):
         src = stage.at[buf]
         if i == 0:
-            src, dst = src.at[:, a0:b0], (k0, s0)[half].at[slot_y % 2, slot_x]
+            src, dst = src.at[:, 0:HALF], (ka, sa)[half].at[slot_x % 2, :, plane]
         elif i == 1:
-            src, dst = src.at[:, a1:b1], (k1, s1)[half].at[slot_x % 2, :, slot_y]
-        elif i == 2:
-            src, dst = src.at[0:2, a2:b2], k2.at[:, slot_y, slot_x]
+            src, dst = src.at[0:2, HALF:rows], kb.at[:, slot_x, plane]
         else:
-            src, dst = src.at[2:4, a2:b2], s2.at[:, slot_y, slot_x]
+            src, dst = src.at[2:4, HALF:rows], sb.at[:, slot_x, plane]
         return pltpu.make_async_copy(src, dst, sems.at[buf, i])
 
     @pl.when(step >= 2)
     def _():
-        for i in range(4):
+        for i in range(3):
             copy(i, buf).wait()
 
-    def row_of(k, count, at):
-        row = lax.broadcasted_iota(jnp.int32, (count, 128), 0)
-        return jnp.where(row == at, gain_ref[pl.ds(4 * step + k, 1), :], 0.0)
-
-    def narrow(start, ks):
-        count = len(ks)
-        rows = at_ref[pl.ds(pl.multiple_of(start, 32), 96 * count), :]
-        for c in range(0, 13, 2):
-            width = min(256, 1664 - 128 * c)
-            res = mm(rows, dqkv_ref[:, 128 * c : 128 * c + width])
-            for i, k in enumerate(ks):
-                for h in range(width // 128):
-                    out_ref[zslot[k], 96 * (c + h) : 96 * (c + h) + 96, :] = res[
-                        96 * i : 96 * i + 96, 128 * h : 128 * h + 128
-                    ].astype(bf16)
-        for k in ks:
-            out_ref[zslot[k], 1248:1280, :] = row_of(k, 32, 0).astype(bf16)
-
-    def wide(ref, start, cot_ref, ks):
-        rows = ref[pl.ds(pl.multiple_of(start, 32), 160 * len(ks)), :]
-        for c in range(0, 8, 2):
-            res = mm(rows, cot_ref[:, 128 * c : 128 * c + 256])
-            for i, k in enumerate(ks):
-                for h in range(2):
-                    b = res[160 * i : 160 * i + 160, 128 * h : 128 * h + 128]
-                    if c + h == 7:
-                        b = b + row_of(k, 160, 0)
-                    at = 160 * (c + h)
-                    out_ref[zslot[k], at : at + 160, :] = b.astype(bf16)
-
-    @pl.when(step < 2)
-    def _():
-        narrow(384 * step, (0, 1, 2, 3))
-
-    @pl.when(step == 2)
-    def _():
-        narrow(768, (0, 1))
-        wide(mixed_ref, 0, dhb_ref, (2, 3))
-
-    @pl.when(step == 3)
-    def _():
-        wide(mixed_ref, 320, dhb_ref, (0, 1, 2, 3))
-
-    @pl.when((step >= 4) & (step < 12))
-    def _():
-        rows = nt_ref[pl.ds(pl.multiple_of(128 * (step - 4), 128), 128), :]
-        for part, ref in enumerate((dgate_ref, dup_ref)):
-            for c in range(0, 20, 2):
-                res = mm(rows, ref[:, 128 * c : 128 * c + 256])
-                for k in range(4):
-                    for h in range(2):
-                        b = res[32 * k : 32 * k + 32, 128 * h : 128 * h + 128]
-                        at = 32 * (20 * part + c + h)
-                        if at == 0:
-                            b = b + row_of(k, 32, 30)
-                        out_ref[zslot[k], at : at + 32, :] = b.astype(bf16)
-
-    @pl.when(step >= 12)
-    def _():
-        wide(mt_ref, 640 * (step - 12), cb_ref, (0, 1, 2, 3))
+    fill(stage.at[buf], zslot)
 
     for half in range(2):
 
-        @pl.when(slot_y // 2 == half)
+        @pl.when(slot_x // 2 == half)
         def _(half=half):
             copy(0, buf, half).start()
 
-        @pl.when(slot_x // 2 == half)
-        def _(half=half):
-            copy(1, buf, half).start()
-
+    copy(1, buf).start()
     copy(2, buf).start()
-    copy(3, buf).start()
-
-    @pl.when(step == 15)
+
+    @pl.when(step == 4 * planes - 1)
     def _():
         for last in (0, 1):
-            for i in range(4):
+            for i in range(3):
                 copy(i, last).wait()
 
 
-def outer(slots, at, dqkv, mixed, dhb, nt, dgate, dup, mt, cb, gains):
+def outer_square(out_ref, zslot, ref, start, cot_ref, ks):
+    rows = ref[pl.ds(pl.multiple_of(start, 32), 160 * len(ks)), :]
+    for c in range(0, 8, 2):
+        res = mm(rows, cot_ref[:, 128 * c : 128 * c + 256])
+        for i, k in enumerate(ks):
+            for h in range(2):
+                b = res[160 * i : 160 * i + 160, 128 * h : 128 * h + 128]
+                at = 160 * (c + h)
+                out_ref[zslot[k], at : at + 160, :] = b.astype(bf16)
+
+
+def outer_feed_kernel(
+    slot_ref, nt_ref, dgate_ref, dup_ref, mt_ref, cb_ref, ka, kb, sa, sb, stage, sems
+):
+    step = pl.program_id(0)
+
+    def fill(out_ref, zslot):
+        @pl.when(step < 8)
+        def _():
+            rows = nt_ref[pl.ds(pl.multiple_of(128 * step, 128), 128), :]
+            for part, ref in enumerate((dgate_ref, dup_ref)):
+                for c in range(0, 20, 2):
+                    res = mm(rows, ref[:, 128 * c : 128 * c + 256])
+                    for k in range(4):
+                        for h in range(2):
+                            b = res[32 * k : 32 * k + 32, 128 * h : 128 * h + 128]
+                            at = 32 * (20 * part + c + h)
+                            out_ref[zslot[k], at : at + 32, :] = b.astype(bf16)
+
+        @pl.when(step >= 8)
+        def _():
+            outer_square(out_ref, zslot, mt_ref, 640 * (step - 8), cb_ref, (0, 1, 2, 3))
+
+    stage_out(step, slot_ref, 3, (ka, kb, sa, sb), stage, sems, fill)
+
+
+def outer_attend_kernel(
+    slot_ref, at_ref, dqkv_ref, mixed_ref, dhb_ref, gain_ref, ka, kb, sa, sb, stage, sems
+):
+    step = pl.program_id(0)
+
+    def fill(out_ref, zslot):
+        def narrow(start, ks):
+            count = len(ks)
+            rows = at_ref[pl.ds(pl.multiple_of(start, 32), 96 * count), :]
+            for c in range(0, 13, 2):
+                width = min(256, 1664 - 128 * c)
+                res = mm(rows, dqkv_ref[:, 128 * c : 128 * c + width])
+                for i, k in enumerate(ks):
+                    for h in range(width // 128):
+                        at = 96 * (c + h)
+                        out_ref[zslot[k], at : at + 96, :] = res[
+                            96 * i : 96 * i + 96, 128 * h : 128 * h + 128
+                        ].astype(bf16)
+            for k in ks:
+                out_ref[zslot[k], 1248:ROWS, :] = jnp.zeros((32, 128), bf16)
+
+        for k in range(4):
+            out_ref[zslot[k], ROWS:PLUS, :] = gain_ref[4 * step + k].astype(bf16)
+
+        @pl.when(step < 2)
+        def _():
+            narrow(384 * step, (0, 1, 2, 3))
+
+        @pl.when(step == 2)
+        def _():
+            narrow(768, (0, 1))
+            outer_square(out_ref, zslot, mixed_ref, 0, dhb_ref, (2, 3))
+
+        @pl.when(step == 3)
+        def _():
+            outer_square(out_ref, zslot, mixed_ref, 320, dhb_ref, (0, 1, 2, 3))
+
+    stage_out(step, slot_ref, 1, (ka, kb, sa, sb), stage, sems, fill)
+
+
+def outer(kernel, name, slots, planes, rows, args):
     whole = lambda v: pl.BlockSpec(v.shape, lambda s, slot: (0,) * v.ndim)
-    args = (at, dqkv, mixed, dhb, nt, dgate, dup, mt, cb, gains)
     shapes = [
-        jax.ShapeDtypeStruct((2, 4, 4, end - begin, 128), bf16) for begin, end in PART_ROWS
+        jax.ShapeDtypeStruct((2, 4, planes, count, 128), bf16) for count in (HALF, rows - HALF)
     ]
     out = pl.pallas_call(
-        outer_kernel,
-        name="outer",
+        kernel,
+        name=name,
         grid_spec=pltpu.PrefetchScalarGridSpec(
             num_scalar_prefetch=1,
-            grid=(16,),
+            grid=(4 * planes,),
             in_specs=[whole(v) for v in args],
-            out_specs=[pl.BlockSpec(memory_space=pl.ANY)] * 6,
+            out_specs=[pl.BlockSpec(memory_space=pl.ANY)] * 4,
             scratch_shapes=[
-                pltpu.VMEM((2, 4, ROWS, 128), bf16),
-                pltpu.SemaphoreType.DMA((2, 4)),
+                pltpu.VMEM((2, 4, rows, 128), bf16),
+                pltpu.SemaphoreType.DMA((2, 3)),
             ],
         ),
         out_shape=shapes * 2,
         compiler_params=pltpu.CompilerParams(vmem_limit_bytes=48 << 20),
         cost_estimate=pl.CostEstimate(
-            flops=2_600_000_000, bytes_accessed=24_000_000, transcendentals=0
+            flops=650_000_000 * planes, bytes_accessed=6_000_000 * planes, transcendentals=0
         ),
     )(slots, *args)
-    return out[:3], out[3:]
+    return list(out[:2]), list(out[2:])
 
 
 def shard_kind(rank):
@@ -766,15 +789,14 @@
 def blocks_shard(blocks, rank):
     def narrow(_):
         w = blocks[:1248].reshape(13, 96, 128).transpose(1, 0, 2).reshape(96, 1664)[:, :1600]
-        return w.reshape(SHARD), blocks[1248, :30]
+        return w.reshape(SHARD)
 
     def square(_):
         w = blocks.reshape(8, 160, 128).transpose(1, 0, 2).reshape(160, 1024)[:, :960]
-        return w.reshape(SHARD), blocks[1120, 64:94]
+        return w.reshape(SHARD)
 
     def broad(_):
-        w = blocks.reshape(40, 32, 128).transpose(1, 0, 2)[:30]
-        return w.reshape(SHARD), blocks[30, :30]
+        return blocks.reshape(40, 32, 128).transpose(1, 0, 2)[:30].reshape(SHARD)
 
     return lax.switch(shard_kind(rank), [narrow, square, broad], 0)
 
@@ -852,6 +874,9 @@
         if tick == 0:
             u = jnp.where(first, u, over(result, 0))
 
+    four = jnp.arange(4, dtype=jnp.int32)
+    slots = jnp.concatenate([slot_of(four ^ at_axis, phase) for at_axis in (x, z)])
+
     cot = out_grad[0]
     d_query = d_kv = None
     for tick in range(2):
@@ -861,10 +886,19 @@
         dgate, dup, dh, dhb, dg_two, d_mixed, cb = feed_back(
             cot, gate, up, hidden, gain_two, pad, gathered
         )
+        if tick:
+            feeds = outer(
+                outer_feed_kernel, "outer_feed", slots, 3, ROWS, (nt, dgate, dup, mt, cb)
+            )
         d_side = jnp.where(active, d_mixed[:QSIDE], over(d_mixed[QSIDE:], layer))
+        if tick:
+            d_side, feeds = lax.optimization_barrier((d_side, feeds))
         d_kv_all, dq_side = attend_back(qt_side, kv_all, bias, d_side, mixed_side, lse)
         dq_new = jnp.concatenate([dq_side, over(dq_side[: D - QSIDE], tick)])
-        dkv_side = scatter_keys(d_kv_all)
+        if tick:
+            dkv_side, feeds = scatter_keys(d_kv_all, feeds)
+        else:
+            dkv_side = scatter_keys(d_kv_all)
         dkv_new = jnp.concatenate([dkv_side, over(dkv_side[:, :256], tick)], axis=1)
         d_query = dq_new if tick == 0 else jnp.where(active, dq_new, d_query)
         d_kv = dkv_new if tick == 0 else jnp.where(active, dkv_new, d_kv)
@@ -874,17 +908,19 @@
         if tick == 0:
             cot = jnp.where(first, over(d_u.astype(bf16), 1).astype(f32), cot)
 
-    gains = jnp.concatenate([dg_one, dg_two], axis=1).reshape(SHARDS, 30)
-    shards = jnp.arange(SHARDS, dtype=jnp.int32)
-    square = (((shards >= 10) & (shards < 16)) | (shards >= 48))[:, None]
-    gains = jnp.where(
-        square, jnp.pad(gains, ((0, 0), (64, 34))), jnp.pad(gains, ((0, 0), (0, 98)))
+    gains = jnp.concatenate([dg_one, dg_two], axis=1).reshape(4, 16, 30).transpose(1, 0, 2)
+    gains = jnp.pad(gains, ((0, 0), (0, 12), (0, 98)))
+    last = outer(
+        outer_attend_kernel, "outer_attend", slots, 1, PLUS, (at, dqkv, mixed, dhb, gains)
     )
-    four = jnp.arange(4, dtype=jnp.int32)
-    slots = jnp.concatenate([slot_of(four ^ at_axis, phase) for at_axis in (y, x, z)])
-    keep, send = outer(slots, at, dqkv, mixed, dhb, nt, dgate, dup, mt, cb, gains)
-    total = scatter_grads(keep, send)
-    param_part, gain_part = blocks_shard(total, rank)
+    last = scatter_planes(last)
+    plane = jnp.concatenate([last[0][0], last[1][0]])
+    feeds = jnp.concatenate(scatter_planes(feeds, (1,)), axis=1)
+    tail = jnp.pad(plane[ROWS : ROWS + 4, None], ((0, 0), (0, 15), (0, 0)))
+    planes = jnp.concatenate([plane[None, :ROWS], feeds])
+    total = scatter_last(jnp.concatenate([planes, tail], axis=1), y, phase)
+    param_part = blocks_shard(total[:ROWS], rank)
+    gain_part = total[ROWS, :30]
     return (result[None, None], d_u[None, None], param_part[None], gain_part[None])
 
 

time: 629 us -> 636 us (1.011)
  starting transfers between devices: 83.5 us -> 106 us
  waiting for transfers between devices: 327 us -> 314 us
    ppermute x54, starting transfers between devices: 62.1 us -> 85.2 us  [swapped(): return lax.ppermute(block, ALL, pairs)]
    ppermute x54, waiting for transfers between devices: 193 us -> 183 us  [swapped(): return lax.ppermute(block, ALL, pairs)]
    unnamed x110 -> x91, local copies, waits for them, and re-layouts: 16.4 us -> 9.17 us
    convert_element_type x15 -> x18, other arithmetic: 13.4 us -> 15.1 us  [summed(): return (mine[at].astype(f32) + got[at].astype(f32)).astype(bf16)]
    pallas_call x1 -> x2, Pallas kernels: 14.2 us -> 15.1 us  [outer(): pl.pallas_call(kernel, name=name, grid_spec=pltpu.PrefetchScalarGridSpec(...]
  transfers between devices with their start and end apart: 69 -> 69, of which waited for: 50 -> 48; matrix products, arithmetic and copies ran while one was open for 5% -> 4% of each run, Pallas kernels for 0% -> 6%
where the time goes in v4:
time: 636 us; the launch traced here: 628 us
  waiting for transfers between devices  314 us (49%)
  Pallas kernels  130 us (20%)
  starting transfers between devices  106 us (17%)
  other arithmetic  37.6 us (6%)
  local copies, waits for them, and re-layouts  21.6 us (3%)
  between operations  17.4 us (3%)
    ppermute x54, waiting for transfers between devices, swapped(): return lax.ppermute(block, ALL, pairs)  183 us
    all_gather x1, waiting for transfers between devices, per_device(): gathered = lax.all_gather(own, ('ctx', 'fsdp'), axis=0)  119 us
    ppermute x54, starting transfers between devices, swapped(): return lax.ppermute(block, ALL, pairs)  85.2 us
    pallas_call x2, Pallas kernels, attend_back(): pl.pallas_call(attend_back_kernel, name='attend_back', grid=(SIDE,), in_s...  31.9 us
    pallas_call x2, Pallas kernels, feed_back(): pl.pallas_call(feed_back_kernel, name='feed_back', grid=(4,), in_specs=[w...  29.7 us
    pallas_call x2, Pallas kernels, feed(): pl.pallas_call(feed_kernel, name='feed', grid=(4,), in_specs=[whole(D, R)...  21.6 us
    ppermute x14, starting transfers between devices, over(): return lax.ppermute(block, 'phase', [(source, 1 - source)])  21.2 us
    pallas_call x2, Pallas kernels, attend(): pl.pallas_call(attend_kernel, name='attend', grid=(SIDE,), in_specs=[pl.B...  17.9 us
  transfers between devices with their start and end apart: 69, of which 48 were waited for; matrix products, arithmetic and copies ran while one was open for 4% of the time, Pallas kernels for 6%

profile of v4, /device:TPU:0, one launch (start us, length us, event | category | flops | bytes accessed | tf_op | source)
XLA Modules:
  0.0 627.6 jit_solution(11373992155140470019)
XLA Ops:
  9.2 8.3 %conditional.2 = (bf16[1280,128]{1,0:T(8,128)(2,1)S(1)}) conditional(s32[]{:T(128)} %clamp.4, (bf16[1,153600]{1,0:T(2,128)(2,1)}, bf16[1,128]{1,0:T(2,128)(2,1)S(1)}) %tuple.46, (bf16[1,153600]{1,0:T(2,128)(2,1)}, bf16[1,128]{1,0:T(2,128)(2,1)S(1)}) %tuple.46, (bf16[1,153600]{1,0:T(2,128)(2,1)}, bf16[1,128]{1,0:T(2,128)(2,1)S(1)}) %tuple.46), branch_computations={%region_1.2_spmd, %region_2.3_spmd, %region_3.5_spmd} | conditional | flops 983040 | bytes 3780876 | solution.py:786
  9.2 7.4 %reduce.15 = bf16[153600]{0:T(1024)(128)(2,1)S(1)} reduce(bf16[1,153600]{1,0:T(2,128)(2,1)} %get-tuple-element.63, bf16[]{:T(256)} %constant.272), dimensions={0}, to_apply=%get-tuple-element.63.reduce_sub_computation | reduce | bytes 614402 | tf_op jit(solution)/shard_map
  24.0 119.0 %all-gather.3.cloned.1.call-done = bf16[81920,128]{1,0:T(8,128)(2,1)} async-done(((bf16[1280,128]{1,0:T(8,128)(2,1)}), bf16[81920,128]{1,0:T(8,128)(2,1)}) %all-gather.3.cloned.1.call-update) | async-done | bytes 20971536 | tf_op jit(solution)/shard_map/all_gather | solution.py:825
  152.2 3.0 collective-permute-start.5
  175.3 4.3 collective-permute-done.8
  182.4 3.3 collective-permute-start.9
  189.9 3.1 collective-permute-done.10
  196.3 9.0 %attend.2 = (bf16[576,128]{1,0:T(8,128)(2,1)S(1)}, f32[3,1,384]{2,1,0:T(1,128)S(1)}) custom-call(bf16[576,128]{1,0:T(8,128)(2,1)S(1)} %slice_select_fusion.3.qt_ref, bf16[4096,384]{1,0:T(8,128)(2,1)S(1)} %bitcast.198, f32[4096,128]{1,0:T(8,128)S(1)} %and_select_fusion.bias_ref), custom_call_target="tpu_custom_call" | custom-call | flops 4000000000 | bytes 8000000 | tf_op jit(solution)/shard_map/attend/pallas_call | solution.py:279
  208.5 11.5 %feed.2 = (bf16[128,960]{1,0:T(8,128)(2,1)S(1)}, f32[128,960]{1,0:T(8,128)}, bf16[1024,128]{1,0:T(8,128)(2,1)}, f32[128,2560]{1,0:T(8,128)}, f32[128,2560]{1,0:T(8,128)}, /*index=5*/bf16[2560,128]{1,0:T(8,128)(2,1)}) custom-call(bf16[960,128]{1,0:T(8,128)(2,1)S(1)} %constant_dynamic-update-slice_fusion.mixed_ref, bf16[128,960]{1,0:T(8,128)(2,1)S(1)} %bitcast.197, ...), custom_call_target="tpu_custom_call" | custom-call | flops 2200000000 | bytes 22000000 | tf_op jit(solution)/shard_map/feed/pallas_call | solution.py:382
  223.3 3.0 project.3
  229.5 3.5 collective-permute-start.18
  241.3 3.7 collective-permute-start.20
  245.3 3.4 collective-permute-done.20
  253.0 4.2 collective-permute-done.21
  259.5 3.7 collective-permute-start.22
  266.5 4.1 collective-permute-done.23
  273.7 9.0 %attend.3 = (bf16[576,128]{1,0:T(8,128)(2,1)S(1)}, f32[3,1,384]{2,1,0:T(1,128)S(1)}) custom-call(bf16[576,128]{1,0:T(8,128)(2,1)S(1)} %slice_select_fusion.2.qt_ref, bf16[4096,384]{1,0:T(8,128)(2,1)S(1)} %bitcast.200, f32[4096,128]{1,0:T(8,128)S(1)} %and_select_fusion.bias_ref), custom_call_target="tpu_custom_call" | custom-call | flops 4000000000 | bytes 8000000 | tf_op jit(solution)/shard_map/attend/pallas_call | solution.py:279
  285.1 10.0 %feed.3 = (bf16[128,960]{1,0:T(8,128)(2,1)S(1)}, f32[128,960]{1,0:T(8,128)S(1)}, bf16[1024,128]{1,0:T(8,128)(2,1)S(1)}, f32[128,2560]{1,0:T(8,128)S(1)}, f32[128...) custom-call(bf16[960,128]{1,0:T(8,128)(2,1)S(1)} %maximum_select_fusion.2.mixed_ref, ...), custom_call_target="tpu_custom_call" | custom-call | flops 2200000000 | bytes 22000000 | tf_op jit(solution)/shard_map/feed/pallas_call | solution.py:382
  297.8 15.3 %feed_back.2 = (bf16[128,2560]{1,0:T(8,128)(2,1)}, bf16[128,2560]{1,0:T(8,128)(2,1)}, f32[128,960]{1,0:T(8,128)S(1)}, bf16[128,1024]{1,0:T(8,128)(2,1)}, f32[1,9...) custom-call(f32[128,960]{1,0:T(8,128)S(1)} %bitcast.195, ...), custom_call_target="tpu_custom_call" | custom-call | flops 2200000000 | bytes 22000000 | tf_op jit(solution)/shard_map/feed_back/pallas_call | solution.py:473
  316.6 15.9 %attend_back.2 = (bf16[4096,384]{1,0:T(8,128)(2,1)S(1)}, f32[576,128]{1,0:T(8,128)S(1)}) custom-call(bf16[576,128]{1,0:T(8,128)(2,1)S(1)} %copy-done.13, bf16[4096,384]{1,0:T(8,128)(2,1)} %bitcast.201, f32[4096,128]{1,0:T(8,128)S(1)} %copy-done.4, f32[576,128]{1,0:T(8,128)S(1)} %slice_select_fusion.1.dot_ref, ...), custom_call_target="tpu_custom_call" | custom-call | flops 10000000000 | bytes 14000000 | tf_op jit(solution)/shard_map/attend_back/pallas_call | solution.py:531
  333.9 3.2 collective-permute-start.27
  337.2 8.9 %collective-permute-done.31 = bf16[8,128,384]{2,1,0:T(8,128)(2,1)S(1)} collective-permute-done((bf16[8,128,384]{2,1,0:T(8,128)(2,1)S(1)}, bf16[8,128,384]{2,1,0:T(8,128)(2,1)S(1)}, u32[]{:S(2)}, u32[]{:S(2)}) %collective-permute-start.31) | collective-permute-done | bytes 786464 | tf_op jit(solution)/shard_map/ppermute | solution.py:57
  347.5 6.7 %collective-permute-done.32 = bf16[4,128,384]{2,1,0:T(8,128)(2,1)S(1)} collective-permute-done((bf16[4,128,384]{2,1,0:T(8,128)(2,1)S(1)}, bf16[4,128,384]{2,1,0:T(8,128)(2,1)S(1)}, u32[]{:S(2)}, u32[]{:S(2)}) %collective-permute-start.32) | collective-permute-done | bytes 393248 | tf_op jit(solution)/shard_map/ppermute | solution.py:57
  354.3 3.3 collective-permute-start.33
  361.5 3.4 collective-permute-done.29
  366.1 3.5 collective-permute-start.35
  375.3 4.2 project_back.2
  385.1 14.4 %feed_back.3 = (bf16[128,2560]{1,0:T(8,128)(2,1)S(1)}, bf16[128,2560]{1,0:T(8,128)(2,1)S(1)}, f32[128,960]{1,0:T(8,128)S(1)}, bf16[128,1024]{1,0:T(8,128)(2,1)S(...) custom-call(f32[128,960]{1,0:T(8,128)S(1)} %convert_select_fusion.c_ref, ...), custom_call_target="tpu_custom_call" | custom-call | flops 2200000000 | bytes 22000000 | tf_op jit(solution)/shard_map/feed_back/pallas_call | solution.py:473
  402.2 10.9 %outer_feed.1 = (bf16[2,4,3,640,128]{4,3,2,1,0:T(8,128)(2,1)}, bf16[2,4,3,640,128]{4,3,2,1,0:T(8,128)(2,1)}, bf16[2,4,3,640,128]{4,3,2,1,0:T(8,128)(2,1)}, bf16[2,4,3,640,128]{4,3,2,1,0:T(8,128)(2,1)}) custom-call(s32[8]{0:T(128)S(1)} %pad_add_fusion.2.slot_ref, bf16[1024,128]{1,0:T(8,128)(2,1)S(1)} %copy-done.19, ...), custom_call_target="tpu_custom_call" | custom-call | flops 1950000000 | bytes 18000000 | tf_op jit(solution)/shard_map/outer_feed/pallas_call | solution.py:742
  413.2 3.3 collective-permute-start.44
  418.4 16.1 %attend_back.3 = (bf16[4096,384]{1,0:T(8,128)(2,1)S(1)}, f32[576,128]{1,0:T(8,128)S(1)}) custom-call(bf16[576,128]{1,0:T(8,128)(2,1)S(1)} %copy-done.11, bf16[4096,384]{1,0:T(8,128)(2,1)} %bitcast.199, f32[4096,128]{1,0:T(8,128)S(1)} %copy-done.5, f32[576,128]{1,0:T(8,128)S(1)} %slice_select_fusion.dot_ref, bf16[576,128]{1,0:T(8,128)(2,1)S(1)} %copy-done.9, ...), custom_call_target="tpu_custom_call" | custom-call | flops 10000000000 | bytes 14000000 | tf_op jit(solution)/shard_map/attend_back/pallas_call | solution.py:531
  434.8 3.2 collective-permute-start.40
  438.3 30.5 %collective-permute-done.40 = bf16[8,128,384]{2,1,0:T(8,128)(2,1)S(1)} collective-permute-done((bf16[8,128,384]{2,1,0:T(8,128)(2,1)S(1)}, bf16[8,128,384]{2,1,0:T(8,128)(2,1)S(1)}, u32[]{:S(2)}, u32[]{:S(2)}) %collective-permute-start.40) | collective-permute-done | bytes 786464 | tf_op jit(solution)/shard_map/ppermute | solution.py:57
  470.5 6.4 %collective-permute-done.41 = bf16[4,128,384]{2,1,0:T(8,128)(2,1)S(1)} collective-permute-done((bf16[4,128,384]{2,1,0:T(8,128)(2,1)S(1)}, bf16[4,128,384]{2,1,0:T(8,128)(2,1)S(1)}, u32[]{:S(2)}, u32[]{:S(2)}) %collective-permute-start.41) | collective-permute-done | bytes 393248 | tf_op jit(solution)/shard_map/ppermute | solution.py:57
  477.4 3.5 fusion.8
  484.3 3.3 collective-permute-start.51
  489.3 7.4 %collective-permute-done.48 = bf16[2,128,384]{2,1,0:T(8,128)(2,1)S(1)} collective-permute-done((bf16[2,128,384]{2,1,0:T(8,128)(2,1)S(1)}, bf16[2,128,384]{2,1,0:T(8,128)(2,1)S(1)}, u32[]{:S(2)}, u32[]{:S(2)}) %collective-permute-start.48) | collective-permute-done | bytes 196640 | tf_op jit(solution)/shard_map/ppermute | solution.py:57
  497.9 12.3 %collective-permute-done.49 = bf16[1,128,384]{2,1,0:T(8,128)(2,1)S(1)} collective-permute-done((bf16[1,128,384]{2,1,0:T(8,128)(2,1)S(1)}, bf16[1,128,384]{2,1,0:T(8,128)(2,1)S(1)}, u32[]{:S(2)}, u32[]{:S(2)}) %collective-permute-start.49) | collective-permute-done | bytes 98336 | tf_op jit(solution)/shard_map/ppermute | solution.py:57
  524.0 3.6 project_back.3
  530.5 4.2 outer_attend.1
  541.6 12.5 %collective-permute-done.65 = bf16[3,640,128]{2,1,0:T(8,128)(2,1)S(1)} collective-permute-done((bf16[3,640,128]{2,1,0:T(8,128)(2,1)S(1)}, bf16[3,640,128]{2,1,0:T(8,128)(2,1)S(1)}, u32[]{:S(2)}, u32[]{:S(2)}) %collective-permute-start.65) | collective-permute-done | bytes 491552 | tf_op jit(solution)/shard_map/ppermute | solution.py:57
  555.3 3.5 collective-permute-done.54
  563.4 6.5 %collective-permute-done.55 = bf16[4,1,640,128]{3,2,1,0:T(8,128)(2,1)S(1)} collective-permute-done((bf16[4,1,640,128]{3,2,1,0:T(8,128)(2,1)S(1)}, bf16[4,1,640,128]{3,2,1,0:T(8,128)(2,1)S(1)}, u32[]{:S(2)}, u32[]{:S(2)}) %collective-permute-start.55) | collective-permute-done | bytes 655392 | tf_op jit(solution)/shard_map/ppermute | solution.py:57
  571.9 3.2 collective-permute-done.59
  578.6 6.9 %collective-permute-done.60 = bf16[2,1,656,128]{3,2,0,1:T(8,128)(2,1)S(1)} collective-permute-done((bf16[2,1,656,128]{3,2,0,1:T(8,128)(2,1)S(1)}, bf16[2,1,656,128]{3,2,0,1:T(8,128)(2,1)S(1)}, u32[]{:S(2)}, u32[]{:S(2)}) %collective-permute-start.60) | collective-permute-done | bytes 335904 | tf_op jit(solution)/shard_map/ppermute | solution.py:57
  585.7 5.3 collective-permute-done.61
  595.6 13.8 %collective-permute-done.66 = bf16[2,1296,128]{2,1,0:T(8,128)(2,1)S(1)} collective-permute-done((bf16[2,1296,128]{2,1,0:T(8,128)(2,1)S(1)}, bf16[2,1296,128]{2,1,0:T(8,128)(2,1)S(1)}, u32[]{:S(2)}, u32[]{:S(2)}) %collective-permute-start.66) | collective-permute-done | bytes 663584 | tf_op jit(solution)/shard_map/ppermute | solution.py:57
  612.1 5.5 collective-permute-done.67
  (352 shorter events, 165.1 us)
Async XLA Ops:
  7.2 135.8 %all-gather.3.cloned.1.call-start = ((), (), s32[]{:S(2)}) async-start(), calls=%async_computation | async-start | bytes 21299200 | tf_op jit(solution)/shard_map/all_gather | solution.py:825
  152.2 6.6 %collective-permute-start.5 = (bf16[128,384]{1,0:T(8,128)(2,1)S(1)}, bf16[128,384]{1,0:T(8,128)(2,1)S(1)}, u32[]{:S(2)}, u32[]{:S(2)}) collective-permute-start(bf16[128,384]{1,0:T(8,128)(2,1)S(1)} %slice_select_fusion.5), channel_id=1, source_target_pairs={{0,2},{1,3},{2,0},{3,1},{4,6},{5,7},{6,4},{7,5},{8,10},{9,11},{10,... | collective-permute-start | bytes 294920 | tf_op jit(solution)/shard_map/ppermute | solution.py:57
  160.3 7.0 %collective-permute-start.3 = (bf16[2,128,384]{2,1,0:T(8,128)(2,1)S(1)}, bf16[2,128,384]{2,1,0:T(8,128)(2,1)S(1)}, u32[]{:S(2)}, u32[]{:S(2)}) collective-permute-start(bf16[2,128,384]{2,1,0:T(8,128)(2,1)S(1)} %pad_maximum_fusion.12), channel_id=1, source_target_pairs={{0,48},{1,49},{2,50},{3,51},{4,52},{5,53},{6,54},{7,55},{8,56},{9,... | collective-permute-start | bytes 589832 | tf_op jit(solution)/shard_map/ppermute | solution.py:57
  163.5 7.0 %collective-permute-start.7 = (bf16[2,128,384]{2,1,0:T(8,128)(2,1)S(1)}, bf16[2,128,384]{2,1,0:T(8,128)(2,1)S(1)}, u32[]{:S(2)}, u32[]{:S(2)}) collective-permute-start(bf16[2,128,384]{2,1,0:T(8,128)(2,1)S(1)} %pad_maximum_fusion.13), channel_id=1, source_target_pairs={{0,12},{1,13},{2,14},{3,15},{4,8},{5,9},{6,10},{7,11},{8,4},{9,5},... | collective-permute-start | bytes 589832 | tf_op jit(solution)/shard_map/ppermute | solution.py:57
  167.3 7.9 %collective-permute-start.4 = (bf16[4,128,384]{2,1,0:T(8,128)(2,1)S(1)}, bf16[4,128,384]{2,1,0:T(8,128)(2,1)S(1)}, u32[]{:S(2)}, u32[]{:S(2)}) collective-permute-start(bf16[4,128,384]{2,1,0:T(8,128)(2,1)S(1)} %pad_maximum_fusion.6), channel_id=1, source_target_pairs={{0,4},{1,5},{2,6},{3,7},{4,0},{5,1},{6,2},{7,3},{8,12},{9,13},{10,... | collective-permute-start | bytes 1179656 | tf_op jit(solution)/shard_map/ppermute | solution.py:57
  170.5 9.1 %collective-permute-start.8 = (bf16[4,128,384]{2,1,0:T(8,128)(2,1)S(1)}, bf16[4,128,384]{2,1,0:T(8,128)(2,1)S(1)}, u32[]{:S(2)}, u32[]{:S(2)}) collective-permute-start(bf16[4,128,384]{2,1,0:T(8,128)(2,1)S(1)} %pad_maximum_fusion.7), channel_id=1, source_target_pairs={{0,16},{1,17},{2,18},{3,19},{4,20},{5,21},{6,22},{7,23},{8,24},{9,... | collective-permute-start | bytes 1179656 | tf_op jit(solution)/shard_map/ppermute | solution.py:57
  179.7 13.3 %collective-permute-start.10 = (bf16[8,128,384]{2,1,0:T(8,128)(2,1)S(1)}, bf16[8,128,384]{2,1,0:T(8,128)(2,1)S(1)}, u32[]{:S(2)}, u32[]{:S(2)}) collective-permute-start(bf16[8,128,384]{2,1,0:T(8,128)(2,1)S(1)} %pad_maximum_fusion.3), channel_id=1, source_target_pairs={{0,48},{1,49},{2,50},{3,51},{4,52},{5,53},{6,54},{7,55},{8,56},{9,... | collective-permute-start | bytes 2359304 | tf_op jit(solution)/shard_map/ppermute | solution.py:57
  182.4 13.3 %collective-permute-start.9 = (bf16[8,128,384]{2,1,0:T(8,128)(2,1)S(1)}, bf16[8,128,384]{2,1,0:T(8,128)(2,1)S(1)}, u32[]{:S(2)}, u32[]{:S(2)}) collective-permute-start(bf16[8,128,384]{2,1,0:T(8,128)(2,1)S(1)} %pad_maximum_fusion.2), channel_id=1, source_target_pairs={{0,12},{1,13},{2,14},{3,15},{4,8},{5,9},{6,10},{7,11},{8,4},{9,5},... | collective-permute-start | bytes 2359304 | tf_op jit(solution)/shard_map/ppermute | solution.py:57
  229.5 6.6 %collective-permute-start.18 = (bf16[128,384]{1,0:T(8,128)(2,1)S(1)}, bf16[128,384]{1,0:T(8,128)(2,1)S(1)}, u32[]{:S(2)}, u32[]{:S(2)}) collective-permute-start(bf16[128,384]{1,0:T(8,128)(2,1)S(1)} %slice_select_fusion.4), channel_id=1, source_target_pairs={{0,2},{1,3},{2,0},{3,1},{4,6},{5,7},{6,4},{7,5},{8,10},{9,11},{10,... | collective-permute-start | bytes 294920 | tf_op jit(solution)/shard_map/ppermute | solution.py:57
  237.7 7.3 %collective-permute-start.16 = (bf16[2,128,384]{2,1,0:T(8,128)(2,1)S(1)}, bf16[2,128,384]{2,1,0:T(8,128)(2,1)S(1)}, u32[]{:S(2)}, u32[]{:S(2)}) collective-permute-start(bf16[2,128,384]{2,1,0:T(8,128)(2,1)S(1)} %pad_maximum_fusion.14), channel_id=1, source_target_pairs={{0,48},{1,49},{2,50},{3,51},{4,52},{5,53},{6,54},{7,55},{8,56},{9,... | collective-permute-start | bytes 589832 | tf_op jit(solution)/shard_map/ppermute | solution.py:57
  241.3 7.3 %collective-permute-start.20 = (bf16[2,128,384]{2,1,0:T(8,128)(2,1)S(1)}, bf16[2,128,384]{2,1,0:T(8,128)(2,1)S(1)}, u32[]{:S(2)}, u32[]{:S(2)}) collective-permute-start(bf16[2,128,384]{2,1,0:T(8,128)(2,1)S(1)} %pad_maximum_fusion.15), channel_id=1, source_target_pairs={{0,12},{1,13},{2,14},{3,15},{4,8},{5,9},{6,10},{7,11},{8,4},{9,5},... | collective-permute-start | bytes 589832 | tf_op jit(solution)/shard_map/ppermute | solution.py:57
  245.1 7.9 %collective-permute-start.17 = (bf16[4,128,384]{2,1,0:T(8,128)(2,1)S(1)}, bf16[4,128,384]{2,1,0:T(8,128)(2,1)S(1)}, u32[]{:S(2)}, u32[]{:S(2)}) collective-permute-start(bf16[4,128,384]{2,1,0:T(8,128)(2,1)S(1)} %pad_maximum_fusion.8), channel_id=1, source_target_pairs={{0,4},{1,5},{2,6},{3,7},{4,0},{5,1},{6,2},{7,3},{8,12},{9,13},{10,... | collective-permute-start | bytes 1179656 | tf_op jit(solution)/shard_map/ppermute | solution.py:57
  248.7 8.5 %collective-permute-start.21 = (bf16[4,128,384]{2,1,0:T(8,128)(2,1)S(1)}, bf16[4,128,384]{2,1,0:T(8,128)(2,1)S(1)}, u32[]{:S(2)}, u32[]{:S(2)}) collective-permute-start(bf16[4,128,384]{2,1,0:T(8,128)(2,1)S(1)} %pad_maximum_fusion.9), channel_id=1, source_target_pairs={{0,16},{1,17},{2,18},{3,19},{4,20},{5,21},{6,22},{7,23},{8,24},{9,... | collective-permute-start | bytes 1179656 | tf_op jit(solution)/shard_map/ppermute | solution.py:57
  257.4 13.3 %collective-permute-start.23 = (bf16[8,128,384]{2,1,0:T(8,128)(2,1)S(1)}, bf16[8,128,384]{2,1,0:T(8,128)(2,1)S(1)}, u32[]{:S(2)}, u32[]{:S(2)}) collective-permute-start(bf16[8,128,384]{2,1,0:T(8,128)(2,1)S(1)} %pad_maximum_fusion.5), channel_id=1, source_target_pairs={{0,48},{1,49},{2,50},{3,51},{4,52},{5,53},{6,54},{7,55},{8,56},{9,... | collective-permute-start | bytes 2359304 | tf_op jit(solution)/shard_map/ppermute | solution.py:57
  259.5 13.7 %collective-permute-start.22 = (bf16[8,128,384]{2,1,0:T(8,128)(2,1)S(1)}, bf16[8,128,384]{2,1,0:T(8,128)(2,1)S(1)}, u32[]{:S(2)}, u32[]{:S(2)}) collective-permute-start(bf16[8,128,384]{2,1,0:T(8,128)(2,1)S(1)} %pad_maximum_fusion.4), channel_id=1, source_target_pairs={{0,12},{1,13},{2,14},{3,15},{4,8},{5,9},{6,10},{7,11},{8,4},{9,5},... | collective-permute-start | bytes 2359304 | tf_op jit(solution)/shard_map/ppermute | solution.py:57
  332.8 13.3 %collective-permute-start.31 = (bf16[8,128,384]{2,1,0:T(8,128)(2,1)S(1)}, bf16[8,128,384]{2,1,0:T(8,128)(2,1)S(1)}, u32[]{:S(2)}, u32[]{:S(2)}) collective-permute-start(bf16[8,128,384]{2,1,0:T(8,128)(2,1)S(1)} %bitcast.285), channel_id=1, source_target_pairs={{0,48},{1,49},{2,50},{3,51},{4,52},{5,53},{6,54},{7,55},{8,56},{9,... | collective-permute-start | bytes 2359304 | tf_op jit(solution)/shard_map/ppermute | solution.py:57
  333.9 13.2 %collective-permute-start.27 = (bf16[8,128,384]{2,1,0:T(8,128)(2,1)S(1)}, bf16[8,128,384]{2,1,0:T(8,128)(2,1)S(1)}, u32[]{:S(2)}, u32[]{:S(2)}) collective-permute-start(bf16[8,128,384]{2,1,0:T(8,128)(2,1)S(1)} %bitcast.283), channel_id=1, source_target_pairs={{0,12},{1,13},{2,14},{3,15},{4,8},{5,9},{6,10},{7,11},{8,4},{9,5},... | collective-permute-start | bytes 2359304 | tf_op jit(solution)/shard_map/ppermute | solution.py:57
  346.3 7.9 %collective-permute-start.32 = (bf16[4,128,384]{2,1,0:T(8,128)(2,1)S(1)}, bf16[4,128,384]{2,1,0:T(8,128)(2,1)S(1)}, u32[]{:S(2)}, u32[]{:S(2)}) collective-permute-start(bf16[4,128,384]{2,1,0:T(8,128)(2,1)S(1)} %slice.609), channel_id=1, source_target_pairs={{0,16},{1,17},{2,18},{3,19},{4,20},{5,21},{6,22},{7,23},{8,24},{9,... | collective-permute-start | bytes 1179656 | tf_op jit(solution)/shard_map/ppermute | solution.py:57
  347.4 10.2 %collective-permute-start.28 = (bf16[4,128,384]{2,1,0:T(8,128)(2,1)S(1)}, bf16[4,128,384]{2,1,0:T(8,128)(2,1)S(1)}, u32[]{:S(2)}, u32[]{:S(2)}) collective-permute-start(bf16[4,128,384]{2,1,0:T(8,128)(2,1)S(1)} %slice.603), channel_id=1, source_target_pairs={{0,4},{1,5},{2,6},{3,7},{4,0},{5,1},{6,2},{7,3},{8,12},{9,13},{10,... | collective-permute-start | bytes 1179656 | tf_op jit(solution)/shard_map/ppermute | solution.py:57
  354.3 7.0 %collective-permute-start.33 = (bf16[2,128,384]{2,1,0:T(8,128)(2,1)S(1)}, bf16[2,128,384]{2,1,0:T(8,128)(2,1)S(1)}, u32[]{:S(2)}, u32[]{:S(2)}) collective-permute-start(bf16[2,128,384]{2,1,0:T(8,128)(2,1)S(1)} %slice.611), channel_id=1, source_target_pairs={{0,12},{1,13},{2,14},{3,15},{4,8},{5,9},{6,10},{7,11},{8,4},{9,5},... | collective-permute-start | bytes 589832 | tf_op jit(solution)/shard_map/ppermute | solution.py:57
  357.8 7.1 %collective-permute-start.29 = (bf16[2,128,384]{2,1,0:T(8,128)(2,1)S(1)}, bf16[2,128,384]{2,1,0:T(8,128)(2,1)S(1)}, u32[]{:S(2)}, u32[]{:S(2)}) collective-permute-start(bf16[2,128,384]{2,1,0:T(8,128)(2,1)S(1)} %slice.605), channel_id=1, source_target_pairs={{0,48},{1,49},{2,50},{3,51},{4,52},{5,53},{6,54},{7,55},{8,56},{9,... | collective-permute-start | bytes 589832 | tf_op jit(solution)/shard_map/ppermute | solution.py:57
  366.1 6.2 collective-permute-start.35
  399.5 13.6 %collective-permute-start.38 = (f32[576,128]{1,0:T(8,128)S(1)}, f32[576,128]{1,0:T(8,128)S(1)}, u32[]{:S(2)}, u32[]{:S(2)}) collective-permute-start(f32[576,128]{1,0:T(8,128)S(1)} %slice.507), channel_id=1, source_target_pairs={{0,64},{1,65},{2,66},{3,67},{4,68},{5,69},{6,70},{7,71},{8,72},{9,... | collective-permute-start | bytes 884744 | tf_op jit(solution)/shard_map/ppermute | solution.py:61
  413.2 64.2 %collective-permute-start.44 = (bf16[2,4,3,640,128]{4,3,2,1,0:T(8,128)(2,1)}, bf16[2,4,3,640,128]{4,3,2,1,0:T(8,128)(2,1)}, u32[]{:S(2)}, u32[]{:S(2)}) collective-permute-start(bf16[2,4,3,640,128]{4,3,2,1,0:T(8,128)(2,1)} %get-tuple-element.171), channel_id=1, source_target_pairs={{0,12},{1,13},{2,14},{3,15},{4,8},{5,9},{6,10},{7,11},{8,4},{9,5},... | collective-permute-start | bytes 11796488 | tf_op jit(solution)/shard_map/ppermute | solution.py:57
  416.5 64.5 %collective-permute-start.45 = (bf16[2,4,3,640,128]{4,3,2,1,0:T(8,128)(2,1)}, bf16[2,4,3,640,128]{4,3,2,1,0:T(8,128)(2,1)S(1)}, u32[]{:S(2)}, u32[]{:S(2)}) collective-permute-start(bf16[2,4,3,640,128]{4,3,2,1,0:T(8,128)(2,1)} %get-tuple-element.173), channel_id=1, source_target_pairs={{0,3},{1,2},{2,1},{3,0},{4,7},{5,6},{6,5},{7,4},{8,11},{9,10},{10,... | collective-permute-start | bytes 11796488 | tf_op jit(solution)/shard_map/ppermute | solution.py:57
  434.8 34.0 %collective-permute-start.40 = (bf16[8,128,384]{2,1,0:T(8,128)(2,1)S(1)}, bf16[8,128,384]{2,1,0:T(8,128)(2,1)S(1)}, u32[]{:S(2)}, u32[]{:S(2)}) collective-permute-start(bf16[8,128,384]{2,1,0:T(8,128)(2,1)S(1)} %bitcast.286), channel_id=1, source_target_pairs={{0,12},{1,13},{2,14},{3,15},{4,8},{5,9},{6,10},{7,11},{8,4},{9,5},... | collective-permute-start | bytes 2359304 | tf_op jit(solution)/shard_map/ppermute | solution.py:57
  438.0 31.2 %collective-permute-start.42 = (bf16[8,128,384]{2,1,0:T(8,128)(2,1)S(1)}, bf16[8,128,384]{2,1,0:T(8,128)(2,1)S(1)}, u32[]{:S(2)}, u32[]{:S(2)}) collective-permute-start(bf16[8,128,384]{2,1,0:T(8,128)(2,1)S(1)} %bitcast.284), channel_id=1, source_target_pairs={{0,48},{1,49},{2,50},{3,51},{4,52},{5,53},{6,54},{7,55},{8,56},{9,... | collective-permute-start | bytes 2359304 | tf_op jit(solution)/shard_map/ppermute | solution.py:57
  469.1 7.9 %collective-permute-start.41 = (bf16[4,128,384]{2,1,0:T(8,128)(2,1)S(1)}, bf16[4,128,384]{2,1,0:T(8,128)(2,1)S(1)}, u32[]{:S(2)}, u32[]{:S(2)}) collective-permute-start(bf16[4,128,384]{2,1,0:T(8,128)(2,1)S(1)} %slice.616), channel_id=1, source_target_pairs={{0,4},{1,5},{2,6},{3,7},{4,0},{5,1},{6,2},{7,3},{8,12},{9,13},{10,... | collective-permute-start | bytes 1179656 | tf_op jit(solution)/shard_map/ppermute | solution.py:57
  469.4 7.9 %collective-permute-start.43 = (bf16[4,128,384]{2,1,0:T(8,128)(2,1)S(1)}, bf16[4,128,384]{2,1,0:T(8,128)(2,1)S(1)}, u32[]{:S(2)}, u32[]{:S(2)}) collective-permute-start(bf16[4,128,384]{2,1,0:T(8,128)(2,1)S(1)} %slice.618), channel_id=1, source_target_pairs={{0,16},{1,17},{2,18},{3,19},{4,20},{5,21},{6,22},{7,23},{8,24},{9,... | collective-permute-start | bytes 1179656 | tf_op jit(solution)/shard_map/ppermute | solution.py:57
  482.3 27.9 %collective-permute-start.50 = (bf16[4,3,640,128]{3,2,1,0:T(8,128)(2,1)S(1)}, bf16[4,3,640,128]{3,2,1,0:T(8,128)(2,1)S(1)}, u32[]{:S(2)}, u32[]{:S(2)}) collective-permute-start(bf16[4,3,640,128]{3,2,1,0:T(8,128)(2,1)S(1)} %get-tuple-element.177), channel_id=1, source_target_pairs={{0,4},{1,5},{2,6},{3,7},{4,0},{5,1},{6,2},{7,3},{8,12},{9,13},{10,... | collective-permute-start | bytes 5898248 | tf_op jit(solution)/shard_map/ppermute | solution.py:57
  484.3 27.3 %collective-permute-start.51 = (bf16[4,3,640,128]{3,2,1,0:T(8,128)(2,1)S(1)}, bf16[4,3,640,128]{3,2,1,0:T(8,128)(2,1)S(1)}, u32[]{:S(2)}, u32[]{:S(2)}) collective-permute-start(bf16[4,3,640,128]{3,2,1,0:T(8,128)(2,1)S(1)} %get-tuple-element.179), channel_id=1, source_target_pairs={{0,1},{1,0},{2,3},{3,2},{4,5},{5,4},{6,7},{7,6},{8,9},{9,8},{10,11... | collective-permute-start | bytes 5898248 | tf_op jit(solution)/shard_map/ppermute | solution.py:57
  487.6 9.1 %collective-permute-start.48 = (bf16[2,128,384]{2,1,0:T(8,128)(2,1)S(1)}, bf16[2,128,384]{2,1,0:T(8,128)(2,1)S(1)}, u32[]{:S(2)}, u32[]{:S(2)}) collective-permute-start(bf16[2,128,384]{2,1,0:T(8,128)(2,1)S(1)} %slice.532), channel_id=1, source_target_pairs={{0,12},{1,13},{2,14},{3,15},{4,8},{5,9},{6,10},{7,11},{8,4},{9,5},... | collective-permute-start | bytes 589832 | tf_op jit(solution)/shard_map/ppermute | solution.py:57
  487.8 9.2 %collective-permute-start.46 = (bf16[2,128,384]{2,1,0:T(8,128)(2,1)S(1)}, bf16[2,128,384]{2,1,0:T(8,128)(2,1)S(1)}, u32[]{:S(2)}, u32[]{:S(2)}) collective-permute-start(bf16[2,128,384]{2,1,0:T(8,128)(2,1)S(1)} %slice.528), channel_id=1, source_target_pairs={{0,48},{1,49},{2,50},{3,51},{4,52},{5,53},{6,54},{7,55},{8,56},{9,... | collective-permute-start | bytes 589832 | tf_op jit(solution)/shard_map/ppermute | solution.py:57
  496.9 13.3 %collective-permute-start.49 = (bf16[1,128,384]{2,1,0:T(8,128)(2,1)S(1)}, bf16[1,128,384]{2,1,0:T(8,128)(2,1)S(1)}, u32[]{:S(2)}, u32[]{:S(2)}) collective-permute-start(bf16[1,128,384]{2,1,0:T(8,128)(2,1)S(1)} %slice.626), channel_id=1, source_target_pairs={{0,4},{1,5},{2,6},{3,7},{4,0},{5,1},{6,2},{7,3},{8,12},{9,13},{10,... | collective-permute-start | bytes 294920 | tf_op jit(solution)/shard_map/ppermute | solution.py:57
  497.0 13.1 %collective-permute-start.47 = (bf16[1,128,384]{2,1,0:T(8,128)(2,1)S(1)}, bf16[1,128,384]{2,1,0:T(8,128)(2,1)S(1)}, u32[]{:S(2)}, u32[]{:S(2)}) collective-permute-start(bf16[1,128,384]{2,1,0:T(8,128)(2,1)S(1)} %slice.624), channel_id=1, source_target_pairs={{0,16},{1,17},{2,18},{3,19},{4,20},{5,21},{6,22},{7,23},{8,24},{9,... | collective-permute-start | bytes 294920 | tf_op jit(solution)/shard_map/ppermute | solution.py:57
  516.7 21.8 %collective-permute-start.64 = (bf16[2,3,640,128]{3,2,1,0:T(8,128)(2,1)}, bf16[2,3,640,128]{3,2,1,0:T(8,128)(2,1)}, u32[]{:S(2)}, u32[]{:S(2)}) collective-permute-start(bf16[2,3,640,128]{3,2,1,0:T(8,128)(2,1)} %get-tuple-element.196), channel_id=1, source_target_pairs={{0,12},{1,13},{2,14},{3,15},{4,8},{5,9},{6,10},{7,11},{8,4},{9,5},... | collective-permute-start | bytes 2949128 | tf_op jit(solution)/shard_map/ppermute | solution.py:57
  521.1 19.1 %collective-permute-start.62 = (bf16[2,3,640,128]{3,2,1,0:T(8,128)(2,1)}, bf16[2,3,640,128]{3,2,1,0:T(8,128)(2,1)}, u32[]{:S(2)}, u32[]{:S(2)}) collective-permute-start(bf16[2,3,640,128]{3,2,1,0:T(8,128)(2,1)} %get-tuple-element.194), channel_id=1, source_target_pairs={{0,3},{1,2},{2,1},{3,0},{4,7},{5,6},{6,5},{7,4},{8,11},{9,10},{10,... | collective-permute-start | bytes 2949128 | tf_op jit(solution)/shard_map/ppermute | solution.py:57
  534.7 24.2 %collective-permute-start.54 = (bf16[2,4,1,640,128]{4,3,1,2,0:T(8,128)(2,1)S(1)}, bf16[2,4,1,640,128]{4,3,1,2,0:T(8,128)(2,1)S(1)}, u32[]{:S(2)}, u32[]{:S(2)}) collective-permute-start(bf16[2,4,1,640,128]{4,3,1,2,0:T(8,128)(2,1)S(1)} %bitcast.206), channel_id=1, source_target_pairs={{0,12},{1,13},{2,14},{3,15},{4,8},{5,9},{6,10},{7,11},{8,4},{9,5},... | collective-permute-start | bytes 3932168 | tf_op jit(solution)/shard_map/ppermute | solution.py:57
  537.1 24.6 %collective-permute-start.58 = (bf16[2,4,1,656,128]{4,3,2,1,0:T(8,128)(2,1)}, bf16[2,4,1,656,128]{4,3,2,1,0:T(8,128)(2,1)S(1)}, u32[]{:S(2)}, u32[]{:S(2)}) collective-permute-start(bf16[2,4,1,656,128]{4,3,2,1,0:T(8,128)(2,1)} %get-tuple-element.192), channel_id=1, source_target_pairs={{0,3},{1,2},{2,1},{3,0},{4,7},{5,6},{6,5},{7,4},{8,11},{9,10},{10,... | collective-permute-start | bytes 4030472 | tf_op jit(solution)/shard_map/ppermute | solution.py:57
  539.8 14.2 %collective-permute-start.65 = (bf16[3,640,128]{2,1,0:T(8,128)(2,1)S(1)}, bf16[3,640,128]{2,1,0:T(8,128)(2,1)S(1)}, u32[]{:S(2)}, u32[]{:S(2)}) collective-permute-start(bf16[3,640,128]{2,1,0:T(8,128)(2,1)S(1)} %fusion.26), channel_id=1, source_target_pairs={{0,4},{1,5},{2,6},{3,7},{4,0},{5,1},{6,2},{7,3},{8,12},{9,13},{10,... | collective-permute-start | bytes 1474568 | tf_op jit(solution)/shard_map/ppermute | solution.py:57
  541.5 20.5 %collective-permute-start.63 = (bf16[3,640,128]{2,1,0:T(8,128)(2,1)S(1)}, bf16[3,640,128]{2,1,0:T(8,128)(2,1)S(1)}, u32[]{:S(2)}, u32[]{:S(2)}) collective-permute-start(bf16[3,640,128]{2,1,0:T(8,128)(2,1)S(1)} %fusion.24), channel_id=1, source_target_pairs={{0,1},{1,0},{2,3},{3,2},{4,5},{5,4},{6,7},{7,6},{8,9},{9,8},{10,11... | collective-permute-start | bytes 1474568 | tf_op jit(solution)/shard_map/ppermute | solution.py:57
  559.2 10.7 %collective-permute-start.55 = (bf16[4,1,640,128]{3,2,1,0:T(8,128)(2,1)S(1)}, bf16[4,1,640,128]{3,2,1,0:T(8,128)(2,1)S(1)}, u32[]{:S(2)}, u32[]{:S(2)}) collective-permute-start(bf16[4,1,640,128]{3,2,1,0:T(8,128)(2,1)S(1)} %get-tuple-element.238), channel_id=1, source_target_pairs={{0,4},{1,5},{2,6},{3,7},{4,0},{5,1},{6,2},{7,3},{8,12},{9,13},{10,... | collective-permute-start | bytes 1966088 | tf_op jit(solution)/shard_map/ppermute | solution.py:57
  561.9 13.2 %collective-permute-start.59 = (bf16[4,1,656,128]{3,2,0,1:T(8,128)(2,1)S(1)}, bf16[4,1,656,128]{3,2,0,1:T(8,128)(2,1)S(1)}, u32[]{:S(2)}, u32[]{:S(2)}) collective-permute-start(bf16[4,1,656,128]{3,2,0,1:T(8,128)(2,1)S(1)} %fusion.17), channel_id=1, source_target_pairs={{0,1},{1,0},{2,3},{3,2},{4,5},{5,4},{6,7},{7,6},{8,9},{9,8},{10,11... | collective-permute-start | bytes 2015240 | tf_op jit(solution)/shard_map/ppermute | solution.py:57
  570.0 8.4 %collective-permute-start.56 = (bf16[2,1,640,128]{3,2,1,0:T(8,128)(2,1)S(1)}, bf16[2,1,640,128]{3,2,1,0:T(8,128)(2,1)S(1)}, u32[]{:S(2)}, u32[]{:S(2)}) collective-permute-start(bf16[2,1,640,128]{3,2,1,0:T(8,128)(2,1)S(1)} %get-tuple-element.240), channel_id=1, source_target_pairs={{0,3},{1,2},{2,1},{3,0},{4,7},{5,6},{6,5},{7,4},{8,11},{9,10},{10,... | collective-permute-start | bytes 983048 | tf_op jit(solution)/shard_map/ppermute | solution.py:57
  575.2 10.3 %collective-permute-start.60 = (bf16[2,1,656,128]{3,2,0,1:T(8,128)(2,1)S(1)}, bf16[2,1,656,128]{3,2,0,1:T(8,128)(2,1)S(1)}, u32[]{:S(2)}, u32[]{:S(2)}) collective-permute-start(bf16[2,1,656,128]{3,2,0,1:T(8,128)(2,1)S(1)} %fusion.18), channel_id=1, source_target_pairs={{0,12},{1,13},{2,14},{3,15},{4,8},{5,9},{6,10},{7,11},{8,4},{9,5},... | collective-permute-start | bytes 1007624 | tf_op jit(solution)/shard_map/ppermute | solution.py:57
  578.5 7.2 %collective-permute-start.57 = (bf16[1,640,128]{2,1,0:T(8,128)(2,1)S(1)}, bf16[1,640,128]{2,1,0:T(8,128)(2,1)S(1)}, u32[]{:S(2)}, u32[]{:S(2)}) collective-permute-start(bf16[1,640,128]{2,1,0:T(8,128)(2,1)S(1)} %fusion.35), channel_id=1, source_target_pairs={{0,1},{1,0},{2,3},{3,2},{4,5},{5,4},{6,7},{7,6},{8,9},{9,8},{10,11... | collective-permute-start | bytes 491528 | tf_op jit(solution)/shard_map/ppermute | solution.py:57
  594.4 15.0 %collective-permute-start.66 = (bf16[2,1296,128]{2,1,0:T(8,128)(2,1)S(1)}, bf16[2,1296,128]{2,1,0:T(8,128)(2,1)S(1)}, u32[]{:S(2)}, u32[]{:S(2)}) collective-permute-start(bf16[2,1296,128]{2,1,0:T(8,128)(2,1)S(1)} %slice.661), channel_id=1, source_target_pairs={{0,48},{1,49},{2,50},{3,51},{4,52},{5,53},{6,54},{7,55},{8,56},{9,... | collective-permute-start | bytes 1990664 | tf_op jit(solution)/shard_map/ppermute | solution.py:57
  610.2 7.3 %collective-permute-start.67 = (bf16[1296,128]{1,0:T(8,128)(2,1)}, bf16[1296,128]{1,0:T(8,128)(2,1)S(1)}, u32[]{:S(2)}, u32[]{:S(2)}) collective-permute-start(bf16[1296,128]{1,0:T(8,128)(2,1)} %fusion.29), channel_id=1, source_target_pairs={{0,16},{1,17},{2,18},{3,19},{4,20},{5,21},{6,22},{7,23},{8,24},{9,... | collective-permute-start | bytes 995336 | tf_op jit(solution)/shard_map/ppermute | solution.py:57
  (61 other events, 502.7 us)
Sparse Core Ops, SparseCore 0:
  18.4 124.5 all-gather.2

commit v5 on v3

--- a/solution.py
+++ b/solution.py
@@ -127,6 +127,28 @@
     return jnp.concatenate(out)
 
 
+HALF = ROWS // 2
+
+
+def gather_front(own, gains, y, phase):
+    row = jnp.pad(gains[None], ((0, 15), (0, 98)))
+    block = jnp.concatenate([own, row])[None]
+    for number in range(2):
+        block = jnp.concatenate([block, swapped(block, along((0, 0), number))])
+    at = slot_of(jnp.arange(4, dtype=jnp.int32) ^ y, phase)
+    front = lax.dynamic_index_in_dim(block, at[0], 0, keepdims=False)
+    rows = jnp.pad(block[:, ROWS][at], ((0, 12), (0, 0)))
+    blocks = [front[None, :HALF], jnp.concatenate([front[HALF:ROWS], rows])[None]]
+    axes = ((1, 2), (2, 1))
+    for leg in range(2):
+        for number in range(2):
+            for part in range(2):
+                axis = axes[part][leg]
+                got = swapped(blocks[part], along((axis, axis), number))
+                blocks[part] = jnp.concatenate([blocks[part], got])
+    return blocks
+
+
 PART_ROWS = ((0, 432), (432, 864), (864, 1280))
 
 
@@ -174,16 +196,26 @@
     return scale, (u * scale * gain).astype(bf16)
 
 
-def project_kernel(u_ref, g_ref, cos_ref, sin_ref, w_ref, qt_ref, kv_ref):
+def front_weight(idx_ref, wa_ref, wb_ref, c):
+    pieces = []
+    for d in range(10):
+        low, high = 96 * c, 96 * c + 96
+        if low < HALF:
+            pieces.append(wa_ref[idx_ref[d], low : min(high, HALF), :])
+        if high > HALF:
+            pieces.append(wb_ref[idx_ref[16 + d], max(low, HALF) - HALF : high - HALF, :])
+    return jnp.concatenate(pieces, axis=0)
+
+
+def project_kernel(idx_ref, u_ref, g_ref, cos_ref, sin_ref, wa_ref, wb_ref, qt_ref, kv_ref):
     u = u_ref[...].astype(f32)
     _, a = normed_of(u, g_ref[...])
     cos, sin = cos_ref[...], sin_ref[...]
     blocks = []
     for c in range(0, 13, 2):
+        w = front_weight(idx_ref, wa_ref, wb_ref, c)
         if c + 1 < 13:
-            w = jnp.concatenate([qkv_weight(w_ref, c), qkv_weight(w_ref, c + 1)], axis=1)
-        else:
-            w = qkv_weight(w_ref, c)
+            w = jnp.concatenate([w, front_weight(idx_ref, wa_ref, wb_ref, c + 1)], axis=1)
         y = mm(a, w)
         for k in range(w.shape[1] // 128):
             b = y[:, 128 * k : 128 * k + 128]
@@ -206,29 +238,31 @@
         kv_ref[:, 128 * g : 128 * g + 128] = jnp.where(lane < 64, k, v).astype(bf16)
 
 
-def project(u, gain, cos, sin, weights):
+def project(u, gain, cos, sin, idx, front):
+    whole = lambda *shape: pl.BlockSpec(shape, lambda i, idx: (0,) * len(shape))
     return pl.pallas_call(
         project_kernel,
         name="project",
-        grid=(1,),
-        in_specs=[
-            pl.BlockSpec((R, D), lambda i: (0, 0)),
-            pl.BlockSpec((1, D), lambda i: (0, 0)),
-            pl.BlockSpec((R, 128), lambda i: (0, 0)),
-            pl.BlockSpec((R, 128), lambda i: (0, 0)),
-            pl.BlockSpec((10, ROWS, 128), lambda i: (0, 0, 0)),
-        ],
-        out_specs=[
-            pl.BlockSpec((QPAD, R), lambda i: (0, 0)),
-            pl.BlockSpec((R, 768), lambda i: (0, 0)),
-        ],
+        grid_spec=pltpu.PrefetchScalarGridSpec(
+            num_scalar_prefetch=1,
+            grid=(1,),
+            in_specs=[
+                whole(R, D),
+                whole(1, D),
+                whole(R, 128),
+                whole(R, 128),
+                whole(16, HALF, 128),
+                whole(16, HALF + 16, 128),
+            ],
+            out_specs=[whole(QPAD, R), whole(R, 768)],
+        ),
         out_shape=[
             jax.ShapeDtypeStruct((QPAD, R), bf16),
             jax.ShapeDtypeStruct((R, 768), bf16),
         ],
         compiler_params=pltpu.CompilerParams(vmem_limit_bytes=48 << 20),
-        cost_estimate=pl.CostEstimate(flops=400_000_000, bytes_accessed=4_000_000, transcendentals=0),
-    )(u, gain, cos, sin, weights)
+        cost_estimate=pl.CostEstimate(flops=400_000_000, bytes_accessed=6_000_000, transcendentals=0),
+    )(idx, u, gain, cos, sin, *front)
 
 
 def heads_wide(ref, low):
@@ -742,23 +776,19 @@
     return jnp.where(rank < 10, 0, jnp.where((rank >= 16) & (rank < 48), 2, 1))
 
 
-def shard_blocks(flat, gains, rank):
-    g = jnp.zeros((1, 128), bf16).at[0, :30].set(gains)
-
+def shard_blocks(flat, rank):
     def narrow(_):
         w = jnp.pad(flat.reshape(96, 1600), ((0, 0), (0, 64)))
         w = w.reshape(96, 13, 128).transpose(1, 0, 2).reshape(1248, 128)
-        return jnp.concatenate([w, jnp.pad(g, ((0, 31), (0, 0)))])
+        return jnp.pad(w, ((0, 32), (0, 0)))
 
     def square(_):
         w = jnp.pad(flat.reshape(160, 960), ((0, 0), (0, 64)))
-        w = w.reshape(160, 8, 128).transpose(1, 0, 2)
-        last = jnp.concatenate([jnp.zeros((1, 64), bf16), g[:, :64]], axis=1)
-        return w.at[7, 0].add(last[0]).reshape(ROWS, 128)
+        return w.reshape(160, 8, 128).transpose(1, 0, 2).reshape(ROWS, 128)
 
     def broad(_):
-        w = jnp.pad(flat.reshape(30, 40, 128), ((0, 2), (0, 0), (0, 0))).transpose(1, 0, 2)
-        return w.at[0, 30].set(g[0]).reshape(ROWS, 128)
+        w = jnp.pad(flat.reshape(30, 40, 128), ((0, 2), (0, 0), (0, 0)))
+        return w.transpose(1, 0, 2).reshape(ROWS, 128)
 
     return lax.switch(shard_kind(rank), [narrow, square, broad], 0)
 
@@ -777,19 +807,6 @@
         return w.reshape(SHARD), blocks[30, :30]
 
     return lax.switch(shard_kind(rank), [narrow, square, broad], 0)
-
-
-def gathered_gains(gathered):
-    rows = jnp.concatenate(
-        [
-            gathered[:10, 1248, :30],
-            gathered[10:16, 1120, 64:94],
-            gathered[16:48, 30, :30],
-            gathered[48:, 1120, 64:94],
-        ]
-    ).astype(f32)
-    flat = rows.reshape(1, 2 * D)
-    return flat[:, :D], flat[:, D:]
 
 
 def per_device(layer_in, out_grad, segment_ids, block_pair, params, norm_gains):
@@ -799,7 +816,7 @@
     y, x, z = rank // 16, (rank // 4) % 4, rank % 4
     zh = z // 2
 
-    own = shard_blocks(params[0], norm_gains[0], rank)
+    own = shard_blocks(params[0], rank)
     gathered = lax.all_gather(own, ("ctx", "fsdp"), axis=0)
 
     seg_row = segment_ids[0]
@@ -831,7 +848,18 @@
     target = jnp.where(spread % 32 < 30, (spread // 32) * 30 + spread % 32, -1)
     pad = (jnp.arange(D, dtype=jnp.int32)[:, None] == target[None, :]).astype(bf16)
 
-    gain_one, gain_two = gathered_gains(gathered)
+    front = gather_front(own, norm_gains[0], y, phase)
+    four = jnp.arange(4, dtype=jnp.int32)
+    slots_y, slots_x, slots_z = (slot_of(four ^ at_axis, phase) for at_axis in (y, x, z))
+    idx = jnp.concatenate(
+        [
+            (slots_x[:, None] + 4 * slots_z[None, :]).reshape(16),
+            (4 * slots_x[:, None] + slots_z[None, :]).reshape(16),
+        ]
+    )
+    gains = front[1][:, HALF : HALF + 4, :30][idx[16:]].astype(f32)
+    gains = gains.transpose(1, 0, 2).reshape(1, 2 * D)
+    gain_one, gain_two = gains[:, :D], gains[:, D:]
     first = phase == 0
 
     u = layer_in[0]
@@ -839,7 +867,7 @@
     kept = []
     for tick in range(2):
         active = phase == tick
-        qt, kv = project(u, gain_one, cos, sin, gathered)
+        qt, kv = project(u, gain_one, cos, sin, idx, front)
         kv_side = jnp.where(active, kv[:, :384], over(kv[:, 384:], tick))
         qt_side = jnp.where(active, qt[:QSIDE], over(qt[QSIDE:], tick))
         kv_all = gather_keys(kv_side)
@@ -880,8 +908,7 @@
     gains = jnp.where(
         square, jnp.pad(gains, ((0, 0), (64, 34))), jnp.pad(gains, ((0, 0), (0, 98)))
     )
-    four = jnp.arange(4, dtype=jnp.int32)
-    slots = jnp.concatenate([slot_of(four ^ at_axis, phase) for at_axis in (y, x, z)])
+    slots = jnp.concatenate([slots_y, slots_x, slots_z])
     keep, send = outer(slots, at, dqkv, mixed, dhb, nt, dgate, dup, mt, cb, gains)
     total = scatter_grads(keep, send)
     param_part, gain_part = blocks_shard(total, rank)

time: 629 us -> 616 us (0.979)
  waiting for transfers between devices: 327 us -> 263 us
  starting transfers between devices: 83.5 us -> 126 us
  local copies, waits for them, and re-layouts: 26.9 us -> 34 us
    all_gather x1, waiting for transfers between devices: 119 us -> 0.02 us  [per_device(): gathered = lax.all_gather(own, ('ctx', 'fsdp'), axis=0)]
    ppermute x54 -> x64, waiting for transfers between devices: 193 us -> 247 us  [swapped(): return lax.ppermute(block, ALL, pairs)]
    ppermute x54 -> x64, starting transfers between devices: 62.1 us -> 105 us  [swapped(): return lax.ppermute(block, ALL, pairs)]
    unnamed x110 -> x142, local copies, waits for them, and re-layouts: 16.4 us -> 20.8 us
  transfers between devices with their start and end apart: 69 -> 79, of which waited for: 50 -> 59; matrix products, arithmetic and copies ran while one was open for 5% -> 8% of each run, Pallas kernels for 0% -> 2%
where the time goes in v5:
time: 616 us; the launch traced here: 607 us
  waiting for transfers between devices  263 us (43%)
  Pallas kernels  127 us (21%)
  starting transfers between devices  126 us (20%)
  other arithmetic  39.6 us (6%)
  local copies, waits for them, and re-layouts  34 us (6%)
  between operations  17.7 us (3%)
    ppermute x64, waiting for transfers between devices, swapped(): return lax.ppermute(block, ALL, pairs)  247 us
    ppermute x64, starting transfers between devices, swapped(): return lax.ppermute(block, ALL, pairs)  105 us
    pallas_call x2, Pallas kernels, attend_back(): pl.pallas_call(attend_back_kernel, name='attend_back', grid=(SIDE,), in_s...  32.1 us
    pallas_call x2, Pallas kernels, feed_back(): pl.pallas_call(feed_back_kernel, name='feed_back', grid=(4,), in_specs=[w...  29.7 us
    pallas_call x2, Pallas kernels, feed(): pl.pallas_call(feed_kernel, name='feed', grid=(4,), in_specs=[whole(D, R)...  21.7 us
    ppermute x14, starting transfers between devices, over(): return lax.ppermute(block, 'phase', [(source, 1 - source)])  20.8 us
    unnamed x142, local copies, waits for them, and re-layouts  20.8 us
    pallas_call x2, Pallas kernels, attend(): pl.pallas_call(attend_kernel, name='attend', grid=(SIDE,), in_specs=[pl.B...  17.9 us
  transfers between devices with their start and end apart: 79, of which 59 were waited for; matrix products, arithmetic and copies ran while one was open for 8% of the time, Pallas kernels for 2%

profile of v5, /device:TPU:0, one launch (start us, length us, event | category | flops | bytes accessed | tf_op | source)
XLA Modules:
  0.0 606.6 jit_solution(8922992997418570655)
XLA Ops:
  7.3 8.8 %conditional.2 = (bf16[1280,128]{1,0:T(8,128)(2,1)}) conditional(s32[]{:T(128)} %clamp.4, bf16[1,153600]{1,0:T(2,128)(2,1)} %param.26, bf16[1,153600]{1,0:T(2,128)(2,1)} %param.26, bf16[1,153600]{1,0:T(2,128)(2,1)} %param.26), branch_computations={%region_0.1_spmd, %region_1.2_spmd, %region_2.3_spmd} | conditional | bytes 3780622 | solution.py:793
  7.3 7.3 %reduce = bf16[153600]{0:T(1024)(128)(2,1)S(1)} reduce(bf16[1,153600]{1,0:T(2,128)(2,1)} %param, bf16[]{:T(256)} %constant.192), dimensions={0}, to_apply=%param.reduce_sub_computation | reduce | bytes 614402 | tf_op jit(solution)/shard_map/shard_map
  27.4 10.8 %collective-permute-done.1 = bf16[2,1296,128]{2,1,0:T(8,128)(2,1)S(1)} collective-permute-done((bf16[2,1296,128]{2,1,0:T(8,128)(2,1)S(1)}, bf16[2,1296,128]{2,1,0:T(8,128)(2,1)S(1)}, u32[]{:S(2)}, u32[]{:S(2)}) %collective-permute-start.1) | collective-permute-done | bytes 663584 | tf_op jit(solution)/shard_map/ppermute | solution.py:57
  47.8 4.6 collective-permute-start.3
  52.4 3.8 collective-permute-done.7
  56.2 4.0 collective-permute-start.8
  60.2 6.1 %collective-permute-done.3 = bf16[2,656,128]{2,1,0:T(8,128)(2,1)S(1)} collective-permute-done((bf16[2,656,128]{2,1,0:T(8,128)(2,1)S(1)}, bf16[2,656,128]{2,1,0:T(8,128)(2,1)S(1)}, u32[]{:S(2)}, u32[]{:S(2)}) %collective-permute-start.3) | collective-permute-done | bytes 335904 | tf_op jit(solution)/shard_map/ppermute | solution.py:57
  68.0 9.1 %collective-permute-done.8 = bf16[4,640,128]{2,1,0:T(8,128)(2,1)S(1)} collective-permute-done((bf16[4,640,128]{2,1,0:T(8,128)(2,1)S(1)}, bf16[4,640,128]{2,1,0:T(8,128)(2,1)S(1)}, u32[]{:S(2)}, u32[]{:S(2)}) %collective-permute-start.8) | collective-permute-done | bytes 655392 | tf_op jit(solution)/shard_map/ppermute | solution.py:57
  89.9 26.5 %collective-permute-done.9 = bf16[8,640,128]{2,1,0:T(8,128)(2,1)} collective-permute-done((bf16[8,640,128]{2,1,0:T(8,128)(2,1)}, bf16[8,640,128]{2,1,0:T(8,128)(2,1)}, u32[]{:S(2)}, u32[]{:S(2)}) %collective-permute-start.9) | collective-permute-done | bytes 1310752 | tf_op jit(solution)/shard_map/ppermute | solution.py:57
  118.9 9.9 %collective-permute-done.5 = bf16[8,656,128]{2,1,0:T(8,128)(2,1)} collective-permute-done((bf16[8,656,128]{2,1,0:T(8,128)(2,1)}, bf16[8,656,128]{2,1,0:T(8,128)(2,1)}, u32[]{:S(2)}, u32[]{:S(2)}) %collective-permute-start.5) | collective-permute-done | bytes 1343520 | tf_op jit(solution)/shard_map/ppermute | solution.py:57
  138.6 8.2 %collective-permute-done.15 = bf16[128,384]{1,0:T(8,128)(2,1)S(1)} collective-permute-done((bf16[128,384]{1,0:T(8,128)(2,1)S(1)}, bf16[128,384]{1,0:T(8,128)(2,1)S(1)}, u32[]{:S(2)}, u32[]{:S(2)}) %collective-permute-start.15) | collective-permute-done | bytes 98336 | tf_op jit(solution)/shard_map/ppermute | solution.py:57
  146.8 4.5 collective-permute-start.13
  153.9 3.7 collective-permute-start.17
  163.2 3.3 collective-permute-done.14
  175.3 4.6 collective-permute-start.20
  185.2 4.6 collective-permute-done.20
  190.4 9.0 %attend.2 = (bf16[576,128]{1,0:T(8,128)(2,1)S(1)}, f32[3,1,384]{2,1,0:T(1,128)S(1)}) custom-call(bf16[576,128]{1,0:T(8,128)(2,1)S(1)} %slice_select_fusion.3.qt_ref, bf16[4096,384]{1,0:T(8,128)(2,1)S(1)} %bitcast.200, f32[4096,128]{1,0:T(8,128)S(1)} %and_select_fusion.bias_ref), custom_call_target="tpu_custom_call" | custom-call | flops 4000000000 | bytes 8000000 | tf_op jit(solution)/shard_map/attend/pallas_call | solution.py:297
  202.7 11.7 %feed.2 = (bf16[128,960]{1,0:T(8,128)(2,1)S(1)}, f32[128,960]{1,0:T(8,128)}, bf16[1024,128]{1,0:T(8,128)(2,1)}, f32[128,2560]{1,0:T(8,128)}, f32[128,2560]{1,0:T(8,128)}, /*index=5*/bf16[2560,128]{1,0:T(8,128)(2,1)}) custom-call(bf16[960,128]{1,0:T(8,128)(2,1)S(1)} %constant_dynamic-update-slice_fusion.10.mixed_ref, bf16[128,960]{1,0:T(8,128)(2,1)S(1)} %bitcast.199, ...), custom_call_target="tpu_custom_call" | custom-call | flops 2200000000 | bytes 22000000 | tf_op jit(solution)/shard_map/feed/pallas_call | solution.py:400
  223.0 5.9 collective-permute-done.28
  243.9 4.5 collective-permute-done.31
  248.7 4.4 collective-permute-start.33
  256.5 5.3 collective-permute-done.32
  263.7 9.0 %attend.3 = (bf16[576,128]{1,0:T(8,128)(2,1)S(1)}, f32[3,1,384]{2,1,0:T(1,128)S(1)}) custom-call(bf16[576,128]{1,0:T(8,128)(2,1)S(1)} %slice_select_fusion.2.qt_ref, bf16[4096,384]{1,0:T(8,128)(2,1)S(1)} %bitcast.202, f32[4096,128]{1,0:T(8,128)S(1)} %copy-done.6), custom_call_target="tpu_custom_call" | custom-call | flops 4000000000 | bytes 8000000 | tf_op jit(solution)/shard_map/attend/pallas_call | solution.py:297
  275.0 10.0 %feed.3 = (bf16[128,960]{1,0:T(8,128)(2,1)S(1)}, f32[128,960]{1,0:T(8,128)S(1)}, bf16[1024,128]{1,0:T(8,128)(2,1)S(1)}, f32[128,2560]{1,0:T(8,128)S(1)}, f32[128...) custom-call(bf16[960,128]{1,0:T(8,128)(2,1)S(1)} %maximum_select_fusion.2.mixed_ref, ...), custom_call_target="tpu_custom_call" | custom-call | flops 2200000000 | bytes 22000000 | tf_op jit(solution)/shard_map/feed/pallas_call | solution.py:400
  286.9 15.4 %feed_back.2 = (bf16[128,2560]{1,0:T(8,128)(2,1)}, bf16[128,2560]{1,0:T(8,128)(2,1)}, f32[128,960]{1,0:T(8,128)S(1)}, bf16[128,1024]{1,0:T(8,128)(2,1)}, f32[1,9...) custom-call(f32[128,960]{1,0:T(8,128)S(1)} %bitcast.197, ...), custom_call_target="tpu_custom_call" | custom-call | flops 2200000000 | bytes 22000000 | tf_op jit(solution)/shard_map/feed_back/pallas_call | solution.py:491
  305.9 16.1 %attend_back.2 = (bf16[4096,384]{1,0:T(8,128)(2,1)S(1)}, f32[576,128]{1,0:T(8,128)S(1)}) custom-call(bf16[576,128]{1,0:T(8,128)(2,1)S(1)} %slice_select_fusion.2.qt_ref, bf16[4096,384]{1,0:T(8,128)(2,1)} %bitcast.203, f32[4096,128]{1,0:T(8,128)S(1)} %copy-done.7, f32[576,128]{1,0:T(8,128)S(1)} %slice_select_fusion.1.dot_ref, ...), custom_call_target="tpu_custom_call" | custom-call | flops 10000000000 | bytes 14000000 | tf_op jit(solution)/shard_map/attend_back/pallas_call | solution.py:549
  322.3 3.3 collective-permute-start.41
  328.7 6.8 %collective-permute-done.41 = bf16[8,128,384]{2,1,0:T(8,128)(2,1)S(1)} collective-permute-done((bf16[8,128,384]{2,1,0:T(8,128)(2,1)S(1)}, bf16[8,128,384]{2,1,0:T(8,128)(2,1)S(1)}, u32[]{:S(2)}, u32[]{:S(2)}) %collective-permute-start.41) | collective-permute-done | bytes 786464 | tf_op jit(solution)/shard_map/ppermute | solution.py:57
  335.9 3.7 collective-permute-done.37
  340.2 3.5 collective-permute-done.42
  351.2 3.7 collective-permute-done.39
  364.1 4.2 project_back.2
  371.9 14.4 %feed_back.3 = (bf16[128,2560]{1,0:T(8,128)(2,1)S(1)}, bf16[128,2560]{1,0:T(8,128)(2,1)S(1)}, f32[128,960]{1,0:T(8,128)S(1)}, bf16[128,1024]{1,0:T(8,128)(2,1)S(...) custom-call(f32[128,960]{1,0:T(8,128)S(1)} %convert_select_fusion.c_ref, ...), custom_call_target="tpu_custom_call" | custom-call | flops 2200000000 | bytes 22000000 | tf_op jit(solution)/shard_map/feed_back/pallas_call | solution.py:491
  390.4 16.1 %attend_back.3 = (bf16[4096,384]{1,0:T(8,128)(2,1)S(1)}, f32[576,128]{1,0:T(8,128)S(1)}) custom-call(bf16[576,128]{1,0:T(8,128)(2,1)S(1)} %copy-done.18, bf16[4096,384]{1,0:T(8,128)(2,1)} %bitcast.201, f32[4096,128]{1,0:T(8,128)S(1)} %copy-done.7, f32[576,128]{1,0:T(8,128)S(1)} %slice_select_fusion.dot_ref, bf16[576,128]{1,0:T(8,128)(2,1)S(1)} %copy-done.12, ...), custom_call_target="tpu_custom_call" | custom-call | flops 10000000000 | bytes 14000000 | tf_op jit(solution)/shard_map/attend_back/pallas_call | solution.py:549
  413.2 6.8 %collective-permute-done.54 = bf16[8,128,384]{2,1,0:T(8,128)(2,1)S(1)} collective-permute-done((bf16[8,128,384]{2,1,0:T(8,128)(2,1)S(1)}, bf16[8,128,384]{2,1,0:T(8,128)(2,1)S(1)}, u32[]{:S(2)}, u32[]{:S(2)}) %collective-permute-start.54) | collective-permute-done | bytes 786464 | tf_op jit(solution)/shard_map/ppermute | solution.py:57
  423.6 4.5 collective-permute-done.55
  428.3 4.7 collective-permute-start.56
  436.9 3.5 collective-permute-done.52
  451.1 3.6 project_back.3
  462.4 14.1 %outer.1 = (bf16[2,4,4,432,128]{4,3,2,1,0:T(8,128)(2,1)}, bf16[2,4,4,432,128]{4,3,2,1,0:T(8,128)(2,1)}, bf16[2,4,4,416,128]{4,3,2,1,0:T(8,128)(2,1)}, bf16[2,4,4...) custom-call(s32[12]{0:T(128)S(1)} %pad_add_fusion.3.slot_ref, ...), custom_call_target="tpu_custom_call" | custom-call | flops 2600000000 | bytes 24000000 | tf_op jit(solution)/shard_map/outer/pallas_call | solution.py:753
  483.2 34.9 %collective-permute-done.72 = bf16[2,4,4,416,128]{4,3,2,1,0:T(8,128)(2,1)S(1)} collective-permute-done((bf16[2,4,4,416,128]{4,3,2,1,0:T(8,128)(2,1)}, bf16[2,4,4,416,128]{4,3,2,1,0:T(8,128)(2,1)S(1)}, u32[]{:S(2)}, u32[]{:S(2)}) %collective-permute-start.72) | collective-permute-done | bytes 3407904 | tf_op jit(solution)/shard_map/ppermute | solution.py:57
  524.4 18.6 %collective-permute-done.73 = bf16[4,4,416,128]{3,2,1,0:T(8,128)(2,1)S(1)} collective-permute-done((bf16[4,4,416,128]{3,2,1,0:T(8,128)(2,1)S(1)}, bf16[4,4,416,128]{3,2,1,0:T(8,128)(2,1)S(1)}, u32[]{:S(2)}, u32[]{:S(2)}) %collective-permute-start.73) | collective-permute-done | bytes 1703968 | tf_op jit(solution)/shard_map/ppermute | solution.py:57
  553.0 4.5 collective-permute-done.74
  563.1 4.0 collective-permute-done.75
  568.2 3.4 collective-permute-start.76
  577.4 6.3 %collective-permute-done.69 = bf16[4,432,128]{2,1,0:T(8,128)(2,1)S(1)} collective-permute-done((bf16[4,432,128]{2,1,0:T(8,128)(2,1)S(1)}, bf16[4,432,128]{2,1,0:T(8,128)(2,1)S(1)}, u32[]{:S(2)}, u32[]{:S(2)}) %collective-permute-start.69) | collective-permute-done | bytes 442400 | tf_op jit(solution)/shard_map/ppermute | solution.py:57
  586.1 6.1 %collective-permute-done.70 = bf16[2,432,128]{2,1,0:T(8,128)(2,1)S(1)} collective-permute-done((bf16[2,432,128]{2,1,0:T(8,128)(2,1)S(1)}, bf16[2,432,128]{2,1,0:T(8,128)(2,1)S(1)}, u32[]{:S(2)}, u32[]{:S(2)}) %collective-permute-start.70) | collective-permute-done | bytes 221216 | tf_op jit(solution)/shard_map/ppermute | solution.py:57
  592.3 4.7 collective-permute-done.71
  (440 shorter events, 212.8 us)
Async XLA Ops:
  7.2 195.5 %all-gather.3.cloned.1.call-start = ((), (), s32[]{:S(2)}) async-start(), calls=%async_computation | async-start | bytes 21299200 | tf_op jit(solution)/shard_map/all_gather | solution.py:820
  17.1 7.3 %collective-permute-start = (bf16[1,1296,128]{2,1,0:T(8,128)(2,1)S(1)}, bf16[1,1296,128]{2,1,0:T(8,128)(2,1)S(1)}, u32[]{:S(2)}, u32[]{:S(2)}) collective-permute-start(bf16[1,1296,128]{2,1,0:T(8,128)(2,1)S(1)} %fusion.26), channel_id=1, source_target_pairs={{0,16},{1,17},{2,18},{3,19},{4,20},{5,21},{6,22},{7,23},{8,24},{9,... | collective-permute-start | bytes 995336 | tf_op jit(solution)/shard_map/ppermute | solution.py:57
  24.5 13.7 %collective-permute-start.1 = (bf16[2,1296,128]{2,1,0:T(8,128)(2,1)S(1)}, bf16[2,1296,128]{2,1,0:T(8,128)(2,1)S(1)}, u32[]{:S(2)}, u32[]{:S(2)}) collective-permute-start(bf16[2,1296,128]{2,1,0:T(8,128)(2,1)S(1)} %pad_maximum_fusion.10), channel_id=1, source_target_pairs={{0,48},{1,49},{2,50},{3,51},{4,52},{5,53},{6,54},{7,55},{8,56},{9,... | collective-permute-start | bytes 1990664 | tf_op jit(solution)/shard_map/ppermute | solution.py:57
  44.8 11.4 %collective-permute-start.7 = (bf16[2,640,128]{2,1,0:T(8,128)(2,1)S(1)}, bf16[2,640,128]{2,1,0:T(8,128)(2,1)S(1)}, u32[]{:S(2)}, u32[]{:S(2)}) collective-permute-start(bf16[2,640,128]{2,1,0:T(8,128)(2,1)S(1)} %pad_maximum_fusion.18), channel_id=1, source_target_pairs={{0,12},{1,13},{2,14},{3,15},{4,8},{5,9},{6,10},{7,11},{8,4},{9,5},... | collective-permute-start | bytes 983048 | tf_op jit(solution)/shard_map/ppermute | solution.py:57
  47.8 18.5 %collective-permute-start.3 = (bf16[2,656,128]{2,1,0:T(8,128)(2,1)S(1)}, bf16[2,656,128]{2,1,0:T(8,128)(2,1)S(1)}, u32[]{:S(2)}, u32[]{:S(2)}) collective-permute-start(bf16[2,656,128]{2,1,0:T(8,128)(2,1)S(1)} %pad_maximum_fusion.17), channel_id=1, source_target_pairs={{0,3},{1,2},{2,1},{3,0},{4,7},{5,6},{6,5},{7,4},{8,11},{9,10},{10,... | collective-permute-start | bytes 1007624 | tf_op jit(solution)/shard_map/ppermute | solution.py:57
  56.2 20.9 %collective-permute-start.8 = (bf16[4,640,128]{2,1,0:T(8,128)(2,1)S(1)}, bf16[4,640,128]{2,1,0:T(8,128)(2,1)S(1)}, u32[]{:S(2)}, u32[]{:S(2)}) collective-permute-start(bf16[4,640,128]{2,1,0:T(8,128)(2,1)S(1)} %pad_maximum_fusion.11), channel_id=1, source_target_pairs={{0,1},{1,0},{2,3},{3,2},{4,5},{5,4},{6,7},{7,6},{8,9},{9,8},{10,11... | collective-permute-start | bytes 1966088 | tf_op jit(solution)/shard_map/ppermute | solution.py:57
  66.4 14.1 %collective-permute-start.4 = (bf16[4,656,128]{2,1,0:T(8,128)(2,1)S(1)}, bf16[4,656,128]{2,1,0:T(8,128)(2,1)S(1)}, u32[]{:S(2)}, u32[]{:S(2)}) collective-permute-start(bf16[4,656,128]{2,1,0:T(8,128)(2,1)S(1)} %pad_maximum_fusion.9), channel_id=1, source_target_pairs={{0,4},{1,5},{2,6},{3,7},{4,0},{5,1},{6,2},{7,3},{8,12},{9,13},{10,... | collective-permute-start | bytes 2015240 | tf_op jit(solution)/shard_map/ppermute | solution.py:57
  78.4 38.0 %collective-permute-start.9 = (bf16[8,640,128]{2,1,0:T(8,128)(2,1)}, bf16[8,640,128]{2,1,0:T(8,128)(2,1)}, u32[]{:S(2)}, u32[]{:S(2)}) collective-permute-start(bf16[8,640,128]{2,1,0:T(8,128)(2,1)} %pad_maximum_fusion.4), channel_id=1, source_target_pairs={{0,3},{1,2},{2,1},{3,0},{4,7},{5,6},{6,5},{7,4},{8,11},{9,10},{10,... | collective-permute-start | bytes 3932168 | tf_op jit(solution)/shard_map/ppermute | solution.py:57
  81.8 46.9 %collective-permute-start.5 = (bf16[8,656,128]{2,1,0:T(8,128)(2,1)}, bf16[8,656,128]{2,1,0:T(8,128)(2,1)}, u32[]{:S(2)}, u32[]{:S(2)}) collective-permute-start(bf16[8,656,128]{2,1,0:T(8,128)(2,1)} %pad_maximum_fusion.2), channel_id=1, source_target_pairs={{0,12},{1,13},{2,14},{3,15},{4,8},{5,9},{6,10},{7,11},{8,4},{9,5},... | collective-permute-start | bytes 4030472 | tf_op jit(solution)/shard_map/ppermute | solution.py:57
  137.7 9.1 %collective-permute-start.15 = (bf16[128,384]{1,0:T(8,128)(2,1)S(1)}, bf16[128,384]{1,0:T(8,128)(2,1)S(1)}, u32[]{:S(2)}, u32[]{:S(2)}) collective-permute-start(bf16[128,384]{1,0:T(8,128)(2,1)S(1)} %slice_select_fusion.5), channel_id=1, source_target_pairs={{0,2},{1,3},{2,0},{3,1},{4,6},{5,7},{6,4},{7,5},{8,10},{9,11},{10,... | collective-permute-start | bytes 294920 | tf_op jit(solution)/shard_map/ppermute | solution.py:57
  137.8 9.0 %collective-permute-start.12 = (bf16[1,128,384]{2,1,0:T(8,128)(2,1)S(1)}, bf16[1,128,384]{2,1,0:T(8,128)(2,1)S(1)}, u32[]{:S(2)}, u32[]{:S(2)}) collective-permute-start(bf16[1,128,384]{2,1,0:T(8,128)(2,1)S(1)} %bitcast.251), channel_id=1, source_target_pairs={{0,16},{1,17},{2,18},{3,19},{4,20},{5,21},{6,22},{7,23},{8,24},{9,... | collective-permute-start | bytes 294920 | tf_op jit(solution)/shard_map/ppermute | solution.py:57
  146.8 10.8 %collective-permute-start.13 = (bf16[2,128,384]{2,1,0:T(8,128)(2,1)S(1)}, bf16[2,128,384]{2,1,0:T(8,128)(2,1)S(1)}, u32[]{:S(2)}, u32[]{:S(2)}) collective-permute-start(bf16[2,128,384]{2,1,0:T(8,128)(2,1)S(1)} %pad_maximum_fusion.20), channel_id=1, source_target_pairs={{0,48},{1,49},{2,50},{3,51},{4,52},{5,53},{6,54},{7,55},{8,56},{9,... | collective-permute-start | bytes 589832 | tf_op jit(solution)/shard_map/ppermute | solution.py:57
  153.9 7.3 %collective-permute-start.17 = (bf16[2,128,384]{2,1,0:T(8,128)(2,1)S(1)}, bf16[2,128,384]{2,1,0:T(8,128)(2,1)S(1)}, u32[]{:S(2)}, u32[]{:S(2)}) collective-permute-start(bf16[2,128,384]{2,1,0:T(8,128)(2,1)S(1)} %pad_maximum_fusion.21), channel_id=1, source_target_pairs={{0,12},{1,13},{2,14},{3,15},{4,8},{5,9},{6,10},{7,11},{8,4},{9,5},... | collective-permute-start | bytes 589832 | tf_op jit(solution)/shard_map/ppermute | solution.py:57
  158.4 8.1 %collective-permute-start.14 = (bf16[4,128,384]{2,1,0:T(8,128)(2,1)}, bf16[4,128,384]{2,1,0:T(8,128)(2,1)}, u32[]{:S(2)}, u32[]{:S(2)}) collective-permute-start(bf16[4,128,384]{2,1,0:T(8,128)(2,1)} %pad_maximum_fusion.13), channel_id=1, source_target_pairs={{0,4},{1,5},{2,6},{3,7},{4,0},{5,1},{6,2},{7,3},{8,12},{9,13},{10,... | collective-permute-start | bytes 1179656 | tf_op jit(solution)/shard_map/ppermute | solution.py:57
  162.7 8.1 %collective-permute-start.18 = (bf16[4,128,384]{2,1,0:T(8,128)(2,1)}, bf16[4,128,384]{2,1,0:T(8,128)(2,1)}, u32[]{:S(2)}, u32[]{:S(2)}) collective-permute-start(bf16[4,128,384]{2,1,0:T(8,128)(2,1)} %pad_maximum_fusion.14), channel_id=1, source_target_pairs={{0,16},{1,17},{2,18},{3,19},{4,20},{5,21},{6,22},{7,23},{8,24},{9,... | collective-permute-start | bytes 1179656 | tf_op jit(solution)/shard_map/ppermute | solution.py:57
  172.0 13.3 %collective-permute-start.19 = (bf16[8,128,384]{2,1,0:T(8,128)(2,1)S(1)}, bf16[8,128,384]{2,1,0:T(8,128)(2,1)S(1)}, u32[]{:S(2)}, u32[]{:S(2)}) collective-permute-start(bf16[8,128,384]{2,1,0:T(8,128)(2,1)S(1)} %pad_maximum_fusion.5), channel_id=1, source_target_pairs={{0,12},{1,13},{2,14},{3,15},{4,8},{5,9},{6,10},{7,11},{8,4},{9,5},... | collective-permute-start | bytes 2359304 | tf_op jit(solution)/shard_map/ppermute | solution.py:57
  175.3 14.6 %collective-permute-start.20 = (bf16[8,128,384]{2,1,0:T(8,128)(2,1)S(1)}, bf16[8,128,384]{2,1,0:T(8,128)(2,1)S(1)}, u32[]{:S(2)}, u32[]{:S(2)}) collective-permute-start(bf16[8,128,384]{2,1,0:T(8,128)(2,1)S(1)} %pad_maximum_fusion.6), channel_id=1, source_target_pairs={{0,48},{1,49},{2,50},{3,51},{4,52},{5,53},{6,54},{7,55},{8,56},{9,... | collective-permute-start | bytes 2359304 | tf_op jit(solution)/shard_map/ppermute | solution.py:57
  236.0 7.9 %collective-permute-start.27 = (bf16[4,128,384]{2,1,0:T(8,128)(2,1)S(1)}, bf16[4,128,384]{2,1,0:T(8,128)(2,1)S(1)}, u32[]{:S(2)}, u32[]{:S(2)}) collective-permute-start(bf16[4,128,384]{2,1,0:T(8,128)(2,1)S(1)} %pad_maximum_fusion.15), channel_id=1, source_target_pairs={{0,4},{1,5},{2,6},{3,7},{4,0},{5,1},{6,2},{7,3},{8,12},{9,13},{10,... | collective-permute-start | bytes 1179656 | tf_op jit(solution)/shard_map/ppermute | solution.py:57
  240.6 7.9 %collective-permute-start.31 = (bf16[4,128,384]{2,1,0:T(8,128)(2,1)S(1)}, bf16[4,128,384]{2,1,0:T(8,128)(2,1)S(1)}, u32[]{:S(2)}, u32[]{:S(2)}) collective-permute-start(bf16[4,128,384]{2,1,0:T(8,128)(2,1)S(1)} %pad_maximum_fusion.16), channel_id=1, source_target_pairs={{0,16},{1,17},{2,18},{3,19},{4,20},{5,21},{6,22},{7,23},{8,24},{9,... | collective-permute-start | bytes 1179656 | tf_op jit(solution)/shard_map/ppermute | solution.py:57
  248.5 13.3 %collective-permute-start.32 = (bf16[8,128,384]{2,1,0:T(8,128)(2,1)S(1)}, bf16[8,128,384]{2,1,0:T(8,128)(2,1)S(1)}, u32[]{:S(2)}, u32[]{:S(2)}) collective-permute-start(bf16[8,128,384]{2,1,0:T(8,128)(2,1)S(1)} %pad_maximum_fusion.7), channel_id=1, source_target_pairs={{0,12},{1,13},{2,14},{3,15},{4,8},{5,9},{6,10},{7,11},{8,4},{9,5},... | collective-permute-start | bytes 2359304 | tf_op jit(solution)/shard_map/ppermute | solution.py:57
  248.7 14.4 %collective-permute-start.33 = (bf16[8,128,384]{2,1,0:T(8,128)(2,1)S(1)}, bf16[8,128,384]{2,1,0:T(8,128)(2,1)S(1)}, u32[]{:S(2)}, u32[]{:S(2)}) collective-permute-start(bf16[8,128,384]{2,1,0:T(8,128)(2,1)S(1)} %pad_maximum_fusion.8), channel_id=1, source_target_pairs={{0,48},{1,49},{2,50},{3,51},{4,52},{5,53},{6,54},{7,55},{8,56},{9,... | collective-permute-start | bytes 2359304 | tf_op jit(solution)/shard_map/ppermute | solution.py:57
  322.3 13.3 %collective-permute-start.41 = (bf16[8,128,384]{2,1,0:T(8,128)(2,1)S(1)}, bf16[8,128,384]{2,1,0:T(8,128)(2,1)S(1)}, u32[]{:S(2)}, u32[]{:S(2)}) collective-permute-start(bf16[8,128,384]{2,1,0:T(8,128)(2,1)S(1)} %bitcast.273), channel_id=1, source_target_pairs={{0,48},{1,49},{2,50},{3,51},{4,52},{5,53},{6,54},{7,55},{8,56},{9,... | collective-permute-start | bytes 2359304 | tf_op jit(solution)/shard_map/ppermute | solution.py:57
  325.6 14.0 %collective-permute-start.37 = (bf16[8,128,384]{2,1,0:T(8,128)(2,1)S(1)}, bf16[8,128,384]{2,1,0:T(8,128)(2,1)S(1)}, u32[]{:S(2)}, u32[]{:S(2)}) collective-permute-start(bf16[8,128,384]{2,1,0:T(8,128)(2,1)S(1)} %bitcast.271), channel_id=1, source_target_pairs={{0,12},{1,13},{2,14},{3,15},{4,8},{5,9},{6,10},{7,11},{8,4},{9,5},... | collective-permute-start | bytes 2359304 | tf_op jit(solution)/shard_map/ppermute | solution.py:57
  335.8 7.9 %collective-permute-start.42 = (bf16[4,128,384]{2,1,0:T(8,128)(2,1)S(1)}, bf16[4,128,384]{2,1,0:T(8,128)(2,1)S(1)}, u32[]{:S(2)}, u32[]{:S(2)}) collective-permute-start(bf16[4,128,384]{2,1,0:T(8,128)(2,1)S(1)} %slice.568), channel_id=1, source_target_pairs={{0,16},{1,17},{2,18},{3,19},{4,20},{5,21},{6,22},{7,23},{8,24},{9,... | collective-permute-start | bytes 1179656 | tf_op jit(solution)/shard_map/ppermute | solution.py:57
  339.8 7.9 %collective-permute-start.38 = (bf16[4,128,384]{2,1,0:T(8,128)(2,1)S(1)}, bf16[4,128,384]{2,1,0:T(8,128)(2,1)S(1)}, u32[]{:S(2)}, u32[]{:S(2)}) collective-permute-start(bf16[4,128,384]{2,1,0:T(8,128)(2,1)S(1)} %slice.562), channel_id=1, source_target_pairs={{0,4},{1,5},{2,6},{3,7},{4,0},{5,1},{6,2},{7,3},{8,12},{9,13},{10,... | collective-permute-start | bytes 1179656 | tf_op jit(solution)/shard_map/ppermute | solution.py:57
  355.7 7.5 %collective-permute-start.36 = (f32[384,128]{1,0:T(8,128)S(1)}, f32[384,128]{1,0:T(8,128)S(1)}, u32[]{:S(2)}, u32[]{:S(2)}) collective-permute-start(f32[384,128]{1,0:T(8,128)S(1)} %slice.440), channel_id=1, source_target_pairs={{0,64},{1,65},{2,66},{3,67},{4,68},{5,69},{6,70},{7,71},{8,72},{9,... | collective-permute-start | bytes 589832 | tf_op jit(solution)/shard_map/ppermute | solution.py:61
  406.8 13.3 %collective-permute-start.54 = (bf16[8,128,384]{2,1,0:T(8,128)(2,1)S(1)}, bf16[8,128,384]{2,1,0:T(8,128)(2,1)S(1)}, u32[]{:S(2)}, u32[]{:S(2)}) collective-permute-start(bf16[8,128,384]{2,1,0:T(8,128)(2,1)S(1)} %bitcast.274), channel_id=1, source_target_pairs={{0,48},{1,49},{2,50},{3,51},{4,52},{5,53},{6,54},{7,55},{8,56},{9,... | collective-permute-start | bytes 2359304 | tf_op jit(solution)/shard_map/ppermute | solution.py:57
  410.1 13.2 %collective-permute-start.50 = (bf16[8,128,384]{2,1,0:T(8,128)(2,1)S(1)}, bf16[8,128,384]{2,1,0:T(8,128)(2,1)S(1)}, u32[]{:S(2)}, u32[]{:S(2)}) collective-permute-start(bf16[8,128,384]{2,1,0:T(8,128)(2,1)S(1)} %bitcast.272), channel_id=1, source_target_pairs={{0,12},{1,13},{2,14},{3,15},{4,8},{5,9},{6,10},{7,11},{8,4},{9,5},... | collective-permute-start | bytes 2359304 | tf_op jit(solution)/shard_map/ppermute | solution.py:57
  420.3 7.9 %collective-permute-start.55 = (bf16[4,128,384]{2,1,0:T(8,128)(2,1)S(1)}, bf16[4,128,384]{2,1,0:T(8,128)(2,1)S(1)}, u32[]{:S(2)}, u32[]{:S(2)}) collective-permute-start(bf16[4,128,384]{2,1,0:T(8,128)(2,1)S(1)} %slice.581), channel_id=1, source_target_pairs={{0,16},{1,17},{2,18},{3,19},{4,20},{5,21},{6,22},{7,23},{8,24},{9,... | collective-permute-start | bytes 1179656 | tf_op jit(solution)/shard_map/ppermute | solution.py:57
  423.5 9.5 %collective-permute-start.51 = (bf16[4,128,384]{2,1,0:T(8,128)(2,1)S(1)}, bf16[4,128,384]{2,1,0:T(8,128)(2,1)S(1)}, u32[]{:S(2)}, u32[]{:S(2)}) collective-permute-start(bf16[4,128,384]{2,1,0:T(8,128)(2,1)S(1)} %slice.575), channel_id=1, source_target_pairs={{0,4},{1,5},{2,6},{3,7},{4,0},{5,1},{6,2},{7,3},{8,12},{9,13},{10,... | collective-permute-start | bytes 1179656 | tf_op jit(solution)/shard_map/ppermute | solution.py:57
  428.3 8.4 %collective-permute-start.56 = (bf16[2,128,384]{2,1,0:T(8,128)(2,1)S(1)}, bf16[2,128,384]{2,1,0:T(8,128)(2,1)S(1)}, u32[]{:S(2)}, u32[]{:S(2)}) collective-permute-start(bf16[2,128,384]{2,1,0:T(8,128)(2,1)S(1)} %slice.583), channel_id=1, source_target_pairs={{0,12},{1,13},{2,14},{3,15},{4,8},{5,9},{6,10},{7,11},{8,4},{9,5},... | collective-permute-start | bytes 589832 | tf_op jit(solution)/shard_map/ppermute | solution.py:57
  441.7 7.6 %collective-permute-start.49 = (f32[384,128]{1,0:T(8,128)S(1)}, f32[384,128]{1,0:T(8,128)S(1)}, u32[]{:S(2)}, u32[]{:S(2)}) collective-permute-start(f32[384,128]{1,0:T(8,128)S(1)} %slice.462), channel_id=1, source_target_pairs={{64,0},{65,1},{66,2},{67,3},{68,4},{69,5},{70,6},{71,7},{72,8},{73... | collective-permute-start | bytes 589832 | tf_op jit(solution)/shard_map/ppermute | solution.py:61
  476.5 41.6 %collective-permute-start.72 = (bf16[2,4,4,416,128]{4,3,2,1,0:T(8,128)(2,1)}, bf16[2,4,4,416,128]{4,3,2,1,0:T(8,128)(2,1)S(1)}, u32[]{:S(2)}, u32[]{:S(2)}) collective-permute-start(bf16[2,4,4,416,128]{4,3,2,1,0:T(8,128)(2,1)} %get-tuple-element.118), channel_id=1, source_target_pairs={{0,3},{1,2},{2,1},{3,0},{4,7},{5,6},{6,5},{7,4},{8,11},{9,10},{10,... | collective-permute-start | bytes 10223624 | tf_op jit(solution)/shard_map/ppermute | solution.py:57
  478.2 43.0 %collective-permute-start.60 = (bf16[2,4,4,432,128]{4,3,2,1,0:T(8,128)(2,1)}, bf16[2,4,4,432,128]{4,3,2,1,0:T(8,128)(2,1)S(1)}, u32[]{:S(2)}, u32[]{:S(2)}) collective-permute-start(bf16[2,4,4,432,128]{4,3,2,1,0:T(8,128)(2,1)} %get-tuple-element.114), channel_id=1, source_target_pairs={{0,48},{1,49},{2,50},{3,51},{4,52},{5,53},{6,54},{7,55},{8,56},{9,... | collective-permute-start | bytes 10616840 | tf_op jit(solution)/shard_map/ppermute | solution.py:57
  480.1 43.3 %collective-permute-start.66 = (bf16[2,4,4,432,128]{4,3,2,1,0:T(8,128)(2,1)}, bf16[2,4,4,432,128]{4,3,2,1,0:T(8,128)(2,1)S(1)}, u32[]{:S(2)}, u32[]{:S(2)}) collective-permute-start(bf16[2,4,4,432,128]{4,3,2,1,0:T(8,128)(2,1)} %get-tuple-element.116), channel_id=1, source_target_pairs={{0,12},{1,13},{2,14},{3,15},{4,8},{5,9},{6,10},{7,11},{8,4},{9,5},... | collective-permute-start | bytes 10616840 | tf_op jit(solution)/shard_map/ppermute | solution.py:57
  521.1 21.9 %collective-permute-start.73 = (bf16[4,4,416,128]{3,2,1,0:T(8,128)(2,1)S(1)}, bf16[4,4,416,128]{3,2,1,0:T(8,128)(2,1)S(1)}, u32[]{:S(2)}, u32[]{:S(2)}) collective-permute-start(bf16[4,4,416,128]{3,2,1,0:T(8,128)(2,1)S(1)} %get-tuple-element.150), channel_id=1, source_target_pairs={{0,1},{1,0},{2,3},{3,2},{4,5},{5,4},{6,7},{7,6},{8,9},{9,8},{10,11... | collective-permute-start | bytes 5111816 | tf_op jit(solution)/shard_map/ppermute | solution.py:57
  522.2 23.2 %collective-permute-start.61 = (bf16[4,4,432,128]{3,2,1,0:T(8,128)(2,1)S(1)}, bf16[4,4,432,128]{3,2,1,0:T(8,128)(2,1)S(1)}, u32[]{:S(2)}, u32[]{:S(2)}) collective-permute-start(bf16[4,4,432,128]{3,2,1,0:T(8,128)(2,1)S(1)} %get-tuple-element.146), channel_id=1, source_target_pairs={{0,16},{1,17},{2,18},{3,19},{4,20},{5,21},{6,22},{7,23},{8,24},{9,... | collective-permute-start | bytes 5308424 | tf_op jit(solution)/shard_map/ppermute | solution.py:57
  524.3 25.6 %collective-permute-start.67 = (bf16[4,4,432,128]{3,2,1,0:T(8,128)(2,1)S(1)}, bf16[4,4,432,128]{3,2,1,0:T(8,128)(2,1)S(1)}, u32[]{:S(2)}, u32[]{:S(2)}) collective-permute-start(bf16[4,4,432,128]{3,2,1,0:T(8,128)(2,1)S(1)} %get-tuple-element.148), channel_id=1, source_target_pairs={{0,4},{1,5},{2,6},{3,7},{4,0},{5,1},{6,2},{7,3},{8,12},{9,13},{10,... | collective-permute-start | bytes 5308424 | tf_op jit(solution)/shard_map/ppermute | solution.py:57
  543.5 14.0 %collective-permute-start.74 = (bf16[2,4,416,128]{3,2,1,0:T(8,128)(2,1)S(1)}, bf16[2,4,416,128]{3,2,1,0:T(8,128)(2,1)S(1)}, u32[]{:S(2)}, u32[]{:S(2)}) collective-permute-start(bf16[2,4,416,128]{3,2,1,0:T(8,128)(2,1)S(1)} %get-tuple-element.156), channel_id=1, source_target_pairs={{0,48},{1,49},{2,50},{3,51},{4,52},{5,53},{6,54},{7,55},{8,56},{9,... | collective-permute-start | bytes 2555912 | tf_op jit(solution)/shard_map/ppermute | solution.py:57
  546.8 14.6 %collective-permute-start.62 = (bf16[2,4,432,128]{3,2,1,0:T(8,128)(2,1)}, bf16[2,4,432,128]{3,2,1,0:T(8,128)(2,1)}, u32[]{:S(2)}, u32[]{:S(2)}) collective-permute-start(bf16[2,4,432,128]{3,2,1,0:T(8,128)(2,1)} %get-tuple-element.152), channel_id=1, source_target_pairs={{0,12},{1,13},{2,14},{3,15},{4,8},{5,9},{6,10},{7,11},{8,4},{9,5},... | collective-permute-start | bytes 2654216 | tf_op jit(solution)/shard_map/ppermute | solution.py:57
  551.3 20.2 %collective-permute-start.68 = (bf16[2,4,432,128]{3,2,1,0:T(8,128)(2,1)}, bf16[2,4,432,128]{3,2,1,0:T(8,128)(2,1)}, u32[]{:S(2)}, u32[]{:S(2)}) collective-permute-start(bf16[2,4,432,128]{3,2,1,0:T(8,128)(2,1)} %get-tuple-element.154), channel_id=1, source_target_pairs={{0,3},{1,2},{2,1},{3,0},{4,7},{5,6},{6,5},{7,4},{8,11},{9,10},{10,... | collective-permute-start | bytes 2654216 | tf_op jit(solution)/shard_map/ppermute | solution.py:57
  558.6 8.4 %collective-permute-start.75 = (bf16[4,416,128]{2,1,0:T(8,128)(2,1)}, bf16[4,416,128]{2,1,0:T(8,128)(2,1)}, u32[]{:S(2)}, u32[]{:S(2)}) collective-permute-start(bf16[4,416,128]{2,1,0:T(8,128)(2,1)} %get-tuple-element.170), channel_id=1, source_target_pairs={{0,16},{1,17},{2,18},{3,19},{4,20},{5,21},{6,22},{7,23},{8,24},{9,... | collective-permute-start | bytes 1277960 | tf_op jit(solution)/shard_map/ppermute | solution.py:57
  562.7 12.8 %collective-permute-start.63 = (bf16[4,432,128]{2,1,0:T(8,128)(2,1)S(1)}, bf16[4,432,128]{2,1,0:T(8,128)(2,1)S(1)}, u32[]{:S(2)}, u32[]{:S(2)}) collective-permute-start(bf16[4,432,128]{2,1,0:T(8,128)(2,1)S(1)} %get-tuple-element.166), channel_id=1, source_target_pairs={{0,4},{1,5},{2,6},{3,7},{4,0},{5,1},{6,2},{7,3},{8,12},{9,13},{10,... | collective-permute-start | bytes 1327112 | tf_op jit(solution)/shard_map/ppermute | solution.py:57
  568.2 7.2 %collective-permute-start.76 = (bf16[2,416,128]{2,1,0:T(8,128)(2,1)S(1)}, bf16[2,416,128]{2,1,0:T(8,128)(2,1)S(1)}, u32[]{:S(2)}, u32[]{:S(2)}) collective-permute-start(bf16[2,416,128]{2,1,0:T(8,128)(2,1)S(1)} %get-tuple-element.177), channel_id=1, source_target_pairs={{0,12},{1,13},{2,14},{3,15},{4,8},{5,9},{6,10},{7,11},{8,4},{9,5},... | collective-permute-start | bytes 638984 | tf_op jit(solution)/shard_map/ppermute | solution.py:57
  573.0 10.8 %collective-permute-start.69 = (bf16[4,432,128]{2,1,0:T(8,128)(2,1)S(1)}, bf16[4,432,128]{2,1,0:T(8,128)(2,1)S(1)}, u32[]{:S(2)}, u32[]{:S(2)}) collective-permute-start(bf16[4,432,128]{2,1,0:T(8,128)(2,1)S(1)} %get-tuple-element.168), channel_id=1, source_target_pairs={{0,1},{1,0},{2,3},{3,2},{4,5},{5,4},{6,7},{7,6},{8,9},{9,8},{10,11... | collective-permute-start | bytes 1327112 | tf_op jit(solution)/shard_map/ppermute | solution.py:57
  575.5 10.2 %collective-permute-start.77 = (bf16[416,128]{1,0:T(8,128)(2,1)S(1)}, bf16[416,128]{1,0:T(8,128)(2,1)S(1)}, u32[]{:S(2)}, u32[]{:S(2)}) collective-permute-start(bf16[416,128]{1,0:T(8,128)(2,1)S(1)} %fusion.34), channel_id=1, source_target_pairs={{0,4},{1,5},{2,6},{3,7},{4,0},{5,1},{6,2},{7,3},{8,12},{9,13},{10,... | collective-permute-start | bytes 319496 | tf_op jit(solution)/shard_map/ppermute | solution.py:57
  575.7 10.0 %collective-permute-start.64 = (bf16[2,432,128]{2,1,0:T(8,128)(2,1)S(1)}, bf16[2,432,128]{2,1,0:T(8,128)(2,1)S(1)}, u32[]{:S(2)}, u32[]{:S(2)}) collective-permute-start(bf16[2,432,128]{2,1,0:T(8,128)(2,1)S(1)} %get-tuple-element.173), channel_id=1, source_target_pairs={{0,3},{1,2},{2,1},{3,0},{4,7},{5,6},{6,5},{7,4},{8,11},{9,10},{10,... | collective-permute-start | bytes 663560 | tf_op jit(solution)/shard_map/ppermute | solution.py:57
  583.9 8.3 %collective-permute-start.70 = (bf16[2,432,128]{2,1,0:T(8,128)(2,1)S(1)}, bf16[2,432,128]{2,1,0:T(8,128)(2,1)S(1)}, u32[]{:S(2)}, u32[]{:S(2)}) collective-permute-start(bf16[2,432,128]{2,1,0:T(8,128)(2,1)S(1)} %get-tuple-element.175), channel_id=1, source_target_pairs={{0,48},{1,49},{2,50},{3,51},{4,52},{5,53},{6,54},{7,55},{8,56},{9,... | collective-permute-start | bytes 663560 | tf_op jit(solution)/shard_map/ppermute | solution.py:57
  (95 other events, 738.5 us)
Sparse Core Ops, SparseCore 0:
  16.2 143.0 all-gather.2

commit v6 on v5

--- a/solution.py
+++ b/solution.py
@@ -135,6 +135,7 @@
     block = jnp.concatenate([own, row])[None]
     for number in range(2):
         block = jnp.concatenate([block, swapped(block, along((0, 0), number))])
+    block, own = lax.optimization_barrier((block, own))
     at = slot_of(jnp.arange(4, dtype=jnp.int32) ^ y, phase)
     front = lax.dynamic_index_in_dim(block, at[0], 0, keepdims=False)
     rows = jnp.pad(block[:, ROWS][at], ((0, 12), (0, 0)))
@@ -146,7 +147,7 @@
                 axis = axes[part][leg]
                 got = swapped(blocks[part], along((axis, axis), number))
                 blocks[part] = jnp.concatenate([blocks[part], got])
-    return blocks
+    return blocks, own
 
 
 PART_ROWS = ((0, 432), (432, 864), (864, 1280))
@@ -271,52 +272,78 @@
     return jnp.concatenate([top, zero] if low else [zero, top], axis=0)
 
 
-def attend_kernel(qt_ref, kv_ref, bias_ref, mixed_ref, lse_ref, s_ref):
+SMALL = 64
+LANES = GRP * R
+
+
+def chunk_of(kv_ref, need_ref, i):
+    rows = [
+        kv_ref[pl.ds(pl.multiple_of(need_ref[CHUNK // SMALL * i + k] * SMALL, SMALL), SMALL), :]
+        for k in range(CHUNK // SMALL)
+    ]
+    return jnp.concatenate(rows, axis=0)
+
+
+def chunk_rows(i):
+    return pl.ds(pl.multiple_of(i * CHUNK, CHUNK), CHUNK)
+
+
+def attend_kernel(need_ref, qt_ref, kv_ref, bias_ref, mixed_ref, lse_ref, s_ref, c_ref):
     q = heads_wide(qt_ref, True)
-    peak = jnp.full((1, GRP * R), masked_fill, f32)
-    for i in range(KEYS // CHUNK):
-        rows = slice(CHUNK * i, CHUNK * i + CHUNK)
-        b = bias_ref[rows, :]
-        s = mm(kv_ref[rows, :], q) + jnp.concatenate([b, b, b], axis=1)
-        s_ref[rows, :] = s
-        peak = jnp.maximum(peak, jnp.max(s, axis=0, keepdims=True))
-    total = jnp.zeros((1, GRP * R), f32)
-    acc = jnp.zeros((128, GRP * R), f32)
-    for i in range(KEYS // CHUNK):
-        rows = slice(CHUNK * i, CHUNK * i + CHUNK)
-        p = jnp.exp(s_ref[rows, :] - peak)
+    count = need_ref[KEYS // SMALL]
+
+    def score(i, peak):
+        kv = chunk_of(kv_ref, need_ref, i)
+        c_ref[chunk_rows(i), :] = kv
+        b = bias_ref[chunk_rows(i), :]
+        s = mm(kv, q) + jnp.concatenate([b, b, b], axis=1)
+        s_ref[chunk_rows(i), :] = s
+        return jnp.maximum(peak, jnp.max(s, axis=0, keepdims=True))
+
+    peak = lax.fori_loop(0, count, score, jnp.full((1, LANES), masked_fill, f32))
+
+    def mix(i, state):
+        total, acc = state
+        p = jnp.exp(s_ref[chunk_rows(i), :] - peak)
         total = total + jnp.sum(p, axis=0, keepdims=True)
-        acc = acc + mm(kv_ref[rows, :].T, p.astype(bf16))
+        return total, acc + mm(c_ref[chunk_rows(i), :].T, p.astype(bf16))
+
+    total, acc = lax.fori_loop(
+        0, count, mix, (jnp.zeros((1, LANES), f32), jnp.zeros((128, LANES), f32))
+    )
     lse_ref[0] = peak + jnp.log(total)
     o = (acc[64:] / total).astype(bf16)
     for h in range(GRP):
         mixed_ref[64 * h : 64 * h + 64, :] = o[:, 128 * h : 128 * h + 128]
 
 
-def attend(qt, kv_all, bias):
+def attend(need, qt, kv_all, bias):
     return pl.pallas_call(
         attend_kernel,
         name="attend",
-        grid=(SIDE,),
-        in_specs=[
-            pl.BlockSpec((GRP * HD, R), lambda g: (g, 0)),
-            pl.BlockSpec((KEYS, 128), lambda g: (0, g)),
-            pl.BlockSpec((KEYS, R), lambda g: (0, 0)),
-        ],
-        out_specs=[
-            pl.BlockSpec((GRP * HD, R), lambda g: (g, 0)),
-            pl.BlockSpec((1, 1, GRP * R), lambda g: (g, 0, 0)),
-        ],
+        grid_spec=pltpu.PrefetchScalarGridSpec(
+            num_scalar_prefetch=1,
+            grid=(SIDE,),
+            in_specs=[
+                pl.BlockSpec((GRP * HD, R), lambda g, n: (g, 0)),
+                pl.BlockSpec((KEYS, 128), lambda g, n: (0, g)),
+                pl.BlockSpec((KEYS, R), lambda g, n: (0, 0)),
+            ],
+            out_specs=[
+                pl.BlockSpec((GRP * HD, R), lambda g, n: (g, 0)),
+                pl.BlockSpec((1, 1, LANES), lambda g, n: (g, 0, 0)),
+            ],
+            scratch_shapes=[pltpu.VMEM((KEYS, LANES), f32), pltpu.VMEM((KEYS, 128), bf16)],
+        ),
         out_shape=[
             jax.ShapeDtypeStruct((QSIDE, R), bf16),
-            jax.ShapeDtypeStruct((SIDE, 1, GRP * R), f32),
+            jax.ShapeDtypeStruct((SIDE, 1, LANES), f32),
         ],
-        scratch_shapes=[pltpu.VMEM((KEYS, GRP * R), f32)],
         compiler_params=pltpu.CompilerParams(vmem_limit_bytes=48 << 20),
         cost_estimate=pl.CostEstimate(
-            flops=4_000_000_000, bytes_accessed=8_000_000, transcendentals=7_900_000
-        ),
-    )(qt, kv_all, bias)
+            flops=2_400_000_000, bytes_accessed=6_000_000, transcendentals=4_700_000
+        ),
+    )(need, qt, kv_all, bias)
 
 
 def out_weight(refs, c):
@@ -521,7 +548,7 @@
 
 
 def attend_back_kernel(
-    qt_ref, kv_ref, bias_ref, dot_ref, mixed_ref, lse_ref, dkv_ref, dqt_ref
+    need_ref, qt_ref, kv_ref, bias_ref, dot_ref, mixed_ref, lse_ref, dkv_ref, dqt_ref
 ):
     q = heads_wide(qt_ref, True)
     d_o = heads_wide(dot_ref, False)
@@ -530,44 +557,52 @@
     d_o = d_o.astype(bf16)
     lse = lse_ref[0]
     both = jnp.concatenate([q, d_o], axis=1)
-    acc = jnp.zeros((128, GRP * R), f32)
-    for i in range(KEYS // CHUNK):
-        rows = slice(CHUNK * i, CHUNK * i + CHUNK)
-        b = bias_ref[rows, :]
-        kv = kv_ref[rows, :]
+    dkv_ref[...] = jnp.zeros_like(dkv_ref)
+
+    def fold(i, acc):
+        kv = chunk_of(kv_ref, need_ref, i)
+        b = bias_ref[chunk_rows(i), :]
         p = jnp.exp(mm(kv, q) + jnp.concatenate([b, b, b], axis=1) - lse)
         ds = (p * (mm(kv, d_o) - delta)).astype(bf16)
-        dkv_ref[rows, :] = mm_nt(jnp.concatenate([ds, p.astype(bf16)], axis=1), both).astype(bf16)
-        acc = acc + mm(kv.T, ds)
+        part = mm_nt(jnp.concatenate([ds, p.astype(bf16)], axis=1), both).astype(bf16)
+        for k in range(CHUNK // SMALL):
+            at = pl.multiple_of(need_ref[CHUNK // SMALL * i + k] * SMALL, SMALL)
+            dkv_ref[pl.ds(at, SMALL), :] = part[SMALL * k : SMALL * k + SMALL]
+        return acc + mm(kv.T, ds)
+
+    acc = lax.fori_loop(0, need_ref[KEYS // SMALL], fold, jnp.zeros((128, LANES), f32))
     acc = acc[:64] * 0.125
     for h in range(GRP):
         dqt_ref[64 * h : 64 * h + 64, :] = acc[:, 128 * h : 128 * h + 128]
 
 
-def attend_back(qt, kv_all, bias, d_mixed, mixed, lse):
-    heads = pl.BlockSpec((GRP * HD, R), lambda g: (g, 0))
+def attend_back(need, qt, kv_all, bias, d_mixed, mixed, lse):
+    heads = pl.BlockSpec((GRP * HD, R), lambda g, n: (g, 0))
     return pl.pallas_call(
         attend_back_kernel,
         name="attend_back",
-        grid=(SIDE,),
-        in_specs=[
-            heads,
-            pl.BlockSpec((KEYS, 128), lambda g: (0, g)),
-            pl.BlockSpec((KEYS, R), lambda g: (0, 0)),
-            heads,
-            heads,
-            pl.BlockSpec((1, 1, GRP * R), lambda g: (g, 0, 0)),
-        ],
-        out_specs=[pl.BlockSpec((KEYS, 128), lambda g: (0, g)), heads],
+        grid_spec=pltpu.PrefetchScalarGridSpec(
+            num_scalar_prefetch=1,
+            grid=(SIDE,),
+            in_specs=[
+                heads,
+                pl.BlockSpec((KEYS, 128), lambda g, n: (0, g)),
+                pl.BlockSpec((KEYS, R), lambda g, n: (0, 0)),
+                heads,
+                heads,
+                pl.BlockSpec((1, 1, LANES), lambda g, n: (g, 0, 0)),
+            ],
+            out_specs=[pl.BlockSpec((KEYS, 128), lambda g, n: (0, g)), heads],
+        ),
         out_shape=[
             jax.ShapeDtypeStruct((KEYS, SIDE * 128), bf16),
             jax.ShapeDtypeStruct((QSIDE, R), f32),
         ],
         compiler_params=pltpu.CompilerParams(vmem_limit_bytes=48 << 20),
         cost_estimate=pl.CostEstimate(
-            flops=10_000_000_000, bytes_accessed=14_000_000, transcendentals=7_900_000
-        ),
-    )(qt, kv_all, bias, d_mixed, mixed, lse)
+            flops=6_000_000_000, bytes_accessed=10_000_000, transcendentals=4_700_000
+        ),
+    )(need, qt, kv_all, bias, d_mixed, mixed, lse)
 
 
 def project_back_kernel(
@@ -817,6 +852,7 @@
     zh = z // 2
 
     own = shard_blocks(params[0], rank)
+    front, own = gather_front(own, norm_gains[0], y, phase)
     gathered = lax.all_gather(own, ("ctx", "fsdp"), axis=0)
 
     seg_row = segment_ids[0]
@@ -831,9 +867,19 @@
     )
     start_q = jnp.sum((seg_row[:, None] < seg_q[None, :]).astype(jnp.int32), axis=0)
     pairs_k = block_pair[key_order(y, x, zh, phase)]
-    place_k = (
-        jnp.stack([pairs_k, 63 - pairs_k], axis=1)[:, :, None] * 64 + within[None, None, :]
-    ).reshape(KEYS)
+    spot_k = jnp.stack([pairs_k, 63 - pairs_k], axis=1).reshape(64)
+    seen_by = lambda at, spot: (spot_k <= spot) & (spot_k * 64 + 63 >= start_q[at])
+    seen = seen_by(0, pair) | seen_by(64, 63 - pair)
+    seen_count = jnp.sum(seen.astype(jnp.int32))
+    before = jnp.arange(64)[:, None] > jnp.arange(64)[None, :]
+    rank_seen = jnp.sum((before & seen[None, :]).astype(jnp.int32), axis=1)
+    rank_k = jnp.where(seen, rank_seen, seen_count + jnp.arange(64) - rank_seen)
+    chosen = rank_k[None, :] == jnp.arange(64)[:, None]
+    order_k = jnp.sum(jnp.where(chosen, jnp.arange(64)[None, :], 0), axis=1)
+    spot_k = jnp.sum(jnp.where(chosen & seen[None, :], spot_k[None, :], 0), axis=1)
+    spot_k = jnp.where(jnp.arange(64) < seen_count, spot_k, 1 << 16)
+    need = jnp.concatenate([order_k, ((seen_count + 7) // 8)[None]]).astype(jnp.int32)
+    place_k = (spot_k[:, None] * 64 + within[None, :]).reshape(KEYS)
     bias = jnp.where(
         (place_k[:, None] <= place_q[None, :]) & (place_k[:, None] >= start_q[None, :]),
         0.0,
@@ -848,7 +894,6 @@
     target = jnp.where(spread % 32 < 30, (spread // 32) * 30 + spread % 32, -1)
     pad = (jnp.arange(D, dtype=jnp.int32)[:, None] == target[None, :]).astype(bf16)
 
-    front = gather_front(own, norm_gains[0], y, phase)
     four = jnp.arange(4, dtype=jnp.int32)
     slots_y, slots_x, slots_z = (slot_of(four ^ at_axis, phase) for at_axis in (y, x, z))
     idx = jnp.concatenate(
@@ -871,7 +916,7 @@
         kv_side = jnp.where(active, kv[:, :384], over(kv[:, 384:], tick))
         qt_side = jnp.where(active, qt[:QSIDE], over(qt[QSIDE:], tick))
         kv_all = gather_keys(kv_side)
-        mixed_side, lse = attend(qt_side, kv_all, bias)
+        mixed_side, lse = attend(need, qt_side, kv_all, bias)
         kept.append((qt_side, kv_all, mixed_side, lse))
         far = over(mixed_side[: D - QSIDE], 1 - tick)
         whole = jnp.concatenate([mixed_side, far])
@@ -890,7 +935,7 @@
             cot, gate, up, hidden, gain_two, pad, gathered
         )
         d_side = jnp.where(active, d_mixed[:QSIDE], over(d_mixed[QSIDE:], layer))
-        d_kv_all, dq_side = attend_back(qt_side, kv_all, bias, d_side, mixed_side, lse)
+        d_kv_all, dq_side = attend_back(need, qt_side, kv_all, bias, d_side, mixed_side, lse)
         dq_new = jnp.concatenate([dq_side, over(dq_side[: D - QSIDE], tick)])
         dkv_side = scatter_keys(d_kv_all)
         dkv_new = jnp.concatenate([dkv_side, over(dkv_side[:, :256], tick)], axis=1)

time: 616 us -> 614 us (level)
  waiting for transfers between devices: 263 us -> 237 us
  starting transfers between devices: 126 us -> 149 us
  other arithmetic: 39.6 us -> 52.9 us
  Pallas kernels: 127 us -> 114 us
    ppermute x64, waiting for transfers between devices: 247 us -> 221 us  [swapped(): return lax.ppermute(block, ALL, pairs)]
    ppermute x64, starting transfers between devices: 105 us -> 129 us  [swapped(): return lax.ppermute(block, ALL, pairs)]
    pallas_call x4, Pallas kernels: 50.1 us -> 37.8 us  [the longest x2 21.9 us: attend_back(): pl.pallas_call(attend_back_kernel, name='attend_back', grid_spec=pltpu.Pr...]
    unnamed x142 -> x124, local copies, waits for them, and re-layouts: 20.8 us -> 19 us
  transfers between devices with their start and end apart: 79 -> 79, of which waited for: 59 -> 56; matrix products, arithmetic and copies ran while one was open for 8% -> 10% of each run, Pallas kernels for 2% -> 2%
where the time goes in v6:
time: 614 us; the launch traced here: 604 us
  waiting for transfers between devices  237 us (39%)
  starting transfers between devices  149 us (24%)
  Pallas kernels  114 us (19%)
  other arithmetic  52.9 us (9%)
  local copies, waits for them, and re-layouts  32.3 us (5%)
  between operations  18.3 us (3%)
    ppermute x64, waiting for transfers between devices, swapped(): return lax.ppermute(block, ALL, pairs)  221 us
    ppermute x64, starting transfers between devices, swapped(): return lax.ppermute(block, ALL, pairs)  129 us
    pallas_call x2, Pallas kernels, feed_back(): pl.pallas_call(feed_back_kernel, name='feed_back', grid=(4,), in_specs=[w...  29.6 us
    pallas_call x2, Pallas kernels, attend_back(): pl.pallas_call(attend_back_kernel, name='attend_back', grid_spec=pltpu.Pr...  21.9 us
    pallas_call x2, Pallas kernels, feed(): pl.pallas_call(feed_kernel, name='feed', grid=(4,), in_specs=[whole(D, R)...  21.6 us
    ppermute x14, starting transfers between devices, over(): return lax.ppermute(block, 'phase', [(source, 1 - source)])  20.3 us
    unnamed x124, local copies, waits for them, and re-layouts  19 us
    ppermute x14, waiting for transfers between devices, over(): return lax.ppermute(block, 'phase', [(source, 1 - source)])  16.1 us
  transfers between devices with their start and end apart: 79, of which 56 were waited for; matrix products, arithmetic and copies ran while one was open for 10% of the time, Pallas kernels for 2%

profile of v6, /device:TPU:0, one launch (start us, length us, event | category | flops | bytes accessed | tf_op | source)
XLA Modules:
  0.0 603.8 jit_solution(17586868678995994829)
XLA Ops:
  7.2 8.0 %conditional.2 = (bf16[1280,128]{1,0:T(8,128)(2,1)S(1)}) conditional(s32[]{:T(128)} %clamp.4, bf16[1,153600]{1,0:T(2,128)(2,1)} %param.26, bf16[1,153600]{1,0:T(2,128)(2,1)} %param.26, bf16[1,153600]{1,0:T(2,128)(2,1)} %param.26), branch_computations={%region_4.5_spmd, %region_5.6_spmd, %region_6.7_spmd} | conditional | bytes 3780622 | solution.py:828
  7.3 7.3 %reduce.1 = bf16[153600]{0:T(1024)(128)(2,1)S(1)} reduce(bf16[1,153600]{1,0:T(2,128)(2,1)} %param, bf16[]{:T(256)} %constant.202), dimensions={0}, to_apply=%param.reduce_sub_computation | reduce | bytes 614402 | tf_op jit(solution)/shard_map/shard_map
  16.6 6.0 collective-permute-done
  25.6 9.0 %collective-permute-done.1 = bf16[2,1296,128]{2,1,0:T(8,128)(2,1)S(1)} collective-permute-done((bf16[2,1296,128]{2,1,0:T(8,128)(2,1)S(1)}, bf16[2,1296,128]{2,1,0:T(8,128)(2,1)S(1)}, u32[]{:S(2)}, u32[]{:S(2)}) %collective-permute-start.1) | collective-permute-done | bytes 663584 | tf_op jit(solution)/shard_map/ppermute | solution.py:57
  53.0 4.4 collective-permute-start.3
  61.4 4.1 collective-permute-done.3
  66.2 6.1 %collective-permute-done.8 = bf16[4,640,128]{2,1,0:T(8,128)(2,1)S(1)} collective-permute-done((bf16[4,640,128]{2,1,0:T(8,128)(2,1)S(1)}, bf16[4,640,128]{2,1,0:T(8,128)(2,1)S(1)}, u32[]{:S(2)}, u32[]{:S(2)}) %collective-permute-start.8) | collective-permute-done | bytes 655392 | tf_op jit(solution)/shard_map/ppermute | solution.py:57
  73.6 7.8 %collective-permute-start.9 = (bf16[8,640,128]{2,1,0:T(8,128)(2,1)}, bf16[8,640,128]{2,1,0:T(8,128)(2,1)}, u32[]{:S(2)}, u32[]{:S(2)}) collective-permute-start(bf16[8,640,128]{2,1,0:T(8,128)(2,1)} %pad_maximum_fusion.4), channel_id=1, source_target_pairs={{0,3},{1,2},{2,1},{3,0},{4,7},{5,6},{6,5},{7,4},{8,11},{9,10},{10,... | collective-permute-start | bytes 3932168 | tf_op jit(solution)/shard_map/ppermute | solution.py:57
  81.3 9.5 %collective-permute-done.4 = bf16[4,656,128]{2,1,0:T(8,128)(2,1)S(1)} collective-permute-done((bf16[4,656,128]{2,1,0:T(8,128)(2,1)S(1)}, bf16[4,656,128]{2,1,0:T(8,128)(2,1)S(1)}, u32[]{:S(2)}, u32[]{:S(2)}) %collective-permute-start.4) | collective-permute-done | bytes 671776 | tf_op jit(solution)/shard_map/ppermute | solution.py:57
  104.5 14.4 %collective-permute-done.5 = bf16[8,656,128]{2,1,0:T(8,128)(2,1)} collective-permute-done((bf16[8,656,128]{2,1,0:T(8,128)(2,1)}, bf16[8,656,128]{2,1,0:T(8,128)(2,1)}, u32[]{:S(2)}, u32[]{:S(2)}) %collective-permute-start.5) | collective-permute-done | bytes 1343520 | tf_op jit(solution)/shard_map/ppermute | solution.py:57
  130.4 6.4 %collective-permute-done.15 = bf16[128,384]{1,0:T(8,128)(2,1)S(1)} collective-permute-done((bf16[128,384]{1,0:T(8,128)(2,1)S(1)}, bf16[128,384]{1,0:T(8,128)(2,1)S(1)}, u32[]{:S(2)}, u32[]{:S(2)}) %collective-permute-start.15) | collective-permute-done | bytes 98336 | tf_op jit(solution)/shard_map/ppermute | solution.py:57
  136.8 10.8 %collective-permute-start.13 = (bf16[2,128,384]{2,1,0:T(8,128)(2,1)S(1)}, bf16[2,128,384]{2,1,0:T(8,128)(2,1)S(1)}, u32[]{:S(2)}, u32[]{:S(2)}) collective-permute-start(bf16[2,128,384]{2,1,0:T(8,128)(2,1)S(1)} %pad_maximum_fusion.20), channel_id=1, source_target_pairs={{0,48},{1,49},{2,50},{3,51},{4,52},{5,53},{6,54},{7,55},{8,56},{9,... | collective-permute-start | bytes 589832 | tf_op jit(solution)/shard_map/ppermute | solution.py:57
  147.8 8.2 %collective-permute-done.13 = bf16[2,128,384]{2,1,0:T(8,128)(2,1)S(1)} collective-permute-done((bf16[2,128,384]{2,1,0:T(8,128)(2,1)S(1)}, bf16[2,128,384]{2,1,0:T(8,128)(2,1)S(1)}, u32[]{:S(2)}, u32[]{:S(2)}) %collective-permute-start.13) | collective-permute-done | bytes 196640 | tf_op jit(solution)/shard_map/ppermute | solution.py:57
  161.1 9.4 %collective-permute-done.14 = bf16[4,128,384]{2,1,0:T(8,128)(2,1)} collective-permute-done((bf16[4,128,384]{2,1,0:T(8,128)(2,1)}, bf16[4,128,384]{2,1,0:T(8,128)(2,1)}, u32[]{:S(2)}, u32[]{:S(2)}) %collective-permute-start.14) | collective-permute-done | bytes 393248 | tf_op jit(solution)/shard_map/ppermute | solution.py:57
  192.3 7.9 %attend.2 = (bf16[576,128]{1,0:T(8,128)(2,1)S(1)}, f32[3,1,384]{2,1,0:T(1,128)S(1)}) custom-call(s32[65]{0:T(128)S(1)} %pad_add_fusion.2.need_ref, bf16[576,128]{1,0:T(8,128)(2,1)S(1)} %slice_select_fusion.3.qt_ref, bf16[4096,384]{1,0:T(8,128)(2,1)S(1)} %bitcast.202, f32[4096,128]{1,0:T(8,128)S(1)} %copy-done.5), custom_call_target="tpu_custom_call" | custom-call | flops 2400000000 | bytes 6000000 | tf_op jit(solution)/shard_map/attend/pallas_call | solution.py:321
  203.6 11.6 %feed.2 = (bf16[128,960]{1,0:T(8,128)(2,1)S(1)}, f32[128,960]{1,0:T(8,128)}, bf16[1024,128]{1,0:T(8,128)(2,1)}, f32[128,2560]{1,0:T(8,128)}, f32[128,2560]{1,0:T(8,128)}, /*index=5*/bf16[2560,128]{1,0:T(8,128)(2,1)}) custom-call(bf16[960,128]{1,0:T(8,128)(2,1)S(1)} %constant_dynamic-update-slice_fusion.10.mixed_ref, bf16[128,960]{1,0:T(8,128)(2,1)S(1)} %bitcast.201, ...), custom_call_target="tpu_custom_call" | custom-call | flops 2200000000 | bytes 22000000 | tf_op jit(solution)/shard_map/feed/pallas_call | solution.py:427
  246.2 3.3 collective-permute-done.31
  249.6 3.4 collective-permute-start.32
  253.1 3.3 collective-permute-start.33
  259.6 3.4 collective-permute-done.32
  263.0 3.3 collective-permute-done.33
  266.9 7.9 %attend.3 = (bf16[576,128]{1,0:T(8,128)(2,1)S(1)}, f32[3,1,384]{2,1,0:T(1,128)S(1)}) custom-call(s32[65]{0:T(128)S(1)} %pad_add_fusion.2.need_ref, bf16[576,128]{1,0:T(8,128)(2,1)S(1)} %slice_select_fusion.2.qt_ref, bf16[4096,384]{1,0:T(8,128)(2,1)S(1)} %bitcast.204, f32[4096,128]{1,0:T(8,128)S(1)} %copy-done.6), custom_call_target="tpu_custom_call" | custom-call | flops 2400000000 | bytes 6000000 | tf_op jit(solution)/shard_map/attend/pallas_call | solution.py:321
  277.1 10.0 %feed.3 = (bf16[128,960]{1,0:T(8,128)(2,1)S(1)}, f32[128,960]{1,0:T(8,128)S(1)}, bf16[1024,128]{1,0:T(8,128)(2,1)S(1)}, f32[128,2560]{1,0:T(8,128)S(1)}, f32[128...) custom-call(bf16[960,128]{1,0:T(8,128)(2,1)S(1)} %maximum_select_fusion.2.mixed_ref, ...), custom_call_target="tpu_custom_call" | custom-call | flops 2200000000 | bytes 22000000 | tf_op jit(solution)/shard_map/feed/pallas_call | solution.py:427
  288.9 15.3 %feed_back.2 = (bf16[128,2560]{1,0:T(8,128)(2,1)}, bf16[128,2560]{1,0:T(8,128)(2,1)}, f32[128,960]{1,0:T(8,128)S(1)}, bf16[128,1024]{1,0:T(8,128)(2,1)}, f32[1,9...) custom-call(f32[128,960]{1,0:T(8,128)S(1)} %bitcast.199, ...), custom_call_target="tpu_custom_call" | custom-call | flops 2200000000 | bytes 22000000 | tf_op jit(solution)/shard_map/feed_back/pallas_call | solution.py:518
  307.8 10.9 %attend_back.2 = (bf16[4096,384]{1,0:T(8,128)(2,1)S(1)}, f32[576,128]{1,0:T(8,128)S(1)}) custom-call(s32[65]{0:T(128)S(1)} %pad_add_fusion.2.need_ref, bf16[576,128]{1,0:T(8,128)(2,1)S(1)} %slice_select_fusion.2.qt_ref, bf16[4096,384]{1,0:T(8,128)(2,1)} %bitcast.205, f32[4096,128]{1,0:T(8,128)S(1)} %copy-done.7, f32[576,128]{1,0:T(8,128)S(1)} %slice_select_fusion.1.dot_ref, ...), custom_call_target="tpu_custom_call" | custom-call | flops 6000000000 | bytes 10000000 | tf_op jit(solution)/shard_map/attend_back/pallas_call | solution.py:581
  319.1 3.3 collective-permute-start.41
  325.5 6.8 %collective-permute-done.41 = bf16[8,128,384]{2,1,0:T(8,128)(2,1)S(1)} collective-permute-done((bf16[8,128,384]{2,1,0:T(8,128)(2,1)S(1)}, bf16[8,128,384]{2,1,0:T(8,128)(2,1)S(1)}, u32[]{:S(2)}, u32[]{:S(2)}) %collective-permute-start.41) | collective-permute-done | bytes 786464 | tf_op jit(solution)/shard_map/ppermute | solution.py:57
  336.6 4.4 collective-permute-start.38
  344.1 3.9 collective-permute-done.38
  350.9 4.2 collective-permute-done.39
  356.5 6.8 %collective-permute-start.45 = (bf16[128,384]{1,0:T(8,128)(2,1)S(1)}, bf16[128,384]{1,0:T(8,128)(2,1)S(1)}, u32[]{:S(2)}, u32[]{:S(2)}) collective-permute-start(bf16[128,384]{1,0:T(8,128)(2,1)S(1)} %fusion.35), channel_id=1, source_target_pairs={{0,2},{1,3},{2,0},{3,1},{4,6},{5,7},{6,4},{7,5},{8,10},{9,11},{10,... | collective-permute-start | bytes 294920 | tf_op jit(solution)/shard_map/ppermute | solution.py:57
  368.2 4.2 project_back.2
  376.0 14.4 %feed_back.3 = (bf16[128,2560]{1,0:T(8,128)(2,1)S(1)}, bf16[128,2560]{1,0:T(8,128)(2,1)S(1)}, f32[128,960]{1,0:T(8,128)S(1)}, bf16[128,1024]{1,0:T(8,128)(2,1)S(...) custom-call(f32[128,960]{1,0:T(8,128)S(1)} %convert_select_fusion.c_ref, ...), custom_call_target="tpu_custom_call" | custom-call | flops 2200000000 | bytes 22000000 | tf_op jit(solution)/shard_map/feed_back/pallas_call | solution.py:518
  393.7 11.0 %attend_back.3 = (bf16[4096,384]{1,0:T(8,128)(2,1)S(1)}, f32[576,128]{1,0:T(8,128)S(1)}) custom-call(s32[65]{0:T(128)S(1)} %pad_add_fusion.2.need_ref, bf16[576,128]{1,0:T(8,128)(2,1)S(1)} %copy-done.16, bf16[4096,384]{1,0:T(8,128)(2,1)} %bitcast.203, f32[4096,128]{1,0:T(8,128)S(1)} %copy-done.7, f32[576,128]{1,0:T(8,128)S(1)} %slice_select_fusion.dot_ref, ...), custom_call_target="tpu_custom_call" | custom-call | flops 6000000000 | bytes 10000000 | tf_op jit(solution)/shard_map/attend_back/pallas_call | solution.py:581
  407.4 10.9 %collective-permute-done.54 = bf16[8,128,384]{2,1,0:T(8,128)(2,1)S(1)} collective-permute-done((bf16[8,128,384]{2,1,0:T(8,128)(2,1)S(1)}, bf16[8,128,384]{2,1,0:T(8,128)(2,1)S(1)}, u32[]{:S(2)}, u32[]{:S(2)}) %collective-permute-start.54) | collective-permute-done | bytes 786464 | tf_op jit(solution)/shard_map/ppermute | solution.py:57
  421.5 5.1 collective-permute-done.55
  430.2 3.5 collective-permute-done.56
  439.7 4.4 collective-permute-start.58
  450.1 3.5 project_back.3
  459.6 14.3 %outer.1 = (bf16[2,4,4,432,128]{4,3,2,1,0:T(8,128)(2,1)}, bf16[2,4,4,432,128]{4,3,2,1,0:T(8,128)(2,1)}, bf16[2,4,4,416,128]{4,3,2,1,0:T(8,128)(2,1)}, bf16[2,4,4...) custom-call(s32[12]{0:T(128)S(1)} %pad_add_fusion.5.slot_ref, ...), custom_call_target="tpu_custom_call" | custom-call | flops 2600000000 | bytes 24000000 | tf_op jit(solution)/shard_map/outer/pallas_call | solution.py:788
  476.9 5.2 collective-permute-start.66
  482.0 33.4 %collective-permute-done.72 = bf16[2,4,4,416,128]{4,3,2,1,0:T(8,128)(2,1)S(1)} collective-permute-done((bf16[2,4,4,416,128]{4,3,2,1,0:T(8,128)(2,1)}, bf16[2,4,4,416,128]{4,3,2,1,0:T(8,128)(2,1)S(1)}, u32[]{:S(2)}, u32[]{:S(2)}) %collective-permute-start.72) | collective-permute-done | bytes 3407904 | tf_op jit(solution)/shard_map/ppermute | solution.py:57
  523.6 16.8 %collective-permute-done.73 = bf16[4,4,416,128]{3,2,1,0:T(8,128)(2,1)S(1)} collective-permute-done((bf16[4,4,416,128]{3,2,1,0:T(8,128)(2,1)S(1)}, bf16[4,4,416,128]{3,2,1,0:T(8,128)(2,1)S(1)}, u32[]{:S(2)}, u32[]{:S(2)}) %collective-permute-start.73) | collective-permute-done | bytes 1703968 | tf_op jit(solution)/shard_map/ppermute | solution.py:57
  546.1 3.5 collective-permute-start.62
  565.7 3.5 collective-permute-start.76
  575.7 5.1 collective-permute-done.69
  586.0 3.3 collective-permute-done.70
  589.5 4.7 collective-permute-done.71
  (430 shorter events, 226.8 us)
Async XLA Ops:
  7.2 196.4 %all-gather.3.cloned.1.call-start = ((), (), s32[]{:S(2)}) async-start(), calls=%async_computation | async-start | bytes 21299200 | tf_op jit(solution)/shard_map/all_gather | solution.py:856
  22.7 12.0 %collective-permute-start.1 = (bf16[2,1296,128]{2,1,0:T(8,128)(2,1)S(1)}, bf16[2,1296,128]{2,1,0:T(8,128)(2,1)S(1)}, u32[]{:S(2)}, u32[]{:S(2)}) collective-permute-start(bf16[2,1296,128]{2,1,0:T(8,128)(2,1)S(1)} %pad_maximum_fusion.10), channel_id=1, source_target_pairs={{0,48},{1,49},{2,50},{3,51},{4,52},{5,53},{6,54},{7,55},{8,56},{9,... | collective-permute-start | bytes 1990664 | tf_op jit(solution)/shard_map/ppermute | solution.py:57
  50.8 9.8 %collective-permute-start.7 = (bf16[2,640,128]{2,1,0:T(8,128)(2,1)S(1)}, bf16[2,640,128]{2,1,0:T(8,128)(2,1)S(1)}, u32[]{:S(2)}, u32[]{:S(2)}) collective-permute-start(bf16[2,640,128]{2,1,0:T(8,128)(2,1)S(1)} %pad_maximum_fusion.18), channel_id=1, source_target_pairs={{0,12},{1,13},{2,14},{3,15},{4,8},{5,9},{6,10},{7,11},{8,4},{9,5},... | collective-permute-start | bytes 983048 | tf_op jit(solution)/shard_map/ppermute | solution.py:57
  53.0 12.4 %collective-permute-start.3 = (bf16[2,656,128]{2,1,0:T(8,128)(2,1)S(1)}, bf16[2,656,128]{2,1,0:T(8,128)(2,1)S(1)}, u32[]{:S(2)}, u32[]{:S(2)}) collective-permute-start(bf16[2,656,128]{2,1,0:T(8,128)(2,1)S(1)} %pad_maximum_fusion.17), channel_id=1, source_target_pairs={{0,3},{1,2},{2,1},{3,0},{4,7},{5,6},{6,5},{7,4},{8,11},{9,10},{10,... | collective-permute-start | bytes 1007624 | tf_op jit(solution)/shard_map/ppermute | solution.py:57
  60.7 11.6 %collective-permute-start.8 = (bf16[4,640,128]{2,1,0:T(8,128)(2,1)S(1)}, bf16[4,640,128]{2,1,0:T(8,128)(2,1)S(1)}, u32[]{:S(2)}, u32[]{:S(2)}) collective-permute-start(bf16[4,640,128]{2,1,0:T(8,128)(2,1)S(1)} %pad_maximum_fusion.11), channel_id=1, source_target_pairs={{0,1},{1,0},{2,3},{3,2},{4,5},{5,4},{6,7},{7,6},{8,9},{9,8},{10,11... | collective-permute-start | bytes 1966088 | tf_op jit(solution)/shard_map/ppermute | solution.py:57
  65.6 25.3 %collective-permute-start.4 = (bf16[4,656,128]{2,1,0:T(8,128)(2,1)S(1)}, bf16[4,656,128]{2,1,0:T(8,128)(2,1)S(1)}, u32[]{:S(2)}, u32[]{:S(2)}) collective-permute-start(bf16[4,656,128]{2,1,0:T(8,128)(2,1)S(1)} %pad_maximum_fusion.9), channel_id=1, source_target_pairs={{0,4},{1,5},{2,6},{3,7},{4,0},{5,1},{6,2},{7,3},{8,12},{9,13},{10,... | collective-permute-start | bytes 2015240 | tf_op jit(solution)/shard_map/ppermute | solution.py:57
  73.6 28.4 %collective-permute-start.9 = (bf16[8,640,128]{2,1,0:T(8,128)(2,1)}, bf16[8,640,128]{2,1,0:T(8,128)(2,1)}, u32[]{:S(2)}, u32[]{:S(2)}) collective-permute-start(bf16[8,640,128]{2,1,0:T(8,128)(2,1)} %pad_maximum_fusion.4), channel_id=1, source_target_pairs={{0,3},{1,2},{2,1},{3,0},{4,7},{5,6},{6,5},{7,4},{8,11},{9,10},{10,... | collective-permute-start | bytes 3932168 | tf_op jit(solution)/shard_map/ppermute | solution.py:57
  92.1 26.7 %collective-permute-start.5 = (bf16[8,656,128]{2,1,0:T(8,128)(2,1)}, bf16[8,656,128]{2,1,0:T(8,128)(2,1)}, u32[]{:S(2)}, u32[]{:S(2)}) collective-permute-start(bf16[8,656,128]{2,1,0:T(8,128)(2,1)} %pad_maximum_fusion.2), channel_id=1, source_target_pairs={{0,12},{1,13},{2,14},{3,15},{4,8},{5,9},{6,10},{7,11},{8,4},{9,5},... | collective-permute-start | bytes 4030472 | tf_op jit(solution)/shard_map/ppermute | solution.py:57
  127.6 9.1 %collective-permute-start.15 = (bf16[128,384]{1,0:T(8,128)(2,1)S(1)}, bf16[128,384]{1,0:T(8,128)(2,1)S(1)}, u32[]{:S(2)}, u32[]{:S(2)}) collective-permute-start(bf16[128,384]{1,0:T(8,128)(2,1)S(1)} %slice_select_fusion.5), channel_id=1, source_target_pairs={{0,2},{1,3},{2,0},{3,1},{4,6},{5,7},{6,4},{7,5},{8,10},{9,11},{10,... | collective-permute-start | bytes 294920 | tf_op jit(solution)/shard_map/ppermute | solution.py:57
  127.7 9.0 %collective-permute-start.12 = (bf16[1,128,384]{2,1,0:T(8,128)(2,1)S(1)}, bf16[1,128,384]{2,1,0:T(8,128)(2,1)S(1)}, u32[]{:S(2)}, u32[]{:S(2)}) collective-permute-start(bf16[1,128,384]{2,1,0:T(8,128)(2,1)S(1)} %bitcast.255), channel_id=1, source_target_pairs={{0,16},{1,17},{2,18},{3,19},{4,20},{5,21},{6,22},{7,23},{8,24},{9,... | collective-permute-start | bytes 294920 | tf_op jit(solution)/shard_map/ppermute | solution.py:57
  136.8 10.8 %collective-permute-start.16 = (bf16[1,128,384]{2,1,0:T(8,128)(2,1)S(1)}, bf16[1,128,384]{2,1,0:T(8,128)(2,1)S(1)}, u32[]{:S(2)}, u32[]{:S(2)}) collective-permute-start(bf16[1,128,384]{2,1,0:T(8,128)(2,1)S(1)} %bitcast.267), channel_id=1, source_target_pairs={{0,4},{1,5},{2,6},{3,7},{4,0},{5,1},{6,2},{7,3},{8,12},{9,13},{10,... | collective-permute-start | bytes 294920 | tf_op jit(solution)/shard_map/ppermute | solution.py:57
  136.8 19.2 %collective-permute-start.13 = (bf16[2,128,384]{2,1,0:T(8,128)(2,1)S(1)}, bf16[2,128,384]{2,1,0:T(8,128)(2,1)S(1)}, u32[]{:S(2)}, u32[]{:S(2)}) collective-permute-start(bf16[2,128,384]{2,1,0:T(8,128)(2,1)S(1)} %pad_maximum_fusion.20), channel_id=1, source_target_pairs={{0,48},{1,49},{2,50},{3,51},{4,52},{5,53},{6,54},{7,55},{8,56},{9,... | collective-permute-start | bytes 589832 | tf_op jit(solution)/shard_map/ppermute | solution.py:57
  147.6 11.1 %collective-permute-start.17 = (bf16[2,128,384]{2,1,0:T(8,128)(2,1)S(1)}, bf16[2,128,384]{2,1,0:T(8,128)(2,1)S(1)}, u32[]{:S(2)}, u32[]{:S(2)}) collective-permute-start(bf16[2,128,384]{2,1,0:T(8,128)(2,1)S(1)} %pad_maximum_fusion.21), channel_id=1, source_target_pairs={{0,12},{1,13},{2,14},{3,15},{4,8},{5,9},{6,10},{7,11},{8,4},{9,5},... | collective-permute-start | bytes 589832 | tf_op jit(solution)/shard_map/ppermute | solution.py:57
  156.8 13.6 %collective-permute-start.14 = (bf16[4,128,384]{2,1,0:T(8,128)(2,1)}, bf16[4,128,384]{2,1,0:T(8,128)(2,1)}, u32[]{:S(2)}, u32[]{:S(2)}) collective-permute-start(bf16[4,128,384]{2,1,0:T(8,128)(2,1)} %pad_maximum_fusion.13), channel_id=1, source_target_pairs={{0,4},{1,5},{2,6},{3,7},{4,0},{5,1},{6,2},{7,3},{8,12},{9,13},{10,... | collective-permute-start | bytes 1179656 | tf_op jit(solution)/shard_map/ppermute | solution.py:57
  160.2 12.3 %collective-permute-start.18 = (bf16[4,128,384]{2,1,0:T(8,128)(2,1)}, bf16[4,128,384]{2,1,0:T(8,128)(2,1)}, u32[]{:S(2)}, u32[]{:S(2)}) collective-permute-start(bf16[4,128,384]{2,1,0:T(8,128)(2,1)} %pad_maximum_fusion.14), channel_id=1, source_target_pairs={{0,16},{1,17},{2,18},{3,19},{4,20},{5,21},{6,22},{7,23},{8,24},{9,... | collective-permute-start | bytes 1179656 | tf_op jit(solution)/shard_map/ppermute | solution.py:57
  174.6 13.5 %collective-permute-start.19 = (bf16[8,128,384]{2,1,0:T(8,128)(2,1)}, bf16[8,128,384]{2,1,0:T(8,128)(2,1)}, u32[]{:S(2)}, u32[]{:S(2)}) collective-permute-start(bf16[8,128,384]{2,1,0:T(8,128)(2,1)} %pad_maximum_fusion.5), channel_id=1, source_target_pairs={{0,12},{1,13},{2,14},{3,15},{4,8},{5,9},{6,10},{7,11},{8,4},{9,5},... | collective-permute-start | bytes 2359304 | tf_op jit(solution)/shard_map/ppermute | solution.py:57
  176.7 13.5 %collective-permute-start.20 = (bf16[8,128,384]{2,1,0:T(8,128)(2,1)}, bf16[8,128,384]{2,1,0:T(8,128)(2,1)}, u32[]{:S(2)}, u32[]{:S(2)}) collective-permute-start(bf16[8,128,384]{2,1,0:T(8,128)(2,1)} %pad_maximum_fusion.6), channel_id=1, source_target_pairs={{0,48},{1,49},{2,50},{3,51},{4,52},{5,53},{6,54},{7,55},{8,56},{9,... | collective-permute-start | bytes 2359304 | tf_op jit(solution)/shard_map/ppermute | solution.py:57
  238.2 7.9 %collective-permute-start.27 = (bf16[4,128,384]{2,1,0:T(8,128)(2,1)S(1)}, bf16[4,128,384]{2,1,0:T(8,128)(2,1)S(1)}, u32[]{:S(2)}, u32[]{:S(2)}) collective-permute-start(bf16[4,128,384]{2,1,0:T(8,128)(2,1)S(1)} %pad_maximum_fusion.15), channel_id=1, source_target_pairs={{0,4},{1,5},{2,6},{3,7},{4,0},{5,1},{6,2},{7,3},{8,12},{9,13},{10,... | collective-permute-start | bytes 1179656 | tf_op jit(solution)/shard_map/ppermute | solution.py:57
  241.6 7.9 %collective-permute-start.31 = (bf16[4,128,384]{2,1,0:T(8,128)(2,1)S(1)}, bf16[4,128,384]{2,1,0:T(8,128)(2,1)S(1)}, u32[]{:S(2)}, u32[]{:S(2)}) collective-permute-start(bf16[4,128,384]{2,1,0:T(8,128)(2,1)S(1)} %pad_maximum_fusion.16), channel_id=1, source_target_pairs={{0,16},{1,17},{2,18},{3,19},{4,20},{5,21},{6,22},{7,23},{8,24},{9,... | collective-permute-start | bytes 1179656 | tf_op jit(solution)/shard_map/ppermute | solution.py:57
  249.6 13.4 %collective-permute-start.32 = (bf16[8,128,384]{2,1,0:T(8,128)(2,1)S(1)}, bf16[8,128,384]{2,1,0:T(8,128)(2,1)S(1)}, u32[]{:S(2)}, u32[]{:S(2)}) collective-permute-start(bf16[8,128,384]{2,1,0:T(8,128)(2,1)S(1)} %pad_maximum_fusion.7), channel_id=1, source_target_pairs={{0,12},{1,13},{2,14},{3,15},{4,8},{5,9},{6,10},{7,11},{8,4},{9,5},... | collective-permute-start | bytes 2359304 | tf_op jit(solution)/shard_map/ppermute | solution.py:57
  253.1 13.3 %collective-permute-start.33 = (bf16[8,128,384]{2,1,0:T(8,128)(2,1)S(1)}, bf16[8,128,384]{2,1,0:T(8,128)(2,1)S(1)}, u32[]{:S(2)}, u32[]{:S(2)}) collective-permute-start(bf16[8,128,384]{2,1,0:T(8,128)(2,1)S(1)} %pad_maximum_fusion.8), channel_id=1, source_target_pairs={{0,48},{1,49},{2,50},{3,51},{4,52},{5,53},{6,54},{7,55},{8,56},{9,... | collective-permute-start | bytes 2359304 | tf_op jit(solution)/shard_map/ppermute | solution.py:57
  319.1 13.3 %collective-permute-start.41 = (bf16[8,128,384]{2,1,0:T(8,128)(2,1)S(1)}, bf16[8,128,384]{2,1,0:T(8,128)(2,1)S(1)}, u32[]{:S(2)}, u32[]{:S(2)}) collective-permute-start(bf16[8,128,384]{2,1,0:T(8,128)(2,1)S(1)} %bitcast.277), channel_id=1, source_target_pairs={{0,48},{1,49},{2,50},{3,51},{4,52},{5,53},{6,54},{7,55},{8,56},{9,... | collective-permute-start | bytes 2359304 | tf_op jit(solution)/shard_map/ppermute | solution.py:57
  322.4 14.0 %collective-permute-start.37 = (bf16[8,128,384]{2,1,0:T(8,128)(2,1)S(1)}, bf16[8,128,384]{2,1,0:T(8,128)(2,1)S(1)}, u32[]{:S(2)}, u32[]{:S(2)}) collective-permute-start(bf16[8,128,384]{2,1,0:T(8,128)(2,1)S(1)} %bitcast.275), channel_id=1, source_target_pairs={{0,12},{1,13},{2,14},{3,15},{4,8},{5,9},{6,10},{7,11},{8,4},{9,5},... | collective-permute-start | bytes 2359304 | tf_op jit(solution)/shard_map/ppermute | solution.py:57
  332.6 8.4 %collective-permute-start.42 = (bf16[4,128,384]{2,1,0:T(8,128)(2,1)S(1)}, bf16[4,128,384]{2,1,0:T(8,128)(2,1)S(1)}, u32[]{:S(2)}, u32[]{:S(2)}) collective-permute-start(bf16[4,128,384]{2,1,0:T(8,128)(2,1)S(1)} %slice.575), channel_id=1, source_target_pairs={{0,16},{1,17},{2,18},{3,19},{4,20},{5,21},{6,22},{7,23},{8,24},{9,... | collective-permute-start | bytes 1179656 | tf_op jit(solution)/shard_map/ppermute | solution.py:57
  336.6 11.4 %collective-permute-start.38 = (bf16[4,128,384]{2,1,0:T(8,128)(2,1)S(1)}, bf16[4,128,384]{2,1,0:T(8,128)(2,1)S(1)}, u32[]{:S(2)}, u32[]{:S(2)}) collective-permute-start(bf16[4,128,384]{2,1,0:T(8,128)(2,1)S(1)} %slice.569), channel_id=1, source_target_pairs={{0,4},{1,5},{2,6},{3,7},{4,0},{5,1},{6,2},{7,3},{8,12},{9,13},{10,... | collective-permute-start | bytes 1179656 | tf_op jit(solution)/shard_map/ppermute | solution.py:57
  348.3 8.1 %collective-permute-start.44 = (bf16[1,128,384]{2,1,0:T(8,128)(2,1)S(1)}, bf16[1,128,384]{2,1,0:T(8,128)(2,1)S(1)}, u32[]{:S(2)}, u32[]{:S(2)}) collective-permute-start(bf16[1,128,384]{2,1,0:T(8,128)(2,1)S(1)} %slice.579), channel_id=1, source_target_pairs={{0,4},{1,5},{2,6},{3,7},{4,0},{5,1},{6,2},{7,3},{8,12},{9,13},{10,... | collective-permute-start | bytes 294920 | tf_op jit(solution)/shard_map/ppermute | solution.py:57
  355.2 9.4 %collective-permute-start.40 = (bf16[1,128,384]{2,1,0:T(8,128)(2,1)S(1)}, bf16[1,128,384]{2,1,0:T(8,128)(2,1)S(1)}, u32[]{:S(2)}, u32[]{:S(2)}) collective-permute-start(bf16[1,128,384]{2,1,0:T(8,128)(2,1)S(1)} %slice.573), channel_id=1, source_target_pairs={{0,16},{1,17},{2,18},{3,19},{4,20},{5,21},{6,22},{7,23},{8,24},{9,... | collective-permute-start | bytes 294920 | tf_op jit(solution)/shard_map/ppermute | solution.py:57
  356.5 9.4 %collective-permute-start.45 = (bf16[128,384]{1,0:T(8,128)(2,1)S(1)}, bf16[128,384]{1,0:T(8,128)(2,1)S(1)}, u32[]{:S(2)}, u32[]{:S(2)}) collective-permute-start(bf16[128,384]{1,0:T(8,128)(2,1)S(1)} %fusion.35), channel_id=1, source_target_pairs={{0,2},{1,3},{2,0},{3,1},{4,6},{5,7},{6,4},{7,5},{8,10},{9,11},{10,... | collective-permute-start | bytes 294920 | tf_op jit(solution)/shard_map/ppermute | solution.py:57
  405.0 13.3 %collective-permute-start.54 = (bf16[8,128,384]{2,1,0:T(8,128)(2,1)S(1)}, bf16[8,128,384]{2,1,0:T(8,128)(2,1)S(1)}, u32[]{:S(2)}, u32[]{:S(2)}) collective-permute-start(bf16[8,128,384]{2,1,0:T(8,128)(2,1)S(1)} %bitcast.278), channel_id=1, source_target_pairs={{0,48},{1,49},{2,50},{3,51},{4,52},{5,53},{6,54},{7,55},{8,56},{9,... | collective-permute-start | bytes 2359304 | tf_op jit(solution)/shard_map/ppermute | solution.py:57
  407.4 13.2 %collective-permute-start.50 = (bf16[8,128,384]{2,1,0:T(8,128)(2,1)S(1)}, bf16[8,128,384]{2,1,0:T(8,128)(2,1)S(1)}, u32[]{:S(2)}, u32[]{:S(2)}) collective-permute-start(bf16[8,128,384]{2,1,0:T(8,128)(2,1)S(1)} %bitcast.276), channel_id=1, source_target_pairs={{0,12},{1,13},{2,14},{3,15},{4,8},{5,9},{6,10},{7,11},{8,4},{9,5},... | collective-permute-start | bytes 2359304 | tf_op jit(solution)/shard_map/ppermute | solution.py:57
  418.6 8.1 %collective-permute-start.55 = (bf16[4,128,384]{2,1,0:T(8,128)(2,1)S(1)}, bf16[4,128,384]{2,1,0:T(8,128)(2,1)S(1)}, u32[]{:S(2)}, u32[]{:S(2)}) collective-permute-start(bf16[4,128,384]{2,1,0:T(8,128)(2,1)S(1)} %slice.588), channel_id=1, source_target_pairs={{0,16},{1,17},{2,18},{3,19},{4,20},{5,21},{6,22},{7,23},{8,24},{9,... | collective-permute-start | bytes 1179656 | tf_op jit(solution)/shard_map/ppermute | solution.py:57
  428.8 8.0 %collective-permute-start.52 = (bf16[2,128,384]{2,1,0:T(8,128)(2,1)S(1)}, bf16[2,128,384]{2,1,0:T(8,128)(2,1)S(1)}, u32[]{:S(2)}, u32[]{:S(2)}) collective-permute-start(bf16[2,128,384]{2,1,0:T(8,128)(2,1)S(1)} %slice.584), channel_id=1, source_target_pairs={{0,48},{1,49},{2,50},{3,51},{4,52},{5,53},{6,54},{7,55},{8,56},{9,... | collective-permute-start | bytes 589832 | tf_op jit(solution)/shard_map/ppermute | solution.py:57
  436.9 8.7 %collective-permute-start.53 = (bf16[1,128,384]{2,1,0:T(8,128)(2,1)S(1)}, bf16[1,128,384]{2,1,0:T(8,128)(2,1)S(1)}, u32[]{:S(2)}, u32[]{:S(2)}) collective-permute-start(bf16[1,128,384]{2,1,0:T(8,128)(2,1)S(1)} %slice.586), channel_id=1, source_target_pairs={{0,16},{1,17},{2,18},{3,19},{4,20},{5,21},{6,22},{7,23},{8,24},{9,... | collective-permute-start | bytes 294920 | tf_op jit(solution)/shard_map/ppermute | solution.py:57
  473.8 41.6 %collective-permute-start.72 = (bf16[2,4,4,416,128]{4,3,2,1,0:T(8,128)(2,1)}, bf16[2,4,4,416,128]{4,3,2,1,0:T(8,128)(2,1)S(1)}, u32[]{:S(2)}, u32[]{:S(2)}) collective-permute-start(bf16[2,4,4,416,128]{4,3,2,1,0:T(8,128)(2,1)} %get-tuple-element.122), channel_id=1, source_target_pairs={{0,3},{1,2},{2,1},{3,0},{4,7},{5,6},{6,5},{7,4},{8,11},{9,10},{10,... | collective-permute-start | bytes 10223624 | tf_op jit(solution)/shard_map/ppermute | solution.py:57
  476.2 44.3 %collective-permute-start.60 = (bf16[2,4,4,432,128]{4,3,2,1,0:T(8,128)(2,1)}, bf16[2,4,4,432,128]{4,3,2,1,0:T(8,128)(2,1)S(1)}, u32[]{:S(2)}, u32[]{:S(2)}) collective-permute-start(bf16[2,4,4,432,128]{4,3,2,1,0:T(8,128)(2,1)} %get-tuple-element.118), channel_id=1, source_target_pairs={{0,48},{1,49},{2,50},{3,51},{4,52},{5,53},{6,54},{7,55},{8,56},{9,... | collective-permute-start | bytes 10616840 | tf_op jit(solution)/shard_map/ppermute | solution.py:57
  476.9 45.6 %collective-permute-start.66 = (bf16[2,4,4,432,128]{4,3,2,1,0:T(8,128)(2,1)}, bf16[2,4,4,432,128]{4,3,2,1,0:T(8,128)(2,1)S(1)}, u32[]{:S(2)}, u32[]{:S(2)}) collective-permute-start(bf16[2,4,4,432,128]{4,3,2,1,0:T(8,128)(2,1)} %get-tuple-element.120), channel_id=1, source_target_pairs={{0,12},{1,13},{2,14},{3,15},{4,8},{5,9},{6,10},{7,11},{8,4},{9,5},... | collective-permute-start | bytes 10616840 | tf_op jit(solution)/shard_map/ppermute | solution.py:57
  518.5 21.9 %collective-permute-start.73 = (bf16[4,4,416,128]{3,2,1,0:T(8,128)(2,1)S(1)}, bf16[4,4,416,128]{3,2,1,0:T(8,128)(2,1)S(1)}, u32[]{:S(2)}, u32[]{:S(2)}) collective-permute-start(bf16[4,4,416,128]{3,2,1,0:T(8,128)(2,1)S(1)} %get-tuple-element.156), channel_id=1, source_target_pairs={{0,1},{1,0},{2,3},{3,2},{4,5},{5,4},{6,7},{7,6},{8,9},{9,8},{10,11... | collective-permute-start | bytes 5111816 | tf_op jit(solution)/shard_map/ppermute | solution.py:57
  521.5 23.2 %collective-permute-start.61 = (bf16[4,4,432,128]{3,2,1,0:T(8,128)(2,1)S(1)}, bf16[4,4,432,128]{3,2,1,0:T(8,128)(2,1)S(1)}, u32[]{:S(2)}, u32[]{:S(2)}) collective-permute-start(bf16[4,4,432,128]{3,2,1,0:T(8,128)(2,1)S(1)} %get-tuple-element.152), channel_id=1, source_target_pairs={{0,16},{1,17},{2,18},{3,19},{4,20},{5,21},{6,22},{7,23},{8,24},{9,... | collective-permute-start | bytes 5308424 | tf_op jit(solution)/shard_map/ppermute | solution.py:57
  523.5 26.1 %collective-permute-start.67 = (bf16[4,4,432,128]{3,2,1,0:T(8,128)(2,1)S(1)}, bf16[4,4,432,128]{3,2,1,0:T(8,128)(2,1)S(1)}, u32[]{:S(2)}, u32[]{:S(2)}) collective-permute-start(bf16[4,4,432,128]{3,2,1,0:T(8,128)(2,1)S(1)} %get-tuple-element.154), channel_id=1, source_target_pairs={{0,4},{1,5},{2,6},{3,7},{4,0},{5,1},{6,2},{7,3},{8,12},{9,13},{10,... | collective-permute-start | bytes 5308424 | tf_op jit(solution)/shard_map/ppermute | solution.py:57
  540.9 14.2 %collective-permute-start.74 = (bf16[2,4,416,128]{3,2,1,0:T(8,128)(2,1)S(1)}, bf16[2,4,416,128]{3,2,1,0:T(8,128)(2,1)S(1)}, u32[]{:S(2)}, u32[]{:S(2)}) collective-permute-start(bf16[2,4,416,128]{3,2,1,0:T(8,128)(2,1)S(1)} %get-tuple-element.162), channel_id=1, source_target_pairs={{0,48},{1,49},{2,50},{3,51},{4,52},{5,53},{6,54},{7,55},{8,56},{9,... | collective-permute-start | bytes 2555912 | tf_op jit(solution)/shard_map/ppermute | solution.py:57
  546.1 14.9 %collective-permute-start.62 = (bf16[2,4,432,128]{3,2,1,0:T(8,128)(2,1)}, bf16[2,4,432,128]{3,2,1,0:T(8,128)(2,1)}, u32[]{:S(2)}, u32[]{:S(2)}) collective-permute-start(bf16[2,4,432,128]{3,2,1,0:T(8,128)(2,1)} %get-tuple-element.158), channel_id=1, source_target_pairs={{0,12},{1,13},{2,14},{3,15},{4,8},{5,9},{6,10},{7,11},{8,4},{9,5},... | collective-permute-start | bytes 2654216 | tf_op jit(solution)/shard_map/ppermute | solution.py:57
  551.0 18.2 %collective-permute-start.68 = (bf16[2,4,432,128]{3,2,1,0:T(8,128)(2,1)}, bf16[2,4,432,128]{3,2,1,0:T(8,128)(2,1)}, u32[]{:S(2)}, u32[]{:S(2)}) collective-permute-start(bf16[2,4,432,128]{3,2,1,0:T(8,128)(2,1)} %get-tuple-element.160), channel_id=1, source_target_pairs={{0,3},{1,2},{2,1},{3,0},{4,7},{5,6},{6,5},{7,4},{8,11},{9,10},{10,... | collective-permute-start | bytes 2654216 | tf_op jit(solution)/shard_map/ppermute | solution.py:57
  556.1 8.4 %collective-permute-start.75 = (bf16[4,416,128]{2,1,0:T(8,128)(2,1)}, bf16[4,416,128]{2,1,0:T(8,128)(2,1)}, u32[]{:S(2)}, u32[]{:S(2)}) collective-permute-start(bf16[4,416,128]{2,1,0:T(8,128)(2,1)} %get-tuple-element.176), channel_id=1, source_target_pairs={{0,16},{1,17},{2,18},{3,19},{4,20},{5,21},{6,22},{7,23},{8,24},{9,... | collective-permute-start | bytes 1277960 | tf_op jit(solution)/shard_map/ppermute | solution.py:57
  562.3 10.8 %collective-permute-start.63 = (bf16[4,432,128]{2,1,0:T(8,128)(2,1)S(1)}, bf16[4,432,128]{2,1,0:T(8,128)(2,1)S(1)}, u32[]{:S(2)}, u32[]{:S(2)}) collective-permute-start(bf16[4,432,128]{2,1,0:T(8,128)(2,1)S(1)} %get-tuple-element.172), channel_id=1, source_target_pairs={{0,4},{1,5},{2,6},{3,7},{4,0},{5,1},{6,2},{7,3},{8,12},{9,13},{10,... | collective-permute-start | bytes 1327112 | tf_op jit(solution)/shard_map/ppermute | solution.py:57
  570.5 10.3 %collective-permute-start.69 = (bf16[4,432,128]{2,1,0:T(8,128)(2,1)S(1)}, bf16[4,432,128]{2,1,0:T(8,128)(2,1)S(1)}, u32[]{:S(2)}, u32[]{:S(2)}) collective-permute-start(bf16[4,432,128]{2,1,0:T(8,128)(2,1)S(1)} %get-tuple-element.174), channel_id=1, source_target_pairs={{0,1},{1,0},{2,3},{3,2},{4,5},{5,4},{6,7},{7,6},{8,9},{9,8},{10,11... | collective-permute-start | bytes 1327112 | tf_op jit(solution)/shard_map/ppermute | solution.py:57
  573.0 10.4 %collective-permute-start.77 = (bf16[416,128]{1,0:T(8,128)(2,1)S(1)}, bf16[416,128]{1,0:T(8,128)(2,1)S(1)}, u32[]{:S(2)}, u32[]{:S(2)}) collective-permute-start(bf16[416,128]{1,0:T(8,128)(2,1)S(1)} %fusion.34), channel_id=1, source_target_pairs={{0,4},{1,5},{2,6},{3,7},{4,0},{5,1},{6,2},{7,3},{8,12},{9,13},{10,... | collective-permute-start | bytes 319496 | tf_op jit(solution)/shard_map/ppermute | solution.py:57
  573.2 10.2 %collective-permute-start.64 = (bf16[2,432,128]{2,1,0:T(8,128)(2,1)S(1)}, bf16[2,432,128]{2,1,0:T(8,128)(2,1)S(1)}, u32[]{:S(2)}, u32[]{:S(2)}) collective-permute-start(bf16[2,432,128]{2,1,0:T(8,128)(2,1)S(1)} %get-tuple-element.179), channel_id=1, source_target_pairs={{0,3},{1,2},{2,1},{3,0},{4,7},{5,6},{6,5},{7,4},{8,11},{9,10},{10,... | collective-permute-start | bytes 663560 | tf_op jit(solution)/shard_map/ppermute | solution.py:57
  580.9 8.4 %collective-permute-start.70 = (bf16[2,432,128]{2,1,0:T(8,128)(2,1)S(1)}, bf16[2,432,128]{2,1,0:T(8,128)(2,1)S(1)}, u32[]{:S(2)}, u32[]{:S(2)}) collective-permute-start(bf16[2,432,128]{2,1,0:T(8,128)(2,1)S(1)} %get-tuple-element.181), channel_id=1, source_target_pairs={{0,48},{1,49},{2,50},{3,51},{4,52},{5,53},{6,54},{7,55},{8,56},{9,... | collective-permute-start | bytes 663560 | tf_op jit(solution)/shard_map/ppermute | solution.py:57
  (86 other events, 700.3 us)
Sparse Core Ops, SparseCore 0:
  34.9 138.9 all-gather.2

commit v7 on v6

--- a/solution.py
+++ b/solution.py
@@ -90,7 +90,7 @@
     return jnp.concatenate(blocks, axis=0).reshape(KEYS, tail[1])
 
 
-def scatter_keys(d_kv):
+def scatter_keys(d_kv, beside=None):
     parts = d_kv.reshape(2, 16, R, d_kv.shape[1])
     orders = (((0, 1), (1, 0)), ((1, 0), (0, 1)))
     blocks = [parts[0], parts[1]]
@@ -102,7 +102,9 @@
                 total = blocks[k][:half].astype(f32) + got.astype(f32)
                 last = k == 0 and half == 1
                 blocks[k] = total if last else total.astype(bf16)
-    return blocks[0][0] + swapped(blocks[1][0], far_z).astype(f32)
+            if beside is not None and leg and number:
+                blocks, beside = lax.optimization_barrier((blocks, beside))
+    return blocks[0][0] + swapped(blocks[1][0], far_z).astype(f32), beside
 
 
 def slot_offsets(phase):
@@ -292,21 +294,25 @@
     q = heads_wide(qt_ref, True)
     count = need_ref[KEYS // SMALL]
 
-    def score(i, peak):
-        kv = chunk_of(kv_ref, need_ref, i)
-        c_ref[chunk_rows(i), :] = kv
-        b = bias_ref[chunk_rows(i), :]
-        s = mm(kv, q) + jnp.concatenate([b, b, b], axis=1)
-        s_ref[chunk_rows(i), :] = s
-        return jnp.maximum(peak, jnp.max(s, axis=0, keepdims=True))
+    def score(pair, peak):
+        for i in (2 * pair, 2 * pair + 1):
+            kv = chunk_of(kv_ref, need_ref, i)
+            c_ref[chunk_rows(i), :] = kv
+            b = bias_ref[chunk_rows(i), :]
+            s = mm(kv, q) + jnp.concatenate([b, b, b], axis=1)
+            s_ref[chunk_rows(i), :] = s
+            peak = jnp.maximum(peak, jnp.max(s, axis=0, keepdims=True))
+        return peak
 
     peak = lax.fori_loop(0, count, score, jnp.full((1, LANES), masked_fill, f32))
 
-    def mix(i, state):
+    def mix(pair, state):
         total, acc = state
-        p = jnp.exp(s_ref[chunk_rows(i), :] - peak)
-        total = total + jnp.sum(p, axis=0, keepdims=True)
-        return total, acc + mm(c_ref[chunk_rows(i), :].T, p.astype(bf16))
+        for i in (2 * pair, 2 * pair + 1):
+            p = jnp.exp(s_ref[chunk_rows(i), :] - peak)
+            total = total + jnp.sum(p, axis=0, keepdims=True)
+            acc = acc + mm(c_ref[chunk_rows(i), :].T, p.astype(bf16))
+        return total, acc
 
     total, acc = lax.fori_loop(
         0, count, mix, (jnp.zeros((1, LANES), f32), jnp.zeros((128, LANES), f32))
@@ -559,16 +565,18 @@
     both = jnp.concatenate([q, d_o], axis=1)
     dkv_ref[...] = jnp.zeros_like(dkv_ref)
 
-    def fold(i, acc):
-        kv = chunk_of(kv_ref, need_ref, i)
-        b = bias_ref[chunk_rows(i), :]
-        p = jnp.exp(mm(kv, q) + jnp.concatenate([b, b, b], axis=1) - lse)
-        ds = (p * (mm(kv, d_o) - delta)).astype(bf16)
-        part = mm_nt(jnp.concatenate([ds, p.astype(bf16)], axis=1), both).astype(bf16)
-        for k in range(CHUNK // SMALL):
-            at = pl.multiple_of(need_ref[CHUNK // SMALL * i + k] * SMALL, SMALL)
-            dkv_ref[pl.ds(at, SMALL), :] = part[SMALL * k : SMALL * k + SMALL]
-        return acc + mm(kv.T, ds)
+    def fold(pair, acc):
+        for i in (2 * pair, 2 * pair + 1):
+            kv = chunk_of(kv_ref, need_ref, i)
+            b = bias_ref[chunk_rows(i), :]
+            p = jnp.exp(mm(kv, q) + jnp.concatenate([b, b, b], axis=1) - lse)
+            ds = (p * (mm(kv, d_o) - delta)).astype(bf16)
+            part = mm_nt(jnp.concatenate([ds, p.astype(bf16)], axis=1), both).astype(bf16)
+            for k in range(CHUNK // SMALL):
+                at = pl.multiple_of(need_ref[CHUNK // SMALL * i + k] * SMALL, SMALL)
+                dkv_ref[pl.ds(at, SMALL), :] = part[SMALL * k : SMALL * k + SMALL]
+            acc = acc + mm(kv.T, ds)
+        return acc
 
     acc = lax.fori_loop(0, need_ref[KEYS // SMALL], fold, jnp.zeros((128, LANES), f32))
     acc = acc[:64] * 0.125
@@ -670,16 +678,15 @@
     )(d_query, d_kv, cos, sin, u, gain, d_hidden, weights)
 
 
-def outer_kernel(
-    slot_ref, at_ref, dqkv_ref, mixed_ref, dhb_ref, nt_ref, dgate_ref, dup_ref, mt_ref, cb_ref,
-    gain_ref, k0, k1, k2, s0, s1, s2, stage, sems,
-):
-    step = pl.program_id(0)
+def outer_steps(begin, end, refs, slot_ref, outs, stage, sems):
+    step = pl.program_id(0) + begin
     buf = step % 2
     slot_y, slot_x = slot_ref[step // 4], slot_ref[4 + step % 4]
     zslot = [slot_ref[8 + k] for k in range(4)]
     out_ref = stage.at[buf]
     (a0, b0), (a1, b1), (a2, b2) = PART_ROWS
+    k0, k1, k2, s0, s1, s2 = outs
+    gain_ref, nt_ref, dgate_ref, dup_ref = refs[:4]
 
     def copy(i, buf, half=0):
         src = stage.at[buf]
@@ -693,7 +700,7 @@
             src, dst = src.at[2:4, a2:b2], s2.at[:, slot_y, slot_x]
         return pltpu.make_async_copy(src, dst, sems.at[buf, i])
 
-    @pl.when(step >= 2)
+    @pl.when(step >= begin + 2)
     def _():
         for i in range(4):
             copy(i, buf).wait()
@@ -728,21 +735,7 @@
                     at = 160 * (c + h)
                     out_ref[zslot[k], at : at + 160, :] = b.astype(bf16)
 
-    @pl.when(step < 2)
-    def _():
-        narrow(384 * step, (0, 1, 2, 3))
-
-    @pl.when(step == 2)
-    def _():
-        narrow(768, (0, 1))
-        wide(mixed_ref, 0, dhb_ref, (2, 3))
-
-    @pl.when(step == 3)
-    def _():
-        wide(mixed_ref, 320, dhb_ref, (0, 1, 2, 3))
-
-    @pl.when((step >= 4) & (step < 12))
-    def _():
+    def broad():
         rows = nt_ref[pl.ds(pl.multiple_of(128 * (step - 4), 128), 128), :]
         for part, ref in enumerate((dgate_ref, dup_ref)):
             for c in range(0, 20, 2):
@@ -755,9 +748,36 @@
                             b = b + row_of(k, 32, 30)
                         out_ref[zslot[k], at : at + 32, :] = b.astype(bf16)
 
-    @pl.when(step >= 12)
-    def _():
-        wide(mt_ref, 640 * (step - 12), cb_ref, (0, 1, 2, 3))
+    if begin == 0:
+        at_ref, dqkv_ref, mixed_ref, dhb_ref = refs[4:]
+
+        @pl.when(step < 2)
+        def _():
+            narrow(384 * step, (0, 1, 2, 3))
+
+        @pl.when(step == 2)
+        def _():
+            narrow(768, (0, 1))
+            wide(mixed_ref, 0, dhb_ref, (2, 3))
+
+        @pl.when(step == 3)
+        def _():
+            wide(mixed_ref, 320, dhb_ref, (0, 1, 2, 3))
+
+        @pl.when(step >= 4)
+        def _():
+            broad()
+
+    else:
+        mt_ref, cb_ref = refs[4:]
+
+        @pl.when(step < 12)
+        def _():
+            broad()
+
+        @pl.when(step >= 12)
+        def _():
+            wide(mt_ref, 640 * (step - 12), cb_ref, (0, 1, 2, 3))
 
     for half in range(2):
 
@@ -772,26 +792,34 @@
     copy(2, buf).start()
     copy(3, buf).start()
 
-    @pl.when(step == 15)
+    @pl.when(step == end - 1)
     def _():
         for last in (0, 1):
             for i in range(4):
                 copy(i, last).wait()
 
 
-def outer(slots, at, dqkv, mixed, dhb, nt, dgate, dup, mt, cb, gains):
+def outer_late_kernel(slot_ref, *refs):
+    outer_steps(0, 8, refs[:8], slot_ref, refs[14:20], *refs[20:])
+
+
+def outer_early_kernel(slot_ref, *refs):
+    outer_steps(8, 16, refs[:6], slot_ref, refs[6:12], *refs[12:])
+
+
+def outer(slots, args, made=None):
     whole = lambda v: pl.BlockSpec(v.shape, lambda s, slot: (0,) * v.ndim)
-    args = (at, dqkv, mixed, dhb, nt, dgate, dup, mt, cb, gains)
     shapes = [
         jax.ShapeDtypeStruct((2, 4, 4, end - begin, 128), bf16) for begin, end in PART_ROWS
     ]
-    out = pl.pallas_call(
-        outer_kernel,
-        name="outer",
+    made = made or []
+    return pl.pallas_call(
+        outer_late_kernel if made else outer_early_kernel,
+        name="outer_late" if made else "outer_early",
         grid_spec=pltpu.PrefetchScalarGridSpec(
             num_scalar_prefetch=1,
-            grid=(16,),
-            in_specs=[whole(v) for v in args],
+            grid=(8,),
+            in_specs=[whole(v) for v in args] + [pl.BlockSpec(memory_space=pl.ANY)] * len(made),
             out_specs=[pl.BlockSpec(memory_space=pl.ANY)] * 6,
             scratch_shapes=[
                 pltpu.VMEM((2, 4, ROWS, 128), bf16),
@@ -799,12 +827,12 @@
             ],
         ),
         out_shape=shapes * 2,
+        input_output_aliases={1 + len(args) + i: i for i in range(len(made))},
         compiler_params=pltpu.CompilerParams(vmem_limit_bytes=48 << 20),
         cost_estimate=pl.CostEstimate(
-            flops=2_600_000_000, bytes_accessed=24_000_000, transcendentals=0
+            flops=1_300_000_000, bytes_accessed=12_000_000, transcendentals=0
         ),
-    )(slots, *args)
-    return out[:3], out[3:]
+    )(slots, *args, *made)
 
 
 def shard_kind(rank):
@@ -842,6 +870,15 @@
         return w.reshape(SHARD), blocks[30, :30]
 
     return lax.switch(shard_kind(rank), [narrow, square, broad], 0)
+
+
+def gain_rows(one, two):
+    gains = jnp.concatenate([one, two], axis=1).reshape(SHARDS, 30)
+    shards = jnp.arange(SHARDS, dtype=jnp.int32)
+    square = (((shards >= 10) & (shards < 16)) | (shards >= 48))[:, None]
+    return jnp.where(
+        square, jnp.pad(gains, ((0, 0), (64, 34))), jnp.pad(gains, ((0, 0), (0, 98)))
+    )
 
 
 def per_device(layer_in, out_grad, segment_ids, block_pair, params, norm_gains):
@@ -878,7 +915,7 @@
     order_k = jnp.sum(jnp.where(chosen, jnp.arange(64)[None, :], 0), axis=1)
     spot_k = jnp.sum(jnp.where(chosen & seen[None, :], spot_k[None, :], 0), axis=1)
     spot_k = jnp.where(jnp.arange(64) < seen_count, spot_k, 1 << 16)
-    need = jnp.concatenate([order_k, ((seen_count + 7) // 8)[None]]).astype(jnp.int32)
+    need = jnp.concatenate([order_k, ((seen_count + 15) // 16)[None]]).astype(jnp.int32)
     place_k = (spot_k[:, None] * 64 + within[None, :]).reshape(KEYS)
     bias = jnp.where(
         (place_k[:, None] <= place_q[None, :]) & (place_k[:, None] >= start_q[None, :]),
@@ -902,6 +939,7 @@
             (4 * slots_x[:, None] + slots_z[None, :]).reshape(16),
         ]
     )
+    slots = jnp.concatenate([slots_y, slots_x, slots_z])
     gains = front[1][:, HALF : HALF + 4, :30][idx[16:]].astype(f32)
     gains = gains.transpose(1, 0, 2).reshape(1, 2 * D)
     gain_one, gain_two = gains[:, :D], gains[:, D:]
@@ -926,7 +964,7 @@
             u = jnp.where(first, u, over(result, 0))
 
     cot = out_grad[0]
-    d_query = d_kv = None
+    d_query = d_kv = made = None
     for tick in range(2):
         layer = 1 - tick
         active = phase == layer
@@ -935,9 +973,11 @@
             cot, gate, up, hidden, gain_two, pad, gathered
         )
         d_side = jnp.where(active, d_mixed[:QSIDE], over(d_mixed[QSIDE:], layer))
+        if tick:
+            made = outer(slots, (gain_rows(dg_two, dg_two), nt, dgate, dup, mt, cb))
         d_kv_all, dq_side = attend_back(need, qt_side, kv_all, bias, d_side, mixed_side, lse)
         dq_new = jnp.concatenate([dq_side, over(dq_side[: D - QSIDE], tick)])
-        dkv_side = scatter_keys(d_kv_all)
+        dkv_side, made = scatter_keys(d_kv_all, made)
         dkv_new = jnp.concatenate([dkv_side, over(dkv_side[:, :256], tick)], axis=1)
         d_query = dq_new if tick == 0 else jnp.where(active, dq_new, d_query)
         d_kv = dkv_new if tick == 0 else jnp.where(active, dkv_new, d_kv)
@@ -947,15 +987,10 @@
         if tick == 0:
             cot = jnp.where(first, over(d_u.astype(bf16), 1).astype(f32), cot)
 
-    gains = jnp.concatenate([dg_one, dg_two], axis=1).reshape(SHARDS, 30)
-    shards = jnp.arange(SHARDS, dtype=jnp.int32)
-    square = (((shards >= 10) & (shards < 16)) | (shards >= 48))[:, None]
-    gains = jnp.where(
-        square, jnp.pad(gains, ((0, 0), (64, 34))), jnp.pad(gains, ((0, 0), (0, 98)))
+    made = outer(
+        slots, (gain_rows(dg_one, dg_two), nt, dgate, dup, at, dqkv, mixed, dhb), list(made)
     )
-    slots = jnp.concatenate([slots_y, slots_x, slots_z])
-    keep, send = outer(slots, at, dqkv, mixed, dhb, nt, dgate, dup, mt, cb, gains)
-    total = scatter_grads(keep, send)
+    total = scatter_grads(made[:3], made[3:])
     param_part, gain_part = blocks_shard(total, rank)
     return (result[None, None], d_u[None, None], param_part[None], gain_part[None])
 

time: 614 us -> 619 us (level); the launches traced: 604 us -> 616 us
  starting transfers between devices: 149 us -> 103 us
  waiting for transfers between devices: 237 us -> 270 us
  local copies, waits for them, and re-layouts: 32.3 us -> 46.4 us
  Pallas kernels: 114 us -> 125 us
    ppermute x64, starting transfers between devices: 129 us -> 82.5 us  [swapped(): return lax.ppermute(block, ALL, pairs)]
    ppermute x64, waiting for transfers between devices: 221 us -> 255 us  [swapped(): return lax.ppermute(block, ALL, pairs)]
    unnamed x124 -> x184, local copies, waits for them, and re-layouts: 19 us -> 31.4 us
    pallas_call x2, Pallas kernels: 21.9 us -> 30.3 us  [attend_back(): pl.pallas_call(attend_back_kernel, name='attend_back', grid_spec=pltpu.Pr...]
    pallas_call x1 -> x2, Pallas kernels: 14.3 us -> 15.2 us  [outer(): pl.pallas_call(outer_late_kernel if made else outer_early_kernel, name='o...]
  transfers between devices with their start and end apart: 79 -> 79, of which waited for: 56 -> 63; matrix products, arithmetic and copies ran while one was open for 10% -> 10% of each run, Pallas kernels for 2% -> 3%
where the time goes in v7:
time: 619 us; the launch traced here: 616 us
  waiting for transfers between devices  270 us (44%)
  Pallas kernels  125 us (20%)
  starting transfers between devices  103 us (17%)
  other arithmetic  52.3 us (8%)
  local copies, waits for them, and re-layouts  46.4 us (7%)
  between operations  18.3 us (3%)
    ppermute x64, waiting for transfers between devices, swapped(): return lax.ppermute(block, ALL, pairs)  255 us
    ppermute x64, starting transfers between devices, swapped(): return lax.ppermute(block, ALL, pairs)  82.5 us
    unnamed x184, local copies, waits for them, and re-layouts  31.4 us
    pallas_call x2, Pallas kernels, attend_back(): pl.pallas_call(attend_back_kernel, name='attend_back', grid_spec=pltpu.Pr...  30.3 us
    pallas_call x2, Pallas kernels, feed_back(): pl.pallas_call(feed_back_kernel, name='feed_back', grid=(4,), in_specs=[w...  29.8 us
    pallas_call x2, Pallas kernels, feed(): pl.pallas_call(feed_kernel, name='feed', grid=(4,), in_specs=[whole(D, R)...  21.7 us
    ppermute x14, starting transfers between devices, over(): return lax.ppermute(block, 'phase', [(source, 1 - source)])  21 us
    pallas_call x2, Pallas kernels, attend(): pl.pallas_call(attend_kernel, name='attend', grid_spec=pltpu.PrefetchScal...  17.3 us
  transfers between devices with their start and end apart: 79, of which 63 were waited for; matrix products, arithmetic and copies ran while one was open for 10% of the time, Pallas kernels for 3%

profile of v7, /device:TPU:0, one launch (start us, length us, event | category | flops | bytes accessed | tf_op | source)
XLA Modules:
  0.0 615.8 jit_solution(16676621023775123543)
XLA Ops:
  7.2 8.0 %conditional.2 = (bf16[1280,128]{1,0:T(8,128)(2,1)S(1)}) conditional(s32[]{:T(128)} %clamp.4, bf16[1,153600]{1,0:T(2,128)(2,1)} %param.26, bf16[1,153600]{1,0:T(2,128)(2,1)} %param.26, bf16[1,153600]{1,0:T(2,128)(2,1)} %param.26), branch_computations={%region_4.5_spmd, %region_5.6_spmd, %region_6.7_spmd} | conditional | bytes 3780622 | solution.py:856
  7.3 7.3 %reduce.1 = bf16[153600]{0:T(1024)(128)(2,1)S(1)} reduce(bf16[1,153600]{1,0:T(2,128)(2,1)} %param, bf16[]{:T(256)} %constant.203), dimensions={0}, to_apply=%param.reduce_sub_computation | reduce | bytes 614402 | tf_op jit(solution)/shard_map/shard_map
  16.6 6.0 collective-permute-done
  25.6 9.0 %collective-permute-done.1 = bf16[2,1296,128]{2,1,0:T(8,128)(2,1)S(1)} collective-permute-done((bf16[2,1296,128]{2,1,0:T(8,128)(2,1)S(1)}, bf16[2,1296,128]{2,1,0:T(8,128)(2,1)S(1)}, u32[]{:S(2)}, u32[]{:S(2)}) %collective-permute-start.1) | collective-permute-done | bytes 663584 | tf_op jit(solution)/shard_map/ppermute | solution.py:57
  53.1 4.7 collective-permute-start.3
  61.6 4.1 collective-permute-done.3
  66.4 5.7 collective-permute-done.8
  73.4 8.4 %collective-permute-start.9 = (bf16[8,640,128]{2,1,0:T(8,128)(2,1)}, bf16[8,640,128]{2,1,0:T(8,128)(2,1)}, u32[]{:S(2)}, u32[]{:S(2)}) collective-permute-start(bf16[8,640,128]{2,1,0:T(8,128)(2,1)} %pad_maximum_fusion.4), channel_id=1, source_target_pairs={{0,3},{1,2},{2,1},{3,0},{4,7},{5,6},{6,5},{7,4},{8,11},{9,10},{10,... | collective-permute-start | bytes 3932168 | tf_op jit(solution)/shard_map/ppermute | solution.py:57
  81.8 9.5 %collective-permute-done.4 = bf16[4,656,128]{2,1,0:T(8,128)(2,1)S(1)} collective-permute-done((bf16[4,656,128]{2,1,0:T(8,128)(2,1)S(1)}, bf16[4,656,128]{2,1,0:T(8,128)(2,1)S(1)}, u32[]{:S(2)}, u32[]{:S(2)}) %collective-permute-start.4) | collective-permute-done | bytes 671776 | tf_op jit(solution)/shard_map/ppermute | solution.py:57
  104.8 17.1 %collective-permute-done.5 = bf16[8,656,128]{2,1,0:T(8,128)(2,1)} collective-permute-done((bf16[8,656,128]{2,1,0:T(8,128)(2,1)}, bf16[8,656,128]{2,1,0:T(8,128)(2,1)}, u32[]{:S(2)}, u32[]{:S(2)}) %collective-permute-start.5) | collective-permute-done | bytes 1343520 | tf_op jit(solution)/shard_map/ppermute | solution.py:57
  133.5 6.5 %collective-permute-done.15 = bf16[128,384]{1,0:T(8,128)(2,1)S(1)} collective-permute-done((bf16[128,384]{1,0:T(8,128)(2,1)S(1)}, bf16[128,384]{1,0:T(8,128)(2,1)S(1)}, u32[]{:S(2)}, u32[]{:S(2)}) %collective-permute-start.15) | collective-permute-done | bytes 98336 | tf_op jit(solution)/shard_map/ppermute | solution.py:57
  140.0 6.9 %collective-permute-start.13 = (bf16[2,128,384]{2,1,0:T(8,128)(2,1)S(1)}, bf16[2,128,384]{2,1,0:T(8,128)(2,1)S(1)}, u32[]{:S(2)}, u32[]{:S(2)}) collective-permute-start(bf16[2,128,384]{2,1,0:T(8,128)(2,1)S(1)} %pad_maximum_fusion.20), channel_id=1, source_target_pairs={{0,48},{1,49},{2,50},{3,51},{4,52},{5,53},{6,54},{7,55},{8,56},{9,... | collective-permute-start | bytes 589832 | tf_op jit(solution)/shard_map/ppermute | solution.py:57
  147.1 8.2 %collective-permute-done.13 = bf16[2,128,384]{2,1,0:T(8,128)(2,1)S(1)} collective-permute-done((bf16[2,128,384]{2,1,0:T(8,128)(2,1)S(1)}, bf16[2,128,384]{2,1,0:T(8,128)(2,1)S(1)}, u32[]{:S(2)}, u32[]{:S(2)}) %collective-permute-start.13) | collective-permute-done | bytes 196640 | tf_op jit(solution)/shard_map/ppermute | solution.py:57
  160.3 9.4 %collective-permute-done.14 = bf16[4,128,384]{2,1,0:T(8,128)(2,1)} collective-permute-done((bf16[4,128,384]{2,1,0:T(8,128)(2,1)}, bf16[4,128,384]{2,1,0:T(8,128)(2,1)}, u32[]{:S(2)}, u32[]{:S(2)}) %collective-permute-start.14) | collective-permute-done | bytes 393248 | tf_op jit(solution)/shard_map/ppermute | solution.py:57
  173.8 3.5 collective-permute-start.20
  187.6 3.2 collective-permute-done.19
  193.0 8.6 %attend.2 = (bf16[576,128]{1,0:T(8,128)(2,1)S(1)}, f32[3,1,384]{2,1,0:T(1,128)S(1)}) custom-call(s32[65]{0:T(128)S(1)} %pad_add_fusion.2.need_ref, bf16[576,128]{1,0:T(8,128)(2,1)S(1)} %slice_select_fusion.3.qt_ref, bf16[4096,384]{1,0:T(8,128)(2,1)S(1)} %bitcast.202, f32[4096,128]{1,0:T(8,128)S(1)} %copy-done.11), custom_call_target="tpu_custom_call" | custom-call | flops 2400000000 | bytes 6000000 | tf_op jit(solution)/shard_map/attend/pallas_call | solution.py:327
  204.9 11.7 %feed.2 = (bf16[128,960]{1,0:T(8,128)(2,1)S(1)}, f32[128,960]{1,0:T(8,128)}, bf16[1024,128]{1,0:T(8,128)(2,1)}, f32[128,2560]{1,0:T(8,128)}, f32[128,2560]{1,0:T(8,128)}, /*index=5*/bf16[2560,128]{1,0:T(8,128)(2,1)}) custom-call(bf16[960,128]{1,0:T(8,128)(2,1)S(1)} %constant_dynamic-update-slice_fusion.10.mixed_ref, bf16[128,960]{1,0:T(8,128)(2,1)S(1)} %bitcast.201, ...), custom_call_target="tpu_custom_call" | custom-call | flops 2200000000 | bytes 22000000 | tf_op jit(solution)/shard_map/feed/pallas_call | solution.py:433
  226.3 4.9 collective-permute-done.28
  231.6 4.8 collective-permute-done.29
  240.3 3.0 collective-permute-done.30
  246.2 5.6 collective-permute-done.31
  256.4 8.9 %collective-permute-done.33 = bf16[8,128,384]{2,1,0:T(8,128)(2,1)S(1)} collective-permute-done((bf16[8,128,384]{2,1,0:T(8,128)(2,1)S(1)}, bf16[8,128,384]{2,1,0:T(8,128)(2,1)S(1)}, u32[]{:S(2)}, u32[]{:S(2)}) %collective-permute-start.33) | collective-permute-done | bytes 786464 | tf_op jit(solution)/shard_map/ppermute | solution.py:57
  265.9 8.6 %attend.3 = (bf16[576,128]{1,0:T(8,128)(2,1)S(1)}, f32[3,1,384]{2,1,0:T(1,128)S(1)}) custom-call(s32[65]{0:T(128)S(1)} %pad_add_fusion.2.need_ref, bf16[576,128]{1,0:T(8,128)(2,1)S(1)} %slice_select_fusion.2.qt_ref, bf16[4096,384]{1,0:T(8,128)(2,1)S(1)} %bitcast.204, f32[4096,128]{1,0:T(8,128)S(1)} %copy-done.12), custom_call_target="tpu_custom_call" | custom-call | flops 2400000000 | bytes 6000000 | tf_op jit(solution)/shard_map/attend/pallas_call | solution.py:327
  276.9 10.0 %feed.3 = (bf16[128,960]{1,0:T(8,128)(2,1)S(1)}, f32[128,960]{1,0:T(8,128)S(1)}, bf16[1024,128]{1,0:T(8,128)(2,1)S(1)}, f32[128,2560]{1,0:T(8,128)S(1)}, f32[128...) custom-call(bf16[960,128]{1,0:T(8,128)(2,1)S(1)} %maximum_select_fusion.2.mixed_ref.refs_6_, ...), custom_call_target="tpu_custom_call" | custom-call | flops 2200000000 | bytes 22000000 | tf_op jit(solution)/shard_map/feed/pallas_call | solution.py:433
  289.4 15.4 %feed_back.2 = (bf16[128,2560]{1,0:T(8,128)(2,1)}, bf16[128,2560]{1,0:T(8,128)(2,1)}, f32[128,960]{1,0:T(8,128)S(1)}, bf16[128,1024]{1,0:T(8,128)(2,1)}, f32[1,9...) custom-call(f32[128,960]{1,0:T(8,128)S(1)} %bitcast.199, ...), custom_call_target="tpu_custom_call" | custom-call | flops 2200000000 | bytes 22000000 | tf_op jit(solution)/shard_map/feed_back/pallas_call | solution.py:524
  308.4 15.2 %attend_back.2 = (bf16[4096,384]{1,0:T(8,128)(2,1)S(1)}, f32[576,128]{1,0:T(8,128)S(1)}) custom-call(s32[65]{0:T(128)S(1)} %pad_add_fusion.2.need_ref, bf16[576,128]{1,0:T(8,128)(2,1)S(1)} %slice_select_fusion.2.qt_ref, bf16[4096,384]{1,0:T(8,128)(2,1)} %bitcast.205, f32[4096,128]{1,0:T(8,128)S(1)} %copy-done.13, f32[576,128]{1,0:T(8,128)S(1)} %slice_select_fusion.1.dot_ref, ...), custom_call_target="tpu_custom_call" | custom-call | flops 6000000000 | bytes 10000000 | tf_op jit(solution)/shard_map/attend_back/pallas_call | solution.py:589
  324.1 13.1 %collective-permute-done.41 = bf16[8,128,384]{2,1,0:T(8,128)(2,1)S(1)} collective-permute-done((bf16[8,128,384]{2,1,0:T(8,128)(2,1)S(1)}, bf16[8,128,384]{2,1,0:T(8,128)(2,1)S(1)}, u32[]{:S(2)}, u32[]{:S(2)}) %collective-permute-start.41) | collective-permute-done | bytes 786464 | tf_op jit(solution)/shard_map/ppermute | solution.py:57
  337.9 7.4 %collective-permute-done.42 = bf16[4,128,384]{2,1,0:T(8,128)(2,1)S(1)} collective-permute-done((bf16[4,128,384]{2,1,0:T(8,128)(2,1)S(1)}, bf16[4,128,384]{2,1,0:T(8,128)(2,1)S(1)}, u32[]{:S(2)}, u32[]{:S(2)}) %collective-permute-start.42) | collective-permute-done | bytes 393248 | tf_op jit(solution)/shard_map/ppermute | solution.py:57
  345.8 8.3 %collective-permute-start.39 = (bf16[2,128,384]{2,1,0:T(8,128)(2,1)S(1)}, bf16[2,128,384]{2,1,0:T(8,128)(2,1)S(1)}, u32[]{:S(2)}, u32[]{:S(2)}) collective-permute-start(bf16[2,128,384]{2,1,0:T(8,128)(2,1)S(1)} %slice.571), channel_id=1, source_target_pairs={{0,48},{1,49},{2,50},{3,51},{4,52},{5,53},{6,54},{7,55},{8,56},{9,... | collective-permute-start | bytes 589832 | tf_op jit(solution)/shard_map/ppermute | solution.py:57
  354.6 3.0 collective-permute-done.39
  368.0 4.2 project_back.2
  375.8 14.4 %feed_back.3 = (bf16[128,2560]{1,0:T(8,128)(2,1)S(1)}, bf16[128,2560]{1,0:T(8,128)(2,1)S(1)}, f32[128,960]{1,0:T(8,128)S(1)}, bf16[128,1024]{1,0:T(8,128)(2,1)S(...) custom-call(f32[128,960]{1,0:T(8,128)S(1)} %convert_select_fusion.c_ref, ...), custom_call_target="tpu_custom_call" | custom-call | flops 2200000000 | bytes 22000000 | tf_op jit(solution)/shard_map/feed_back/pallas_call | solution.py:524
  394.9 15.2 %attend_back.3 = (bf16[4096,384]{1,0:T(8,128)(2,1)S(1)}, f32[576,128]{1,0:T(8,128)S(1)}) custom-call(s32[65]{0:T(128)S(1)} %pad_add_fusion.2.need_ref, bf16[576,128]{1,0:T(8,128)(2,1)S(1)} %copy-done.46, bf16[4096,384]{1,0:T(8,128)(2,1)} %bitcast.203, f32[4096,128]{1,0:T(8,128)S(1)} %copy-done.13, f32[576,128]{1,0:T(8,128)S(1)} %slice_select_fusion.dot_ref, ...), custom_call_target="tpu_custom_call" | custom-call | flops 6000000000 | bytes 10000000 | tf_op jit(solution)/shard_map/attend_back/pallas_call | solution.py:589
  417.5 7.7 %outer_early.1 = (bf16[2,4,4,432,128]{4,3,2,1,0:T(8,128)(2,1)}, bf16[2,4,4,432,128]{4,3,2,1,0:T(8,128)(2,1)}, bf16[2,4,4,416,128]{4,3,2,1,0:T(8,128)(2,1)S(1)}, ...) custom-call(s32[12]{0:T(128)S(1)} %pad_add_fusion.5.slot_ref, ...), custom_call_target="tpu_custom_call" | custom-call | flops 1300000000 | bytes 12000000 | tf_op jit(solution)/shard_map/outer_early/pallas_call | solution.py:816
  428.2 3.4 collective-permute-start.55
  431.7 5.6 collective-permute-done.55
  439.6 3.1 collective-permute-start.53
  452.1 3.4 collective-permute-done.58
  458.9 3.5 project_back.3
  471.9 7.5 %outer_late.1 = (bf16[2,4,4,432,128]{4,3,2,1,0:T(8,128)(2,1)}, bf16[2,4,4,432,128]{4,3,2,1,0:T(8,128)(2,1)}, bf16[2,4,4,416,128]{4,3,2,1,0:T(8,128)(2,1)S(1)}, b...) custom-call(s32[12]{0:T(128)S(1)} %pad_add_fusion.5.slot_ref, ...), custom_call_target="tpu_custom_call", output_to_operand_aliasing={{0}: (9, {}), {1}: (10, {}), {2}: (11, {}), {3}: (12, {}), ... | custom-call | flops 1300000000 | bytes 12000000 | tf_op jit(solution)/shard_map/outer_late/pallas_call | solution.py:816
  479.4 14.8 %collective-permute-start.72 = (bf16[2,4,4,416,128]{4,3,2,1,0:T(8,128)(2,1)}, bf16[2,4,4,416,128]{4,3,2,1,0:T(8,128)(2,1)S(1)}, u32[]{:S(2)}, u32[]{:S(2)}) collective-permute-start(bf16[2,4,4,416,128]{4,3,2,1,0:T(8,128)(2,1)} %get-tuple-element.150), channel_id=1, source_target_pairs={{0,3},{1,2},{2,1},{3,0},{4,7},{5,6},{6,5},{7,4},{8,11},{9,10},{10,... | collective-permute-start | bytes 10223624 | tf_op jit(solution)/shard_map/ppermute | solution.py:57
  494.3 38.3 %collective-permute-done.72 = bf16[2,4,4,416,128]{4,3,2,1,0:T(8,128)(2,1)S(1)} collective-permute-done((bf16[2,4,4,416,128]{4,3,2,1,0:T(8,128)(2,1)}, bf16[2,4,4,416,128]{4,3,2,1,0:T(8,128)(2,1)S(1)}, u32[]{:S(2)}, u32[]{:S(2)}) %collective-permute-start.72) | collective-permute-done | bytes 3407904 | tf_op jit(solution)/shard_map/ppermute | solution.py:57
  533.5 3.6 collective-permute-done.66
  540.9 14.4 %collective-permute-done.73 = bf16[4,4,416,128]{3,2,1,0:T(8,128)(2,1)S(1)} collective-permute-done((bf16[4,4,416,128]{3,2,1,0:T(8,128)(2,1)S(1)}, bf16[4,4,416,128]{3,2,1,0:T(8,128)(2,1)S(1)}, u32[]{:S(2)}, u32[]{:S(2)}) %collective-permute-start.73) | collective-permute-done | bytes 1703968 | tf_op jit(solution)/shard_map/ppermute | solution.py:57
  555.9 4.8 collective-permute-done.67
  562.7 5.7 collective-permute-done.61
  586.7 4.5 collective-permute-done.76
  (494 shorter events, 206.5 us)
Async XLA Ops:
  7.2 197.8 %all-gather.3.cloned.1.call-start = ((), (), s32[]{:S(2)}) async-start(), calls=%async_computation | async-start | bytes 21299200 | tf_op jit(solution)/shard_map/all_gather | solution.py:893
  22.7 12.0 %collective-permute-start.1 = (bf16[2,1296,128]{2,1,0:T(8,128)(2,1)S(1)}, bf16[2,1296,128]{2,1,0:T(8,128)(2,1)S(1)}, u32[]{:S(2)}, u32[]{:S(2)}) collective-permute-start(bf16[2,1296,128]{2,1,0:T(8,128)(2,1)S(1)} %pad_maximum_fusion.10), channel_id=1, source_target_pairs={{0,48},{1,49},{2,50},{3,51},{4,52},{5,53},{6,54},{7,55},{8,56},{9,... | collective-permute-start | bytes 1990664 | tf_op jit(solution)/shard_map/ppermute | solution.py:57
  50.9 9.7 %collective-permute-start.7 = (bf16[2,640,128]{2,1,0:T(8,128)(2,1)S(1)}, bf16[2,640,128]{2,1,0:T(8,128)(2,1)S(1)}, u32[]{:S(2)}, u32[]{:S(2)}) collective-permute-start(bf16[2,640,128]{2,1,0:T(8,128)(2,1)S(1)} %pad_maximum_fusion.18), channel_id=1, source_target_pairs={{0,12},{1,13},{2,14},{3,15},{4,8},{5,9},{6,10},{7,11},{8,4},{9,5},... | collective-permute-start | bytes 983048 | tf_op jit(solution)/shard_map/ppermute | solution.py:57
  53.1 12.6 %collective-permute-start.3 = (bf16[2,656,128]{2,1,0:T(8,128)(2,1)S(1)}, bf16[2,656,128]{2,1,0:T(8,128)(2,1)S(1)}, u32[]{:S(2)}, u32[]{:S(2)}) collective-permute-start(bf16[2,656,128]{2,1,0:T(8,128)(2,1)S(1)} %pad_maximum_fusion.17), channel_id=1, source_target_pairs={{0,3},{1,2},{2,1},{3,0},{4,7},{5,6},{6,5},{7,4},{8,11},{9,10},{10,... | collective-permute-start | bytes 1007624 | tf_op jit(solution)/shard_map/ppermute | solution.py:57
  60.7 11.4 %collective-permute-start.8 = (bf16[4,640,128]{2,1,0:T(8,128)(2,1)S(1)}, bf16[4,640,128]{2,1,0:T(8,128)(2,1)S(1)}, u32[]{:S(2)}, u32[]{:S(2)}) collective-permute-start(bf16[4,640,128]{2,1,0:T(8,128)(2,1)S(1)} %pad_maximum_fusion.11), channel_id=1, source_target_pairs={{0,1},{1,0},{2,3},{3,2},{4,5},{5,4},{6,7},{7,6},{8,9},{9,8},{10,11... | collective-permute-start | bytes 1966088 | tf_op jit(solution)/shard_map/ppermute | solution.py:57
  65.8 25.6 %collective-permute-start.4 = (bf16[4,656,128]{2,1,0:T(8,128)(2,1)S(1)}, bf16[4,656,128]{2,1,0:T(8,128)(2,1)S(1)}, u32[]{:S(2)}, u32[]{:S(2)}) collective-permute-start(bf16[4,656,128]{2,1,0:T(8,128)(2,1)S(1)} %pad_maximum_fusion.9), channel_id=1, source_target_pairs={{0,4},{1,5},{2,6},{3,7},{4,0},{5,1},{6,2},{7,3},{8,12},{9,13},{10,... | collective-permute-start | bytes 2015240 | tf_op jit(solution)/shard_map/ppermute | solution.py:57
  73.4 29.0 %collective-permute-start.9 = (bf16[8,640,128]{2,1,0:T(8,128)(2,1)}, bf16[8,640,128]{2,1,0:T(8,128)(2,1)}, u32[]{:S(2)}, u32[]{:S(2)}) collective-permute-start(bf16[8,640,128]{2,1,0:T(8,128)(2,1)} %pad_maximum_fusion.4), channel_id=1, source_target_pairs={{0,3},{1,2},{2,1},{3,0},{4,7},{5,6},{6,5},{7,4},{8,11},{9,10},{10,... | collective-permute-start | bytes 3932168 | tf_op jit(solution)/shard_map/ppermute | solution.py:57
  92.6 29.3 %collective-permute-start.5 = (bf16[8,656,128]{2,1,0:T(8,128)(2,1)}, bf16[8,656,128]{2,1,0:T(8,128)(2,1)}, u32[]{:S(2)}, u32[]{:S(2)}) collective-permute-start(bf16[8,656,128]{2,1,0:T(8,128)(2,1)} %pad_maximum_fusion.2), channel_id=1, source_target_pairs={{0,12},{1,13},{2,14},{3,15},{4,8},{5,9},{6,10},{7,11},{8,4},{9,5},... | collective-permute-start | bytes 4030472 | tf_op jit(solution)/shard_map/ppermute | solution.py:57
  130.8 9.1 %collective-permute-start.15 = (bf16[128,384]{1,0:T(8,128)(2,1)S(1)}, bf16[128,384]{1,0:T(8,128)(2,1)S(1)}, u32[]{:S(2)}, u32[]{:S(2)}) collective-permute-start(bf16[128,384]{1,0:T(8,128)(2,1)S(1)} %slice_select_fusion.5), channel_id=1, source_target_pairs={{0,2},{1,3},{2,0},{3,1},{4,6},{5,7},{6,4},{7,5},{8,10},{9,11},{10,... | collective-permute-start | bytes 294920 | tf_op jit(solution)/shard_map/ppermute | solution.py:57
  130.9 9.0 %collective-permute-start.12 = (bf16[1,128,384]{2,1,0:T(8,128)(2,1)S(1)}, bf16[1,128,384]{2,1,0:T(8,128)(2,1)S(1)}, u32[]{:S(2)}, u32[]{:S(2)}) collective-permute-start(bf16[1,128,384]{2,1,0:T(8,128)(2,1)S(1)} %bitcast.255), channel_id=1, source_target_pairs={{0,16},{1,17},{2,18},{3,19},{4,20},{5,21},{6,22},{7,23},{8,24},{9,... | collective-permute-start | bytes 294920 | tf_op jit(solution)/shard_map/ppermute | solution.py:57
  140.0 15.4 %collective-permute-start.13 = (bf16[2,128,384]{2,1,0:T(8,128)(2,1)S(1)}, bf16[2,128,384]{2,1,0:T(8,128)(2,1)S(1)}, u32[]{:S(2)}, u32[]{:S(2)}) collective-permute-start(bf16[2,128,384]{2,1,0:T(8,128)(2,1)S(1)} %pad_maximum_fusion.20), channel_id=1, source_target_pairs={{0,48},{1,49},{2,50},{3,51},{4,52},{5,53},{6,54},{7,55},{8,56},{9,... | collective-permute-start | bytes 589832 | tf_op jit(solution)/shard_map/ppermute | solution.py:57
  146.9 11.1 %collective-permute-start.17 = (bf16[2,128,384]{2,1,0:T(8,128)(2,1)S(1)}, bf16[2,128,384]{2,1,0:T(8,128)(2,1)S(1)}, u32[]{:S(2)}, u32[]{:S(2)}) collective-permute-start(bf16[2,128,384]{2,1,0:T(8,128)(2,1)S(1)} %pad_maximum_fusion.21), channel_id=1, source_target_pairs={{0,12},{1,13},{2,14},{3,15},{4,8},{5,9},{6,10},{7,11},{8,4},{9,5},... | collective-permute-start | bytes 589832 | tf_op jit(solution)/shard_map/ppermute | solution.py:57
  156.1 13.5 %collective-permute-start.14 = (bf16[4,128,384]{2,1,0:T(8,128)(2,1)}, bf16[4,128,384]{2,1,0:T(8,128)(2,1)}, u32[]{:S(2)}, u32[]{:S(2)}) collective-permute-start(bf16[4,128,384]{2,1,0:T(8,128)(2,1)} %pad_maximum_fusion.13), channel_id=1, source_target_pairs={{0,4},{1,5},{2,6},{3,7},{4,0},{5,1},{6,2},{7,3},{8,12},{9,13},{10,... | collective-permute-start | bytes 1179656 | tf_op jit(solution)/shard_map/ppermute | solution.py:57
  159.5 12.1 %collective-permute-start.18 = (bf16[4,128,384]{2,1,0:T(8,128)(2,1)}, bf16[4,128,384]{2,1,0:T(8,128)(2,1)}, u32[]{:S(2)}, u32[]{:S(2)}) collective-permute-start(bf16[4,128,384]{2,1,0:T(8,128)(2,1)} %pad_maximum_fusion.14), channel_id=1, source_target_pairs={{0,16},{1,17},{2,18},{3,19},{4,20},{5,21},{6,22},{7,23},{8,24},{9,... | collective-permute-start | bytes 1179656 | tf_op jit(solution)/shard_map/ppermute | solution.py:57
  173.8 13.8 %collective-permute-start.20 = (bf16[8,128,384]{2,1,0:T(8,128)(2,1)}, bf16[8,128,384]{2,1,0:T(8,128)(2,1)}, u32[]{:S(2)}, u32[]{:S(2)}) collective-permute-start(bf16[8,128,384]{2,1,0:T(8,128)(2,1)} %pad_maximum_fusion.6), channel_id=1, source_target_pairs={{0,48},{1,49},{2,50},{3,51},{4,52},{5,53},{6,54},{7,55},{8,56},{9,... | collective-permute-start | bytes 2359304 | tf_op jit(solution)/shard_map/ppermute | solution.py:57
  177.3 13.5 %collective-permute-start.19 = (bf16[8,128,384]{2,1,0:T(8,128)(2,1)}, bf16[8,128,384]{2,1,0:T(8,128)(2,1)}, u32[]{:S(2)}, u32[]{:S(2)}) collective-permute-start(bf16[8,128,384]{2,1,0:T(8,128)(2,1)} %pad_maximum_fusion.5), channel_id=1, source_target_pairs={{0,12},{1,13},{2,14},{3,15},{4,8},{5,9},{6,10},{7,11},{8,4},{9,5},... | collective-permute-start | bytes 2359304 | tf_op jit(solution)/shard_map/ppermute | solution.py:57
  238.2 7.9 %collective-permute-start.27 = (bf16[4,128,384]{2,1,0:T(8,128)(2,1)S(1)}, bf16[4,128,384]{2,1,0:T(8,128)(2,1)S(1)}, u32[]{:S(2)}, u32[]{:S(2)}) collective-permute-start(bf16[4,128,384]{2,1,0:T(8,128)(2,1)S(1)} %pad_maximum_fusion.15), channel_id=1, source_target_pairs={{0,4},{1,5},{2,6},{3,7},{4,0},{5,1},{6,2},{7,3},{8,12},{9,13},{10,... | collective-permute-start | bytes 1179656 | tf_op jit(solution)/shard_map/ppermute | solution.py:57
  243.4 8.4 %collective-permute-start.31 = (bf16[4,128,384]{2,1,0:T(8,128)(2,1)S(1)}, bf16[4,128,384]{2,1,0:T(8,128)(2,1)S(1)}, u32[]{:S(2)}, u32[]{:S(2)}) collective-permute-start(bf16[4,128,384]{2,1,0:T(8,128)(2,1)S(1)} %pad_maximum_fusion.16), channel_id=1, source_target_pairs={{0,16},{1,17},{2,18},{3,19},{4,20},{5,21},{6,22},{7,23},{8,24},{9,... | collective-permute-start | bytes 1179656 | tf_op jit(solution)/shard_map/ppermute | solution.py:57
  251.9 13.3 %collective-permute-start.33 = (bf16[8,128,384]{2,1,0:T(8,128)(2,1)S(1)}, bf16[8,128,384]{2,1,0:T(8,128)(2,1)S(1)}, u32[]{:S(2)}, u32[]{:S(2)}) collective-permute-start(bf16[8,128,384]{2,1,0:T(8,128)(2,1)S(1)} %pad_maximum_fusion.8), channel_id=1, source_target_pairs={{0,48},{1,49},{2,50},{3,51},{4,52},{5,53},{6,54},{7,55},{8,56},{9,... | collective-permute-start | bytes 2359304 | tf_op jit(solution)/shard_map/ppermute | solution.py:57
  252.0 13.3 %collective-permute-start.32 = (bf16[8,128,384]{2,1,0:T(8,128)(2,1)S(1)}, bf16[8,128,384]{2,1,0:T(8,128)(2,1)S(1)}, u32[]{:S(2)}, u32[]{:S(2)}) collective-permute-start(bf16[8,128,384]{2,1,0:T(8,128)(2,1)S(1)} %pad_maximum_fusion.7), channel_id=1, source_target_pairs={{0,12},{1,13},{2,14},{3,15},{4,8},{5,9},{6,10},{7,11},{8,4},{9,5},... | collective-permute-start | bytes 2359304 | tf_op jit(solution)/shard_map/ppermute | solution.py:57
  323.9 13.3 %collective-permute-start.41 = (bf16[8,128,384]{2,1,0:T(8,128)(2,1)S(1)}, bf16[8,128,384]{2,1,0:T(8,128)(2,1)S(1)}, u32[]{:S(2)}, u32[]{:S(2)}) collective-permute-start(bf16[8,128,384]{2,1,0:T(8,128)(2,1)S(1)} %bitcast.276), channel_id=1, source_target_pairs={{0,48},{1,49},{2,50},{3,51},{4,52},{5,53},{6,54},{7,55},{8,56},{9,... | collective-permute-start | bytes 2359304 | tf_op jit(solution)/shard_map/ppermute | solution.py:57
  324.0 13.5 %collective-permute-start.37 = (bf16[8,128,384]{2,1,0:T(8,128)(2,1)S(1)}, bf16[8,128,384]{2,1,0:T(8,128)(2,1)S(1)}, u32[]{:S(2)}, u32[]{:S(2)}) collective-permute-start(bf16[8,128,384]{2,1,0:T(8,128)(2,1)S(1)} %bitcast.275), channel_id=1, source_target_pairs={{0,12},{1,13},{2,14},{3,15},{4,8},{5,9},{6,10},{7,11},{8,4},{9,5},... | collective-permute-start | bytes 2359304 | tf_op jit(solution)/shard_map/ppermute | solution.py:57
  337.4 7.9 %collective-permute-start.42 = (bf16[4,128,384]{2,1,0:T(8,128)(2,1)S(1)}, bf16[4,128,384]{2,1,0:T(8,128)(2,1)S(1)}, u32[]{:S(2)}, u32[]{:S(2)}) collective-permute-start(bf16[4,128,384]{2,1,0:T(8,128)(2,1)S(1)} %slice.575), channel_id=1, source_target_pairs={{0,16},{1,17},{2,18},{3,19},{4,20},{5,21},{6,22},{7,23},{8,24},{9,... | collective-permute-start | bytes 1179656 | tf_op jit(solution)/shard_map/ppermute | solution.py:57
  337.8 7.9 %collective-permute-start.38 = (bf16[4,128,384]{2,1,0:T(8,128)(2,1)S(1)}, bf16[4,128,384]{2,1,0:T(8,128)(2,1)S(1)}, u32[]{:S(2)}, u32[]{:S(2)}) collective-permute-start(bf16[4,128,384]{2,1,0:T(8,128)(2,1)S(1)} %slice.569), channel_id=1, source_target_pairs={{0,4},{1,5},{2,6},{3,7},{4,0},{5,1},{6,2},{7,3},{8,12},{9,13},{10,... | collective-permute-start | bytes 1179656 | tf_op jit(solution)/shard_map/ppermute | solution.py:57
  345.4 8.6 %collective-permute-start.43 = (bf16[2,128,384]{2,1,0:T(8,128)(2,1)S(1)}, bf16[2,128,384]{2,1,0:T(8,128)(2,1)S(1)}, u32[]{:S(2)}, u32[]{:S(2)}) collective-permute-start(bf16[2,128,384]{2,1,0:T(8,128)(2,1)S(1)} %slice.577), channel_id=1, source_target_pairs={{0,12},{1,13},{2,14},{3,15},{4,8},{5,9},{6,10},{7,11},{8,4},{9,5},... | collective-permute-start | bytes 589832 | tf_op jit(solution)/shard_map/ppermute | solution.py:57
  345.8 11.9 %collective-permute-start.39 = (bf16[2,128,384]{2,1,0:T(8,128)(2,1)S(1)}, bf16[2,128,384]{2,1,0:T(8,128)(2,1)S(1)}, u32[]{:S(2)}, u32[]{:S(2)}) collective-permute-start(bf16[2,128,384]{2,1,0:T(8,128)(2,1)S(1)} %slice.571), channel_id=1, source_target_pairs={{0,48},{1,49},{2,50},{3,51},{4,52},{5,53},{6,54},{7,55},{8,56},{9,... | collective-permute-start | bytes 589832 | tf_op jit(solution)/shard_map/ppermute | solution.py:57
  358.9 7.5 %collective-permute-start.36 = (f32[384,128]{1,0:T(8,128)S(1)}, f32[384,128]{1,0:T(8,128)S(1)}, u32[]{:S(2)}, u32[]{:S(2)}) collective-permute-start(f32[384,128]{1,0:T(8,128)S(1)} %slice.448), channel_id=1, source_target_pairs={{0,64},{1,65},{2,66},{3,67},{4,68},{5,69},{6,70},{7,71},{8,72},{9,... | collective-permute-start | bytes 589832 | tf_op jit(solution)/shard_map/ppermute | solution.py:61
  411.9 13.5 %collective-permute-start.50 = (bf16[8,128,384]{2,1,0:T(8,128)(2,1)}, bf16[8,128,384]{2,1,0:T(8,128)(2,1)}, u32[]{:S(2)}, u32[]{:S(2)}) collective-permute-start(bf16[8,128,384]{2,1,0:T(8,128)(2,1)} %bitcast.53), channel_id=1, source_target_pairs={{0,12},{1,13},{2,14},{3,15},{4,8},{5,9},{6,10},{7,11},{8,4},{9,5},... | collective-permute-start | bytes 2359304 | tf_op jit(solution)/shard_map/ppermute | solution.py:57
  411.9 14.9 %collective-permute-start.51 = (bf16[8,128,384]{2,1,0:T(8,128)(2,1)}, bf16[8,128,384]{2,1,0:T(8,128)(2,1)}, u32[]{:S(2)}, u32[]{:S(2)}) collective-permute-start(bf16[8,128,384]{2,1,0:T(8,128)(2,1)} %bitcast.55), channel_id=1, source_target_pairs={{0,48},{1,49},{2,50},{3,51},{4,52},{5,53},{6,54},{7,55},{8,56},{9,... | collective-permute-start | bytes 2359304 | tf_op jit(solution)/shard_map/ppermute | solution.py:57
  428.2 9.2 %collective-permute-start.55 = (bf16[4,128,384]{2,1,0:T(8,128)(2,1)S(1)}, bf16[4,128,384]{2,1,0:T(8,128)(2,1)S(1)}, u32[]{:S(2)}, u32[]{:S(2)}) collective-permute-start(bf16[4,128,384]{2,1,0:T(8,128)(2,1)S(1)} %slice.484), channel_id=1, source_target_pairs={{0,16},{1,17},{2,18},{3,19},{4,20},{5,21},{6,22},{7,23},{8,24},{9,... | collective-permute-start | bytes 1179656 | tf_op jit(solution)/shard_map/ppermute | solution.py:57
  431.6 7.9 %collective-permute-start.52 = (bf16[4,128,384]{2,1,0:T(8,128)(2,1)S(1)}, bf16[4,128,384]{2,1,0:T(8,128)(2,1)S(1)}, u32[]{:S(2)}, u32[]{:S(2)}) collective-permute-start(bf16[4,128,384]{2,1,0:T(8,128)(2,1)S(1)} %slice.478), channel_id=1, source_target_pairs={{0,4},{1,5},{2,6},{3,7},{4,0},{5,1},{6,2},{7,3},{8,12},{9,13},{10,... | collective-permute-start | bytes 1179656 | tf_op jit(solution)/shard_map/ppermute | solution.py:57
  439.6 7.7 %collective-permute-start.53 = (bf16[2,128,384]{2,1,0:T(8,128)(2,1)S(1)}, bf16[2,128,384]{2,1,0:T(8,128)(2,1)S(1)}, u32[]{:S(2)}, u32[]{:S(2)}) collective-permute-start(bf16[2,128,384]{2,1,0:T(8,128)(2,1)S(1)} %slice.582), channel_id=1, source_target_pairs={{0,48},{1,49},{2,50},{3,51},{4,52},{5,53},{6,54},{7,55},{8,56},{9,... | collective-permute-start | bytes 589832 | tf_op jit(solution)/shard_map/ppermute | solution.py:57
  449.4 7.8 %collective-permute-start.49 = (f32[384,128]{1,0:T(8,128)S(1)}, f32[384,128]{1,0:T(8,128)S(1)}, u32[]{:S(2)}, u32[]{:S(2)}) collective-permute-start(f32[384,128]{1,0:T(8,128)S(1)} %slice.470), channel_id=1, source_target_pairs={{64,0},{65,1},{66,2},{67,3},{68,4},{69,5},{70,6},{71,7},{72,8},{73... | collective-permute-start | bytes 589832 | tf_op jit(solution)/shard_map/ppermute | solution.py:61
  479.4 53.1 %collective-permute-start.72 = (bf16[2,4,4,416,128]{4,3,2,1,0:T(8,128)(2,1)}, bf16[2,4,4,416,128]{4,3,2,1,0:T(8,128)(2,1)S(1)}, u32[]{:S(2)}, u32[]{:S(2)}) collective-permute-start(bf16[2,4,4,416,128]{4,3,2,1,0:T(8,128)(2,1)} %get-tuple-element.150), channel_id=1, source_target_pairs={{0,3},{1,2},{2,1},{3,0},{4,7},{5,6},{6,5},{7,4},{8,11},{9,10},{10,... | collective-permute-start | bytes 10223624 | tf_op jit(solution)/shard_map/ppermute | solution.py:57
  494.3 42.9 %collective-permute-start.66 = (bf16[2,4,4,432,128]{4,3,2,1,0:T(8,128)(2,1)}, bf16[2,4,4,432,128]{4,3,2,1,0:T(8,128)(2,1)S(1)}, u32[]{:S(2)}, u32[]{:S(2)}) collective-permute-start(bf16[2,4,4,432,128]{4,3,2,1,0:T(8,128)(2,1)} %get-tuple-element.148), channel_id=1, source_target_pairs={{0,12},{1,13},{2,14},{3,15},{4,8},{5,9},{6,10},{7,11},{8,4},{9,5},... | collective-permute-start | bytes 10616840 | tf_op jit(solution)/shard_map/ppermute | solution.py:57
  494.3 43.9 %collective-permute-start.60 = (bf16[2,4,4,432,128]{4,3,2,1,0:T(8,128)(2,1)}, bf16[2,4,4,432,128]{4,3,2,1,0:T(8,128)(2,1)S(1)}, u32[]{:S(2)}, u32[]{:S(2)}) collective-permute-start(bf16[2,4,4,432,128]{4,3,2,1,0:T(8,128)(2,1)} %get-tuple-element.146), channel_id=1, source_target_pairs={{0,48},{1,49},{2,50},{3,51},{4,52},{5,53},{6,54},{7,55},{8,56},{9,... | collective-permute-start | bytes 10616840 | tf_op jit(solution)/shard_map/ppermute | solution.py:57
  533.4 21.9 %collective-permute-start.73 = (bf16[4,4,416,128]{3,2,1,0:T(8,128)(2,1)S(1)}, bf16[4,4,416,128]{3,2,1,0:T(8,128)(2,1)S(1)}, u32[]{:S(2)}, u32[]{:S(2)}) collective-permute-start(bf16[4,4,416,128]{3,2,1,0:T(8,128)(2,1)S(1)} %get-tuple-element.184), channel_id=1, source_target_pairs={{0,1},{1,0},{2,3},{3,2},{4,5},{5,4},{6,7},{7,6},{8,9},{9,8},{10,11... | collective-permute-start | bytes 5111816 | tf_op jit(solution)/shard_map/ppermute | solution.py:57
  538.1 22.6 %collective-permute-start.67 = (bf16[4,4,432,128]{3,2,1,0:T(8,128)(2,1)S(1)}, bf16[4,4,432,128]{3,2,1,0:T(8,128)(2,1)S(1)}, u32[]{:S(2)}, u32[]{:S(2)}) collective-permute-start(bf16[4,4,432,128]{3,2,1,0:T(8,128)(2,1)S(1)} %get-tuple-element.182), channel_id=1, source_target_pairs={{0,4},{1,5},{2,6},{3,7},{4,0},{5,1},{6,2},{7,3},{8,12},{9,13},{10,... | collective-permute-start | bytes 5308424 | tf_op jit(solution)/shard_map/ppermute | solution.py:57
  540.1 28.3 %collective-permute-start.61 = (bf16[4,4,432,128]{3,2,1,0:T(8,128)(2,1)S(1)}, bf16[4,4,432,128]{3,2,1,0:T(8,128)(2,1)S(1)}, u32[]{:S(2)}, u32[]{:S(2)}) collective-permute-start(bf16[4,4,432,128]{3,2,1,0:T(8,128)(2,1)S(1)} %get-tuple-element.180), channel_id=1, source_target_pairs={{0,16},{1,17},{2,18},{3,19},{4,20},{5,21},{6,22},{7,23},{8,24},{9,... | collective-permute-start | bytes 5308424 | tf_op jit(solution)/shard_map/ppermute | solution.py:57
  555.8 16.8 %collective-permute-start.74 = (bf16[2,4,416,128]{3,2,1,0:T(8,128)(2,1)S(1)}, bf16[2,4,416,128]{3,2,1,0:T(8,128)(2,1)S(1)}, u32[]{:S(2)}, u32[]{:S(2)}) collective-permute-start(bf16[2,4,416,128]{3,2,1,0:T(8,128)(2,1)S(1)} %get-tuple-element.190), channel_id=1, source_target_pairs={{0,48},{1,49},{2,50},{3,51},{4,52},{5,53},{6,54},{7,55},{8,56},{9,... | collective-permute-start | bytes 2555912 | tf_op jit(solution)/shard_map/ppermute | solution.py:57
  562.1 14.6 %collective-permute-start.68 = (bf16[2,4,432,128]{3,2,1,0:T(8,128)(2,1)}, bf16[2,4,432,128]{3,2,1,0:T(8,128)(2,1)}, u32[]{:S(2)}, u32[]{:S(2)}) collective-permute-start(bf16[2,4,432,128]{3,2,1,0:T(8,128)(2,1)} %get-tuple-element.188), channel_id=1, source_target_pairs={{0,3},{1,2},{2,1},{3,0},{4,7},{5,6},{6,5},{7,4},{8,11},{9,10},{10,... | collective-permute-start | bytes 2654216 | tf_op jit(solution)/shard_map/ppermute | solution.py:57
  569.8 14.6 %collective-permute-start.62 = (bf16[2,4,432,128]{3,2,1,0:T(8,128)(2,1)}, bf16[2,4,432,128]{3,2,1,0:T(8,128)(2,1)}, u32[]{:S(2)}, u32[]{:S(2)}) collective-permute-start(bf16[2,4,432,128]{3,2,1,0:T(8,128)(2,1)} %get-tuple-element.186), channel_id=1, source_target_pairs={{0,12},{1,13},{2,14},{3,15},{4,8},{5,9},{6,10},{7,11},{8,4},{9,5},... | collective-permute-start | bytes 2654216 | tf_op jit(solution)/shard_map/ppermute | solution.py:57
  572.9 8.3 %collective-permute-start.75 = (bf16[4,416,128]{2,1,0:T(8,128)(2,1)S(1)}, bf16[4,416,128]{2,1,0:T(8,128)(2,1)}, u32[]{:S(2)}, u32[]{:S(2)}) collective-permute-start(bf16[4,416,128]{2,1,0:T(8,128)(2,1)S(1)} %get-tuple-element.204), channel_id=1, source_target_pairs={{0,16},{1,17},{2,18},{3,19},{4,20},{5,21},{6,22},{7,23},{8,24},{9,... | collective-permute-start | bytes 1277960 | tf_op jit(solution)/shard_map/ppermute | solution.py:57
  578.1 13.2 %collective-permute-start.69 = (bf16[4,432,128]{2,1,0:T(8,128)(2,1)S(1)}, bf16[4,432,128]{2,1,0:T(8,128)(2,1)S(1)}, u32[]{:S(2)}, u32[]{:S(2)}) collective-permute-start(bf16[4,432,128]{2,1,0:T(8,128)(2,1)S(1)} %get-tuple-element.202), channel_id=1, source_target_pairs={{0,1},{1,0},{2,3},{3,2},{4,5},{5,4},{6,7},{7,6},{8,9},{9,8},{10,11... | collective-permute-start | bytes 1327112 | tf_op jit(solution)/shard_map/ppermute | solution.py:57
  582.3 8.9 %collective-permute-start.76 = (bf16[2,416,128]{2,1,0:T(8,128)(2,1)S(1)}, bf16[2,416,128]{2,1,0:T(8,128)(2,1)S(1)}, u32[]{:S(2)}, u32[]{:S(2)}) collective-permute-start(bf16[2,416,128]{2,1,0:T(8,128)(2,1)S(1)} %get-tuple-element.211), channel_id=1, source_target_pairs={{0,12},{1,13},{2,14},{3,15},{4,8},{5,9},{6,10},{7,11},{8,4},{9,5},... | collective-permute-start | bytes 638984 | tf_op jit(solution)/shard_map/ppermute | solution.py:57
  585.8 8.4 %collective-permute-start.63 = (bf16[4,432,128]{2,1,0:T(8,128)(2,1)S(1)}, bf16[4,432,128]{2,1,0:T(8,128)(2,1)S(1)}, u32[]{:S(2)}, u32[]{:S(2)}) collective-permute-start(bf16[4,432,128]{2,1,0:T(8,128)(2,1)S(1)} %get-tuple-element.200), channel_id=1, source_target_pairs={{0,4},{1,5},{2,6},{3,7},{4,0},{5,1},{6,2},{7,3},{8,12},{9,13},{10,... | collective-permute-start | bytes 1327112 | tf_op jit(solution)/shard_map/ppermute | solution.py:57
  591.4 7.2 %collective-permute-start.70 = (bf16[2,432,128]{2,1,0:T(8,128)(2,1)S(1)}, bf16[2,432,128]{2,1,0:T(8,128)(2,1)S(1)}, u32[]{:S(2)}, u32[]{:S(2)}) collective-permute-start(bf16[2,432,128]{2,1,0:T(8,128)(2,1)S(1)} %get-tuple-element.209), channel_id=1, source_target_pairs={{0,48},{1,49},{2,50},{3,51},{4,52},{5,53},{6,54},{7,55},{8,56},{9,... | collective-permute-start | bytes 663560 | tf_op jit(solution)/shard_map/ppermute | solution.py:57
  594.3 7.2 %collective-permute-start.64 = (bf16[2,432,128]{2,1,0:T(8,128)(2,1)S(1)}, bf16[2,432,128]{2,1,0:T(8,128)(2,1)S(1)}, u32[]{:S(2)}, u32[]{:S(2)}) collective-permute-start(bf16[2,432,128]{2,1,0:T(8,128)(2,1)S(1)} %get-tuple-element.207), channel_id=1, source_target_pairs={{0,3},{1,2},{2,1},{3,0},{4,7},{5,6},{6,5},{7,4},{8,11},{9,10},{10,... | collective-permute-start | bytes 663560 | tf_op jit(solution)/shard_map/ppermute | solution.py:57
  (116 other events, 984.5 us)
Sparse Core Ops, SparseCore 0:
  34.9 140.0 all-gather.2

commit v8 on v7

--- a/solution.py
+++ b/solution.py
@@ -137,7 +137,6 @@
     block = jnp.concatenate([own, row])[None]
     for number in range(2):
         block = jnp.concatenate([block, swapped(block, along((0, 0), number))])
-    block, own = lax.optimization_barrier((block, own))
     at = slot_of(jnp.arange(4, dtype=jnp.int32) ^ y, phase)
     front = lax.dynamic_index_in_dim(block, at[0], 0, keepdims=False)
     rows = jnp.pad(block[:, ROWS][at], ((0, 12), (0, 0)))
@@ -188,10 +187,6 @@
 def half_swapped(block):
     lane = lane_of(block.shape)
     return jnp.where(lane % HD < HD // 2, pltpu.roll(block, 96, 1), pltpu.roll(block, 32, 1))
-
-
-def qkv_weight(w_ref, c):
-    return w_ref[:, 96 * c : 96 * c + 96, :].reshape(D, 128)
 
 
 def normed_of(u, gain):
@@ -263,7 +258,7 @@
             jax.ShapeDtypeStruct((QPAD, R), bf16),
             jax.ShapeDtypeStruct((R, 768), bf16),
         ],
-        compiler_params=pltpu.CompilerParams(vmem_limit_bytes=48 << 20),
+        compiler_params=pltpu.CompilerParams(vmem_limit_bytes=22 << 20),
         cost_estimate=pl.CostEstimate(flops=400_000_000, bytes_accessed=6_000_000, transcendentals=0),
     )(idx, u, gain, cos, sin, *front)
 
@@ -345,7 +340,7 @@
             jax.ShapeDtypeStruct((QSIDE, R), bf16),
             jax.ShapeDtypeStruct((SIDE, 1, LANES), f32),
         ],
-        compiler_params=pltpu.CompilerParams(vmem_limit_bytes=48 << 20),
+        compiler_params=pltpu.CompilerParams(vmem_limit_bytes=24 << 20),
         cost_estimate=pl.CostEstimate(
             flops=2_400_000_000, bytes_accessed=6_000_000, transcendentals=4_700_000
         ),
@@ -452,7 +447,7 @@
             jax.ShapeDtypeStruct((FF, R), bf16),
         ],
         scratch_shapes=[pltpu.VMEM((R, PADD), bf16), pltpu.VMEM((R, PADD), f32)],
-        compiler_params=pltpu.CompilerParams(vmem_limit_bytes=48 << 20),
+        compiler_params=pltpu.CompilerParams(vmem_limit_bytes=30 << 20),
         cost_estimate=pl.CostEstimate(
             flops=2_200_000_000, bytes_accessed=22_000_000, transcendentals=400_000
         ),
@@ -546,7 +541,7 @@
             jax.ShapeDtypeStruct((R, PADD), bf16),
         ],
         scratch_shapes=[pltpu.VMEM((R, PADD), f32)],
-        compiler_params=pltpu.CompilerParams(vmem_limit_bytes=48 << 20),
+        compiler_params=pltpu.CompilerParams(vmem_limit_bytes=30 << 20),
         cost_estimate=pl.CostEstimate(
             flops=2_200_000_000, bytes_accessed=22_000_000, transcendentals=400_000
         ),
@@ -565,20 +560,18 @@
     both = jnp.concatenate([q, d_o], axis=1)
     dkv_ref[...] = jnp.zeros_like(dkv_ref)
 
-    def fold(pair, acc):
-        for i in (2 * pair, 2 * pair + 1):
-            kv = chunk_of(kv_ref, need_ref, i)
-            b = bias_ref[chunk_rows(i), :]
-            p = jnp.exp(mm(kv, q) + jnp.concatenate([b, b, b], axis=1) - lse)
-            ds = (p * (mm(kv, d_o) - delta)).astype(bf16)
-            part = mm_nt(jnp.concatenate([ds, p.astype(bf16)], axis=1), both).astype(bf16)
-            for k in range(CHUNK // SMALL):
-                at = pl.multiple_of(need_ref[CHUNK // SMALL * i + k] * SMALL, SMALL)
-                dkv_ref[pl.ds(at, SMALL), :] = part[SMALL * k : SMALL * k + SMALL]
-            acc = acc + mm(kv.T, ds)
-        return acc
-
-    acc = lax.fori_loop(0, need_ref[KEYS // SMALL], fold, jnp.zeros((128, LANES), f32))
+    def fold(i, acc):
+        kv = chunk_of(kv_ref, need_ref, i)
+        b = bias_ref[chunk_rows(i), :]
+        p = jnp.exp(mm(kv, q) + jnp.concatenate([b, b, b], axis=1) - lse)
+        ds = (p * (mm(kv, d_o) - delta)).astype(bf16)
+        part = mm_nt(jnp.concatenate([ds, p.astype(bf16)], axis=1), both).astype(bf16)
+        for k in range(CHUNK // SMALL):
+            at = pl.multiple_of(need_ref[CHUNK // SMALL * i + k] * SMALL, SMALL)
+            dkv_ref[pl.ds(at, SMALL), :] = part[SMALL * k : SMALL * k + SMALL]
+        return acc + mm(kv.T, ds)
+
+    acc = lax.fori_loop(0, need_ref[KEYS // SMALL + 1], fold, jnp.zeros((128, LANES), f32))
     acc = acc[:64] * 0.125
     for h in range(GRP):
         dqt_ref[64 * h : 64 * h + 64, :] = acc[:, 128 * h : 128 * h + 128]
@@ -606,7 +599,7 @@
             jax.ShapeDtypeStruct((KEYS, SIDE * 128), bf16),
             jax.ShapeDtypeStruct((QSIDE, R), f32),
         ],
-        compiler_params=pltpu.CompilerParams(vmem_limit_bytes=48 << 20),
+        compiler_params=pltpu.CompilerParams(vmem_limit_bytes=24 << 20),
         cost_estimate=pl.CostEstimate(
             flops=6_000_000_000, bytes_accessed=10_000_000, transcendentals=4_700_000
         ),
@@ -614,7 +607,7 @@
 
 
 def project_back_kernel(
-    dqt_ref, dkv_ref, cos_ref, sin_ref, u_ref, g_ref, dh_ref, w_ref,
+    idx_ref, dqt_ref, dkv_ref, cos_ref, sin_ref, u_ref, g_ref, dh_ref, wa_ref, wb_ref,
     du_ref, dqkv_ref, at_ref, dg_ref,
 ):
     cos, sin = cos_ref[...], sin_ref[...]
@@ -634,11 +627,10 @@
     blocks.append(jnp.where(low, rolled[4], zero))
     da = jnp.zeros((R, D), f32)
     for c in range(0, 13, 2):
+        d, w = blocks[c].astype(bf16), front_weight(idx_ref, wa_ref, wb_ref, c)
         if c + 1 < 13:
-            d = jnp.concatenate([blocks[c], blocks[c + 1]], axis=1).astype(bf16)
-            w = jnp.concatenate([qkv_weight(w_ref, c), qkv_weight(w_ref, c + 1)], axis=1)
-        else:
-            d, w = blocks[c].astype(bf16), qkv_weight(w_ref, c)
+            d = jnp.concatenate([d, blocks[c + 1].astype(bf16)], axis=1)
+            w = jnp.concatenate([w, front_weight(idx_ref, wa_ref, wb_ref, c + 1)], axis=1)
         dqkv_ref[:, 128 * c : 128 * c + d.shape[1]] = d
         da = da + mm_nt(d, w)
     u = u_ref[...].astype(f32)
@@ -650,32 +642,36 @@
     du_ref[...] = dh_ref[...] + d_u
 
 
-def project_back(d_query, d_kv, cos, sin, u, gain, d_hidden, weights):
-    whole = lambda *shape: pl.BlockSpec(shape, lambda j: (0,) * len(shape))
+def project_back(d_query, d_kv, cos, sin, u, gain, d_hidden, idx, front):
+    whole = lambda *shape: pl.BlockSpec(shape, lambda j, idx: (0,) * len(shape))
     return pl.pallas_call(
         project_back_kernel,
         name="project_back",
-        grid=(1,),
-        in_specs=[
-            whole(D, R),
-            whole(R, 640),
-            whole(R, 128),
-            whole(R, 128),
-            whole(R, D),
-            whole(1, D),
-            whole(R, D),
-            whole(10, ROWS, 128),
-        ],
-        out_specs=[whole(R, D), whole(R, 13 * 128), whole(D, R), whole(1, D)],
+        grid_spec=pltpu.PrefetchScalarGridSpec(
+            num_scalar_prefetch=1,
+            grid=(1,),
+            in_specs=[
+                whole(D, R),
+                whole(R, 640),
+                whole(R, 128),
+                whole(R, 128),
+                whole(R, D),
+                whole(1, D),
+                whole(R, D),
+                whole(16, HALF, 128),
+                whole(16, HALF + 16, 128),
+            ],
+            out_specs=[whole(R, D), whole(R, 13 * 128), whole(D, R), whole(1, D)],
+        ),
         out_shape=[
             jax.ShapeDtypeStruct((R, D), f32),
             jax.ShapeDtypeStruct((R, 13 * 128), bf16),
             jax.ShapeDtypeStruct((D, R), bf16),
             jax.ShapeDtypeStruct((1, D), f32),
         ],
-        compiler_params=pltpu.CompilerParams(vmem_limit_bytes=48 << 20),
-        cost_estimate=pl.CostEstimate(flops=400_000_000, bytes_accessed=5_000_000, transcendentals=0),
-    )(d_query, d_kv, cos, sin, u, gain, d_hidden, weights)
+        compiler_params=pltpu.CompilerParams(vmem_limit_bytes=24 << 20),
+        cost_estimate=pl.CostEstimate(flops=400_000_000, bytes_accessed=7_000_000, transcendentals=0),
+    )(idx, d_query, d_kv, cos, sin, u, gain, d_hidden, *front)
 
 
 def outer_steps(begin, end, refs, slot_ref, outs, stage, sems):
@@ -828,7 +824,7 @@
         ),
         out_shape=shapes * 2,
         input_output_aliases={1 + len(args) + i: i for i in range(len(made))},
-        compiler_params=pltpu.CompilerParams(vmem_limit_bytes=48 << 20),
+        compiler_params=pltpu.CompilerParams(vmem_limit_bytes=20 << 20),
         cost_estimate=pl.CostEstimate(
             flops=1_300_000_000, bytes_accessed=12_000_000, transcendentals=0
         ),
@@ -915,7 +911,8 @@
     order_k = jnp.sum(jnp.where(chosen, jnp.arange(64)[None, :], 0), axis=1)
     spot_k = jnp.sum(jnp.where(chosen & seen[None, :], spot_k[None, :], 0), axis=1)
     spot_k = jnp.where(jnp.arange(64) < seen_count, spot_k, 1 << 16)
-    need = jnp.concatenate([order_k, ((seen_count + 15) // 16)[None]]).astype(jnp.int32)
+    turns = jnp.stack([(seen_count + 15) // 16, (seen_count + 7) // 8])
+    need = jnp.concatenate([order_k, turns]).astype(jnp.int32)
     place_k = (spot_k[:, None] * 64 + within[None, :]).reshape(KEYS)
     bias = jnp.where(
         (place_k[:, None] <= place_q[None, :]) & (place_k[:, None] >= start_q[None, :]),
@@ -982,7 +979,7 @@
         d_query = dq_new if tick == 0 else jnp.where(active, dq_new, d_query)
         d_kv = dkv_new if tick == 0 else jnp.where(active, dkv_new, d_kv)
         d_u, dqkv, at, dg_one = project_back(
-            d_query, d_kv, cos, sin, u, gain_one, dh, gathered
+            d_query, d_kv, cos, sin, u, gain_one, dh, idx, front
         )
         if tick == 0:
             cot = jnp.where(first, over(d_u.astype(bf16), 1).astype(f32), cot)

time: 619 us -> 623 us (level); the launches traced: 616 us -> 612 us
  starting transfers between devices: 103 us -> 135 us
  waiting for transfers between devices: 270 us -> 245 us
  Pallas kernels: 125 us -> 104 us
  local copies, waits for them, and re-layouts: 46.4 us -> 58.6 us
    ppermute x64, starting transfers between devices: 82.5 us -> 114 us  [swapped(): return lax.ppermute(block, ALL, pairs)]
    ppermute x64, waiting for transfers between devices: 255 us -> 230 us  [swapped(): return lax.ppermute(block, ALL, pairs)]
    pallas_call x2, Pallas kernels: 30.3 us -> 16.6 us  [attend_back(): pl.pallas_call(attend_back_kernel, name='attend_back', grid_spec=pltpu.Pr...]
    unnamed x184 -> x210, local copies, waits for them, and re-layouts: 31.4 us -> 42.5 us
  transfers between devices with their start and end apart: 79 -> 79, of which waited for: 63 -> 51; matrix products, arithmetic and copies ran while one was open for 10% -> 9% of each run, Pallas kernels for 3% -> 3%
where the time goes in v8:
time: 623 us; the launch traced here: 612 us
  waiting for transfers between devices  245 us (39%)
  starting transfers between devices  135 us (22%)
  Pallas kernels  104 us (17%)
  local copies, waits for them, and re-layouts  58.6 us (9%)
  other arithmetic  50.2 us (8%)
  between operations  19 us (3%)
    ppermute x64, waiting for transfers between devices, swapped(): return lax.ppermute(block, ALL, pairs)  230 us
    ppermute x64, starting transfers between devices, swapped(): return lax.ppermute(block, ALL, pairs)  114 us
    unnamed x210, local copies, waits for them, and re-layouts  42.5 us
    pallas_call x2, Pallas kernels, feed_back(): pl.pallas_call(feed_back_kernel, name='feed_back', grid=(4,), in_specs=[w...  28.6 us
    ppermute x14, starting transfers between devices, over(): return lax.ppermute(block, 'phase', [(source, 1 - source)])  21 us
    pallas_call x2, Pallas kernels, feed(): pl.pallas_call(feed_kernel, name='feed', grid=(4,), in_specs=[whole(D, R)...  20.6 us
    pallas_call x2, Pallas kernels, outer(): pl.pallas_call(outer_late_kernel if made else outer_early_kernel, name='o...  17.7 us
    pallas_call x2, Pallas kernels, attend_back(): pl.pallas_call(attend_back_kernel, name='attend_back', grid_spec=pltpu.Pr...  16.6 us
  transfers between devices with their start and end apart: 79, of which 51 were waited for; matrix products, arithmetic and copies ran while one was open for 9% of the time, Pallas kernels for 3%

profile of v8, /device:TPU:0, one launch (start us, length us, event | category | flops | bytes accessed | tf_op | source)
XLA Modules:
  0.0 612.2 jit_solution(12097932518339330358)
XLA Ops:
  7.3 8.0 %conditional.2 = (bf16[1280,128]{1,0:T(8,128)(2,1)S(1)}) conditional(s32[]{:T(128)} %clamp.4, bf16[1,153600]{1,0:T(2,128)(2,1)} %param.26, bf16[1,153600]{1,0:T(2,128)(2,1)} %param.26, bf16[1,153600]{1,0:T(2,128)(2,1)} %param.26), branch_computations={%region_4.5_spmd, %region_5.6_spmd, %region_6.7_spmd} | conditional | bytes 3780622 | solution.py:852
  7.3 7.3 %reduce.1 = bf16[153600]{0:T(1024)(128)(2,1)S(1)} reduce(bf16[1,153600]{1,0:T(2,128)(2,1)} %param, bf16[]{:T(256)} %constant.214), dimensions={0}, to_apply=%param.reduce_sub_computation | reduce | bytes 614402 | tf_op jit(solution)/shard_map/shard_map
  28.7 12.1 %collective-permute-done.1 = bf16[2,1296,128]{2,1,0:T(8,128)(2,1)S(1)} collective-permute-done((bf16[2,1296,128]{2,1,0:T(8,128)(2,1)S(1)}, bf16[2,1296,128]{2,1,0:T(8,128)(2,1)S(1)}, u32[]{:S(2)}, u32[]{:S(2)}) %collective-permute-start.1) | collective-permute-done | bytes 663584 | tf_op jit(solution)/shard_map/ppermute | solution.py:57
  52.1 3.3 collective-permute-start.3
  55.5 9.6 %collective-permute-done.7 = bf16[2,640,128]{2,1,0:T(8,128)(2,1)S(1)} collective-permute-done((bf16[2,640,128]{2,1,0:T(8,128)(2,1)S(1)}, bf16[2,640,128]{2,1,0:T(8,128)(2,1)S(1)}, u32[]{:S(2)}, u32[]{:S(2)}) %collective-permute-start.7) | collective-permute-done | bytes 327712 | tf_op jit(solution)/shard_map/ppermute | solution.py:57
  69.1 8.3 %collective-permute-done.8 = bf16[4,640,128]{2,1,0:T(8,128)(2,1)S(1)} collective-permute-done((bf16[4,640,128]{2,1,0:T(8,128)(2,1)S(1)}, bf16[4,640,128]{2,1,0:T(8,128)(2,1)S(1)}, u32[]{:S(2)}, u32[]{:S(2)}) %collective-permute-start.8) | collective-permute-done | bytes 655392 | tf_op jit(solution)/shard_map/ppermute | solution.py:57
  92.7 27.9 %collective-permute-done.9 = bf16[8,640,128]{2,1,0:T(8,128)(2,1)} collective-permute-done((bf16[8,640,128]{2,1,0:T(8,128)(2,1)}, bf16[8,640,128]{2,1,0:T(8,128)(2,1)}, u32[]{:S(2)}, u32[]{:S(2)}) %collective-permute-start.9) | collective-permute-done | bytes 1310752 | tf_op jit(solution)/shard_map/ppermute | solution.py:57
  123.2 7.1 %collective-permute-done.5 = bf16[8,656,128]{2,1,0:T(8,128)(2,1)} collective-permute-done((bf16[8,656,128]{2,1,0:T(8,128)(2,1)}, bf16[8,656,128]{2,1,0:T(8,128)(2,1)}, u32[]{:S(2)}, u32[]{:S(2)}) %collective-permute-start.5) | collective-permute-done | bytes 1343520 | tf_op jit(solution)/shard_map/ppermute | solution.py:57
  142.0 6.3 %collective-permute-done.15 = bf16[128,384]{1,0:T(8,128)(2,1)S(1)} collective-permute-done((bf16[128,384]{1,0:T(8,128)(2,1)S(1)}, bf16[128,384]{1,0:T(8,128)(2,1)S(1)}, u32[]{:S(2)}, u32[]{:S(2)}) %collective-permute-start.15) | collective-permute-done | bytes 98336 | tf_op jit(solution)/shard_map/ppermute | solution.py:57
  149.3 6.8 %collective-permute-done.16 = bf16[1,128,384]{2,1,0:T(8,128)(2,1)S(1)} collective-permute-done((bf16[1,128,384]{2,1,0:T(8,128)(2,1)S(1)}, bf16[1,128,384]{2,1,0:T(8,128)(2,1)S(1)}, u32[]{:S(2)}, u32[]{:S(2)}) %collective-permute-start.16) | collective-permute-done | bytes 98336 | tf_op jit(solution)/shard_map/ppermute | solution.py:57
  158.6 4.5 collective-permute-done.17
  167.4 3.6 collective-permute-done.18
  176.4 2.9 and_select_fusion.bias_ref
  189.7 6.2 %attend.2 = (bf16[576,128]{1,0:T(8,128)(2,1)S(1)}, f32[3,1,384]{2,1,0:T(1,128)S(1)}) custom-call(s32[66]{0:T(128)S(1)} %pad_add_fusion.2.need_ref, bf16[576,128]{1,0:T(8,128)(2,1)S(1)} %slice_select_fusion.3.qt_ref, bf16[4096,384]{1,0:T(8,128)(2,1)S(1)} %bitcast.203, f32[4096,128]{1,0:T(8,128)S(1)} %copy-done.26), custom_call_target="tpu_custom_call" | custom-call | flops 2400000000 | bytes 6000000 | tf_op jit(solution)/shard_map/attend/pallas_call | solution.py:322
  199.2 11.1 %feed.2 = (bf16[128,960]{1,0:T(8,128)(2,1)S(1)}, f32[128,960]{1,0:T(8,128)}, bf16[1024,128]{1,0:T(8,128)(2,1)}, f32[128,2560]{1,0:T(8,128)}, f32[128,2560]{1,0:T(8,128)}, /*index=5*/bf16[2560,128]{1,0:T(8,128)(2,1)}) custom-call(bf16[960,128]{1,0:T(8,128)(2,1)S(1)} %constant_dynamic-update-slice_fusion.10.mixed_ref, bf16[128,960]{1,0:T(8,128)(2,1)S(1)} %bitcast.202, ...), custom_call_target="tpu_custom_call" | custom-call | flops 2200000000 | bytes 22000000 | tf_op jit(solution)/shard_map/feed/pallas_call | solution.py:428
  218.4 4.7 collective-permute-start.28
  223.2 4.2 collective-permute-start.25
  232.5 4.4 collective-permute-done.26
  239.4 3.7 collective-permute-start.31
  244.9 5.1 collective-permute-done.31
  253.9 9.5 %collective-permute-done.32 = bf16[8,128,384]{2,1,0:T(8,128)(2,1)S(1)} collective-permute-done((bf16[8,128,384]{2,1,0:T(8,128)(2,1)S(1)}, bf16[8,128,384]{2,1,0:T(8,128)(2,1)S(1)}, u32[]{:S(2)}, u32[]{:S(2)}) %collective-permute-start.32) | collective-permute-done | bytes 786464 | tf_op jit(solution)/shard_map/ppermute | solution.py:57
  264.0 6.2 %attend.3 = (bf16[576,128]{1,0:T(8,128)(2,1)S(1)}, f32[3,1,384]{2,1,0:T(1,128)S(1)}) custom-call(s32[66]{0:T(128)S(1)} %pad_add_fusion.2.need_ref, bf16[576,128]{1,0:T(8,128)(2,1)S(1)} %slice_select_fusion.2.qt_ref, bf16[4096,384]{1,0:T(8,128)(2,1)S(1)} %bitcast.205, f32[4096,128]{1,0:T(8,128)S(1)} %copy-done.27), custom_call_target="tpu_custom_call" | custom-call | flops 2400000000 | bytes 6000000 | tf_op jit(solution)/shard_map/attend/pallas_call | solution.py:322
  273.0 9.5 %feed.3 = (bf16[128,960]{1,0:T(8,128)(2,1)S(1)}, f32[128,960]{1,0:T(8,128)S(1)}, bf16[1024,128]{1,0:T(8,128)(2,1)S(1)}, f32[128,2560]{1,0:T(8,128)S(1)}, f32[128...) custom-call(bf16[960,128]{1,0:T(8,128)(2,1)S(1)} %maximum_select_fusion.2.mixed_ref.refs_6_, ...), custom_call_target="tpu_custom_call" | custom-call | flops 2200000000 | bytes 22000000 | tf_op jit(solution)/shard_map/feed/pallas_call | solution.py:428
  283.3 14.8 %feed_back.2 = (bf16[128,2560]{1,0:T(8,128)(2,1)}, bf16[128,2560]{1,0:T(8,128)(2,1)}, f32[128,960]{1,0:T(8,128)S(1)}, bf16[128,1024]{1,0:T(8,128)(2,1)}, f32[1,9...) custom-call(f32[128,960]{1,0:T(8,128)S(1)} %bitcast.200, ...), custom_call_target="tpu_custom_call" | custom-call | flops 2200000000 | bytes 22000000 | tf_op jit(solution)/shard_map/feed_back/pallas_call | solution.py:519
  301.8 8.3 %attend_back.2 = (bf16[4096,384]{1,0:T(8,128)(2,1)S(1)}, f32[576,128]{1,0:T(8,128)S(1)}) custom-call(s32[66]{0:T(128)S(1)} %pad_add_fusion.2.need_ref, bf16[576,128]{1,0:T(8,128)(2,1)S(1)} %copy-done.63, bf16[4096,384]{1,0:T(8,128)(2,1)S(1)} %bitcast.206, f32[4096,128]{1,0:T(8,128)S(1)} %copy-done.28, f32[576,128]{1,0:T(8,128)S(1)} %slice_select_fusion.1.dot_ref, ...), custom_call_target="tpu_custom_call" | custom-call | flops 6000000000 | bytes 10000000 | tf_op jit(solution)/shard_map/attend_back/pallas_call | solution.py:582
  310.8 2.9 collective-permute-start.37
  313.7 10.0 %collective-permute-done.41 = bf16[8,128,384]{2,1,0:T(8,128)(2,1)S(1)} collective-permute-done((bf16[8,128,384]{2,1,0:T(8,128)(2,1)S(1)}, bf16[8,128,384]{2,1,0:T(8,128)(2,1)S(1)}, u32[]{:S(2)}, u32[]{:S(2)}) %collective-permute-start.41) | collective-permute-done | bytes 786464 | tf_op jit(solution)/shard_map/ppermute | solution.py:57
  325.3 3.8 collective-permute-start.38
  331.9 3.2 collective-permute-start.43
  335.5 3.4 collective-permute-done.43
  343.7 13.4 %collective-permute-start.45 = (bf16[128,384]{1,0:T(8,128)(2,1)S(1)}, bf16[128,384]{1,0:T(8,128)(2,1)S(1)}, u32[]{:S(2)}, u32[]{:S(2)}) collective-permute-start(bf16[128,384]{1,0:T(8,128)(2,1)S(1)} %fusion.35), channel_id=1, source_target_pairs={{0,2},{1,3},{2,0},{3,1},{4,6},{5,7},{6,4},{7,5},{8,10},{9,11},{10,... | collective-permute-start | bytes 294920 | tf_op jit(solution)/shard_map/ppermute | solution.py:57
  362.2 2.9 project_back.2
  368.6 13.8 %feed_back.3 = (bf16[128,2560]{1,0:T(8,128)(2,1)S(1)}, bf16[128,2560]{1,0:T(8,128)(2,1)S(1)}, f32[128,960]{1,0:T(8,128)S(1)}, bf16[128,1024]{1,0:T(8,128)(2,1)S(...) custom-call(f32[128,960]{1,0:T(8,128)S(1)} %convert_select_fusion.c_ref, ...), custom_call_target="tpu_custom_call" | custom-call | flops 2200000000 | bytes 22000000 | tf_op jit(solution)/shard_map/feed_back/pallas_call | solution.py:519
  387.9 8.3 %attend_back.3 = (bf16[4096,384]{1,0:T(8,128)(2,1)S(1)}, f32[576,128]{1,0:T(8,128)S(1)}) custom-call(s32[66]{0:T(128)S(1)} %pad_add_fusion.2.need_ref, bf16[576,128]{1,0:T(8,128)(2,1)S(1)} %copy-done.61, bf16[4096,384]{1,0:T(8,128)(2,1)S(1)} %bitcast.204, f32[4096,128]{1,0:T(8,128)S(1)} %copy-done.28, f32[576,128]{1,0:T(8,128)S(1)} %slice_select_fusion.dot_ref, ...), custom_call_target="tpu_custom_call" | custom-call | flops 6000000000 | bytes 10000000 | tf_op jit(solution)/shard_map/attend_back/pallas_call | solution.py:582
  406.4 8.7 %outer_early.1 = (bf16[2,4,4,432,128]{4,3,2,1,0:T(8,128)(2,1)S(1)}, bf16[2,4,4,432,128]{4,3,2,1,0:T(8,128)(2,1)S(1)}, bf16[2,4,4,416,128]{4,3,2,1,0:T(8,128)(2,1...) custom-call(s32[12]{0:T(128)S(1)} %pad_add_fusion.5.slot_ref, ...), custom_call_target="tpu_custom_call" | custom-call | flops 1300000000 | bytes 12000000 | tf_op jit(solution)/shard_map/outer_early/pallas_call | solution.py:812
  426.3 3.9 collective-permute-done.55
  430.4 3.2 collective-permute-start.56
  437.5 5.0 collective-permute-start.57
  445.1 3.0 collective-permute-start.58
  475.1 9.0 %outer_late.1 = (bf16[2,4,4,432,128]{4,3,2,1,0:T(8,128)(2,1)S(1)}, bf16[2,4,4,432,128]{4,3,2,1,0:T(8,128)(2,1)S(1)}, bf16[2,4,4,416,128]{4,3,2,1,0:T(8,128)(2,1)...) custom-call(s32[12]{0:T(128)S(1)} %pad_add_fusion.5.slot_ref, ...), custom_call_target="tpu_custom_call", output_to_operand_aliasing={{0}: (9, {}), {1}: (10, {}), {2}: (11, {}), {3}: (12, {}), ... | custom-call | flops 1300000000 | bytes 12000000 | tf_op jit(solution)/shard_map/outer_late/pallas_call | solution.py:812
  489.3 3.0 collective-permute-start.66
  492.4 34.9 %collective-permute-done.72 = bf16[2,4,4,416,128]{4,3,2,1,0:T(8,128)(2,1)S(1)} collective-permute-done((bf16[2,4,4,416,128]{4,3,2,1,0:T(8,128)(2,1)S(1)}, bf16[2,4,4,416,128]{4,3,2,1,0:T(8,128)(2,1)S(1)}, u32[]{:S(2)}, u32[]{:S(2)}) %collective-permute-start.72) | collective-permute-done | bytes 3407904 | tf_op jit(solution)/shard_map/ppermute | solution.py:57
  533.9 16.2 %collective-permute-done.73 = bf16[4,4,416,128]{3,2,1,0:T(8,128)(2,1)S(1)} collective-permute-done((bf16[4,4,416,128]{3,2,1,0:T(8,128)(2,1)S(1)}, bf16[4,4,416,128]{3,2,1,0:T(8,128)(2,1)S(1)}, u32[]{:S(2)}, u32[]{:S(2)}) %collective-permute-start.73) | collective-permute-done | bytes 1703968 | tf_op jit(solution)/shard_map/ppermute | solution.py:57
  551.6 5.9 collective-permute-done.61
  567.4 6.9 %collective-permute-done.62 = bf16[2,4,432,128]{3,2,1,0:T(8,128)(2,1)} collective-permute-done((bf16[2,4,432,128]{3,2,1,0:T(8,128)(2,1)}, bf16[2,4,432,128]{3,2,1,0:T(8,128)(2,1)}, u32[]{:S(2)}, u32[]{:S(2)}) %collective-permute-start.62) | collective-permute-done | bytes 884768 | tf_op jit(solution)/shard_map/ppermute | solution.py:57
  580.1 4.0 collective-permute-start.69
  586.4 3.0 collective-permute-start.64
  594.7 3.3 collective-permute-done.70
  (520 shorter events, 235.2 us)
Async XLA Ops:
  7.2 192.0 %all-gather.3.cloned.1.call-start = ((), (), s32[]{:S(2)}) async-start(), calls=%async_computation | async-start | bytes 21299200 | tf_op jit(solution)/shard_map/all_gather | solution.py:889
  17.1 9.2 %collective-permute-start = (bf16[1,1296,128]{2,1,0:T(8,128)(2,1)S(1)}, bf16[1,1296,128]{2,1,0:T(8,128)(2,1)S(1)}, u32[]{:S(2)}, u32[]{:S(2)}) collective-permute-start(bf16[1,1296,128]{2,1,0:T(8,128)(2,1)S(1)} %fusion.26), channel_id=1, source_target_pairs={{0,16},{1,17},{2,18},{3,19},{4,20},{5,21},{6,22},{7,23},{8,24},{9,... | collective-permute-start | bytes 995336 | tf_op jit(solution)/shard_map/ppermute | solution.py:57
  26.4 14.5 %collective-permute-start.1 = (bf16[2,1296,128]{2,1,0:T(8,128)(2,1)S(1)}, bf16[2,1296,128]{2,1,0:T(8,128)(2,1)S(1)}, u32[]{:S(2)}, u32[]{:S(2)}) collective-permute-start(bf16[2,1296,128]{2,1,0:T(8,128)(2,1)S(1)} %pad_maximum_fusion.10), channel_id=1, source_target_pairs={{0,48},{1,49},{2,50},{3,51},{4,52},{5,53},{6,54},{7,55},{8,56},{9,... | collective-permute-start | bytes 1990664 | tf_op jit(solution)/shard_map/ppermute | solution.py:57
  41.7 8.2 %collective-permute-start.6 = (bf16[1,640,128]{2,1,0:T(8,128)(2,1)S(1)}, bf16[1,640,128]{2,1,0:T(8,128)(2,1)S(1)}, u32[]{:S(2)}, u32[]{:S(2)}) collective-permute-start(bf16[1,640,128]{2,1,0:T(8,128)(2,1)S(1)} %get-tuple-element.172), channel_id=1, source_target_pairs={{0,4},{1,5},{2,6},{3,7},{4,0},{5,1},{6,2},{7,3},{8,12},{9,13},{10,... | collective-permute-start | bytes 491528 | tf_op jit(solution)/shard_map/ppermute | solution.py:57
  49.9 15.2 %collective-permute-start.7 = (bf16[2,640,128]{2,1,0:T(8,128)(2,1)S(1)}, bf16[2,640,128]{2,1,0:T(8,128)(2,1)S(1)}, u32[]{:S(2)}, u32[]{:S(2)}) collective-permute-start(bf16[2,640,128]{2,1,0:T(8,128)(2,1)S(1)} %pad_maximum_fusion.18), channel_id=1, source_target_pairs={{0,12},{1,13},{2,14},{3,15},{4,8},{5,9},{6,10},{7,11},{8,4},{9,5},... | collective-permute-start | bytes 983048 | tf_op jit(solution)/shard_map/ppermute | solution.py:57
  52.1 15.5 %collective-permute-start.3 = (bf16[2,656,128]{2,1,0:T(8,128)(2,1)S(1)}, bf16[2,656,128]{2,1,0:T(8,128)(2,1)S(1)}, u32[]{:S(2)}, u32[]{:S(2)}) collective-permute-start(bf16[2,656,128]{2,1,0:T(8,128)(2,1)S(1)} %pad_maximum_fusion.17), channel_id=1, source_target_pairs={{0,3},{1,2},{2,1},{3,0},{4,7},{5,6},{6,5},{7,4},{8,11},{9,10},{10,... | collective-permute-start | bytes 1007624 | tf_op jit(solution)/shard_map/ppermute | solution.py:57
  65.2 12.1 %collective-permute-start.8 = (bf16[4,640,128]{2,1,0:T(8,128)(2,1)S(1)}, bf16[4,640,128]{2,1,0:T(8,128)(2,1)S(1)}, u32[]{:S(2)}, u32[]{:S(2)}) collective-permute-start(bf16[4,640,128]{2,1,0:T(8,128)(2,1)S(1)} %pad_maximum_fusion.11), channel_id=1, source_target_pairs={{0,1},{1,0},{2,3},{3,2},{4,5},{5,4},{6,7},{7,6},{8,9},{9,8},{10,11... | collective-permute-start | bytes 1966088 | tf_op jit(solution)/shard_map/ppermute | solution.py:57
  67.7 13.4 %collective-permute-start.4 = (bf16[4,656,128]{2,1,0:T(8,128)(2,1)S(1)}, bf16[4,656,128]{2,1,0:T(8,128)(2,1)S(1)}, u32[]{:S(2)}, u32[]{:S(2)}) collective-permute-start(bf16[4,656,128]{2,1,0:T(8,128)(2,1)S(1)} %pad_maximum_fusion.9), channel_id=1, source_target_pairs={{0,4},{1,5},{2,6},{3,7},{4,0},{5,1},{6,2},{7,3},{8,12},{9,13},{10,... | collective-permute-start | bytes 2015240 | tf_op jit(solution)/shard_map/ppermute | solution.py:57
  78.6 42.0 %collective-permute-start.9 = (bf16[8,640,128]{2,1,0:T(8,128)(2,1)}, bf16[8,640,128]{2,1,0:T(8,128)(2,1)}, u32[]{:S(2)}, u32[]{:S(2)}) collective-permute-start(bf16[8,640,128]{2,1,0:T(8,128)(2,1)} %pad_maximum_fusion.4), channel_id=1, source_target_pairs={{0,3},{1,2},{2,1},{3,0},{4,7},{5,6},{6,5},{7,4},{8,11},{9,10},{10,... | collective-permute-start | bytes 3932168 | tf_op jit(solution)/shard_map/ppermute | solution.py:57
  82.5 47.7 %collective-permute-start.5 = (bf16[8,656,128]{2,1,0:T(8,128)(2,1)}, bf16[8,656,128]{2,1,0:T(8,128)(2,1)}, u32[]{:S(2)}, u32[]{:S(2)}) collective-permute-start(bf16[8,656,128]{2,1,0:T(8,128)(2,1)} %pad_maximum_fusion.2), channel_id=1, source_target_pairs={{0,12},{1,13},{2,14},{3,15},{4,8},{5,9},{6,10},{7,11},{8,4},{9,5},... | collective-permute-start | bytes 4030472 | tf_op jit(solution)/shard_map/ppermute | solution.py:57
  139.2 9.1 %collective-permute-start.15 = (bf16[128,384]{1,0:T(8,128)(2,1)S(1)}, bf16[128,384]{1,0:T(8,128)(2,1)S(1)}, u32[]{:S(2)}, u32[]{:S(2)}) collective-permute-start(bf16[128,384]{1,0:T(8,128)(2,1)S(1)} %slice_select_fusion.5), channel_id=1, source_target_pairs={{0,2},{1,3},{2,0},{3,1},{4,6},{5,7},{6,4},{7,5},{8,10},{9,11},{10,... | collective-permute-start | bytes 294920 | tf_op jit(solution)/shard_map/ppermute | solution.py:57
  139.3 9.0 %collective-permute-start.12 = (bf16[1,128,384]{2,1,0:T(8,128)(2,1)S(1)}, bf16[1,128,384]{2,1,0:T(8,128)(2,1)S(1)}, u32[]{:S(2)}, u32[]{:S(2)}) collective-permute-start(bf16[1,128,384]{2,1,0:T(8,128)(2,1)S(1)} %bitcast.254), channel_id=1, source_target_pairs={{0,16},{1,17},{2,18},{3,19},{4,20},{5,21},{6,22},{7,23},{8,24},{9,... | collective-permute-start | bytes 294920 | tf_op jit(solution)/shard_map/ppermute | solution.py:57
  148.4 7.7 %collective-permute-start.16 = (bf16[1,128,384]{2,1,0:T(8,128)(2,1)S(1)}, bf16[1,128,384]{2,1,0:T(8,128)(2,1)S(1)}, u32[]{:S(2)}, u32[]{:S(2)}) collective-permute-start(bf16[1,128,384]{2,1,0:T(8,128)(2,1)S(1)} %bitcast.266), channel_id=1, source_target_pairs={{0,4},{1,5},{2,6},{3,7},{4,0},{5,1},{6,2},{7,3},{8,12},{9,13},{10,... | collective-permute-start | bytes 294920 | tf_op jit(solution)/shard_map/ppermute | solution.py:57
  148.4 10.0 %collective-permute-start.13 = (bf16[2,128,384]{2,1,0:T(8,128)(2,1)S(1)}, bf16[2,128,384]{2,1,0:T(8,128)(2,1)S(1)}, u32[]{:S(2)}, u32[]{:S(2)}) collective-permute-start(bf16[2,128,384]{2,1,0:T(8,128)(2,1)S(1)} %pad_maximum_fusion.20), channel_id=1, source_target_pairs={{0,48},{1,49},{2,50},{3,51},{4,52},{5,53},{6,54},{7,55},{8,56},{9,... | collective-permute-start | bytes 589832 | tf_op jit(solution)/shard_map/ppermute | solution.py:57
  158.5 7.9 %collective-permute-start.14 = (bf16[4,128,384]{2,1,0:T(8,128)(2,1)S(1)}, bf16[4,128,384]{2,1,0:T(8,128)(2,1)S(1)}, u32[]{:S(2)}, u32[]{:S(2)}) collective-permute-start(bf16[4,128,384]{2,1,0:T(8,128)(2,1)S(1)} %pad_maximum_fusion.13), channel_id=1, source_target_pairs={{0,4},{1,5},{2,6},{3,7},{4,0},{5,1},{6,2},{7,3},{8,12},{9,13},{10,... | collective-permute-start | bytes 1179656 | tf_op jit(solution)/shard_map/ppermute | solution.py:57
  163.1 7.9 %collective-permute-start.18 = (bf16[4,128,384]{2,1,0:T(8,128)(2,1)S(1)}, bf16[4,128,384]{2,1,0:T(8,128)(2,1)S(1)}, u32[]{:S(2)}, u32[]{:S(2)}) collective-permute-start(bf16[4,128,384]{2,1,0:T(8,128)(2,1)S(1)} %pad_maximum_fusion.14), channel_id=1, source_target_pairs={{0,16},{1,17},{2,18},{3,19},{4,20},{5,21},{6,22},{7,23},{8,24},{9,... | collective-permute-start | bytes 1179656 | tf_op jit(solution)/shard_map/ppermute | solution.py:57
  172.0 13.5 %collective-permute-start.19 = (bf16[8,128,384]{2,1,0:T(8,128)(2,1)}, bf16[8,128,384]{2,1,0:T(8,128)(2,1)}, u32[]{:S(2)}, u32[]{:S(2)}) collective-permute-start(bf16[8,128,384]{2,1,0:T(8,128)(2,1)} %pad_maximum_fusion.5), channel_id=1, source_target_pairs={{0,12},{1,13},{2,14},{3,15},{4,8},{5,9},{6,10},{7,11},{8,4},{9,5},... | collective-permute-start | bytes 2359304 | tf_op jit(solution)/shard_map/ppermute | solution.py:57
  174.1 13.5 %collective-permute-start.20 = (bf16[8,128,384]{2,1,0:T(8,128)(2,1)}, bf16[8,128,384]{2,1,0:T(8,128)(2,1)}, u32[]{:S(2)}, u32[]{:S(2)}) collective-permute-start(bf16[8,128,384]{2,1,0:T(8,128)(2,1)} %pad_maximum_fusion.6), channel_id=1, source_target_pairs={{0,48},{1,49},{2,50},{3,51},{4,52},{5,53},{6,54},{7,55},{8,56},{9,... | collective-permute-start | bytes 2359304 | tf_op jit(solution)/shard_map/ppermute | solution.py:57
  218.4 8.9 %collective-permute-start.28 = (bf16[128,384]{1,0:T(8,128)(2,1)S(1)}, bf16[128,384]{1,0:T(8,128)(2,1)S(1)}, u32[]{:S(2)}, u32[]{:S(2)}) collective-permute-start(bf16[128,384]{1,0:T(8,128)(2,1)S(1)} %slice_select_fusion.4), channel_id=1, source_target_pairs={{0,2},{1,3},{2,0},{3,1},{4,6},{5,7},{6,4},{7,5},{8,10},{9,11},{10,... | collective-permute-start | bytes 294920 | tf_op jit(solution)/shard_map/ppermute | solution.py:57
  237.0 7.9 %collective-permute-start.27 = (bf16[4,128,384]{2,1,0:T(8,128)(2,1)S(1)}, bf16[4,128,384]{2,1,0:T(8,128)(2,1)S(1)}, u32[]{:S(2)}, u32[]{:S(2)}) collective-permute-start(bf16[4,128,384]{2,1,0:T(8,128)(2,1)S(1)} %pad_maximum_fusion.15), channel_id=1, source_target_pairs={{0,4},{1,5},{2,6},{3,7},{4,0},{5,1},{6,2},{7,3},{8,12},{9,13},{10,... | collective-permute-start | bytes 1179656 | tf_op jit(solution)/shard_map/ppermute | solution.py:57
  239.4 10.6 %collective-permute-start.31 = (bf16[4,128,384]{2,1,0:T(8,128)(2,1)S(1)}, bf16[4,128,384]{2,1,0:T(8,128)(2,1)S(1)}, u32[]{:S(2)}, u32[]{:S(2)}) collective-permute-start(bf16[4,128,384]{2,1,0:T(8,128)(2,1)S(1)} %pad_maximum_fusion.16), channel_id=1, source_target_pairs={{0,16},{1,17},{2,18},{3,19},{4,20},{5,21},{6,22},{7,23},{8,24},{9,... | collective-permute-start | bytes 1179656 | tf_op jit(solution)/shard_map/ppermute | solution.py:57
  250.1 13.3 %collective-permute-start.32 = (bf16[8,128,384]{2,1,0:T(8,128)(2,1)S(1)}, bf16[8,128,384]{2,1,0:T(8,128)(2,1)S(1)}, u32[]{:S(2)}, u32[]{:S(2)}) collective-permute-start(bf16[8,128,384]{2,1,0:T(8,128)(2,1)S(1)} %pad_maximum_fusion.7), channel_id=1, source_target_pairs={{0,12},{1,13},{2,14},{3,15},{4,8},{5,9},{6,10},{7,11},{8,4},{9,5},... | collective-permute-start | bytes 2359304 | tf_op jit(solution)/shard_map/ppermute | solution.py:57
  250.2 13.3 %collective-permute-start.33 = (bf16[8,128,384]{2,1,0:T(8,128)(2,1)S(1)}, bf16[8,128,384]{2,1,0:T(8,128)(2,1)S(1)}, u32[]{:S(2)}, u32[]{:S(2)}) collective-permute-start(bf16[8,128,384]{2,1,0:T(8,128)(2,1)S(1)} %pad_maximum_fusion.8), channel_id=1, source_target_pairs={{0,48},{1,49},{2,50},{3,51},{4,52},{5,53},{6,54},{7,55},{8,56},{9,... | collective-permute-start | bytes 2359304 | tf_op jit(solution)/shard_map/ppermute | solution.py:57
  310.4 13.3 %collective-permute-start.41 = (bf16[8,128,384]{2,1,0:T(8,128)(2,1)S(1)}, bf16[8,128,384]{2,1,0:T(8,128)(2,1)S(1)}, u32[]{:S(2)}, u32[]{:S(2)}) collective-permute-start(bf16[8,128,384]{2,1,0:T(8,128)(2,1)S(1)} %bitcast.275), channel_id=1, source_target_pairs={{0,48},{1,49},{2,50},{3,51},{4,52},{5,53},{6,54},{7,55},{8,56},{9,... | collective-permute-start | bytes 2359304 | tf_op jit(solution)/shard_map/ppermute | solution.py:57
  310.8 14.2 %collective-permute-start.37 = (bf16[8,128,384]{2,1,0:T(8,128)(2,1)S(1)}, bf16[8,128,384]{2,1,0:T(8,128)(2,1)S(1)}, u32[]{:S(2)}, u32[]{:S(2)}) collective-permute-start(bf16[8,128,384]{2,1,0:T(8,128)(2,1)S(1)} %bitcast.274), channel_id=1, source_target_pairs={{0,12},{1,13},{2,14},{3,15},{4,8},{5,9},{6,10},{7,11},{8,4},{9,5},... | collective-permute-start | bytes 2359304 | tf_op jit(solution)/shard_map/ppermute | solution.py:57
  323.9 7.9 %collective-permute-start.42 = (bf16[4,128,384]{2,1,0:T(8,128)(2,1)S(1)}, bf16[4,128,384]{2,1,0:T(8,128)(2,1)S(1)}, u32[]{:S(2)}, u32[]{:S(2)}) collective-permute-start(bf16[4,128,384]{2,1,0:T(8,128)(2,1)S(1)} %slice.576), channel_id=1, source_target_pairs={{0,16},{1,17},{2,18},{3,19},{4,20},{5,21},{6,22},{7,23},{8,24},{9,... | collective-permute-start | bytes 1179656 | tf_op jit(solution)/shard_map/ppermute | solution.py:57
  325.3 9.9 %collective-permute-start.38 = (bf16[4,128,384]{2,1,0:T(8,128)(2,1)S(1)}, bf16[4,128,384]{2,1,0:T(8,128)(2,1)S(1)}, u32[]{:S(2)}, u32[]{:S(2)}) collective-permute-start(bf16[4,128,384]{2,1,0:T(8,128)(2,1)S(1)} %slice.570), channel_id=1, source_target_pairs={{0,4},{1,5},{2,6},{3,7},{4,0},{5,1},{6,2},{7,3},{8,12},{9,13},{10,... | collective-permute-start | bytes 1179656 | tf_op jit(solution)/shard_map/ppermute | solution.py:57
  342.3 16.1 %collective-permute-start.40 = (bf16[1,128,384]{2,1,0:T(8,128)(2,1)S(1)}, bf16[1,128,384]{2,1,0:T(8,128)(2,1)S(1)}, u32[]{:S(2)}, u32[]{:S(2)}) collective-permute-start(bf16[1,128,384]{2,1,0:T(8,128)(2,1)S(1)} %slice.574), channel_id=1, source_target_pairs={{0,16},{1,17},{2,18},{3,19},{4,20},{5,21},{6,22},{7,23},{8,24},{9,... | collective-permute-start | bytes 294920 | tf_op jit(solution)/shard_map/ppermute | solution.py:57
  343.7 16.0 %collective-permute-start.45 = (bf16[128,384]{1,0:T(8,128)(2,1)S(1)}, bf16[128,384]{1,0:T(8,128)(2,1)S(1)}, u32[]{:S(2)}, u32[]{:S(2)}) collective-permute-start(bf16[128,384]{1,0:T(8,128)(2,1)S(1)} %fusion.35), channel_id=1, source_target_pairs={{0,2},{1,3},{2,0},{3,1},{4,6},{5,7},{6,4},{7,5},{8,10},{9,11},{10,... | collective-permute-start | bytes 294920 | tf_op jit(solution)/shard_map/ppermute | solution.py:57
  398.0 20.5 %collective-permute-start.51 = (bf16[8,128,384]{2,1,0:T(8,128)(2,1)}, bf16[8,128,384]{2,1,0:T(8,128)(2,1)}, u32[]{:S(2)}, u32[]{:S(2)}) collective-permute-start(bf16[8,128,384]{2,1,0:T(8,128)(2,1)} %bitcast.56), channel_id=1, source_target_pairs={{0,48},{1,49},{2,50},{3,51},{4,52},{5,53},{6,54},{7,55},{8,56},{9,... | collective-permute-start | bytes 2359304 | tf_op jit(solution)/shard_map/ppermute | solution.py:57
  400.6 19.9 %collective-permute-start.50 = (bf16[8,128,384]{2,1,0:T(8,128)(2,1)}, bf16[8,128,384]{2,1,0:T(8,128)(2,1)}, u32[]{:S(2)}, u32[]{:S(2)}) collective-permute-start(bf16[8,128,384]{2,1,0:T(8,128)(2,1)} %bitcast.54), channel_id=1, source_target_pairs={{0,12},{1,13},{2,14},{3,15},{4,8},{5,9},{6,10},{7,11},{8,4},{9,5},... | collective-permute-start | bytes 2359304 | tf_op jit(solution)/shard_map/ppermute | solution.py:57
  422.4 7.9 %collective-permute-start.55 = (bf16[4,128,384]{2,1,0:T(8,128)(2,1)S(1)}, bf16[4,128,384]{2,1,0:T(8,128)(2,1)S(1)}, u32[]{:S(2)}, u32[]{:S(2)}) collective-permute-start(bf16[4,128,384]{2,1,0:T(8,128)(2,1)S(1)} %slice.484), channel_id=1, source_target_pairs={{0,16},{1,17},{2,18},{3,19},{4,20},{5,21},{6,22},{7,23},{8,24},{9,... | collective-permute-start | bytes 1179656 | tf_op jit(solution)/shard_map/ppermute | solution.py:57
  424.0 9.5 %collective-permute-start.52 = (bf16[4,128,384]{2,1,0:T(8,128)(2,1)S(1)}, bf16[4,128,384]{2,1,0:T(8,128)(2,1)S(1)}, u32[]{:S(2)}, u32[]{:S(2)}) collective-permute-start(bf16[4,128,384]{2,1,0:T(8,128)(2,1)S(1)} %slice.478), channel_id=1, source_target_pairs={{0,4},{1,5},{2,6},{3,7},{4,0},{5,1},{6,2},{7,3},{8,12},{9,13},{10,... | collective-permute-start | bytes 1179656 | tf_op jit(solution)/shard_map/ppermute | solution.py:57
  433.7 8.8 %collective-permute-start.53 = (bf16[2,128,384]{2,1,0:T(8,128)(2,1)S(1)}, bf16[2,128,384]{2,1,0:T(8,128)(2,1)S(1)}, u32[]{:S(2)}, u32[]{:S(2)}) collective-permute-start(bf16[2,128,384]{2,1,0:T(8,128)(2,1)S(1)} %slice.583), channel_id=1, source_target_pairs={{0,48},{1,49},{2,50},{3,51},{4,52},{5,53},{6,54},{7,55},{8,56},{9,... | collective-permute-start | bytes 589832 | tf_op jit(solution)/shard_map/ppermute | solution.py:57
  486.0 41.3 %collective-permute-start.72 = (bf16[2,4,4,416,128]{4,3,2,1,0:T(8,128)(2,1)S(1)}, bf16[2,4,4,416,128]{4,3,2,1,0:T(8,128)(2,1)S(1)}, u32[]{:S(2)}, u32[]{:S(2)}) collective-permute-start(bf16[2,4,4,416,128]{4,3,2,1,0:T(8,128)(2,1)S(1)} %get-tuple-element.146), channel_id=1, source_target_pairs={{0,3},{1,2},{2,1},{3,0},{4,7},{5,6},{6,5},{7,4},{8,11},{9,10},{10,... | collective-permute-start | bytes 10223624 | tf_op jit(solution)/shard_map/ppermute | solution.py:57
  487.9 42.9 %collective-permute-start.60 = (bf16[2,4,4,432,128]{4,3,2,1,0:T(8,128)(2,1)}, bf16[2,4,4,432,128]{4,3,2,1,0:T(8,128)(2,1)S(1)}, u32[]{:S(2)}, u32[]{:S(2)}) collective-permute-start(bf16[2,4,4,432,128]{4,3,2,1,0:T(8,128)(2,1)} %get-tuple-element.142), channel_id=1, source_target_pairs={{0,48},{1,49},{2,50},{3,51},{4,52},{5,53},{6,54},{7,55},{8,56},{9,... | collective-permute-start | bytes 10616840 | tf_op jit(solution)/shard_map/ppermute | solution.py:57
  489.3 43.0 %collective-permute-start.66 = (bf16[2,4,4,432,128]{4,3,2,1,0:T(8,128)(2,1)}, bf16[2,4,4,432,128]{4,3,2,1,0:T(8,128)(2,1)S(1)}, u32[]{:S(2)}, u32[]{:S(2)}) collective-permute-start(bf16[2,4,4,432,128]{4,3,2,1,0:T(8,128)(2,1)} %get-tuple-element.144), channel_id=1, source_target_pairs={{0,12},{1,13},{2,14},{3,15},{4,8},{5,9},{6,10},{7,11},{8,4},{9,5},... | collective-permute-start | bytes 10616840 | tf_op jit(solution)/shard_map/ppermute | solution.py:57
  528.3 21.9 %collective-permute-start.73 = (bf16[4,4,416,128]{3,2,1,0:T(8,128)(2,1)S(1)}, bf16[4,4,416,128]{3,2,1,0:T(8,128)(2,1)S(1)}, u32[]{:S(2)}, u32[]{:S(2)}) collective-permute-start(bf16[4,4,416,128]{3,2,1,0:T(8,128)(2,1)S(1)} %get-tuple-element.180), channel_id=1, source_target_pairs={{0,1},{1,0},{2,3},{3,2},{4,5},{5,4},{6,7},{7,6},{8,9},{9,8},{10,11... | collective-permute-start | bytes 5111816 | tf_op jit(solution)/shard_map/ppermute | solution.py:57
  531.7 25.8 %collective-permute-start.61 = (bf16[4,4,432,128]{3,2,1,0:T(8,128)(2,1)S(1)}, bf16[4,4,432,128]{3,2,1,0:T(8,128)(2,1)S(1)}, u32[]{:S(2)}, u32[]{:S(2)}) collective-permute-start(bf16[4,4,432,128]{3,2,1,0:T(8,128)(2,1)S(1)} %get-tuple-element.176), channel_id=1, source_target_pairs={{0,16},{1,17},{2,18},{3,19},{4,20},{5,21},{6,22},{7,23},{8,24},{9,... | collective-permute-start | bytes 5308424 | tf_op jit(solution)/shard_map/ppermute | solution.py:57
  533.7 27.4 %collective-permute-start.67 = (bf16[4,4,432,128]{3,2,1,0:T(8,128)(2,1)S(1)}, bf16[4,4,432,128]{3,2,1,0:T(8,128)(2,1)S(1)}, u32[]{:S(2)}, u32[]{:S(2)}) collective-permute-start(bf16[4,4,432,128]{3,2,1,0:T(8,128)(2,1)S(1)} %get-tuple-element.178), channel_id=1, source_target_pairs={{0,4},{1,5},{2,6},{3,7},{4,0},{5,1},{6,2},{7,3},{8,12},{9,13},{10,... | collective-permute-start | bytes 5308424 | tf_op jit(solution)/shard_map/ppermute | solution.py:57
  550.6 14.2 %collective-permute-start.74 = (bf16[2,4,416,128]{3,2,1,0:T(8,128)(2,1)S(1)}, bf16[2,4,416,128]{3,2,1,0:T(8,128)(2,1)S(1)}, u32[]{:S(2)}, u32[]{:S(2)}) collective-permute-start(bf16[2,4,416,128]{3,2,1,0:T(8,128)(2,1)S(1)} %get-tuple-element.186), channel_id=1, source_target_pairs={{0,48},{1,49},{2,50},{3,51},{4,52},{5,53},{6,54},{7,55},{8,56},{9,... | collective-permute-start | bytes 2555912 | tf_op jit(solution)/shard_map/ppermute | solution.py:57
  558.9 15.4 %collective-permute-start.62 = (bf16[2,4,432,128]{3,2,1,0:T(8,128)(2,1)}, bf16[2,4,432,128]{3,2,1,0:T(8,128)(2,1)}, u32[]{:S(2)}, u32[]{:S(2)}) collective-permute-start(bf16[2,4,432,128]{3,2,1,0:T(8,128)(2,1)} %get-tuple-element.182), channel_id=1, source_target_pairs={{0,12},{1,13},{2,14},{3,15},{4,8},{5,9},{6,10},{7,11},{8,4},{9,5},... | collective-permute-start | bytes 2654216 | tf_op jit(solution)/shard_map/ppermute | solution.py:57
  562.5 16.2 %collective-permute-start.68 = (bf16[2,4,432,128]{3,2,1,0:T(8,128)(2,1)}, bf16[2,4,432,128]{3,2,1,0:T(8,128)(2,1)}, u32[]{:S(2)}, u32[]{:S(2)}) collective-permute-start(bf16[2,4,432,128]{3,2,1,0:T(8,128)(2,1)} %get-tuple-element.184), channel_id=1, source_target_pairs={{0,3},{1,2},{2,1},{3,0},{4,7},{5,6},{6,5},{7,4},{8,11},{9,10},{10,... | collective-permute-start | bytes 2654216 | tf_op jit(solution)/shard_map/ppermute | solution.py:57
  565.0 10.8 %collective-permute-start.75 = (bf16[4,416,128]{2,1,0:T(8,128)(2,1)S(1)}, bf16[4,416,128]{2,1,0:T(8,128)(2,1)}, u32[]{:S(2)}, u32[]{:S(2)}) collective-permute-start(bf16[4,416,128]{2,1,0:T(8,128)(2,1)S(1)} %get-tuple-element.200), channel_id=1, source_target_pairs={{0,16},{1,17},{2,18},{3,19},{4,20},{5,21},{6,22},{7,23},{8,24},{9,... | collective-permute-start | bytes 1277960 | tf_op jit(solution)/shard_map/ppermute | solution.py:57
  575.7 10.6 %collective-permute-start.63 = (bf16[4,432,128]{2,1,0:T(8,128)(2,1)S(1)}, bf16[4,432,128]{2,1,0:T(8,128)(2,1)S(1)}, u32[]{:S(2)}, u32[]{:S(2)}) collective-permute-start(bf16[4,432,128]{2,1,0:T(8,128)(2,1)S(1)} %get-tuple-element.196), channel_id=1, source_target_pairs={{0,4},{1,5},{2,6},{3,7},{4,0},{5,1},{6,2},{7,3},{8,12},{9,13},{10,... | collective-permute-start | bytes 1327112 | tf_op jit(solution)/shard_map/ppermute | solution.py:57
  577.0 8.4 %collective-permute-start.76 = (bf16[2,416,128]{2,1,0:T(8,128)(2,1)S(1)}, bf16[2,416,128]{2,1,0:T(8,128)(2,1)S(1)}, u32[]{:S(2)}, u32[]{:S(2)}) collective-permute-start(bf16[2,416,128]{2,1,0:T(8,128)(2,1)S(1)} %get-tuple-element.207), channel_id=1, source_target_pairs={{0,12},{1,13},{2,14},{3,15},{4,8},{5,9},{6,10},{7,11},{8,4},{9,5},... | collective-permute-start | bytes 638984 | tf_op jit(solution)/shard_map/ppermute | solution.py:57
  580.1 10.5 %collective-permute-start.69 = (bf16[4,432,128]{2,1,0:T(8,128)(2,1)S(1)}, bf16[4,432,128]{2,1,0:T(8,128)(2,1)S(1)}, u32[]{:S(2)}, u32[]{:S(2)}) collective-permute-start(bf16[4,432,128]{2,1,0:T(8,128)(2,1)S(1)} %get-tuple-element.198), channel_id=1, source_target_pairs={{0,1},{1,0},{2,3},{3,2},{4,5},{5,4},{6,7},{7,6},{8,9},{9,8},{10,11... | collective-permute-start | bytes 1327112 | tf_op jit(solution)/shard_map/ppermute | solution.py:57
  585.4 7.9 %collective-permute-start.77 = (bf16[416,128]{1,0:T(8,128)(2,1)S(1)}, bf16[416,128]{1,0:T(8,128)(2,1)S(1)}, u32[]{:S(2)}, u32[]{:S(2)}) collective-permute-start(bf16[416,128]{1,0:T(8,128)(2,1)S(1)} %fusion.34), channel_id=1, source_target_pairs={{0,4},{1,5},{2,6},{3,7},{4,0},{5,1},{6,2},{7,3},{8,12},{9,13},{10,... | collective-permute-start | bytes 319496 | tf_op jit(solution)/shard_map/ppermute | solution.py:57
  (129 other events, 1680.5 us)
Sparse Core Ops, SparseCore 0:
  16.2 143.6 all-gather.2

commit v9 on v8

--- a/solution.py
+++ b/solution.py
@@ -90,7 +90,7 @@
     return jnp.concatenate(blocks, axis=0).reshape(KEYS, tail[1])
 
 
-def scatter_keys(d_kv, beside=None):
+def scatter_keys(d_kv):
     parts = d_kv.reshape(2, 16, R, d_kv.shape[1])
     orders = (((0, 1), (1, 0)), ((1, 0), (0, 1)))
     blocks = [parts[0], parts[1]]
@@ -102,9 +102,7 @@
                 total = blocks[k][:half].astype(f32) + got.astype(f32)
                 last = k == 0 and half == 1
                 blocks[k] = total if last else total.astype(bf16)
-            if beside is not None and leg and number:
-                blocks, beside = lax.optimization_barrier((blocks, beside))
-    return blocks[0][0] + swapped(blocks[1][0], far_z).astype(f32), beside
+    return blocks[0][0] + swapped(blocks[1][0], far_z).astype(f32)
 
 
 def slot_offsets(phase):
@@ -674,15 +672,16 @@
     )(idx, d_query, d_kv, cos, sin, u, gain, d_hidden, *front)
 
 
-def outer_steps(begin, end, refs, slot_ref, outs, stage, sems):
-    step = pl.program_id(0) + begin
+def outer_kernel(
+    slot_ref, at_ref, dqkv_ref, mixed_ref, dhb_ref, nt_ref, dgate_ref, dup_ref, mt_ref, cb_ref,
+    gain_ref, k0, k1, k2, s0, s1, s2, stage, sems,
+):
+    step = pl.program_id(0)
     buf = step % 2
     slot_y, slot_x = slot_ref[step // 4], slot_ref[4 + step % 4]
     zslot = [slot_ref[8 + k] for k in range(4)]
     out_ref = stage.at[buf]
     (a0, b0), (a1, b1), (a2, b2) = PART_ROWS
-    k0, k1, k2, s0, s1, s2 = outs
-    gain_ref, nt_ref, dgate_ref, dup_ref = refs[:4]
 
     def copy(i, buf, half=0):
         src = stage.at[buf]
@@ -696,7 +695,7 @@
             src, dst = src.at[2:4, a2:b2], s2.at[:, slot_y, slot_x]
         return pltpu.make_async_copy(src, dst, sems.at[buf, i])
 
-    @pl.when(step >= begin + 2)
+    @pl.when(step >= 2)
     def _():
         for i in range(4):
             copy(i, buf).wait()
@@ -731,7 +730,21 @@
                     at = 160 * (c + h)
                     out_ref[zslot[k], at : at + 160, :] = b.astype(bf16)
 
-    def broad():
+    @pl.when(step < 2)
+    def _():
+        narrow(384 * step, (0, 1, 2, 3))
+
+    @pl.when(step == 2)
+    def _():
+        narrow(768, (0, 1))
+        wide(mixed_ref, 0, dhb_ref, (2, 3))
+
+    @pl.when(step == 3)
+    def _():
+        wide(mixed_ref, 320, dhb_ref, (0, 1, 2, 3))
+
+    @pl.when((step >= 4) & (step < 12))
+    def _():
         rows = nt_ref[pl.ds(pl.multiple_of(128 * (step - 4), 128), 128), :]
         for part, ref in enumerate((dgate_ref, dup_ref)):
             for c in range(0, 20, 2):
@@ -744,36 +757,9 @@
                             b = b + row_of(k, 32, 30)
                         out_ref[zslot[k], at : at + 32, :] = b.astype(bf16)
 
-    if begin == 0:
-        at_ref, dqkv_ref, mixed_ref, dhb_ref = refs[4:]
-
-        @pl.when(step < 2)
-        def _():
-            narrow(384 * step, (0, 1, 2, 3))
-
-        @pl.when(step == 2)
-        def _():
-            narrow(768, (0, 1))
-            wide(mixed_ref, 0, dhb_ref, (2, 3))
-
-        @pl.when(step == 3)
-        def _():
-            wide(mixed_ref, 320, dhb_ref, (0, 1, 2, 3))
-
-        @pl.when(step >= 4)
-        def _():
-            broad()
-
-    else:
-        mt_ref, cb_ref = refs[4:]
-
-        @pl.when(step < 12)
-        def _():
-            broad()
-
-        @pl.when(step >= 12)
-        def _():
-            wide(mt_ref, 640 * (step - 12), cb_ref, (0, 1, 2, 3))
+    @pl.when(step >= 12)
+    def _():
+        wide(mt_ref, 640 * (step - 12), cb_ref, (0, 1, 2, 3))
 
     for half in range(2):
 
@@ -788,34 +774,26 @@
     copy(2, buf).start()
     copy(3, buf).start()
 
-    @pl.when(step == end - 1)
+    @pl.when(step == 15)
     def _():
         for last in (0, 1):
             for i in range(4):
                 copy(i, last).wait()
 
 
-def outer_late_kernel(slot_ref, *refs):
-    outer_steps(0, 8, refs[:8], slot_ref, refs[14:20], *refs[20:])
-
-
-def outer_early_kernel(slot_ref, *refs):
-    outer_steps(8, 16, refs[:6], slot_ref, refs[6:12], *refs[12:])
-
-
-def outer(slots, args, made=None):
+def outer(slots, at, dqkv, mixed, dhb, nt, dgate, dup, mt, cb, gains):
     whole = lambda v: pl.BlockSpec(v.shape, lambda s, slot: (0,) * v.ndim)
+    args = (at, dqkv, mixed, dhb, nt, dgate, dup, mt, cb, gains)
     shapes = [
         jax.ShapeDtypeStruct((2, 4, 4, end - begin, 128), bf16) for begin, end in PART_ROWS
     ]
-    made = made or []
-    return pl.pallas_call(
-        outer_late_kernel if made else outer_early_kernel,
-        name="outer_late" if made else "outer_early",
+    out = pl.pallas_call(
+        outer_kernel,
+        name="outer",
         grid_spec=pltpu.PrefetchScalarGridSpec(
             num_scalar_prefetch=1,
-            grid=(8,),
-            in_specs=[whole(v) for v in args] + [pl.BlockSpec(memory_space=pl.ANY)] * len(made),
+            grid=(16,),
+            in_specs=[whole(v) for v in args],
             out_specs=[pl.BlockSpec(memory_space=pl.ANY)] * 6,
             scratch_shapes=[
                 pltpu.VMEM((2, 4, ROWS, 128), bf16),
@@ -823,12 +801,12 @@
             ],
         ),
         out_shape=shapes * 2,
-        input_output_aliases={1 + len(args) + i: i for i in range(len(made))},
         compiler_params=pltpu.CompilerParams(vmem_limit_bytes=20 << 20),
         cost_estimate=pl.CostEstimate(
-            flops=1_300_000_000, bytes_accessed=12_000_000, transcendentals=0
-        ),
-    )(slots, *args, *made)
+            flops=2_600_000_000, bytes_accessed=24_000_000, transcendentals=0
+        ),
+    )(slots, *args)
+    return out[:3], out[3:]
 
 
 def shard_kind(rank):
@@ -961,7 +939,7 @@
             u = jnp.where(first, u, over(result, 0))
 
     cot = out_grad[0]
-    d_query = d_kv = made = None
+    d_query = d_kv = None
     for tick in range(2):
         layer = 1 - tick
         active = phase == layer
@@ -970,11 +948,9 @@
             cot, gate, up, hidden, gain_two, pad, gathered
         )
         d_side = jnp.where(active, d_mixed[:QSIDE], over(d_mixed[QSIDE:], layer))
-        if tick:
-            made = outer(slots, (gain_rows(dg_two, dg_two), nt, dgate, dup, mt, cb))
         d_kv_all, dq_side = attend_back(need, qt_side, kv_all, bias, d_side, mixed_side, lse)
         dq_new = jnp.concatenate([dq_side, over(dq_side[: D - QSIDE], tick)])
-        dkv_side, made = scatter_keys(d_kv_all, made)
+        dkv_side = scatter_keys(d_kv_all)
         dkv_new = jnp.concatenate([dkv_side, over(dkv_side[:, :256], tick)], axis=1)
         d_query = dq_new if tick == 0 else jnp.where(active, dq_new, d_query)
         d_kv = dkv_new if tick == 0 else jnp.where(active, dkv_new, d_kv)
@@ -984,10 +960,10 @@
         if tick == 0:
             cot = jnp.where(first, over(d_u.astype(bf16), 1).astype(f32), cot)
 
-    made = outer(
-        slots, (gain_rows(dg_one, dg_two), nt, dgate, dup, at, dqkv, mixed, dhb), list(made)
+    keep, send = outer(
+        slots, at, dqkv, mixed, dhb, nt, dgate, dup, mt, cb, gain_rows(dg_one, dg_two)
     )
-    total = scatter_grads(made[:3], made[3:])
+    total = scatter_grads(keep, send)
     param_part, gain_part = blocks_shard(total, rank)
     return (result[None, None], d_u[None, None], param_part[None], gain_part[None])
 

time: 623 us -> 610 us (0.979)
  local copies, waits for them, and re-layouts: 58.6 us -> 37.4 us
  starting transfers between devices: 135 us -> 147 us
  Pallas kernels: 104 us -> 94.9 us
  waiting for transfers between devices: 245 us -> 253 us
    unnamed x210 -> x144, local copies, waits for them, and re-layouts: 42.5 us -> 24.1 us
    ppermute x64, starting transfers between devices: 114 us -> 126 us  [swapped(): return lax.ppermute(block, ALL, pairs)]
    ppermute x64, waiting for transfers between devices: 230 us -> 238 us  [swapped(): return lax.ppermute(block, ALL, pairs)]
    pallas_call x2 -> x1, Pallas kernels: 17.7 us -> 17.7 us  [outer(): pl.pallas_call(outer_kernel, name='outer', grid_spec=pltpu.PrefetchScalar...]
  transfers between devices with their start and end apart: 79 -> 79, of which waited for: 51 -> 53; matrix products, arithmetic and copies ran while one was open for 9% -> 10% of each run, Pallas kernels for 3% -> 1%
where the time goes in v9:
time: 610 us; the launch traced here: 601 us
  waiting for transfers between devices  253 us (41%)
  starting transfers between devices  147 us (24%)
  Pallas kernels  94.9 us (16%)
  other arithmetic  49.6 us (8%)
  local copies, waits for them, and re-layouts  37.4 us (6%)
  between operations  19 us (3%)
    ppermute x64, waiting for transfers between devices, swapped(): return lax.ppermute(block, ALL, pairs)  238 us
    ppermute x64, starting transfers between devices, swapped(): return lax.ppermute(block, ALL, pairs)  126 us
    pallas_call x2, Pallas kernels, feed_back(): pl.pallas_call(feed_back_kernel, name='feed_back', grid=(4,), in_specs=[w...  28.3 us
    unnamed x144, local copies, waits for them, and re-layouts  24.1 us
    ppermute x14, starting transfers between devices, over(): return lax.ppermute(block, 'phase', [(source, 1 - source)])  20.6 us
    pallas_call x2, Pallas kernels, feed(): pl.pallas_call(feed_kernel, name='feed', grid=(4,), in_specs=[whole(D, R)...  20.6 us
    pallas_call x1, Pallas kernels, outer(): pl.pallas_call(outer_kernel, name='outer', grid_spec=pltpu.PrefetchScalar...  17.7 us
    ppermute x14, waiting for transfers between devices, over(): return lax.ppermute(block, 'phase', [(source, 1 - source)])  15.3 us
  transfers between devices with their start and end apart: 79, of which 53 were waited for; matrix products, arithmetic and copies ran while one was open for 10% of the time, Pallas kernels for 1%

profile of v9, /device:TPU:0, one launch (start us, length us, event | category | flops | bytes accessed | tf_op | source)
XLA Modules:
  0.0 600.7 jit_solution(16619361441459312522)
XLA Ops:
  7.3 8.0 %conditional.2 = (bf16[1280,128]{1,0:T(8,128)(2,1)S(1)}) conditional(s32[]{:T(128)} %clamp.4, bf16[1,153600]{1,0:T(2,128)(2,1)} %param.26, bf16[1,153600]{1,0:T(2,128)(2,1)} %param.26, bf16[1,153600]{1,0:T(2,128)(2,1)} %param.26), branch_computations={%region_4.5_spmd, %region_5.6_spmd, %region_6.7_spmd} | conditional | bytes 3780622 | solution.py:830
  7.3 7.3 %reduce.1 = bf16[153600]{0:T(1024)(128)(2,1)S(1)} reduce(bf16[1,153600]{1,0:T(2,128)(2,1)} %param, bf16[]{:T(256)} %constant.210), dimensions={0}, to_apply=%param.reduce_sub_computation | reduce | bytes 614402 | tf_op jit(solution)/shard_map/shard_map
  28.7 12.1 %collective-permute-done.1 = bf16[2,1296,128]{2,1,0:T(8,128)(2,1)S(1)} collective-permute-done((bf16[2,1296,128]{2,1,0:T(8,128)(2,1)S(1)}, bf16[2,1296,128]{2,1,0:T(8,128)(2,1)S(1)}, u32[]{:S(2)}, u32[]{:S(2)}) %collective-permute-start.1) | collective-permute-done | bytes 663584 | tf_op jit(solution)/shard_map/ppermute | solution.py:57
  52.1 3.2 collective-permute-start.3
  55.3 9.7 %collective-permute-done.7 = bf16[2,640,128]{2,1,0:T(8,128)(2,1)S(1)} collective-permute-done((bf16[2,640,128]{2,1,0:T(8,128)(2,1)S(1)}, bf16[2,640,128]{2,1,0:T(8,128)(2,1)S(1)}, u32[]{:S(2)}, u32[]{:S(2)}) %collective-permute-start.7) | collective-permute-done | bytes 327712 | tf_op jit(solution)/shard_map/ppermute | solution.py:57
  69.0 8.1 %collective-permute-done.8 = bf16[4,640,128]{2,1,0:T(8,128)(2,1)S(1)} collective-permute-done((bf16[4,640,128]{2,1,0:T(8,128)(2,1)S(1)}, bf16[4,640,128]{2,1,0:T(8,128)(2,1)S(1)}, u32[]{:S(2)}, u32[]{:S(2)}) %collective-permute-start.8) | collective-permute-done | bytes 655392 | tf_op jit(solution)/shard_map/ppermute | solution.py:57
  93.5 26.7 %collective-permute-done.9 = bf16[8,640,128]{2,1,0:T(8,128)(2,1)} collective-permute-done((bf16[8,640,128]{2,1,0:T(8,128)(2,1)}, bf16[8,640,128]{2,1,0:T(8,128)(2,1)}, u32[]{:S(2)}, u32[]{:S(2)}) %collective-permute-start.9) | collective-permute-done | bytes 1310752 | tf_op jit(solution)/shard_map/ppermute | solution.py:57
  122.6 7.1 %collective-permute-done.5 = bf16[8,656,128]{2,1,0:T(8,128)(2,1)} collective-permute-done((bf16[8,656,128]{2,1,0:T(8,128)(2,1)}, bf16[8,656,128]{2,1,0:T(8,128)(2,1)}, u32[]{:S(2)}, u32[]{:S(2)}) %collective-permute-start.5) | collective-permute-done | bytes 1343520 | tf_op jit(solution)/shard_map/ppermute | solution.py:57
  141.6 6.3 %collective-permute-done.15 = bf16[128,384]{1,0:T(8,128)(2,1)S(1)} collective-permute-done((bf16[128,384]{1,0:T(8,128)(2,1)S(1)}, bf16[128,384]{1,0:T(8,128)(2,1)S(1)}, u32[]{:S(2)}, u32[]{:S(2)}) %collective-permute-start.15) | collective-permute-done | bytes 98336 | tf_op jit(solution)/shard_map/ppermute | solution.py:57
  149.3 6.4 %collective-permute-done.16 = bf16[1,128,384]{2,1,0:T(8,128)(2,1)S(1)} collective-permute-done((bf16[1,128,384]{2,1,0:T(8,128)(2,1)S(1)}, bf16[1,128,384]{2,1,0:T(8,128)(2,1)S(1)}, u32[]{:S(2)}, u32[]{:S(2)}) %collective-permute-start.16) | collective-permute-done | bytes 98336 | tf_op jit(solution)/shard_map/ppermute | solution.py:57
  158.3 4.3 collective-permute-done.17
  167.1 3.5 collective-permute-done.18
  189.4 3.7 attend.2
  196.4 11.1 %feed.2 = (bf16[128,960]{1,0:T(8,128)(2,1)S(1)}, f32[128,960]{1,0:T(8,128)}, bf16[1024,128]{1,0:T(8,128)(2,1)}, f32[128,2560]{1,0:T(8,128)}, f32[128,2560]{1,0:T(8,128)}, /*index=5*/bf16[2560,128]{1,0:T(8,128)(2,1)}) custom-call(bf16[960,128]{1,0:T(8,128)(2,1)S(1)} %constant_dynamic-update-slice_fusion.10.mixed_ref, bf16[128,960]{1,0:T(8,128)(2,1)S(1)} %bitcast.202, ...), custom_call_target="tpu_custom_call" | custom-call | flops 2200000000 | bytes 22000000 | tf_op jit(solution)/shard_map/feed/pallas_call | solution.py:426
  215.7 9.6 %collective-permute-start.28 = (bf16[128,384]{1,0:T(8,128)(2,1)S(1)}, bf16[128,384]{1,0:T(8,128)(2,1)S(1)}, u32[]{:S(2)}, u32[]{:S(2)}) collective-permute-start(bf16[128,384]{1,0:T(8,128)(2,1)S(1)} %slice_select_fusion.4), channel_id=1, source_target_pairs={{0,2},{1,3},{2,0},{3,1},{4,6},{5,7},{6,4},{7,5},{8,10},{9,11},{10,... | collective-permute-start | bytes 294920 | tf_op jit(solution)/shard_map/ppermute | solution.py:57
  225.3 3.1 collective-permute-done.28
  233.7 3.2 collective-permute-done.26
  237.6 3.0 collective-permute-done.30
  240.7 4.1 collective-permute-done.27
  244.9 3.8 collective-permute-done.31
  252.4 9.7 %collective-permute-done.32 = bf16[8,128,384]{2,1,0:T(8,128)(2,1)S(1)} collective-permute-done((bf16[8,128,384]{2,1,0:T(8,128)(2,1)S(1)}, bf16[8,128,384]{2,1,0:T(8,128)(2,1)S(1)}, u32[]{:S(2)}, u32[]{:S(2)}) %collective-permute-start.32) | collective-permute-done | bytes 786464 | tf_op jit(solution)/shard_map/ppermute | solution.py:57
  262.8 3.7 attend.3
  269.6 9.5 %feed.3 = (bf16[128,960]{1,0:T(8,128)(2,1)S(1)}, f32[128,960]{1,0:T(8,128)S(1)}, bf16[1024,128]{1,0:T(8,128)(2,1)S(1)}, f32[128,2560]{1,0:T(8,128)S(1)}, f32[128...) custom-call(bf16[960,128]{1,0:T(8,128)(2,1)S(1)} %maximum_select_fusion.2.mixed_ref, ...), custom_call_target="tpu_custom_call" | custom-call | flops 2200000000 | bytes 22000000 | tf_op jit(solution)/shard_map/feed/pallas_call | solution.py:426
  280.7 14.6 %feed_back.2 = (bf16[128,2560]{1,0:T(8,128)(2,1)}, bf16[128,2560]{1,0:T(8,128)(2,1)}, f32[128,960]{1,0:T(8,128)S(1)}, bf16[128,1024]{1,0:T(8,128)(2,1)}, f32[1,9...) custom-call(f32[128,960]{1,0:T(8,128)S(1)} %bitcast.200, ...), custom_call_target="tpu_custom_call" | custom-call | flops 2200000000 | bytes 22000000 | tf_op jit(solution)/shard_map/feed_back/pallas_call | solution.py:517
  298.8 6.3 %attend_back.2 = (bf16[4096,384]{1,0:T(8,128)(2,1)S(1)}, f32[576,128]{1,0:T(8,128)S(1)}) custom-call(s32[66]{0:T(128)S(1)} %pad_add_fusion.2.need_ref, bf16[576,128]{1,0:T(8,128)(2,1)S(1)} %copy-done.24, bf16[4096,384]{1,0:T(8,128)(2,1)S(1)} %bitcast.206, f32[4096,128]{1,0:T(8,128)S(1)} %copy-done.12, f32[576,128]{1,0:T(8,128)S(1)} %slice_select_fusion.1.dot_ref, ...), custom_call_target="tpu_custom_call" | custom-call | flops 6000000000 | bytes 10000000 | tf_op jit(solution)/shard_map/attend_back/pallas_call | solution.py:580
  305.5 9.7 %collective-permute-start.37 = (bf16[8,128,384]{2,1,0:T(8,128)(2,1)S(1)}, bf16[8,128,384]{2,1,0:T(8,128)(2,1)S(1)}, u32[]{:S(2)}, u32[]{:S(2)}) collective-permute-start(bf16[8,128,384]{2,1,0:T(8,128)(2,1)S(1)} %bitcast.274), channel_id=1, source_target_pairs={{0,12},{1,13},{2,14},{3,15},{4,8},{5,9},{6,10},{7,11},{8,4},{9,5},... | collective-permute-start | bytes 2359304 | tf_op jit(solution)/shard_map/ppermute | solution.py:57
  315.2 3.5 collective-permute-done.41
  321.7 6.7 %collective-permute-done.37 = bf16[8,128,384]{2,1,0:T(8,128)(2,1)S(1)} collective-permute-done((bf16[8,128,384]{2,1,0:T(8,128)(2,1)S(1)}, bf16[8,128,384]{2,1,0:T(8,128)(2,1)S(1)}, u32[]{:S(2)}, u32[]{:S(2)}) %collective-permute-start.37) | collective-permute-done | bytes 786464 | tf_op jit(solution)/shard_map/ppermute | solution.py:57
  328.9 4.6 collective-permute-start.43
  333.5 4.8 collective-permute-done.38
  338.8 6.7 %collective-permute-done.39 = bf16[2,128,384]{2,1,0:T(8,128)(2,1)S(1)} collective-permute-done((bf16[2,128,384]{2,1,0:T(8,128)(2,1)S(1)}, bf16[2,128,384]{2,1,0:T(8,128)(2,1)S(1)}, u32[]{:S(2)}, u32[]{:S(2)}) %collective-permute-start.39) | collective-permute-done | bytes 196640 | tf_op jit(solution)/shard_map/ppermute | solution.py:57
  345.7 10.1 %collective-permute-start.45 = (bf16[128,384]{1,0:T(8,128)(2,1)S(1)}, bf16[128,384]{1,0:T(8,128)(2,1)S(1)}, u32[]{:S(2)}, u32[]{:S(2)}) collective-permute-start(bf16[128,384]{1,0:T(8,128)(2,1)S(1)} %fusion.35), channel_id=1, source_target_pairs={{0,2},{1,3},{2,0},{3,1},{4,6},{5,7},{6,4},{7,5},{8,10},{9,11},{10,... | collective-permute-start | bytes 294920 | tf_op jit(solution)/shard_map/ppermute | solution.py:57
  367.2 13.8 %feed_back.3 = (bf16[128,2560]{1,0:T(8,128)(2,1)S(1)}, bf16[128,2560]{1,0:T(8,128)(2,1)S(1)}, f32[128,960]{1,0:T(8,128)S(1)}, bf16[128,1024]{1,0:T(8,128)(2,1)S(...) custom-call(f32[128,960]{1,0:T(8,128)S(1)} %convert_select_fusion.c_ref, ...), custom_call_target="tpu_custom_call" | custom-call | flops 2200000000 | bytes 22000000 | tf_op jit(solution)/shard_map/feed_back/pallas_call | solution.py:517
  385.7 6.3 %attend_back.3 = (bf16[4096,384]{1,0:T(8,128)(2,1)S(1)}, f32[576,128]{1,0:T(8,128)S(1)}) custom-call(s32[66]{0:T(128)S(1)} %pad_add_fusion.2.need_ref, bf16[576,128]{1,0:T(8,128)(2,1)S(1)} %copy-done.22, bf16[4096,384]{1,0:T(8,128)(2,1)S(1)} %bitcast.204, f32[4096,128]{1,0:T(8,128)S(1)} %copy-done.12, f32[576,128]{1,0:T(8,128)S(1)} %slice_select_fusion.dot_ref, ...), custom_call_target="tpu_custom_call" | custom-call | flops 6000000000 | bytes 10000000 | tf_op jit(solution)/shard_map/attend_back/pallas_call | solution.py:580
  392.6 7.0 %collective-permute-start.50 = (bf16[8,128,384]{2,1,0:T(8,128)(2,1)S(1)}, bf16[8,128,384]{2,1,0:T(8,128)(2,1)S(1)}, u32[]{:S(2)}, u32[]{:S(2)}) collective-permute-start(bf16[8,128,384]{2,1,0:T(8,128)(2,1)S(1)} %bitcast.275), channel_id=1, source_target_pairs={{0,12},{1,13},{2,14},{3,15},{4,8},{5,9},{6,10},{7,11},{8,4},{9,5},... | collective-permute-start | bytes 2359304 | tf_op jit(solution)/shard_map/ppermute | solution.py:57
  399.7 5.9 collective-permute-done.54
  405.8 4.6 collective-permute-start.55
  412.1 4.1 collective-permute-done.55
  429.0 7.4 %collective-permute-start.58 = (bf16[128,384]{1,0:T(8,128)(2,1)S(1)}, bf16[128,384]{1,0:T(8,128)(2,1)S(1)}, u32[]{:S(2)}, u32[]{:S(2)}) collective-permute-start(bf16[128,384]{1,0:T(8,128)(2,1)S(1)} %fusion.36), channel_id=1, source_target_pairs={{0,2},{1,3},{2,0},{3,1},{4,6},{5,7},{6,4},{7,5},{8,10},{9,11},{10,... | collective-permute-start | bytes 294920 | tf_op jit(solution)/shard_map/ppermute | solution.py:57
  452.2 17.7 %outer.1 = (bf16[2,4,4,432,128]{4,3,2,1,0:T(8,128)(2,1)S(1)}, bf16[2,4,4,432,128]{4,3,2,1,0:T(8,128)(2,1)S(1)}, bf16[2,4,4,416,128]{4,3,2,1,0:T(8,128)(2,1)S(1)}...) custom-call(s32[12]{0:T(128)S(1)} %pad_add_fusion.5.slot_ref, ...), custom_call_target="tpu_custom_call" | custom-call | flops 2600000000 | bytes 24000000 | tf_op jit(solution)/shard_map/outer/pallas_call | solution.py:790
  476.6 34.7 %collective-permute-done.72 = bf16[2,4,4,416,128]{4,3,2,1,0:T(8,128)(2,1)} collective-permute-done((bf16[2,4,4,416,128]{4,3,2,1,0:T(8,128)(2,1)S(1)}, bf16[2,4,4,416,128]{4,3,2,1,0:T(8,128)(2,1)}, u32[]{:S(2)}, u32[]{:S(2)}) %collective-permute-start.72) | collective-permute-done | bytes 3407904 | tf_op jit(solution)/shard_map/ppermute | solution.py:57
  521.3 14.8 %collective-permute-done.73 = bf16[4,4,416,128]{3,2,1,0:T(8,128)(2,1)S(1)} collective-permute-done((bf16[4,4,416,128]{3,2,1,0:T(8,128)(2,1)S(1)}, bf16[4,4,416,128]{3,2,1,0:T(8,128)(2,1)S(1)}, u32[]{:S(2)}, u32[]{:S(2)}) %collective-permute-start.73) | collective-permute-done | bytes 1703968 | tf_op jit(solution)/shard_map/ppermute | solution.py:57
  539.1 5.6 collective-permute-done.61
  554.6 6.0 collective-permute-done.62
  564.7 3.0 collective-permute-start.76
  573.3 3.1 collective-permute-start.64
  582.5 3.7 collective-permute-done.70
  587.1 3.9 collective-permute-done.71
  (450 shorter events, 215.1 us)
Async XLA Ops:
  7.2 189.3 %all-gather.3.cloned.1.call-start = ((), (), s32[]{:S(2)}) async-start(), calls=%async_computation | async-start | bytes 21299200 | tf_op jit(solution)/shard_map/all_gather | solution.py:867
  17.1 9.2 %collective-permute-start = (bf16[1,1296,128]{2,1,0:T(8,128)(2,1)S(1)}, bf16[1,1296,128]{2,1,0:T(8,128)(2,1)S(1)}, u32[]{:S(2)}, u32[]{:S(2)}) collective-permute-start(bf16[1,1296,128]{2,1,0:T(8,128)(2,1)S(1)} %fusion.26), channel_id=1, source_target_pairs={{0,16},{1,17},{2,18},{3,19},{4,20},{5,21},{6,22},{7,23},{8,24},{9,... | collective-permute-start | bytes 995336 | tf_op jit(solution)/shard_map/ppermute | solution.py:57
  26.4 14.5 %collective-permute-start.1 = (bf16[2,1296,128]{2,1,0:T(8,128)(2,1)S(1)}, bf16[2,1296,128]{2,1,0:T(8,128)(2,1)S(1)}, u32[]{:S(2)}, u32[]{:S(2)}) collective-permute-start(bf16[2,1296,128]{2,1,0:T(8,128)(2,1)S(1)} %pad_maximum_fusion.10), channel_id=1, source_target_pairs={{0,48},{1,49},{2,50},{3,51},{4,52},{5,53},{6,54},{7,55},{8,56},{9,... | collective-permute-start | bytes 1990664 | tf_op jit(solution)/shard_map/ppermute | solution.py:57
  41.7 8.1 %collective-permute-start.6 = (bf16[1,640,128]{2,1,0:T(8,128)(2,1)S(1)}, bf16[1,640,128]{2,1,0:T(8,128)(2,1)S(1)}, u32[]{:S(2)}, u32[]{:S(2)}) collective-permute-start(bf16[1,640,128]{2,1,0:T(8,128)(2,1)S(1)} %get-tuple-element.144), channel_id=1, source_target_pairs={{0,4},{1,5},{2,6},{3,7},{4,0},{5,1},{6,2},{7,3},{8,12},{9,13},{10,... | collective-permute-start | bytes 491528 | tf_op jit(solution)/shard_map/ppermute | solution.py:57
  49.9 15.2 %collective-permute-start.7 = (bf16[2,640,128]{2,1,0:T(8,128)(2,1)S(1)}, bf16[2,640,128]{2,1,0:T(8,128)(2,1)S(1)}, u32[]{:S(2)}, u32[]{:S(2)}) collective-permute-start(bf16[2,640,128]{2,1,0:T(8,128)(2,1)S(1)} %pad_maximum_fusion.18), channel_id=1, source_target_pairs={{0,12},{1,13},{2,14},{3,15},{4,8},{5,9},{6,10},{7,11},{8,4},{9,5},... | collective-permute-start | bytes 983048 | tf_op jit(solution)/shard_map/ppermute | solution.py:57
  52.1 15.5 %collective-permute-start.3 = (bf16[2,656,128]{2,1,0:T(8,128)(2,1)S(1)}, bf16[2,656,128]{2,1,0:T(8,128)(2,1)S(1)}, u32[]{:S(2)}, u32[]{:S(2)}) collective-permute-start(bf16[2,656,128]{2,1,0:T(8,128)(2,1)S(1)} %pad_maximum_fusion.17), channel_id=1, source_target_pairs={{0,3},{1,2},{2,1},{3,0},{4,7},{5,6},{6,5},{7,4},{8,11},{9,10},{10,... | collective-permute-start | bytes 1007624 | tf_op jit(solution)/shard_map/ppermute | solution.py:57
  65.1 12.0 %collective-permute-start.8 = (bf16[4,640,128]{2,1,0:T(8,128)(2,1)S(1)}, bf16[4,640,128]{2,1,0:T(8,128)(2,1)S(1)}, u32[]{:S(2)}, u32[]{:S(2)}) collective-permute-start(bf16[4,640,128]{2,1,0:T(8,128)(2,1)S(1)} %pad_maximum_fusion.11), channel_id=1, source_target_pairs={{0,1},{1,0},{2,3},{3,2},{4,5},{5,4},{6,7},{7,6},{8,9},{9,8},{10,11... | collective-permute-start | bytes 1966088 | tf_op jit(solution)/shard_map/ppermute | solution.py:57
  67.7 13.4 %collective-permute-start.4 = (bf16[4,656,128]{2,1,0:T(8,128)(2,1)S(1)}, bf16[4,656,128]{2,1,0:T(8,128)(2,1)S(1)}, u32[]{:S(2)}, u32[]{:S(2)}) collective-permute-start(bf16[4,656,128]{2,1,0:T(8,128)(2,1)S(1)} %pad_maximum_fusion.9), channel_id=1, source_target_pairs={{0,4},{1,5},{2,6},{3,7},{4,0},{5,1},{6,2},{7,3},{8,12},{9,13},{10,... | collective-permute-start | bytes 2015240 | tf_op jit(solution)/shard_map/ppermute | solution.py:57
  78.3 41.9 %collective-permute-start.9 = (bf16[8,640,128]{2,1,0:T(8,128)(2,1)}, bf16[8,640,128]{2,1,0:T(8,128)(2,1)}, u32[]{:S(2)}, u32[]{:S(2)}) collective-permute-start(bf16[8,640,128]{2,1,0:T(8,128)(2,1)} %pad_maximum_fusion.4), channel_id=1, source_target_pairs={{0,3},{1,2},{2,1},{3,0},{4,7},{5,6},{6,5},{7,4},{8,11},{9,10},{10,... | collective-permute-start | bytes 3932168 | tf_op jit(solution)/shard_map/ppermute | solution.py:57
  82.3 47.4 %collective-permute-start.5 = (bf16[8,656,128]{2,1,0:T(8,128)(2,1)}, bf16[8,656,128]{2,1,0:T(8,128)(2,1)}, u32[]{:S(2)}, u32[]{:S(2)}) collective-permute-start(bf16[8,656,128]{2,1,0:T(8,128)(2,1)} %pad_maximum_fusion.2), channel_id=1, source_target_pairs={{0,12},{1,13},{2,14},{3,15},{4,8},{5,9},{6,10},{7,11},{8,4},{9,5},... | collective-permute-start | bytes 4030472 | tf_op jit(solution)/shard_map/ppermute | solution.py:57
  138.8 9.1 %collective-permute-start.15 = (bf16[128,384]{1,0:T(8,128)(2,1)S(1)}, bf16[128,384]{1,0:T(8,128)(2,1)S(1)}, u32[]{:S(2)}, u32[]{:S(2)}) collective-permute-start(bf16[128,384]{1,0:T(8,128)(2,1)S(1)} %slice_select_fusion.5), channel_id=1, source_target_pairs={{0,2},{1,3},{2,0},{3,1},{4,6},{5,7},{6,4},{7,5},{8,10},{9,11},{10,... | collective-permute-start | bytes 294920 | tf_op jit(solution)/shard_map/ppermute | solution.py:57
  138.9 9.0 %collective-permute-start.12 = (bf16[1,128,384]{2,1,0:T(8,128)(2,1)S(1)}, bf16[1,128,384]{2,1,0:T(8,128)(2,1)S(1)}, u32[]{:S(2)}, u32[]{:S(2)}) collective-permute-start(bf16[1,128,384]{2,1,0:T(8,128)(2,1)S(1)} %bitcast.254), channel_id=1, source_target_pairs={{0,16},{1,17},{2,18},{3,19},{4,20},{5,21},{6,22},{7,23},{8,24},{9,... | collective-permute-start | bytes 294920 | tf_op jit(solution)/shard_map/ppermute | solution.py:57
  147.9 10.2 %collective-permute-start.13 = (bf16[2,128,384]{2,1,0:T(8,128)(2,1)S(1)}, bf16[2,128,384]{2,1,0:T(8,128)(2,1)S(1)}, u32[]{:S(2)}, u32[]{:S(2)}) collective-permute-start(bf16[2,128,384]{2,1,0:T(8,128)(2,1)S(1)} %pad_maximum_fusion.20), channel_id=1, source_target_pairs={{0,48},{1,49},{2,50},{3,51},{4,52},{5,53},{6,54},{7,55},{8,56},{9,... | collective-permute-start | bytes 589832 | tf_op jit(solution)/shard_map/ppermute | solution.py:57
  158.2 7.9 %collective-permute-start.14 = (bf16[4,128,384]{2,1,0:T(8,128)(2,1)S(1)}, bf16[4,128,384]{2,1,0:T(8,128)(2,1)S(1)}, u32[]{:S(2)}, u32[]{:S(2)}) collective-permute-start(bf16[4,128,384]{2,1,0:T(8,128)(2,1)S(1)} %pad_maximum_fusion.13), channel_id=1, source_target_pairs={{0,4},{1,5},{2,6},{3,7},{4,0},{5,1},{6,2},{7,3},{8,12},{9,13},{10,... | collective-permute-start | bytes 1179656 | tf_op jit(solution)/shard_map/ppermute | solution.py:57
  171.5 13.5 %collective-permute-start.19 = (bf16[8,128,384]{2,1,0:T(8,128)(2,1)}, bf16[8,128,384]{2,1,0:T(8,128)(2,1)}, u32[]{:S(2)}, u32[]{:S(2)}) collective-permute-start(bf16[8,128,384]{2,1,0:T(8,128)(2,1)} %pad_maximum_fusion.5), channel_id=1, source_target_pairs={{0,12},{1,13},{2,14},{3,15},{4,8},{5,9},{6,10},{7,11},{8,4},{9,5},... | collective-permute-start | bytes 2359304 | tf_op jit(solution)/shard_map/ppermute | solution.py:57
  173.8 13.5 %collective-permute-start.20 = (bf16[8,128,384]{2,1,0:T(8,128)(2,1)}, bf16[8,128,384]{2,1,0:T(8,128)(2,1)}, u32[]{:S(2)}, u32[]{:S(2)}) collective-permute-start(bf16[8,128,384]{2,1,0:T(8,128)(2,1)} %pad_maximum_fusion.6), channel_id=1, source_target_pairs={{0,48},{1,49},{2,50},{3,51},{4,52},{5,53},{6,54},{7,55},{8,56},{9,... | collective-permute-start | bytes 2359304 | tf_op jit(solution)/shard_map/ppermute | solution.py:57
  215.7 12.7 %collective-permute-start.28 = (bf16[128,384]{1,0:T(8,128)(2,1)S(1)}, bf16[128,384]{1,0:T(8,128)(2,1)S(1)}, u32[]{:S(2)}, u32[]{:S(2)}) collective-permute-start(bf16[128,384]{1,0:T(8,128)(2,1)S(1)} %slice_select_fusion.4), channel_id=1, source_target_pairs={{0,2},{1,3},{2,0},{3,1},{4,6},{5,7},{6,4},{7,5},{8,10},{9,11},{10,... | collective-permute-start | bytes 294920 | tf_op jit(solution)/shard_map/ppermute | solution.py:57
  237.0 7.9 %collective-permute-start.27 = (bf16[4,128,384]{2,1,0:T(8,128)(2,1)S(1)}, bf16[4,128,384]{2,1,0:T(8,128)(2,1)S(1)}, u32[]{:S(2)}, u32[]{:S(2)}) collective-permute-start(bf16[4,128,384]{2,1,0:T(8,128)(2,1)S(1)} %pad_maximum_fusion.15), channel_id=1, source_target_pairs={{0,4},{1,5},{2,6},{3,7},{4,0},{5,1},{6,2},{7,3},{8,12},{9,13},{10,... | collective-permute-start | bytes 1179656 | tf_op jit(solution)/shard_map/ppermute | solution.py:57
  240.6 8.1 %collective-permute-start.31 = (bf16[4,128,384]{2,1,0:T(8,128)(2,1)S(1)}, bf16[4,128,384]{2,1,0:T(8,128)(2,1)S(1)}, u32[]{:S(2)}, u32[]{:S(2)}) collective-permute-start(bf16[4,128,384]{2,1,0:T(8,128)(2,1)S(1)} %pad_maximum_fusion.16), channel_id=1, source_target_pairs={{0,16},{1,17},{2,18},{3,19},{4,20},{5,21},{6,22},{7,23},{8,24},{9,... | collective-permute-start | bytes 1179656 | tf_op jit(solution)/shard_map/ppermute | solution.py:57
  248.9 13.3 %collective-permute-start.32 = (bf16[8,128,384]{2,1,0:T(8,128)(2,1)S(1)}, bf16[8,128,384]{2,1,0:T(8,128)(2,1)S(1)}, u32[]{:S(2)}, u32[]{:S(2)}) collective-permute-start(bf16[8,128,384]{2,1,0:T(8,128)(2,1)S(1)} %pad_maximum_fusion.7), channel_id=1, source_target_pairs={{0,12},{1,13},{2,14},{3,15},{4,8},{5,9},{6,10},{7,11},{8,4},{9,5},... | collective-permute-start | bytes 2359304 | tf_op jit(solution)/shard_map/ppermute | solution.py:57
  249.0 13.3 %collective-permute-start.33 = (bf16[8,128,384]{2,1,0:T(8,128)(2,1)S(1)}, bf16[8,128,384]{2,1,0:T(8,128)(2,1)S(1)}, u32[]{:S(2)}, u32[]{:S(2)}) collective-permute-start(bf16[8,128,384]{2,1,0:T(8,128)(2,1)S(1)} %pad_maximum_fusion.8), channel_id=1, source_target_pairs={{0,48},{1,49},{2,50},{3,51},{4,52},{5,53},{6,54},{7,55},{8,56},{9,... | collective-permute-start | bytes 2359304 | tf_op jit(solution)/shard_map/ppermute | solution.py:57
  305.4 13.3 %collective-permute-start.41 = (bf16[8,128,384]{2,1,0:T(8,128)(2,1)S(1)}, bf16[8,128,384]{2,1,0:T(8,128)(2,1)S(1)}, u32[]{:S(2)}, u32[]{:S(2)}) collective-permute-start(bf16[8,128,384]{2,1,0:T(8,128)(2,1)S(1)} %bitcast.276), channel_id=1, source_target_pairs={{0,48},{1,49},{2,50},{3,51},{4,52},{5,53},{6,54},{7,55},{8,56},{9,... | collective-permute-start | bytes 2359304 | tf_op jit(solution)/shard_map/ppermute | solution.py:57
  305.5 22.9 %collective-permute-start.37 = (bf16[8,128,384]{2,1,0:T(8,128)(2,1)S(1)}, bf16[8,128,384]{2,1,0:T(8,128)(2,1)S(1)}, u32[]{:S(2)}, u32[]{:S(2)}) collective-permute-start(bf16[8,128,384]{2,1,0:T(8,128)(2,1)S(1)} %bitcast.274), channel_id=1, source_target_pairs={{0,12},{1,13},{2,14},{3,15},{4,8},{5,9},{6,10},{7,11},{8,4},{9,5},... | collective-permute-start | bytes 2359304 | tf_op jit(solution)/shard_map/ppermute | solution.py:57
  319.0 9.8 %collective-permute-start.42 = (bf16[4,128,384]{2,1,0:T(8,128)(2,1)S(1)}, bf16[4,128,384]{2,1,0:T(8,128)(2,1)S(1)}, u32[]{:S(2)}, u32[]{:S(2)}) collective-permute-start(bf16[4,128,384]{2,1,0:T(8,128)(2,1)S(1)} %slice.576), channel_id=1, source_target_pairs={{0,16},{1,17},{2,18},{3,19},{4,20},{5,21},{6,22},{7,23},{8,24},{9,... | collective-permute-start | bytes 1179656 | tf_op jit(solution)/shard_map/ppermute | solution.py:57
  328.7 9.7 %collective-permute-start.38 = (bf16[4,128,384]{2,1,0:T(8,128)(2,1)S(1)}, bf16[4,128,384]{2,1,0:T(8,128)(2,1)S(1)}, u32[]{:S(2)}, u32[]{:S(2)}) collective-permute-start(bf16[4,128,384]{2,1,0:T(8,128)(2,1)S(1)} %slice.570), channel_id=1, source_target_pairs={{0,4},{1,5},{2,6},{3,7},{4,0},{5,1},{6,2},{7,3},{8,12},{9,13},{10,... | collective-permute-start | bytes 1179656 | tf_op jit(solution)/shard_map/ppermute | solution.py:57
  328.9 9.7 %collective-permute-start.43 = (bf16[2,128,384]{2,1,0:T(8,128)(2,1)S(1)}, bf16[2,128,384]{2,1,0:T(8,128)(2,1)S(1)}, u32[]{:S(2)}, u32[]{:S(2)}) collective-permute-start(bf16[2,128,384]{2,1,0:T(8,128)(2,1)S(1)} %slice.578), channel_id=1, source_target_pairs={{0,12},{1,13},{2,14},{3,15},{4,8},{5,9},{6,10},{7,11},{8,4},{9,5},... | collective-permute-start | bytes 589832 | tf_op jit(solution)/shard_map/ppermute | solution.py:57
  345.5 11.6 %collective-permute-start.40 = (bf16[1,128,384]{2,1,0:T(8,128)(2,1)S(1)}, bf16[1,128,384]{2,1,0:T(8,128)(2,1)S(1)}, u32[]{:S(2)}, u32[]{:S(2)}) collective-permute-start(bf16[1,128,384]{2,1,0:T(8,128)(2,1)S(1)} %slice.574), channel_id=1, source_target_pairs={{0,16},{1,17},{2,18},{3,19},{4,20},{5,21},{6,22},{7,23},{8,24},{9,... | collective-permute-start | bytes 294920 | tf_op jit(solution)/shard_map/ppermute | solution.py:57
  345.7 12.7 %collective-permute-start.45 = (bf16[128,384]{1,0:T(8,128)(2,1)S(1)}, bf16[128,384]{1,0:T(8,128)(2,1)S(1)}, u32[]{:S(2)}, u32[]{:S(2)}) collective-permute-start(bf16[128,384]{1,0:T(8,128)(2,1)S(1)} %fusion.35), channel_id=1, source_target_pairs={{0,2},{1,3},{2,0},{3,1},{4,6},{5,7},{6,4},{7,5},{8,10},{9,11},{10,... | collective-permute-start | bytes 294920 | tf_op jit(solution)/shard_map/ppermute | solution.py:57
  392.3 13.3 %collective-permute-start.54 = (bf16[8,128,384]{2,1,0:T(8,128)(2,1)S(1)}, bf16[8,128,384]{2,1,0:T(8,128)(2,1)S(1)}, u32[]{:S(2)}, u32[]{:S(2)}) collective-permute-start(bf16[8,128,384]{2,1,0:T(8,128)(2,1)S(1)} %bitcast.277), channel_id=1, source_target_pairs={{0,48},{1,49},{2,50},{3,51},{4,52},{5,53},{6,54},{7,55},{8,56},{9,... | collective-permute-start | bytes 2359304 | tf_op jit(solution)/shard_map/ppermute | solution.py:57
  392.6 17.8 %collective-permute-start.50 = (bf16[8,128,384]{2,1,0:T(8,128)(2,1)S(1)}, bf16[8,128,384]{2,1,0:T(8,128)(2,1)S(1)}, u32[]{:S(2)}, u32[]{:S(2)}) collective-permute-start(bf16[8,128,384]{2,1,0:T(8,128)(2,1)S(1)} %bitcast.275), channel_id=1, source_target_pairs={{0,12},{1,13},{2,14},{3,15},{4,8},{5,9},{6,10},{7,11},{8,4},{9,5},... | collective-permute-start | bytes 2359304 | tf_op jit(solution)/shard_map/ppermute | solution.py:57
  405.8 10.4 %collective-permute-start.55 = (bf16[4,128,384]{2,1,0:T(8,128)(2,1)S(1)}, bf16[4,128,384]{2,1,0:T(8,128)(2,1)S(1)}, u32[]{:S(2)}, u32[]{:S(2)}) collective-permute-start(bf16[4,128,384]{2,1,0:T(8,128)(2,1)S(1)} %slice.589), channel_id=1, source_target_pairs={{0,16},{1,17},{2,18},{3,19},{4,20},{5,21},{6,22},{7,23},{8,24},{9,... | collective-permute-start | bytes 1179656 | tf_op jit(solution)/shard_map/ppermute | solution.py:57
  418.7 8.0 %collective-permute-start.52 = (bf16[2,128,384]{2,1,0:T(8,128)(2,1)S(1)}, bf16[2,128,384]{2,1,0:T(8,128)(2,1)S(1)}, u32[]{:S(2)}, u32[]{:S(2)}) collective-permute-start(bf16[2,128,384]{2,1,0:T(8,128)(2,1)S(1)} %slice.585), channel_id=1, source_target_pairs={{0,48},{1,49},{2,50},{3,51},{4,52},{5,53},{6,54},{7,55},{8,56},{9,... | collective-permute-start | bytes 589832 | tf_op jit(solution)/shard_map/ppermute | solution.py:57
  426.8 11.0 %collective-permute-start.53 = (bf16[1,128,384]{2,1,0:T(8,128)(2,1)S(1)}, bf16[1,128,384]{2,1,0:T(8,128)(2,1)S(1)}, u32[]{:S(2)}, u32[]{:S(2)}) collective-permute-start(bf16[1,128,384]{2,1,0:T(8,128)(2,1)S(1)} %slice.587), channel_id=1, source_target_pairs={{0,16},{1,17},{2,18},{3,19},{4,20},{5,21},{6,22},{7,23},{8,24},{9,... | collective-permute-start | bytes 294920 | tf_op jit(solution)/shard_map/ppermute | solution.py:57
  429.0 10.0 %collective-permute-start.58 = (bf16[128,384]{1,0:T(8,128)(2,1)S(1)}, bf16[128,384]{1,0:T(8,128)(2,1)S(1)}, u32[]{:S(2)}, u32[]{:S(2)}) collective-permute-start(bf16[128,384]{1,0:T(8,128)(2,1)S(1)} %fusion.36), channel_id=1, source_target_pairs={{0,2},{1,3},{2,0},{3,1},{4,6},{5,7},{6,4},{7,5},{8,10},{9,11},{10,... | collective-permute-start | bytes 294920 | tf_op jit(solution)/shard_map/ppermute | solution.py:57
  469.8 41.5 %collective-permute-start.72 = (bf16[2,4,4,416,128]{4,3,2,1,0:T(8,128)(2,1)S(1)}, bf16[2,4,4,416,128]{4,3,2,1,0:T(8,128)(2,1)}, u32[]{:S(2)}, u32[]{:S(2)}) collective-permute-start(bf16[2,4,4,416,128]{4,3,2,1,0:T(8,128)(2,1)S(1)} %get-tuple-element.118), channel_id=1, source_target_pairs={{0,3},{1,2},{2,1},{3,0},{4,7},{5,6},{6,5},{7,4},{8,11},{9,10},{10,... | collective-permute-start | bytes 10223624 | tf_op jit(solution)/shard_map/ppermute | solution.py:57
  472.2 44.0 %collective-permute-start.60 = (bf16[2,4,4,432,128]{4,3,2,1,0:T(8,128)(2,1)S(1)}, bf16[2,4,4,432,128]{4,3,2,1,0:T(8,128)(2,1)}, u32[]{:S(2)}, u32[]{:S(2)}) collective-permute-start(bf16[2,4,4,432,128]{4,3,2,1,0:T(8,128)(2,1)S(1)} %get-tuple-element.114), channel_id=1, source_target_pairs={{0,48},{1,49},{2,50},{3,51},{4,52},{5,53},{6,54},{7,55},{8,56},{9,... | collective-permute-start | bytes 10616840 | tf_op jit(solution)/shard_map/ppermute | solution.py:57
  474.7 45.5 %collective-permute-start.66 = (bf16[2,4,4,432,128]{4,3,2,1,0:T(8,128)(2,1)S(1)}, bf16[2,4,4,432,128]{4,3,2,1,0:T(8,128)(2,1)S(1)}, u32[]{:S(2)}, u32[]{:S(2)}) collective-permute-start(bf16[2,4,4,432,128]{4,3,2,1,0:T(8,128)(2,1)S(1)} %get-tuple-element.116), channel_id=1, source_target_pairs={{0,12},{1,13},{2,14},{3,15},{4,8},{5,9},{6,10},{7,11},{8,4},{9,5},... | collective-permute-start | bytes 10616840 | tf_op jit(solution)/shard_map/ppermute | solution.py:57
  514.2 21.9 %collective-permute-start.73 = (bf16[4,4,416,128]{3,2,1,0:T(8,128)(2,1)S(1)}, bf16[4,4,416,128]{3,2,1,0:T(8,128)(2,1)S(1)}, u32[]{:S(2)}, u32[]{:S(2)}) collective-permute-start(bf16[4,4,416,128]{3,2,1,0:T(8,128)(2,1)S(1)} %get-tuple-element.152), channel_id=1, source_target_pairs={{0,1},{1,0},{2,3},{3,2},{4,5},{5,4},{6,7},{7,6},{8,9},{9,8},{10,11... | collective-permute-start | bytes 5111816 | tf_op jit(solution)/shard_map/ppermute | solution.py:57
  519.1 25.5 %collective-permute-start.61 = (bf16[4,4,432,128]{3,2,1,0:T(8,128)(2,1)S(1)}, bf16[4,4,432,128]{3,2,1,0:T(8,128)(2,1)S(1)}, u32[]{:S(2)}, u32[]{:S(2)}) collective-permute-start(bf16[4,4,432,128]{3,2,1,0:T(8,128)(2,1)S(1)} %get-tuple-element.148), channel_id=1, source_target_pairs={{0,16},{1,17},{2,18},{3,19},{4,20},{5,21},{6,22},{7,23},{8,24},{9,... | collective-permute-start | bytes 5308424 | tf_op jit(solution)/shard_map/ppermute | solution.py:57
  521.1 27.4 %collective-permute-start.67 = (bf16[4,4,432,128]{3,2,1,0:T(8,128)(2,1)S(1)}, bf16[4,4,432,128]{3,2,1,0:T(8,128)(2,1)S(1)}, u32[]{:S(2)}, u32[]{:S(2)}) collective-permute-start(bf16[4,4,432,128]{3,2,1,0:T(8,128)(2,1)S(1)} %get-tuple-element.150), channel_id=1, source_target_pairs={{0,4},{1,5},{2,6},{3,7},{4,0},{5,1},{6,2},{7,3},{8,12},{9,13},{10,... | collective-permute-start | bytes 5308424 | tf_op jit(solution)/shard_map/ppermute | solution.py:57
  536.6 14.0 %collective-permute-start.74 = (bf16[2,4,416,128]{3,2,1,0:T(8,128)(2,1)S(1)}, bf16[2,4,416,128]{3,2,1,0:T(8,128)(2,1)S(1)}, u32[]{:S(2)}, u32[]{:S(2)}) collective-permute-start(bf16[2,4,416,128]{3,2,1,0:T(8,128)(2,1)S(1)} %get-tuple-element.158), channel_id=1, source_target_pairs={{0,48},{1,49},{2,50},{3,51},{4,52},{5,53},{6,54},{7,55},{8,56},{9,... | collective-permute-start | bytes 2555912 | tf_op jit(solution)/shard_map/ppermute | solution.py:57
  546.0 14.6 %collective-permute-start.62 = (bf16[2,4,432,128]{3,2,1,0:T(8,128)(2,1)}, bf16[2,4,432,128]{3,2,1,0:T(8,128)(2,1)}, u32[]{:S(2)}, u32[]{:S(2)}) collective-permute-start(bf16[2,4,432,128]{3,2,1,0:T(8,128)(2,1)} %get-tuple-element.154), channel_id=1, source_target_pairs={{0,12},{1,13},{2,14},{3,15},{4,8},{5,9},{6,10},{7,11},{8,4},{9,5},... | collective-permute-start | bytes 2654216 | tf_op jit(solution)/shard_map/ppermute | solution.py:57
  549.9 17.8 %collective-permute-start.68 = (bf16[2,4,432,128]{3,2,1,0:T(8,128)(2,1)}, bf16[2,4,432,128]{3,2,1,0:T(8,128)(2,1)}, u32[]{:S(2)}, u32[]{:S(2)}) collective-permute-start(bf16[2,4,432,128]{3,2,1,0:T(8,128)(2,1)} %get-tuple-element.156), channel_id=1, source_target_pairs={{0,3},{1,2},{2,1},{3,0},{4,7},{5,6},{6,5},{7,4},{8,11},{9,10},{10,... | collective-permute-start | bytes 2654216 | tf_op jit(solution)/shard_map/ppermute | solution.py:57
  550.8 12.8 %collective-permute-start.75 = (bf16[4,416,128]{2,1,0:T(8,128)(2,1)S(1)}, bf16[4,416,128]{2,1,0:T(8,128)(2,1)}, u32[]{:S(2)}, u32[]{:S(2)}) collective-permute-start(bf16[4,416,128]{2,1,0:T(8,128)(2,1)S(1)} %get-tuple-element.172), channel_id=1, source_target_pairs={{0,16},{1,17},{2,18},{3,19},{4,20},{5,21},{6,22},{7,23},{8,24},{9,... | collective-permute-start | bytes 1277960 | tf_op jit(solution)/shard_map/ppermute | solution.py:57
  562.0 11.2 %collective-permute-start.63 = (bf16[4,432,128]{2,1,0:T(8,128)(2,1)S(1)}, bf16[4,432,128]{2,1,0:T(8,128)(2,1)S(1)}, u32[]{:S(2)}, u32[]{:S(2)}) collective-permute-start(bf16[4,432,128]{2,1,0:T(8,128)(2,1)S(1)} %get-tuple-element.168), channel_id=1, source_target_pairs={{0,4},{1,5},{2,6},{3,7},{4,0},{5,1},{6,2},{7,3},{8,12},{9,13},{10,... | collective-permute-start | bytes 1327112 | tf_op jit(solution)/shard_map/ppermute | solution.py:57
  564.7 8.3 %collective-permute-start.76 = (bf16[2,416,128]{2,1,0:T(8,128)(2,1)S(1)}, bf16[2,416,128]{2,1,0:T(8,128)(2,1)S(1)}, u32[]{:S(2)}, u32[]{:S(2)}) collective-permute-start(bf16[2,416,128]{2,1,0:T(8,128)(2,1)S(1)} %get-tuple-element.179), channel_id=1, source_target_pairs={{0,12},{1,13},{2,14},{3,15},{4,8},{5,9},{6,10},{7,11},{8,4},{9,5},... | collective-permute-start | bytes 638984 | tf_op jit(solution)/shard_map/ppermute | solution.py:57
  569.1 9.7 %collective-permute-start.69 = (bf16[4,432,128]{2,1,0:T(8,128)(2,1)S(1)}, bf16[4,432,128]{2,1,0:T(8,128)(2,1)S(1)}, u32[]{:S(2)}, u32[]{:S(2)}) collective-permute-start(bf16[4,432,128]{2,1,0:T(8,128)(2,1)S(1)} %get-tuple-element.170), channel_id=1, source_target_pairs={{0,1},{1,0},{2,3},{3,2},{4,5},{5,4},{6,7},{7,6},{8,9},{9,8},{10,11... | collective-permute-start | bytes 1327112 | tf_op jit(solution)/shard_map/ppermute | solution.py:57
  573.3 8.3 %collective-permute-start.64 = (bf16[2,432,128]{2,1,0:T(8,128)(2,1)S(1)}, bf16[2,432,128]{2,1,0:T(8,128)(2,1)S(1)}, u32[]{:S(2)}, u32[]{:S(2)}) collective-permute-start(bf16[2,432,128]{2,1,0:T(8,128)(2,1)S(1)} %get-tuple-element.175), channel_id=1, source_target_pairs={{0,3},{1,2},{2,1},{3,0},{4,7},{5,6},{6,5},{7,4},{8,11},{9,10},{10,... | collective-permute-start | bytes 663560 | tf_op jit(solution)/shard_map/ppermute | solution.py:57
  (96 other events, 762.4 us)
Sparse Core Ops, SparseCore 0:
  16.2 143.4 all-gather.2
